TPU v7x, 32 devices: a whole 2x2x4 slice. The times are simulated.
32 devices in a mesh: grp: 2 (over y), garm: 4 (over z), body: 2 (over x), frame: 2 (over core).
Axes of the slice: x: 2, y: 2, z: 4, core: 2. Of those that a mesh axis runs over, the one named last changes fastest.
Arguments:
- garment: float32 [4, 3, 32768], P(('grp', 'frame'), None, ('garm', 'body')), parts along dimension 0, may hold values from -6 to 6
- cotangent: float32 [4, 32768], P(('grp', 'frame'), ('garm', 'body')), parts along dimension 0, may hold values from -6 to 6
- body_points: float32 [4, 3, 16384], P(('grp', 'frame'), None, ('garm', 'body')), parts along dimension 0, may hold values from -6 to 6
- stiffness: float32 [32768], P(('grp', 'garm', 'body')), parts along dimension 0, may hold values from 0.2 to 2
- pair_garment: int32 [4, 8, 8, 4], P(('grp', 'frame'), ('garm', 'body')), parts along dimension 0, may hold values from 0 to 31
- pair_body: int32 [4, 8, 8, 4], P(('grp', 'frame'), ('garm', 'body')), parts along dimension 0, may hold values from 0 to 15
- pair_count: int32 [4, 8, 8], P(('grp', 'frame'), ('garm', 'body')), parts along dimension 0, may hold values from 0 to 4, as said below
Outputs:
- garment_grad: float32 [4, 3, 32768], P(('grp', 'frame'), None, ('garm', 'body')), parts along dimension 0
- body_grad: float32 [4, 3, 16384], P(('grp', 'frame'), None, ('garm', 'body')), parts along dimension 0
- stiffness_grad: float32 [32768], P(('grp', 'garm', 'body')), parts along dimension 0
There are 2 independent parts, one for each index of `grp`. A program takes and returns all parts, laid end to end along the dimension named above; each array names one. Nothing has to cross between parts.
Inputs may be any that keep to these rules, and one draw needn't show every extreme that they name: pair_count gives the live slots; in every frame one receiving owner gets 4 live slots from every sending owner. `pair_garment`: slots at or past the count are unused and hold arbitrary block numbers. `pair_body`: slots at or past the count are unused and hold arbitrary block numbers.
All inputs are finite; a program needn't handle non-finite values.
Results may differ from a plain program's by a relative error of at most 0.00016.
Values sent between devices are 32-bit elements; how exact they have to be, the bound alone decides.
No kernel may reach another device: no remote copies, remote signals or barrier semaphores. Data moves between devices by JAX's collectives and lax.ppermute only.
A program may use at most 64 MiB of HBM per device.

v0:
```python
import math

import jax
import jax.numpy as jnp
from jax import lax
from jax.sharding import PartitionSpec as P

BLOCK = 128
CAP = 4
GB_DEV = 32
BB_DEV = 16


amplitude = 0.05
width_sq = 4.0


def pair_terms(garm_pos, cot_vals, body_pos, stiff_vals):
    distance = jnp.zeros((garm_pos.shape[0], garm_pos.shape[2], body_pos.shape[2]), jnp.float32)
    for coord in range(3):
        delta = garm_pos[:, coord, :, None] - body_pos[:, coord, None, :]
        distance = distance + delta * delta
    kernel = jnp.exp(-distance / width_sq)
    coupled = amplitude * cot_vals[:, :, None] * stiff_vals[:, None, :] * kernel
    row_sums = jnp.sum(coupled, axis=2)
    col_sums = jnp.sum(coupled, axis=1)
    pulled_body = jnp.einsum("nij,naj->nai", coupled, body_pos, precision=lax.Precision.HIGHEST)
    pulled_garm = jnp.einsum("nij,nai->naj", coupled, garm_pos, precision=lax.Precision.HIGHEST)
    factor = -2.0 / width_sq
    garm_grad = factor * (garm_pos * row_sums[:, None, :] - pulled_body)
    body_part = factor * (body_pos * col_sums[:, None, :] - pulled_garm)
    stiff_part = amplitude * jnp.einsum(
        "ni,nij->nj", cot_vals, kernel, precision=lax.Precision.HIGHEST
    )
    return (garm_grad, body_part, stiff_part)


def take_rows(lookup, indices):
    return lookup[indices]


def per_device(garment, cotangent, body_points, stiffness, pair_garment, pair_body, pair_count):
    owners = lax.axis_size(("garm", "body"))
    frames = garment.shape[0]
    garm_table = garment.reshape(frames, 3, GB_DEV, BLOCK).transpose(0, 2, 1, 3)
    cot_table = cotangent.reshape(frames, GB_DEV, 1, BLOCK)
    packed = jnp.concatenate([garm_table, cot_table], axis=2)
    garm_sel = pair_garment[:, 0]
    targets = pair_body[:, 0]
    is_live = (
        jnp.arange(CAP, dtype=jnp.int32)[None, None, :] < pair_count[:, 0][:, :, None]
    ).astype(jnp.float32)
    chosen = jax.vmap(take_rows)(packed, garm_sel)
    outgoing = jnp.concatenate(
        [chosen[:, :, :, :3], chosen[:, :, :, 3:] * is_live[:, :, :, None, None]], axis=3
    )
    body_table = body_points.reshape(frames, 3, BB_DEV, BLOCK).transpose(0, 2, 1, 3)
    stiff_table = stiffness.reshape(BB_DEV, BLOCK)
    incoming = lax.all_to_all(outgoing, ("garm", "body"), split_axis=1, concat_axis=1, tiled=True)
    indices = lax.all_to_all(targets, ("garm", "body"), split_axis=1, concat_axis=1, tiled=True)
    slot_count = incoming.shape[2]
    partner = jax.vmap(take_rows)(body_table, indices)
    stiff_vals = stiff_table[indices]
    total_pairs = frames * owners * slot_count
    per_turn = math.gcd(total_pairs, 64)
    turns = total_pairs // per_turn
    garm_pos = incoming[:, :, :, :3].reshape(turns, per_turn, 3, BLOCK)
    cot_vals = incoming[:, :, :, 3].reshape(turns, per_turn, BLOCK)
    body_pos = partner.reshape(turns, per_turn, 3, BLOCK)
    stiff_flat = stiff_vals.reshape(turns, per_turn, BLOCK)

    def one_turn(inputs):
        return pair_terms(inputs[0], inputs[1], inputs[2], inputs[3])

    garm_grad, body_part, stiff_part = lax.map(one_turn, (garm_pos, cot_vals, body_pos, stiff_flat))
    garm_grad = garm_grad.reshape(frames, owners, slot_count, 3, BLOCK)
    merged = jnp.concatenate(
        [
            body_part.reshape(frames, owners, slot_count, 3, BLOCK),
            stiff_part.reshape(frames, owners, slot_count, 1, BLOCK),
        ],
        axis=3,
    )
    onehot = (indices[..., None] == jnp.arange(BB_DEV, dtype=jnp.int32)).astype(jnp.float32)
    partial_value = jnp.einsum("fosk,fosan->faskn", onehot, merged, precision=lax.Precision.HIGHEST)
    garm_grad, partial_value = (
        garm_grad,
        partial_value.reshape(frames, 4, slot_count, BB_DEV * BLOCK),
    )
    returned_here = lax.all_to_all(
        garm_grad, ("garm", "body"), split_axis=1, concat_axis=1, tiled=True
    )
    returned, partial_value = (returned_here, partial_value)
    garm_onehot = (garm_sel[..., None] == jnp.arange(GB_DEV, dtype=jnp.int32)).astype(jnp.float32)
    garm_sum = jnp.einsum(
        "fosk,fosan->fakn", garm_onehot, returned, precision=lax.Precision.HIGHEST
    )
    garment_grad = garm_sum.reshape(frames, 3, GB_DEV * BLOCK)
    totals = jnp.sum(partial_value, axis=2)
    body_grad = totals[:, :3]
    stiff_local = jnp.sum(totals[:, 3], axis=0)
    stiffness_grad = lax.psum(stiff_local, "frame")
    return (garment_grad, body_grad, stiffness_grad)


def solution(mesh):
    in_specs = (
        P(("grp", "frame"), None, ("garm", "body")),
        P(("grp", "frame"), ("garm", "body")),
        P(("grp", "frame"), None, ("garm", "body")),
        P(("grp", "garm", "body")),
        P(("grp", "frame"), ("garm", "body"), None, None),
        P(("grp", "frame"), ("garm", "body"), None, None),
        P(("grp", "frame"), ("garm", "body"), None),
    )
    out_specs = (
        P(("grp", "frame"), None, ("garm", "body")),
        P(("grp", "frame"), None, ("garm", "body")),
        P(("grp", "garm", "body")),
    )
    return jax.shard_map(
        per_device, mesh=mesh, in_specs=in_specs, out_specs=out_specs, check_vma=False
    )
```

profile of v0, /device:TPU:0, one launch (start us, length us, event | category | flops | bytes accessed | tf_op | source)
XLA Modules:
  0.0 54.5 jit_solution(11758936058117778686)
XLA Ops:
  0.7 1.4 %copy.38 = s32[1,8,4]{2,0,1:T(1,128)} copy(s32[1,8,4]{1,2,0:T(4,128)} %bitcast.123) | data formatting | bytes 256 | tf_op jit(solution)/shard_map/squeeze | solution.py:49
  2.0 7.3 %all-to-all-start.1 = ((s32[1,8,4]{2,0,1:T(1,128)}), s32[1,8,4]{2,0,1:T(1,128)S(1)}, u32[]{:S(2)}, u32[]{:S(2)}) async-start(s32[1,8,4]{2,0,1:T(1,128)} %copy.38), calls=%async_computation.1 | async-start | bytes 8192 | tf_op jit(solution)/shard_map/all_to_all | solution.py:60
  9.3 0.8 %copy.58 = f32[1,3,32,128]{3,1,2,0:T(4,128)S(1)} copy(f32[1,3,32,128]{3,2,0,1:T(8,128)} %bitcast.93) | data formatting | bytes 98304 | tf_op jit(solution)/shard_map/reshape | solution.py:45
  10.5 0.6 %gather_fusion.1 = f32[32,4,128]{2,1,0:T(4,128)S(1)} fusion(f32[1,32,4,128]{3,2,1,0:T(4,128)S(1)} %pad_maximum_fusion, s32[32]{0:T(128)S(1)} %reshape.175), kind=kCustom, calls=%fused_computation.1 | custom fusion | bytes 131328 | tf_op jit(solution)/shard_map/vmap()/gather | solution.py:39
  11.1 0.1 slice_multiply_fusion
  11.2 0.7 %pad_maximum_fusion.1 = f32[1,8,4,4,128]{4,3,2,0,1:T(4,128)} fusion(f32[1,8,4,1,128]{4,3,2,0,1:T(1,128)S(1)} %slice_multiply_fusion, f32[1,8,4,3,128]{4,3,2,0,1:T(4,128)S(1)} %bitcast.80), kind=kLoop, calls=%fused_computation.20 | loop fusion | flops 16384 | bytes 131072 | tf_op jit(solution)/shard_map/concatenate | solution.py:54
  11.9 3.7 %all-to-all-done.1 = s32[1,8,4]{2,0,1:T(1,128)S(1)} async-done(((s32[1,8,4]{2,0,1:T(1,128)}), s32[1,8,4]{2,0,1:T(1,128)S(1)}, u32[]{:S(2)}, u32[]{:S(2)}) %all-to-all-start.1) | async-done | bytes 160 | tf_op jit(solution)/shard_map/all_to_all | solution.py:60
  15.7 3.3 %all-to-all-start = ((f32[1,8,4,4,128]{4,3,2,0,1:T(4,128)}), f32[1,8,4,4,128]{4,3,2,0,1:T(4,128)S(1)}, u32[]{:S(2)}, u32[]{:S(2)}) async-start(f32[1,8,4,4,128]{4,3,2,0,1:T(4,128)} %pad_maximum_fusion.1), calls=%async_computation | async-start | bytes 131072 | tf_op jit(solution)/shard_map/all_to_all | solution.py:59
  19.0 0.5 broadcast.147
  19.5 0.7 %fusion.35 = (s32[8,4]{1,0:T(8,128)S(1)}, s32[1,8,4]{2,0,1:T(1,128)S(1)}) fusion(s32[]{:T(128)} %broadcast.147, s32[1,8,4]{2,0,1:T(1,128)S(1)} %all-to-all-done.1), kind=kLoop, calls=%fused_computation.60 | loop fusion | flops 96 | bytes 388 | tf_op jit(solution)/shard_map/vmap()/select_n | solution.py:39
  20.6 0.6 %gather_fusion.2 = f32[32,3,128]{2,1,0:T(4,128)S(1)} fusion(f32[1,16,3,128]{3,2,1,0:T(4,128)S(1)} %bitcast.81, s32[32]{0:T(128)S(1)} %reshape.183), kind=kCustom, calls=%fused_computation.2 | custom fusion | bytes 98560 | tf_op jit(solution)/shard_map/vmap()/gather | solution.py:39
  21.2 0.6 %gather_fusion = f32[32,128]{1,0:T(8,128)S(1)} fusion(f32[16,128]{1,0:T(8,128)S(1)} %bitcast.78, s32[1024]{0:T(1024)S(1)} %pad_clamp_fusion), kind=kCustom, calls=%fused_computation | custom fusion | bytes 32896 | tf_op jit(solution)/shard_map/gather | solution.py:63
  21.9 4.0 %all-to-all-done = f32[1,8,4,4,128]{4,3,2,0,1:T(4,128)S(1)} async-done(((f32[1,8,4,4,128]{4,3,2,0,1:T(4,128)}), f32[1,8,4,4,128]{4,3,2,0,1:T(4,128)S(1)}, u32[]{:S(2)}, u32[]{:S(2)}) %all-to-all-start) | async-done | bytes 65568 | tf_op jit(solution)/shard_map/all_to_all | solution.py:59
  25.9 3.2 %fusion.10 = (f32[32,128]{1,0:T(8,128)S(1)}, f32[32,128]{1,0:T(8,128)S(1)}) fusion(f32[32,128]{1,0:T(8,128)S(1)} %bitcast.102, f32[32,128]{1,0:T(8,128)S(1)} %bitcast.114, f32[32,128]{1,0:T(8,128)S(1)} %bitcast.106, f32[32,128]{1,0:T(8,128)S(1)} %bitcast.118, f32[32,128]{1,0:T(8,128)S(1)} %bitcast.98, f32[32,128]{1,0:T(8,128)S(1)} %bitcast.110, ...), kind=kLoop, calls=%fused_computation.17 | loop fusion | flops 7331840 | bytes 163840 | tf_op jit(solution)/shard_map/while/body/eval_jaxpr/reduce_sum | solution.py:26
  29.1 4.3 %fusion.1 = f32[32,3,128]{2,1,0:T(4,128)S(1)} fusion(f32[32,3,128]{2,1,0:T(4,128)S(1)} %bitcast.83, f32[32,128]{1,0:T(8,128)S(1)} %gather_fusion, f32[32,128]{1,0:T(8,128)S(1)} %bitcast.103, f32[32,128]{1,0:T(8,128)S(1)} %bitcast.115, f32[32,128]{1,0:T(8,128)S(1)} %bitcast.107, f32[32,128]{1,0:T(8,128)S(1)} %bitcast.119, f32[32,128]{1,0:T(8,128)S(1)} %bitcast.99, ...), kind=kOutput, calls=%fused_computation.7 | convolution fusion | flops 25202688 | bytes 294912 | tf_op jit(solution)/shard_map/while/body/eval_jaxpr/nij,nai->naj/dot_general | solution.py:28
  33.4 3.8 %fusion = f32[32,1,128]{2,1,0:T(1,128)S(1)} fusion(f32[32,128,1]{1,2,0:T(1,128)S(1)} %bitcast.91, f32[32,128]{1,0:T(8,128)S(1)} %bitcast.104, f32[32,128]{1,0:T(8,128)S(1)} %bitcast.116, f32[32,128]{1,0:T(8,128)S(1)} %bitcast.108, f32[32,128]{1,0:T(8,128)S(1)} %bitcast.120, f32[32,128]{1,0:T(8,128)S(1)} %bitcast.100, f32[32,128]{1,0:T(8,128)S(1)} %bitcast.112), kind=kOutput, calls=%fused_computation.5 | convolution fusion | flops 11534336 | bytes 131072 | tf_op jit(solution)/shard_map/while/body/eval_jaxpr/ni,nij->nj/dot_general | solution.py:32
  37.2 5.6 %fusion.2 = f32[32,3,128]{2,1,0:T(4,128)S(1)} fusion(f32[32,3,128]{2,1,0:T(4,128)S(1)} %gather_fusion.2, f32[32,128]{1,0:T(8,128)S(1)} %gather_fusion, f32[32,128]{1,0:T(8,128)S(1)} %bitcast.105, f32[32,128]{1,0:T(8,128)S(1)} %bitcast.117, f32[32,128]{1,0:T(8,128)S(1)} %bitcast.109, f32[32,128]{1,0:T(8,128)S(1)} %bitcast.121, f32[32,128]{1,0:T(8,128)S(1)} %bitcast.101, ...), kind=kOutput, calls=%fused_computation.9 | convolution fusion | flops 25202688 | bytes 294912 | tf_op jit(solution)/shard_map/while/body/eval_jaxpr/nij,naj->nai/dot_general | solution.py:27
  42.8 0.7 %copy.42 = f32[1,8,4,3,128]{4,2,3,0,1:T(4,128)} copy(f32[1,8,4,3,128]{4,3,2,1,0:T(4,128)S(1)} %bitcast.88) | data formatting | bytes 98304 | tf_op jit(solution)/shard_map/reshape | solution.py:76
  43.5 3.3 %all-to-all-start.2 = ((f32[1,8,4,3,128]{4,2,3,0,1:T(4,128)}), f32[1,8,4,3,128]{4,2,3,0,1:T(4,128)S(1)}, u32[]{:S(2)}, u32[]{:S(2)}) async-start(f32[1,8,4,3,128]{4,2,3,0,1:T(4,128)} %copy.42), calls=%async_computation.2 | async-start | bytes 98304 | tf_op jit(solution)/shard_map/all_to_all | solution.py:90
  46.8 0.3 fusion.12
  47.1 0.6 %slice.74 = f32[1,3,2048]{2,0,1:T(1,128)} slice(f32[1,4,2048]{2,0,1:T(1,128)S(1)} %bitcast.87), slice={[0:1], [0:3], [0:2048]} | slice | bytes 49152 | tf_op jit(solution)/shard_map/slice | solution.py:100
  47.8 3.0 %psum.7 = f32[2048]{0:T(1024)} all-reduce(f32[2048]{0:T(1024)S(1)} %bitcast.94), channel_id=1, replica_groups=mesh['grp'=2,'garm'=4,'body'=2,'frame'=2] {'frame'}, use_global_device_ids=true, to_apply=%region_2.3 | all-reduce | flops 2048 | bytes 16384 | tf_op jit(solution)/shard_map/psum | solution.py:102
  50.8 2.8 %all-to-all-done.2 = f32[1,8,4,3,128]{4,2,3,0,1:T(4,128)S(1)} async-done(((f32[1,8,4,3,128]{4,2,3,0,1:T(4,128)}), f32[1,8,4,3,128]{4,2,3,0,1:T(4,128)S(1)}, u32[]{:S(2)}, u32[]{:S(2)}) %all-to-all-start.2) | async-done | bytes 49184 | tf_op jit(solution)/shard_map/all_to_all | solution.py:90
  53.6 0.9 %fusion.15 = f32[3,128,32,1]{1,2,3,0:T(8,128)} fusion(f32[1,8,4,3,128]{4,2,3,0,1:T(4,128)S(1)} %all-to-all-done.2, s32[8,4]{0,1:T(4,128)S(1)} %bitcast.125), kind=kOutput, calls=%fused_computation.26 | convolution fusion | flops 4719616 | bytes 98432 | tf_op jit(solution)/shard_map/fosk,fosan->fakn/dot_general | solution.py:95
  (35 shorter events, 1.0 us)
Async XLA Ops:
  0.6 20.5 %copy-start = (f32[2048]{0:T(1024)S(1)}, f32[2048]{0:T(1024)}, u32[]{:S(2)}) copy-start(f32[2048]{0:T(1024)} %param.10) | copy-start | bytes 24580
  0.6 9.5 %copy-start.3 = (s32[1,1,8,4]{2,3,1,0:T(4,128)S(1)}, s32[1,1,8,4]{2,3,1,0:T(4,128)}, u32[]{:S(2)}) copy-start(s32[1,1,8,4]{2,3,1,0:T(4,128)} %param.11) | copy-start | bytes 388
  2.0 13.6 %all-to-all-start.1 = ((s32[1,8,4]{2,0,1:T(1,128)}), s32[1,8,4]{2,0,1:T(1,128)S(1)}, u32[]{:S(2)}, u32[]{:S(2)}) async-start(s32[1,8,4]{2,0,1:T(1,128)} %copy.38), calls=%async_computation.1 | async-start | bytes 8192 | tf_op jit(solution)/shard_map/all_to_all | solution.py:60
  9.3 1.1 %copy-start.4 = (s32[1,1,8]{2,1,0:T(1,128)S(1)}, s32[1,1,8]{2,1,0:T(1,128)}, u32[]{:S(2)}) copy-start(s32[1,1,8]{2,1,0:T(1,128)} %param.13) | copy-start | bytes 100
  9.3 1.1 %copy-start.2 = (f32[1,4096]{1,0:T(1,128)S(1)}, f32[1,4096]{1,0:T(1,128)}, u32[]{:S(2)}) copy-start(f32[1,4096]{1,0:T(1,128)} %param.8) | copy-start | bytes 49156
  11.2 0.7 %copy-start.1 = (f32[1,3,2048]{2,0,1:T(1,128)S(1)}, f32[1,3,2048]{2,0,1:T(1,128)}, u32[]{:S(2)}) copy-start(f32[1,3,2048]{2,0,1:T(1,128)} %param.9) | copy-start | bytes 73732
  15.7 10.2 %all-to-all-start = ((f32[1,8,4,4,128]{4,3,2,0,1:T(4,128)}), f32[1,8,4,4,128]{4,3,2,0,1:T(4,128)S(1)}, u32[]{:S(2)}, u32[]{:S(2)}) async-start(f32[1,8,4,4,128]{4,3,2,0,1:T(4,128)} %pad_maximum_fusion.1), calls=%async_computation | async-start | bytes 131072 | tf_op jit(solution)/shard_map/all_to_all | solution.py:59
  43.5 10.1 %all-to-all-start.2 = ((f32[1,8,4,3,128]{4,2,3,0,1:T(4,128)}), f32[1,8,4,3,128]{4,2,3,0,1:T(4,128)S(1)}, u32[]{:S(2)}, u32[]{:S(2)}) async-start(f32[1,8,4,3,128]{4,2,3,0,1:T(4,128)} %copy.42), calls=%async_computation.2 | async-start | bytes 98304 | tf_op jit(solution)/shard_map/all_to_all | solution.py:90
where the time goes:
time: 55 us; the launch traced here: 54.5 us
  matrix products  14.8 us (27%)
  starting transfers between devices  13.9 us (25%)
  waiting for transfers between devices  10.5 us (19%)
  local copies, waits for them, and re-layouts  6.65 us (12%)
  other arithmetic  4.72 us (9%)
  blocking collectives  3.05 us (6%)
  between operations  0.83 us (2%)
    all_to_all x1, starting transfers between devices, per_device(): lax.all_to_all(targets, ('garm', 'body'), split_axis=1, concat_axis=1, ti...  7.25 us
    dot_general x1, matrix products, pair_terms(): jnp.einsum('nij,naj->nai', coupled, body_pos, precision=lax.Precision.HIG...  5.62 us
    dot_general x1, matrix products, pair_terms(): jnp.einsum('nij,nai->naj', coupled, garm_pos, precision=lax.Precision.HIG...  4.29 us
    all_to_all x1, waiting for transfers between devices, per_device(): lax.all_to_all(outgoing, ('garm', 'body'), split_axis=1, concat_axis=1, t...  3.97 us
    dot_general x1, matrix products, pair_terms(): jnp.einsum('ni,nij->nj', cot_vals, kernel, precision=lax.Precision.HIGHEST)  3.76 us
    all_to_all x1, waiting for transfers between devices, per_device(): lax.all_to_all(targets, ('garm', 'body'), split_axis=1, concat_axis=1, ti...  3.71 us
    all_to_all x1, starting transfers between devices, per_device(): lax.all_to_all(outgoing, ('garm', 'body'), split_axis=1, concat_axis=1, t...  3.35 us
    all_to_all x1, starting transfers between devices, per_device(): lax.all_to_all(garm_grad, ('garm', 'body'), split_axis=1, concat_axis=1,...  3.35 us
  transfers between devices with their start and end apart: 3, of which 3 were waited for; matrix products, arithmetic and copies ran while one was open for 11% of the time, Pallas kernels for 0%

commit v1 on v0

v1 whole, which is shorter than its diff:
```python
import math

import jax
import jax.numpy as jnp
from jax import lax
from jax.experimental import pallas as pl
from jax.experimental.pallas import tpu as pltpu
from jax.sharding import PartitionSpec as P

BLOCK = 128
SUB = 8

amplitude = 0.05
width_sq = 4.0

SCALE = math.sqrt(math.log2(math.e) / width_sq)
FACTOR = -2.0 / width_sq * amplitude

f32 = jnp.float32
bf16 = jnp.bfloat16


def pieces(value, count):
    out = []
    for _ in range(count - 1):
        top = value.astype(bf16).astype(f32)
        out.append(top)
        value = value - top
    out.append(value)
    return out


def features(left, right):
    lpos = [left[c] * SCALE for c in range(3)]
    rpos = [right[c] * SCALE for c in range(3)]
    lnorm = -(lpos[0] * lpos[0] + lpos[1] * lpos[1] + lpos[2] * lpos[2])
    rnorm = -(rpos[0] * rpos[0] + rpos[1] * rpos[1] + rpos[2] * rpos[2])
    one = jnp.ones_like(lnorm)
    lrows, rrows = [], []
    for c in range(3):
        l1, l2, l3 = pieces(lpos[c] * 2.0, 3)
        r1, r2, r3 = pieces(rpos[c], 3)
        lrows += [l1, l1, l2, l2, l1, l3]
        rrows += [r1, r2, r1, r2, r3, r1]
    lrows += pieces(lnorm, 3) + [one] * 3
    rrows += [one] * 3 + pieces(rnorm, 3)
    return (
        jnp.concatenate(lrows, axis=0).astype(bf16),
        jnp.concatenate(rrows, axis=0).astype(bf16),
    )


def pull(left, right):
    lfeat, rfeat = features(left, right)
    depth = lfeat.shape[0]
    weight = left[3]
    coeff = jnp.concatenate([weight * left[c] for c in range(3)] + [weight], axis=0)
    chi, clo = pieces(coeff, 2)
    chi, clo = chi.astype(bf16), clo.astype(bf16)
    lhs = jnp.concatenate(
        [
            jnp.concatenate([chi, chi], axis=1),
            jnp.concatenate([clo, jnp.zeros_like(clo)], axis=1),
        ],
        axis=0,
    )
    lfeat_t = lfeat.T
    row = lax.broadcasted_iota(jnp.int32, (depth, BLOCK), 0) % SUB
    sub = lax.broadcasted_iota(jnp.int32, (4 * SUB, BLOCK), 0) % SUB
    total = jnp.zeros((4 * SUB, BLOCK), f32)
    for pair in range(0, SUB, 2):
        rhs = jnp.concatenate(
            [rfeat * (row == pair + k).astype(f32).astype(bf16) for k in range(2)], axis=1
        )
        exponent = jnp.dot(lfeat_t, rhs, preferred_element_type=f32)
        kernel = jnp.exp2(exponent)
        khi = kernel.astype(bf16)
        klo = (kernel - khi.astype(f32)).astype(bf16)
        sums = jnp.dot(lhs, jnp.concatenate([khi, klo], axis=0), preferred_element_type=f32)
        sums = sums[: 4 * SUB] + sums[4 * SUB :]
        for k in range(2):
            total = jnp.where(sub == pair + k, sums[:, k * BLOCK : (k + 1) * BLOCK], total)
    return [total[c * SUB : (c + 1) * SUB] for c in range(4)]


def run_batches(left_ref, right_ref, grad_ref):
    batches = left_ref.shape[1] // SUB

    def step(k, carry):
        rows = pl.ds(pl.multiple_of(k * SUB, SUB), SUB)
        left = [left_ref[c, rows, :] for c in range(4)]
        right = [right_ref[c, rows, :] for c in range(4)]
        total = pull(left, right)
        for c in range(3):
            grad_ref[rows, c * BLOCK : (c + 1) * BLOCK] = (
                FACTOR * right[3] * (right[c] * total[3] - total[c])
            )
        grad_ref[rows, 3 * BLOCK :] = amplitude * total[3]
        return carry

    if batches <= 4:
        for k in range(batches):
            step(k, 0)
    else:
        lax.fori_loop(0, batches, step, 0)


def scatter(index, grad_ref, blocks):
    lane = lax.broadcasted_iota(jnp.int32, index.shape, 1).astype(f32)
    onehot_t = (index == lane).astype(f32).T[:blocks].astype(bf16)
    parts = [
        jnp.dot(onehot_t, part.astype(bf16), preferred_element_type=f32)
        for part in pieces(grad_ref[...], 3)
    ]
    return parts[0] + parts[1] + parts[2]


def pack_kernel(pg_ref, pb_ref, pc_ref, garm_ref, cot_ref, body_ref, stiff_ref, out_ref):
    cap, owners = pg_ref.shape
    tiles = stiff_ref.shape[0] // cap

    def one(d, carry):
        for s in range(cap):
            row = pl.ds(pg_ref[s, d], 1)
            for c in range(3):
                out_ref[d, c, s : s + 1, :] = garm_ref[c, row, :]
            out_ref[d, 3, s : s + 1, :] = jnp.where(s < pc_ref[0, d], cot_ref[row, :], 0.0)
            out_ref[d, 4 + 4 * tiles, s : s + 1, :] = jnp.full(
                (1, BLOCK), pb_ref[s, d].astype(f32), f32
            )
        for q in range(tiles):
            rows = slice(q * cap, (q + 1) * cap)
            for c in range(3):
                out_ref[d, 4 + c * tiles + q] = body_ref[c, rows, :]
            out_ref[d, 4 + 3 * tiles + q] = stiff_ref[rows, :]
        return carry

    if owners <= 8:
        for d in range(owners):
            one(d, 0)
    else:
        lax.fori_loop(0, owners, one, 0)


def over(count, fn):
    if count <= 8:
        for d in range(count):
            fn(d)
    else:
        lax.fori_loop(0, count, lambda d, carry: (fn(d), carry)[1], 0)


def body_kernel(own_ref, in_ref, out_ref, stiff_ref, left, right, table, index, grad):
    owners, tiles, cap, _ = in_ref.shape
    blocks = tiles - 5

    def take(d):
        rows = pl.ds(d * cap, cap)
        for c in range(4):
            left[c, rows, :] = in_ref[d, c]
        index[rows, :] = in_ref[d, tiles - 1]

    over(owners, take)
    for c in range(4):
        for q in range(blocks // 4):
            table[4 * q : 4 * q + 4, c * BLOCK : (c + 1) * BLOCK] = own_ref[
                0, 4 + c * (blocks // 4) + q
            ]
    lane = lax.broadcasted_iota(jnp.int32, index.shape, 1).astype(f32)
    onehot = (index[...] == lane).astype(f32)[:, :blocks].astype(bf16)
    chosen = [
        jnp.dot(onehot, part.astype(bf16), preferred_element_type=f32)
        for part in pieces(table[...], 3)
    ]
    chosen = chosen[0] + chosen[1] + chosen[2]
    for c in range(4):
        right[c] = chosen[:, c * BLOCK : (c + 1) * BLOCK]
    run_batches(left, right, grad)
    total = scatter(index[...], grad, blocks)
    for c in range(3):
        out_ref[c] = total[:, c * BLOCK : (c + 1) * BLOCK]
    stiff_ref[...] = total[:, 3 * BLOCK :]


def garm_kernel(pg_ref, pb_ref, own_ref, in_ref, out_ref, left, right, index, grad):
    owners, tiles, cap, _ = in_ref.shape
    blocks = tiles - 5
    garm_blocks = out_ref.shape[1]

    def take(d):
        rows = pl.ds(d * cap, cap)
        for c in range(4):
            right[c, rows, :] = own_ref[d, c]
        for s in range(cap):
            b = pb_ref[s, d]
            for c in range(4):
                left[c, pl.ds(d * cap + s, 1), :] = in_ref[
                    d, 4 + c * (blocks // 4) + b // 4, pl.ds(b % 4, 1), :
                ]
            index[pl.ds(d * cap + s, 1), :] = jnp.full((1, BLOCK), pg_ref[s, d].astype(f32), f32)

    over(owners, take)
    run_batches(left, right, grad)
    total = scatter(index[...], grad, garm_blocks)
    for c in range(3):
        out_ref[c] = total[:, c * BLOCK : (c + 1) * BLOCK]


def call(kernel, out_shape, scratch, scalars, arrays):
    specs = [pl.BlockSpec(memory_space=pltpu.SMEM)] * len(scalars)
    specs += [pl.BlockSpec(memory_space=pltpu.VMEM)] * len(arrays)
    return pl.pallas_call(
        kernel,
        out_shape=out_shape,
        in_specs=specs,
        out_specs=jax.tree.map(lambda _: pl.BlockSpec(memory_space=pltpu.VMEM), out_shape),
        scratch_shapes=scratch,
        compiler_params=pltpu.CompilerParams(vmem_limit_bytes=32 * 1024 * 1024),
    )(*scalars, *arrays)


def per_device(garment, cotangent, body_points, stiffness, pair_garment, pair_body, pair_count):
    owners = lax.axis_size(("garm", "body"))
    verts = garment.shape[2]
    points = body_points.shape[2]
    blocks = points // BLOCK
    cap = pair_garment.shape[3]
    slots = owners * cap
    pg = pair_garment.reshape(owners, cap).T
    pb = pair_body.reshape(owners, cap).T
    pc = pair_count.reshape(1, owners)
    message = call(
        pack_kernel,
        jax.ShapeDtypeStruct((owners, 5 + blocks, cap, BLOCK), f32),
        [],
        (pg, pb, pc),
        (
            garment.reshape(3, verts // BLOCK, BLOCK),
            cotangent.reshape(verts // BLOCK, BLOCK),
            body_points.reshape(3, blocks, BLOCK),
            stiffness.reshape(blocks, BLOCK),
        ),
    )
    arrived = lax.all_to_all(message, ("garm", "body"), split_axis=0, concat_axis=0, tiled=True)
    rows = pltpu.VMEM((4, slots, BLOCK), f32)
    grad = pltpu.VMEM((slots, 4 * BLOCK), f32)
    index = pltpu.VMEM((slots, BLOCK), f32)
    body_grad, stiff = call(
        body_kernel,
        (
            jax.ShapeDtypeStruct((3, blocks, BLOCK), f32),
            jax.ShapeDtypeStruct((blocks, BLOCK), f32),
        ),
        [rows, rows, pltpu.VMEM((blocks, 4 * BLOCK), f32), index, grad],
        (),
        (message, arrived),
    )
    other = lax.ppermute(stiff, "frame", [(0, 1), (1, 0)])
    garm_grad = call(
        garm_kernel,
        jax.ShapeDtypeStruct((3, verts // BLOCK, BLOCK), f32),
        [rows, rows, index, grad],
        (pg, pb),
        (message, arrived),
    )
    return (
        garm_grad.reshape(1, 3, verts),
        body_grad.reshape(1, 3, points),
        (stiff + other).reshape(points),
    )


def solution(mesh):
    in_specs = (
        P(("grp", "frame"), None, ("garm", "body")),
        P(("grp", "frame"), ("garm", "body")),
        P(("grp", "frame"), None, ("garm", "body")),
        P(("grp", "garm", "body")),
        P(("grp", "frame"), ("garm", "body"), None, None),
        P(("grp", "frame"), ("garm", "body"), None, None),
        P(("grp", "frame"), ("garm", "body"), None),
    )
    out_specs = (
        P(("grp", "frame"), None, ("garm", "body")),
        P(("grp", "frame"), None, ("garm", "body")),
        P(("grp", "garm", "body")),
    )
    return jax.shard_map(
        per_device, mesh=mesh, in_specs=in_specs, out_specs=out_specs, check_vma=False
    )
```

time: 55 us -> 27.9 us (0.51)
  blocking collectives: 3.05 us -> 18.2 us
  matrix products: 14.8 us -> 0 us
  starting transfers between devices: 13.9 us -> 0.01 us
  waiting for transfers between devices: 10.5 us -> 0.01 us
  Pallas kernels: 0 us -> 4.97 us
  other arithmetic: 4.72 us -> 0.6 us
  local copies, waits for them, and re-layouts: 6.65 us -> 2.94 us
    all_to_all x0 -> x1, blocking collectives: none -> 18.2 us  [per_device(): lax.all_to_all(message, ('garm', 'body'), split_axis=0, concat_axis=0, ti...]
    dot_general x5 -> x0, matrix products: 14.8 us -> none  [the longest x1 5.62 us: pair_terms(): jnp.einsum('nij,naj->nai', coupled, body_pos, precision=lax.Precision.HIG...]
    all_to_all x3 -> x0, starting transfers between devices: 13.9 us -> none  [the longest x1 7.25 us: per_device(): lax.all_to_all(targets, ('garm', 'body'), split_axis=1, concat_axis=1, ti...]
    all_to_all x3 -> x0, waiting for transfers between devices: 10.5 us -> none  [the longest x1 3.97 us: per_device(): lax.all_to_all(outgoing, ('garm', 'body'), split_axis=1, concat_axis=1, t...]
    pallas_call x0 -> x3, Pallas kernels: none -> 4.97 us  [call(): pl.pallas_call(kernel, out_shape=out_shape, in_specs=specs, out_specs=jax...]
    reduce_sum x1 -> x0, other arithmetic: 3.17 us -> none  [pair_terms(): col_sums = jnp.sum(coupled, axis=1)]
    psum x1 -> x0, blocking collectives: 3.05 us -> none  [per_device(): stiffness_grad = lax.psum(stiff_local, 'frame')]
    unnamed x10 -> x14, local copies, waits for them, and re-layouts: 0.11 us -> 2.94 us
  transfers between devices with their start and end apart: 3 -> 1, of which waited for: 3 -> 0; matrix products, arithmetic and copies ran while one was open for 11% -> 0% of each run, Pallas kernels for 0% -> 9%
where the time goes in v1:
time: 27.9 us; the launch traced here: 27.4 us
  blocking collectives  18.2 us (65%)
  Pallas kernels  4.97 us (18%)
  local copies, waits for them, and re-layouts  2.94 us (11%)
  between operations  0.68 us (2%)
  other arithmetic  0.6 us (2%)
    all_to_all x1, blocking collectives, per_device(): lax.all_to_all(message, ('garm', 'body'), split_axis=0, concat_axis=0, ti...  18.2 us
    pallas_call x3, Pallas kernels, call(): pl.pallas_call(kernel, out_shape=out_shape, in_specs=specs, out_specs=jax...  4.97 us
    unnamed x14, local copies, waits for them, and re-layouts  2.94 us
    reshape x1, other arithmetic, per_device(): (stiff + other).reshape(points)  0.6 us
  transfers between devices with their start and end apart: 1, of which 0 were waited for; matrix products, arithmetic and copies ran while one was open for 0% of the time, Pallas kernels for 9%

profile of v1, /device:TPU:0, one launch (start us, length us, event | category | flops | bytes accessed | tf_op | source)
XLA Modules:
  0.0 27.4 jit_solution(17848130780136730774)
XLA Ops:
  0.6 0.0 copy-start.3
  0.6 0.0 copy-start.5
  0.7 0.0 copy-start.4
  0.7 0.0 copy-start.6
  0.7 0.7 %copy-done.3 = f32[2048]{0:T(1024)S(1)} copy-done((f32[2048]{0:T(1024)S(1)}, f32[2048]{0:T(1024)}, u32[]{:S(2)}) %copy-start.3) | copy-done | bytes 8216
  1.3 0.0 copy-done.5
  1.3 0.0 copy-done.4
  1.3 0.0 copy-done.6
  1.4 0.0 copy-start
  1.4 0.8 %copy-done = f32[1,3,4096]{2,0,1:T(1,128)S(1)} copy-done((f32[1,3,4096]{2,0,1:T(1,128)S(1)}, f32[1,3,4096]{2,0,1:T(1,128)}, u32[]{:S(2)}) %copy-start) | copy-done | bytes 49176
  2.1 0.0 copy-start.1
  2.2 0.7 %copy-done.1 = f32[1,3,2048]{2,0,1:T(1,128)S(1)} copy-done((f32[1,3,2048]{2,0,1:T(1,128)S(1)}, f32[1,3,2048]{2,0,1:T(1,128)}, u32[]{:S(2)}) %copy-start.1) | copy-done | bytes 24600
  2.9 0.0 copy-start.2
  2.9 0.7 %copy-done.2 = f32[1,4096]{1,0:T(1,128)S(1)} copy-done((f32[1,4096]{1,0:T(1,128)S(1)}, f32[1,4096]{1,0:T(1,128)}, u32[]{:S(2)}) %copy-start.2) | copy-done | bytes 16408
  3.6 0.7 %shard_map.94.own_ref = f32[8,21,4,128]{3,2,1,0:T(4,128)S(1)} custom-call(s32[4,8]{1,0:T(4,128)S(1)} %bitcast.19, s32[4,8]{1,0:T(4,128)S(1)} %bitcast.21, s32[1,8]{1,0:T(1,128)S(1)} %bitcast.23, f32[3,32,128]{2,1,0:T(8,128)S(1)} %bitcast.15, f32[32,128]{1,0:T(8,128)S(1)} %bitcast.17, f32[3,16,128]{2,1,0:T(8,128)S(1)} %bitcast.16, f32[16,128]{1,0:T(8,128)S(1)} %bitcast.18), custom_call_target="tpu_custom_call" | custom-call | tf_op jit(solution)/shard_map/pallas_call | solution.py:212
  4.3 18.2 %all_to_all.5.in_ref = f32[8,21,4,128]{3,2,1,0:T(4,128)S(1)} all-to-all(f32[8,21,4,128]{3,2,1,0:T(4,128)S(1)} %shard_map.94.own_ref), channel_id=1, replica_groups=mesh['grp'=2,'garm'=4,'body'=2,'frame'=2] {'garm','body'}, dimensions={0} | all-to-all | bytes 688128 | tf_op jit(solution)/shard_map/all_to_all | solution.py:244
  22.6 1.9 %shard_map.96 = (f32[3,16,128]{2,1,0:T(8,128)}, f32[16,128]{1,0:T(8,128)S(1)}) custom-call(f32[8,21,4,128]{3,2,1,0:T(4,128)S(1)} %shard_map.94.own_ref, f32[8,21,4,128]{3,2,1,0:T(4,128)S(1)} %all_to_all.5.in_ref), custom_call_target="tpu_custom_call" | custom-call | tf_op jit(solution)/shard_map/pallas_call | solution.py:212
  24.4 0.0 collective-permute-start
  24.4 2.4 %shard_map.95 = f32[3,32,128]{2,1,0:T(8,128)} custom-call(s32[4,8]{1,0:T(4,128)S(1)} %bitcast.20, s32[4,8]{1,0:T(4,128)S(1)} %bitcast.22, f32[8,21,4,128]{3,2,1,0:T(4,128)S(1)} %shard_map.94.own_ref, f32[8,21,4,128]{3,2,1,0:T(4,128)S(1)} %all_to_all.5.in_ref), custom_call_target="tpu_custom_call" | custom-call | tf_op jit(solution)/shard_map/pallas_call | solution.py:212
  26.8 0.0 collective-permute-done
  26.8 0.6 %add_bitcast_fusion = f32[2048]{0:T(1024)} fusion(f32[16,128]{1,0:T(8,128)S(1)} %get-tuple-element.6, f32[16,128]{1,0:T(8,128)S(1)} %collective-permute-done), kind=kLoop, calls=%fused_computation | loop fusion | flops 2048 | bytes 24576 | tf_op jit(solution)/shard_map/reshape | solution.py:269
Async XLA Ops:
  0.6 0.7 %copy-start.3 = (f32[2048]{0:T(1024)S(1)}, f32[2048]{0:T(1024)}, u32[]{:S(2)}) copy-start(f32[2048]{0:T(1024)} %param.10) | copy-start | bytes 24580
  0.6 0.7 %copy-start.5 = (s32[1,1,8,4]{2,3,1,0:T(4,128)S(1)}, s32[1,1,8,4]{2,3,1,0:T(4,128)}, u32[]{:S(2)}) copy-start(s32[1,1,8,4]{2,3,1,0:T(4,128)} %param.12) | copy-start | bytes 388
  0.7 0.7 %copy-start.4 = (s32[1,1,8,4]{2,3,1,0:T(4,128)S(1)}, s32[1,1,8,4]{2,3,1,0:T(4,128)}, u32[]{:S(2)}) copy-start(s32[1,1,8,4]{2,3,1,0:T(4,128)} %param.11) | copy-start | bytes 388
  0.7 0.7 %copy-start.6 = (s32[1,1,8]{2,1,0:T(1,128)S(1)}, s32[1,1,8]{2,1,0:T(1,128)}, u32[]{:S(2)}) copy-start(s32[1,1,8]{2,1,0:T(1,128)} %param.13) | copy-start | bytes 100
  1.4 0.8 %copy-start = (f32[1,3,4096]{2,0,1:T(1,128)S(1)}, f32[1,3,4096]{2,0,1:T(1,128)}, u32[]{:S(2)}) copy-start(f32[1,3,4096]{2,0,1:T(1,128)} %param.7) | copy-start | bytes 147460
  2.1 0.7 %copy-start.1 = (f32[1,3,2048]{2,0,1:T(1,128)S(1)}, f32[1,3,2048]{2,0,1:T(1,128)}, u32[]{:S(2)}) copy-start(f32[1,3,2048]{2,0,1:T(1,128)} %param.9) | copy-start | bytes 73732
  2.9 0.7 %copy-start.2 = (f32[1,4096]{1,0:T(1,128)S(1)}, f32[1,4096]{1,0:T(1,128)}, u32[]{:S(2)}) copy-start(f32[1,4096]{1,0:T(1,128)} %param.8) | copy-start | bytes 49156
  24.4 2.4 %collective-permute-start = (f32[16,128]{1,0:T(8,128)S(1)}, f32[16,128]{1,0:T(8,128)S(1)}, u32[]{:S(2)}, u32[]{:S(2)}) collective-permute-start(f32[16,128]{1,0:T(8,128)S(1)} %get-tuple-element.6), channel_id=1, source_target_pairs={{0,1},{1,0},{2,3},{3,2},{4,5},{5,4},{6,7},{7,6},{8,9},{9,8},{10,11... | collective-permute-start | bytes 24584 | tf_op jit(solution)/shard_map/ppermute | solution.py:258

commit v2 on v1

--- a/solution.py
+++ b/solution.py
@@ -1,3 +1,4 @@
+import functools
 import math
 
 import jax
@@ -83,6 +84,12 @@
     return [total[c * SUB : (c + 1) * SUB] for c in range(4)]
 
 
+def gradients(left, right):
+    total = pull(left, right)
+    out = [FACTOR * right[3] * (right[c] * total[3] - total[c]) for c in range(3)]
+    return out + [amplitude * total[3]]
+
+
 def run_batches(left_ref, right_ref, grad_ref):
     batches = left_ref.shape[1] // SUB
 
@@ -90,12 +97,8 @@
         rows = pl.ds(pl.multiple_of(k * SUB, SUB), SUB)
         left = [left_ref[c, rows, :] for c in range(4)]
         right = [right_ref[c, rows, :] for c in range(4)]
-        total = pull(left, right)
-        for c in range(3):
-            grad_ref[rows, c * BLOCK : (c + 1) * BLOCK] = (
-                FACTOR * right[3] * (right[c] * total[3] - total[c])
-            )
-        grad_ref[rows, 3 * BLOCK :] = amplitude * total[3]
+        for c, value in enumerate(gradients(left, right)):
+            grad_ref[rows, c * BLOCK : (c + 1) * BLOCK] = value
         return carry
 
     if batches <= 4:
@@ -105,12 +108,12 @@
         lax.fori_loop(0, batches, step, 0)
 
 
-def scatter(index, grad_ref, blocks):
+def scatter(index, grads, blocks):
     lane = lax.broadcasted_iota(jnp.int32, index.shape, 1).astype(f32)
     onehot_t = (index == lane).astype(f32).T[:blocks].astype(bf16)
     parts = [
         jnp.dot(onehot_t, part.astype(bf16), preferred_element_type=f32)
-        for part in pieces(grad_ref[...], 3)
+        for part in pieces(grads, 3)
     ]
     return parts[0] + parts[1] + parts[2]
 
@@ -176,7 +179,7 @@
     for c in range(4):
         right[c] = chosen[:, c * BLOCK : (c + 1) * BLOCK]
     run_batches(left, right, grad)
-    total = scatter(index[...], grad, blocks)
+    total = scatter(index[...], grad[...], blocks)
     for c in range(3):
         out_ref[c] = total[:, c * BLOCK : (c + 1) * BLOCK]
     stiff_ref[...] = total[:, 3 * BLOCK :]
@@ -201,9 +204,195 @@
 
     over(owners, take)
     run_batches(left, right, grad)
-    total = scatter(index[...], grad, garm_blocks)
+    total = scatter(index[...], grad[...], garm_blocks)
     for c in range(3):
         out_ref[c] = total[:, c * BLOCK : (c + 1) * BLOCK]
+
+
+def read_table(message_ref):
+    tiles = (message_ref.shape[0] - 5) // 4
+    columns = []
+    for c in range(4):
+        start = 4 + c * tiles
+        columns.append(jnp.concatenate([message_ref[start + q] for q in range(tiles)], axis=0))
+    return jnp.concatenate(columns, axis=1)
+
+
+def choose(index, table):
+    lane = lax.broadcasted_iota(jnp.int32, index.shape, 1).astype(f32)
+    onehot = (index == lane).astype(f32)[:, : table.shape[0]].astype(bf16)
+    parts = [
+        jnp.dot(onehot, part.astype(bf16), preferred_element_type=f32)
+        for part in pieces(table, 3)
+    ]
+    rows = parts[0] + parts[1] + parts[2]
+    return [rows[:, c * BLOCK : (c + 1) * BLOCK] for c in range(4)]
+
+
+def mix(same_ref, other_ref, tile):
+    row = lax.broadcasted_iota(jnp.int32, (SUB, BLOCK), 0)
+    return jnp.where(row < SUB // 2, same_ref[tile], other_ref[tile])
+
+
+def body_batch(same_ref, other_ref, own_ref):
+    left = [mix(same_ref, other_ref, c) for c in range(4)]
+    index = mix(same_ref, other_ref, same_ref.shape[0] - 1)
+    right = choose(index, read_table(own_ref))
+    return jnp.concatenate(gradients(left, right), axis=1), index
+
+
+def garm_batch(same_ref, other_ref, sent_ref):
+    right = [sent_ref[c] for c in range(4)]
+    same, other = read_table(same_ref), read_table(other_ref)
+    row = lax.broadcasted_iota(jnp.int32, (SUB, BLOCK), 0)
+    index = sent_ref[sent_ref.shape[0] - 1]
+    index = index + jnp.where(row < SUB // 2, 0, same.shape[0]).astype(f32)
+    left = choose(index, jnp.concatenate([same, other], axis=0))
+    return jnp.concatenate(gradients(left, right)[:3], axis=1)
+
+
+def both_kernel(same_ref, other_ref, own_ref, sent_ref, bgrad_ref, bindex_ref, ggrad_ref):
+    bgrad_ref[...], bindex_ref[...] = body_batch(same_ref, other_ref, own_ref)
+    ggrad_ref[...] = garm_batch(same_ref, other_ref, sent_ref)
+
+
+def last_body_kernel(same_ref, other_ref, own_ref, *refs):
+    *earlier, out_ref, stiff_ref = refs
+    grad, index = body_batch(same_ref, other_ref, own_ref)
+    count = len(earlier) // 2
+    grads = jnp.concatenate([ref[...] for ref in earlier[:count]] + [grad], axis=0)
+    index = jnp.concatenate([ref[...] for ref in earlier[count:]] + [index], axis=0)
+    total = scatter(index, grads, out_ref.shape[1])
+    for c in range(3):
+        out_ref[c] = total[:, c * BLOCK : (c + 1) * BLOCK]
+    stiff_ref[...] = total[:, 3 * BLOCK :]
+
+
+def last_garm_kernel(same_ref, other_ref, sent_ref, index_ref, *refs):
+    *earlier, out_ref = refs
+    grad = garm_batch(same_ref, other_ref, sent_ref)
+    grads = jnp.concatenate([ref[...] for ref in earlier] + [grad], axis=0)
+    index = jnp.concatenate([index_ref[k] for k in range(index_ref.shape[0])], axis=0)
+    total = scatter(index, grads, out_ref.shape[1])
+    for c in range(3):
+        out_ref[c] = total[:, c * BLOCK : (c + 1) * BLOCK]
+
+
+def final_kernel(garm_ref, body_ref, mine_ref, other_ref, garm_out, body_out, stiff_out):
+    stiff_out[...] = mine_ref[...] + other_ref[...]
+    body_out[...] = body_ref[...]
+    garm_out[...] = garm_ref[...]
+
+
+def stage_kernel(order, *refs):
+    hbm, (index_ref, *out_refs), vmem, sems = refs[:7], refs[7:12], refs[12:19], refs[19]
+    copies = [
+        pltpu.make_async_copy(src, dst, sems.at[k]) for k, (src, dst) in enumerate(zip(hbm, vmem))
+    ]
+    for copy in copies:
+        copy.start()
+    for copy in copies:
+        copy.wait()
+    pg_ref, pb_ref, pc_ref, garm_ref, cot_ref, body_ref, stiff_ref = vmem
+    cap = pg_ref.shape[0]
+    tiles = stiff_ref.shape[0]
+    width = lax.axis_size("body")
+    here, column = lax.axis_index("garm"), lax.axis_index("body")
+    for k, out_ref in enumerate(out_refs):
+        for q in range(3 * tiles):
+            out_ref[4 + q] = body_ref[q]
+        for q in range(tiles):
+            out_ref[4 + 3 * tiles + q] = stiff_ref[q]
+        for x in range(2):
+            owner = (here ^ k) * width + (column ^ x)
+            live = pc_ref[0, owner]
+            for s in range(cap):
+                g = pg_ref[s, owner]
+                row, place = pl.ds(g, 1), pl.ds(x * cap + s, 1)
+                for c in range(3):
+                    out_ref[c, place, :] = garm_ref[c, row, :]
+                out_ref[3, place, :] = jnp.where(s < live, cot_ref[row, :], 0.0)
+                out_ref[4 + 4 * tiles, place, :] = jnp.full(
+                    (1, BLOCK), pb_ref[s, owner].astype(f32), f32
+                )
+                index_ref[order.index(k), place, :] = jnp.full((1, BLOCK), g.astype(f32), f32)
+
+
+def staged(garment, cotangent, body_points, stiffness, pg, pb, pc):
+    verts = garment.shape[2]
+    points = body_points.shape[2]
+    blocks = points // BLOCK
+    tiles = blocks // SUB
+    garm_n = lax.axis_size("garm")
+    order = (0, 3, 1, 2)
+    message = jax.ShapeDtypeStruct((5 + 4 * tiles, SUB, BLOCK), f32)
+    arrays = (
+        pg,
+        pb,
+        pc,
+        garment.reshape(3, verts // BLOCK, BLOCK),
+        cotangent.reshape(verts // BLOCK, BLOCK),
+        body_points.reshape(3 * tiles, SUB, BLOCK),
+        stiffness.reshape(tiles, SUB, BLOCK),
+    )
+    index, *sent = pl.pallas_call(
+        functools.partial(stage_kernel, order),
+        out_shape=[jax.ShapeDtypeStruct((garm_n, SUB, BLOCK), f32)] + [message] * garm_n,
+        in_specs=[pl.BlockSpec(memory_space=pltpu.HBM)] * len(arrays),
+        out_specs=[pl.BlockSpec(memory_space=pltpu.VMEM)] * (garm_n + 1),
+        scratch_shapes=[
+            (pltpu.SMEM if k < 3 else pltpu.VMEM)(a.shape, a.dtype) for k, a in enumerate(arrays)
+        ]
+        + [pltpu.SemaphoreType.DMA((len(arrays),))],
+    )(*[pltpu.with_memory_space_constraint(a, pltpu.HBM) for a in arrays])
+
+    def along_garm(k):
+        return lax.ppermute(sent[k], "garm", [(z, z ^ k) for z in range(garm_n)])
+
+    def along_body(value):
+        return lax.ppermute(value, "body", [(0, 1), (1, 0)])
+
+    same = {k: along_garm(k) for k in (3, 2, 1)}
+    same[0] = sent[0]
+    other = {k: along_body(same[k]) for k in (0, 1, 2, 3)}
+    body_grads, body_index, garm_grads = [], [], []
+    for k in order[:-1]:
+        out = call(
+            both_kernel,
+            (
+                jax.ShapeDtypeStruct((SUB, 4 * BLOCK), f32),
+                jax.ShapeDtypeStruct((SUB, BLOCK), f32),
+                jax.ShapeDtypeStruct((SUB, 3 * BLOCK), f32),
+            ),
+            [],
+            (),
+            (same[k], other[k], sent[0], sent[k]),
+        )
+        body_grads.append(out[0])
+        body_index.append(out[1])
+        garm_grads.append(out[2])
+    k = order[-1]
+    body_shape = jax.ShapeDtypeStruct((3, blocks, BLOCK), f32)
+    stiff_shape = jax.ShapeDtypeStruct((blocks, BLOCK), f32)
+    garm_shape = jax.ShapeDtypeStruct((3, verts // BLOCK, BLOCK), f32)
+    body_total, stiff = call(
+        last_body_kernel,
+        (body_shape, stiff_shape),
+        [],
+        (),
+        (same[k], other[k], sent[0], *body_grads, *body_index),
+    )
+    stiff_other = lax.ppermute(stiff, "frame", [(0, 1), (1, 0)])
+    garm_total = call(
+        last_garm_kernel, garm_shape, [], (), (same[k], other[k], sent[k], index, *garm_grads)
+    )
+    return call(
+        final_kernel,
+        (garm_shape, body_shape, stiff_shape),
+        [],
+        (),
+        (garm_total, body_total, stiff, stiff_other),
+    )
 
 
 def call(kernel, out_shape, scratch, scalars, arrays):
@@ -229,6 +418,15 @@
     pg = pair_garment.reshape(owners, cap).T
     pb = pair_body.reshape(owners, cap).T
     pc = pair_count.reshape(1, owners)
+    if (lax.axis_size("garm"), lax.axis_size("body")) == (4, 2) and cap == SUB // 2:
+        garm_grad, body_grad, stiff = staged(
+            garment, cotangent, body_points, stiffness, pg, pb, pc
+        )
+        return (
+            garm_grad.reshape(1, 3, verts),
+            body_grad.reshape(1, 3, points),
+            stiff.reshape(points),
+        )
     message = call(
         pack_kernel,
         jax.ShapeDtypeStruct((owners, 5 + blocks, cap, BLOCK), f32),

time: 27.9 us -> 22.2 us (0.80)
  blocking collectives: 18.2 us -> 0 us
  starting transfers between devices: 0.01 us -> 10.7 us
  waiting for transfers between devices: 0.01 us -> 2.56 us
  Pallas kernels: 4.97 us -> 7.08 us
  local copies, waits for them, and re-layouts: 2.94 us -> 0.91 us
  other arithmetic: 0.6 us -> 0 us
    all_to_all x1 -> x0, blocking collectives: 18.2 us -> none  [per_device(): lax.all_to_all(message, ('garm', 'body'), split_axis=0, concat_axis=0, ti...]
    ppermute x1 -> x8, starting transfers between devices: 0.01 us -> 10.7 us  [the longest x3 5.68 us: along_garm(): return lax.ppermute(sent[k], 'garm', [(z, z ^ k) for z in range(garm_n)])]
    ppermute x1 -> x8, waiting for transfers between devices: 0.01 us -> 2.56 us  [the longest x3 2.19 us: along_garm(): return lax.ppermute(sent[k], 'garm', [(z, z ^ k) for z in range(garm_n)])]
    unnamed x14 -> x10, local copies, waits for them, and re-layouts: 2.94 us -> 0.91 us
    pallas_call x0 -> x1, Pallas kernels: none -> 1.66 us  [staged(): pl.pallas_call(functools.partial(stage_kernel, order), out_shape=[jax.Sha...]
    reshape x1 -> x0, other arithmetic: 0.6 us -> none  [per_device(): (stiff + other).reshape(points)]
    pallas_call x3 -> x6, Pallas kernels: 4.97 us -> 5.41 us  [call(): pl.pallas_call(kernel, out_shape=out_shape, in_specs=specs, out_specs=jax...]
  transfers between devices with their start and end apart: 1 -> 8, of which waited for: 0 -> 2; matrix products, arithmetic and copies ran while one was open for 0% -> 0% of each run, Pallas kernels for 9% -> 19%
where the time goes in v2:
time: 22.2 us; the launch traced here: 21.9 us
  starting transfers between devices  10.7 us (48%)
  Pallas kernels  7.08 us (32%)
  waiting for transfers between devices  2.56 us (12%)
  local copies, waits for them, and re-layouts  0.91 us (4%)
  between operations  0.72 us (3%)
    ppermute x3, starting transfers between devices, along_garm(): return lax.ppermute(sent[k], 'garm', [(z, z ^ k) for z in range(garm_n)])  5.68 us
    pallas_call x6, Pallas kernels, call(): pl.pallas_call(kernel, out_shape=out_shape, in_specs=specs, out_specs=jax...  5.41 us
    ppermute x4, starting transfers between devices, along_body(): return lax.ppermute(value, 'body', [(0, 1), (1, 0)])  5.01 us
    ppermute x3, waiting for transfers between devices, along_garm(): return lax.ppermute(sent[k], 'garm', [(z, z ^ k) for z in range(garm_n)])  2.19 us
    pallas_call x1, Pallas kernels, staged(): pl.pallas_call(functools.partial(stage_kernel, order), out_shape=[jax.Sha...  1.66 us
    unnamed x10, local copies, waits for them, and re-layouts  0.91 us
  transfers between devices with their start and end apart: 8, of which 2 were waited for; matrix products, arithmetic and copies ran while one was open for 0% of the time, Pallas kernels for 19%

profile of v2, /device:TPU:0, one launch (start us, length us, event | category | flops | bytes accessed | tf_op | source)
XLA Modules:
  0.0 21.9 jit_solution(6232011273449212576)
XLA Ops:
  0.6 1.7 %shard_map.94 = (f32[4,8,128]{2,1,0:T(8,128)}, f32[13,8,128]{2,1,0:T(8,128)}, f32[13,8,128]{2,1,0:T(8,128)}, f32[13,8,128]{2,1,0:T(8,128)}, f32[13,8,128]{2,1,0:T(8,128)}) custom-call(s32[4,8]{1,0:T(4,128)} %bitcast.18, s32[4,8]{1,0:T(4,128)} %bitcast.19, s32[1,8]{1,0:T(1,128)} %bitcast.20, f32[3,32,128]{2,1,0:T(8,128)} %bitcast.14, f32[32,128]{1,0:T(8,128)} %bitcast.16, ...), custom_call_target="tpu_custom_call" | custom-call | tf_op jit(solution)/shard_map/pallas_call | solution.py:338
  2.3 3.1 %collective-permute-start.5 = (f32[13,8,128]{2,1,0:T(8,128)}, f32[13,8,128]{2,1,0:T(8,128)S(1)}, u32[]{:S(2)}, u32[]{:S(2)}) collective-permute-start(f32[13,8,128]{2,1,0:T(8,128)} %get-tuple-element.28.sent_ref), channel_id=1, source_target_pairs={{0,4},{4,0},{8,12},{12,8},{1,5},{5,1},{9,13},{13,9},{2,6},{6,2},{1... | collective-permute-start | bytes 159752 | tf_op jit(solution)/shard_map/ppermute | solution.py:350
  5.4 2.5 %collective-permute-start.3 = (f32[13,8,128]{2,1,0:T(8,128)}, f32[13,8,128]{2,1,0:T(8,128)S(1)}, u32[]{:S(2)}, u32[]{:S(2)}) collective-permute-start(f32[13,8,128]{2,1,0:T(8,128)} %get-tuple-element.26.sent_ref), channel_id=1, source_target_pairs={{0,12},{4,8},{8,4},{12,0},{1,13},{5,9},{9,5},{13,1},{2,14},{6,10},... | collective-permute-start | bytes 159752 | tf_op jit(solution)/shard_map/ppermute | solution.py:350
  7.9 0.1 collective-permute-start
  8.0 1.5 %collective-permute-start.2 = (f32[13,8,128]{2,1,0:T(8,128)}, f32[13,8,128]{2,1,0:T(8,128)S(1)}, u32[]{:S(2)}, u32[]{:S(2)}) collective-permute-start(f32[13,8,128]{2,1,0:T(8,128)} %get-tuple-element.24.same_ref.own_ref.sent_ref), channel_id=1, source_target_pairs={{0,2},{2,0},{1,3},{3,1},{4,6},{6,4},{5,7},{7,5},{8,10},{10,8},{9,1... | collective-permute-start | bytes 159752 | tf_op jit(solution)/shard_map/ppermute | solution.py:353
  9.5 0.0 collective-permute-done.5.same_ref
  9.5 0.5 %collective-permute-start.6 = (f32[13,8,128]{2,1,0:T(8,128)S(1)}, f32[13,8,128]{2,1,0:T(8,128)S(1)}, u32[]{:S(2)}, u32[]{:S(2)}) collective-permute-start(f32[13,8,128]{2,1,0:T(8,128)S(1)} %collective-permute-done.5.same_ref), channel_id=1, source_target_pairs={{0,2},{2,0},{1,3},{3,1},{4,6},{6,4},{5,7},{7,5},{8,10},{10,8},{9,1... | collective-permute-start | bytes 159752 | tf_op jit(solution)/shard_map/ppermute | solution.py:353
  10.0 2.2 %collective-permute-done.3.same_ref = f32[13,8,128]{2,1,0:T(8,128)S(1)} collective-permute-done((f32[13,8,128]{2,1,0:T(8,128)}, f32[13,8,128]{2,1,0:T(8,128)S(1)}, u32[]{:S(2)}, u32[]{:S(2)}) %collective-permute-start.3) | collective-permute-done | bytes 53280 | tf_op jit(solution)/shard_map/ppermute | solution.py:350
  12.2 1.5 %collective-permute-start.4 = (f32[13,8,128]{2,1,0:T(8,128)S(1)}, f32[13,8,128]{2,1,0:T(8,128)S(1)}, u32[]{:S(2)}, u32[]{:S(2)}) collective-permute-start(f32[13,8,128]{2,1,0:T(8,128)S(1)} %collective-permute-done.3.same_ref), channel_id=1, source_target_pairs={{0,2},{2,0},{1,3},{3,1},{4,6},{6,4},{5,7},{7,5},{8,10},{10,8},{9,1... | collective-permute-start | bytes 159752 | tf_op jit(solution)/shard_map/ppermute | solution.py:353
  13.7 0.0 collective-permute-done.same_ref
  13.7 1.5 %collective-permute-start.1 = (f32[13,8,128]{2,1,0:T(8,128)S(1)}, f32[13,8,128]{2,1,0:T(8,128)S(1)}, u32[]{:S(2)}, u32[]{:S(2)}) collective-permute-start(f32[13,8,128]{2,1,0:T(8,128)S(1)} %collective-permute-done.same_ref), channel_id=1, source_target_pairs={{0,2},{2,0},{1,3},{3,1},{4,6},{6,4},{5,7},{7,5},{8,10},{10,8},{9,1... | collective-permute-start | bytes 159752 | tf_op jit(solution)/shard_map/ppermute | solution.py:353
  15.2 0.8 %copy-done = f32[13,8,128]{2,1,0:T(8,128)S(1)} copy-done((f32[13,8,128]{2,1,0:T(8,128)S(1)}, f32[13,8,128]{2,1,0:T(8,128)}, u32[]{:S(2)}) %copy-start) | copy-done | bytes 53272
  16.0 1.1 %shard_map.95 = (f32[8,512]{1,0:T(8,128)S(1)}, f32[8,128]{1,0:T(8,128)S(1)}, f32[8,384]{1,0:T(8,128)S(1)}) custom-call(f32[13,8,128]{2,1,0:T(8,128)S(1)} %copy-done, f32[13,8,128]{2,1,0:T(8,128)S(1)} %collective-permute-done.2.other_ref, f32[13,8,128]{2,1,0:T(8,128)S(1)} %copy-done, f32[13,8,128]{2,1,0:T(8,128)S(1)} %copy-done), custom_call_target="tpu_custom_call" | custom-call | tf_op jit(solution)/shard_map/pallas_call | solution.py:401
  17.1 0.0 copy-start.2
  17.1 1.1 %shard_map.97 = (f32[8,512]{1,0:T(8,128)S(1)}, f32[8,128]{1,0:T(8,128)S(1)}, f32[8,384]{1,0:T(8,128)S(1)}) custom-call(f32[13,8,128]{2,1,0:T(8,128)S(1)} %collective-permute-done.5.same_ref, f32[13,8,128]{2,1,0:T(8,128)S(1)} %collective-permute-done.6.other_ref, f32[13,8,128]{2,1,0:T(8,128)S(1)} %copy-done, f32[13,8,128]{2,1,0:T(8,128)S(1)} %copy-done.3), custom_call_target="tpu_custom_call" | custom-call | tf_op jit(solution)/shard_map/pallas_call | solution.py:401
  18.2 0.0 collective-permute-done.4.other_ref
  18.3 1.1 %shard_map.96 = (f32[8,512]{1,0:T(8,128)S(1)}, f32[8,128]{1,0:T(8,128)S(1)}, f32[8,384]{1,0:T(8,128)S(1)}) custom-call(f32[13,8,128]{2,1,0:T(8,128)S(1)} %collective-permute-done.3.same_ref, f32[13,8,128]{2,1,0:T(8,128)S(1)} %collective-permute-done.4.other_ref, f32[13,8,128]{2,1,0:T(8,128)S(1)} %copy-done, f32[13,8,128]{2,1,0:T(8,128)S(1)} %copy-done.2), custom_call_target="tpu_custom_call" | custom-call | tf_op jit(solution)/shard_map/pallas_call | solution.py:401
  19.4 0.0 collective-permute-done.1.other_ref
  19.4 0.0 copy-start.4
  19.4 0.7 %shard_map.99 = (f32[3,16,128]{2,1,0:T(8,128)S(1)}, f32[16,128]{1,0:T(8,128)S(1)}) custom-call(f32[13,8,128]{2,1,0:T(8,128)S(1)} %collective-permute-done.same_ref, f32[13,8,128]{2,1,0:T(8,128)S(1)} %collective-permute-done.1.other_ref, f32[13,8,128]{2,1,0:T(8,128)S(1)} %copy-done, f32[8,512]{1,0:T(8,128)S(1)} %get-tuple-element.30.refs_0_, ...), custom_call_target="tpu_custom_call" | custom-call | tf_op jit(solution)/shard_map/pallas_call | solution.py:401
  20.1 0.1 copy-done.1
  20.2 0.8 %shard_map.98.garm_ref = f32[3,32,128]{2,1,0:T(8,128)S(1)} custom-call(f32[13,8,128]{2,1,0:T(8,128)S(1)} %collective-permute-done.same_ref, f32[13,8,128]{2,1,0:T(8,128)S(1)} %collective-permute-done.1.other_ref, f32[13,8,128]{2,1,0:T(8,128)S(1)} %copy-done.1, f32[4,8,128]{2,1,0:T(8,128)S(1)} %copy-done.4, f32[8,384]{1,0:T(8,128)S(1)} %get-tuple-element.25.refs_0_, ...), custom_call_target="tpu_custom_call" | custom-call | tf_op jit(solution)/shard_map/pallas_call | solution.py:401
  21.0 0.3 %collective-permute-done.7.other_ref = f32[16,128]{1,0:T(8,128)S(1)} collective-permute-done((f32[16,128]{1,0:T(8,128)S(1)}, f32[16,128]{1,0:T(8,128)S(1)}, u32[]{:S(2)}, u32[]{:S(2)}) %collective-permute-start.7) | collective-permute-done | bytes 8224 | tf_op jit(solution)/shard_map/ppermute | solution.py:385
  21.3 0.6 %shard_map.100 = (f32[3,32,128]{2,1,0:T(8,128)}, f32[3,16,128]{2,1,0:T(8,128)}, f32[16,128]{1,0:T(8,128)}) custom-call(f32[3,32,128]{2,1,0:T(8,128)S(1)} %shard_map.98.garm_ref, f32[3,16,128]{2,1,0:T(8,128)S(1)} %get-tuple-element.36.body_ref, f32[16,128]{1,0:T(8,128)S(1)} %get-tuple-element.37.mine_ref, f32[16,128]{1,0:T(8,128)S(1)} %collective-permute-done.7.other_ref), custom_call_target="tpu_custom_call" | custom-call | tf_op jit(solution)/shard_map/pallas_call | solution.py:401
  (9 shorter events, 0.0 us)
Async XLA Ops:
  2.3 7.2 %collective-permute-start.5 = (f32[13,8,128]{2,1,0:T(8,128)}, f32[13,8,128]{2,1,0:T(8,128)S(1)}, u32[]{:S(2)}, u32[]{:S(2)}) collective-permute-start(f32[13,8,128]{2,1,0:T(8,128)} %get-tuple-element.28.sent_ref), channel_id=1, source_target_pairs={{0,4},{4,0},{8,12},{12,8},{1,5},{5,1},{9,13},{13,9},{2,6},{6,2},{1... | collective-permute-start | bytes 159752 | tf_op jit(solution)/shard_map/ppermute | solution.py:350
  5.4 6.8 %collective-permute-start.3 = (f32[13,8,128]{2,1,0:T(8,128)}, f32[13,8,128]{2,1,0:T(8,128)S(1)}, u32[]{:S(2)}, u32[]{:S(2)}) collective-permute-start(f32[13,8,128]{2,1,0:T(8,128)} %get-tuple-element.26.sent_ref), channel_id=1, source_target_pairs={{0,12},{4,8},{8,4},{12,0},{1,13},{5,9},{9,5},{13,1},{2,14},{6,10},... | collective-permute-start | bytes 159752 | tf_op jit(solution)/shard_map/ppermute | solution.py:350
  7.9 5.8 %collective-permute-start = (f32[13,8,128]{2,1,0:T(8,128)}, f32[13,8,128]{2,1,0:T(8,128)S(1)}, u32[]{:S(2)}, u32[]{:S(2)}) collective-permute-start(f32[13,8,128]{2,1,0:T(8,128)} %get-tuple-element.22.sent_ref), channel_id=1, source_target_pairs={{0,8},{4,12},{8,0},{12,4},{1,9},{5,13},{9,1},{13,5},{2,10},{6,14},... | collective-permute-start | bytes 159752 | tf_op jit(solution)/shard_map/ppermute | solution.py:350
  8.0 7.2 %collective-permute-start.2 = (f32[13,8,128]{2,1,0:T(8,128)}, f32[13,8,128]{2,1,0:T(8,128)S(1)}, u32[]{:S(2)}, u32[]{:S(2)}) collective-permute-start(f32[13,8,128]{2,1,0:T(8,128)} %get-tuple-element.24.same_ref.own_ref.sent_ref), channel_id=1, source_target_pairs={{0,2},{2,0},{1,3},{3,1},{4,6},{6,4},{5,7},{7,5},{8,10},{10,8},{9,1... | collective-permute-start | bytes 159752 | tf_op jit(solution)/shard_map/ppermute | solution.py:353
  9.5 7.6 %collective-permute-start.6 = (f32[13,8,128]{2,1,0:T(8,128)S(1)}, f32[13,8,128]{2,1,0:T(8,128)S(1)}, u32[]{:S(2)}, u32[]{:S(2)}) collective-permute-start(f32[13,8,128]{2,1,0:T(8,128)S(1)} %collective-permute-done.5.same_ref), channel_id=1, source_target_pairs={{0,2},{2,0},{1,3},{3,1},{4,6},{6,4},{5,7},{7,5},{8,10},{10,8},{9,1... | collective-permute-start | bytes 159752 | tf_op jit(solution)/shard_map/ppermute | solution.py:353
  12.2 6.1 %collective-permute-start.4 = (f32[13,8,128]{2,1,0:T(8,128)S(1)}, f32[13,8,128]{2,1,0:T(8,128)S(1)}, u32[]{:S(2)}, u32[]{:S(2)}) collective-permute-start(f32[13,8,128]{2,1,0:T(8,128)S(1)} %collective-permute-done.3.same_ref), channel_id=1, source_target_pairs={{0,2},{2,0},{1,3},{3,1},{4,6},{6,4},{5,7},{7,5},{8,10},{10,8},{9,1... | collective-permute-start | bytes 159752 | tf_op jit(solution)/shard_map/ppermute | solution.py:353
  13.7 5.7 %collective-permute-start.1 = (f32[13,8,128]{2,1,0:T(8,128)S(1)}, f32[13,8,128]{2,1,0:T(8,128)S(1)}, u32[]{:S(2)}, u32[]{:S(2)}) collective-permute-start(f32[13,8,128]{2,1,0:T(8,128)S(1)} %collective-permute-done.same_ref), channel_id=1, source_target_pairs={{0,2},{2,0},{1,3},{3,1},{4,6},{6,4},{5,7},{7,5},{8,10},{10,8},{9,1... | collective-permute-start | bytes 159752 | tf_op jit(solution)/shard_map/ppermute | solution.py:353
  15.2 0.8 %copy-start = (f32[13,8,128]{2,1,0:T(8,128)S(1)}, f32[13,8,128]{2,1,0:T(8,128)}, u32[]{:S(2)}) copy-start(f32[13,8,128]{2,1,0:T(8,128)} %get-tuple-element.24.same_ref.own_ref.sent_ref) | copy-start | bytes 159748
  16.0 1.1 %copy-start.3 = (f32[13,8,128]{2,1,0:T(8,128)S(1)}, f32[13,8,128]{2,1,0:T(8,128)}, u32[]{:S(2)}) copy-start(f32[13,8,128]{2,1,0:T(8,128)} %get-tuple-element.28.sent_ref) | copy-start | bytes 159748
  17.1 1.2 %copy-start.2 = (f32[13,8,128]{2,1,0:T(8,128)S(1)}, f32[13,8,128]{2,1,0:T(8,128)}, u32[]{:S(2)}) copy-start(f32[13,8,128]{2,1,0:T(8,128)} %get-tuple-element.26.sent_ref) | copy-start | bytes 159748
  19.4 0.8 %copy-start.1 = (f32[13,8,128]{2,1,0:T(8,128)S(1)}, f32[13,8,128]{2,1,0:T(8,128)}, u32[]{:S(2)}) copy-start(f32[13,8,128]{2,1,0:T(8,128)} %get-tuple-element.22.sent_ref) | copy-start | bytes 159748
  19.4 0.8 %copy-start.4 = (f32[4,8,128]{2,1,0:T(8,128)S(1)}, f32[4,8,128]{2,1,0:T(8,128)}, u32[]{:S(2)}) copy-start(f32[4,8,128]{2,1,0:T(8,128)} %get-tuple-element.23.index_ref) | copy-start | bytes 49156
  20.1 1.2 %collective-permute-start.7 = (f32[16,128]{1,0:T(8,128)S(1)}, f32[16,128]{1,0:T(8,128)S(1)}, u32[]{:S(2)}, u32[]{:S(2)}) collective-permute-start(f32[16,128]{1,0:T(8,128)S(1)} %get-tuple-element.37.mine_ref), channel_id=1, source_target_pairs={{0,1},{1,0},{2,3},{3,2},{4,5},{5,4},{6,7},{7,6},{8,9},{9,8},{10,11... | collective-permute-start | bytes 24584 | tf_op jit(solution)/shard_map/ppermute | solution.py:385

commit v3 on v2

--- a/solution.py
+++ b/solution.py
@@ -10,6 +10,7 @@
 
 BLOCK = 128
 SUB = 8
+VMEM_LIMIT = 32 * 1024 * 1024
 
 amplitude = 0.05
 width_sq = 4.0
@@ -344,6 +345,7 @@
             (pltpu.SMEM if k < 3 else pltpu.VMEM)(a.shape, a.dtype) for k, a in enumerate(arrays)
         ]
         + [pltpu.SemaphoreType.DMA((len(arrays),))],
+        compiler_params=pltpu.CompilerParams(vmem_limit_bytes=VMEM_LIMIT),
     )(*[pltpu.with_memory_space_constraint(a, pltpu.HBM) for a in arrays])
 
     def along_garm(k):
@@ -404,7 +406,7 @@
         in_specs=specs,
         out_specs=jax.tree.map(lambda _: pl.BlockSpec(memory_space=pltpu.VMEM), out_shape),
         scratch_shapes=scratch,
-        compiler_params=pltpu.CompilerParams(vmem_limit_bytes=32 * 1024 * 1024),
+        compiler_params=pltpu.CompilerParams(vmem_limit_bytes=VMEM_LIMIT),
     )(*scalars, *arrays)
 
 

time: 22.2 us -> 20.4 us (0.919)
  local copies, waits for them, and re-layouts: 0.91 us -> 0 us
  Pallas kernels: 7.08 us -> 6.42 us
    unnamed x10 -> x0, local copies, waits for them, and re-layouts: 0.91 us -> none
    pallas_call x1, Pallas kernels: 1.66 us -> 0.99 us  [staged(): pl.pallas_call(functools.partial(stage_kernel, order), out_shape=[jax.Sha...]
  transfers between devices with their start and end apart: 8 -> 8, of which waited for: 2 -> 2; matrix products, arithmetic and copies ran while one was open for 0% -> 0% of each run, Pallas kernels for 19% -> 20%
where the time goes in v3:
time: 20.4 us; the launch traced here: 20.2 us
  starting transfers between devices  10.7 us (52%)
  Pallas kernels  6.42 us (31%)
  waiting for transfers between devices  2.42 us (12%)
  between operations  0.67 us (3%)
    ppermute x3, starting transfers between devices, along_garm(): return lax.ppermute(sent[k], 'garm', [(z, z ^ k) for z in range(garm_n)])  5.68 us
    pallas_call x6, Pallas kernels, call(): pl.pallas_call(kernel, out_shape=out_shape, in_specs=specs, out_specs=jax...  5.43 us
    ppermute x4, starting transfers between devices, along_body(): return lax.ppermute(value, 'body', [(0, 1), (1, 0)])  5.01 us
    ppermute x3, waiting for transfers between devices, along_garm(): return lax.ppermute(sent[k], 'garm', [(z, z ^ k) for z in range(garm_n)])  1.98 us
    pallas_call x1, Pallas kernels, staged(): pl.pallas_call(functools.partial(stage_kernel, order), out_shape=[jax.Sha...  0.99 us
  transfers between devices with their start and end apart: 8, of which 2 were waited for; matrix products, arithmetic and copies ran while one was open for 0% of the time, Pallas kernels for 20%

profile of v3, /device:TPU:0, one launch (start us, length us, event | category | flops | bytes accessed | tf_op | source)
XLA Modules:
  0.0 20.2 jit_solution(16674100651490367578)
XLA Ops:
  0.6 1.0 %shard_map.94 = (f32[4,8,128]{2,1,0:T(8,128)S(1)}, f32[13,8,128]{2,1,0:T(8,128)S(1)}, f32[13,8,128]{2,1,0:T(8,128)S(1)}, f32[13,8,128]{2,1,0:T(8,128)S(1)}, f32[13,8,128]{2,1,0:T(8,128)S(1)}) custom-call(s32[4,8]{1,0:T(4,128)} %bitcast.18, s32[4,8]{1,0:T(4,128)} %bitcast.19, s32[1,8]{1,0:T(1,128)} %bitcast.20, f32[3,32,128]{2,1,0:T(8,128)} %bitcast.14, ...), custom_call_target="tpu_custom_call" | custom-call | tf_op jit(solution)/shard_map/pallas_call | solution.py:339
  1.6 3.1 %collective-permute-start.5 = (f32[13,8,128]{2,1,0:T(8,128)S(1)}, f32[13,8,128]{2,1,0:T(8,128)S(1)}, u32[]{:S(2)}, u32[]{:S(2)}) collective-permute-start(f32[13,8,128]{2,1,0:T(8,128)S(1)} %get-tuple-element.28.sent_ref), channel_id=1, source_target_pairs={{0,4},{4,0},{8,12},{12,8},{1,5},{5,1},{9,13},{13,9},{2,6},{6,2},{1... | collective-permute-start | bytes 159752 | tf_op jit(solution)/shard_map/ppermute | solution.py:352
  4.7 2.5 %collective-permute-start.3 = (f32[13,8,128]{2,1,0:T(8,128)S(1)}, f32[13,8,128]{2,1,0:T(8,128)S(1)}, u32[]{:S(2)}, u32[]{:S(2)}) collective-permute-start(f32[13,8,128]{2,1,0:T(8,128)S(1)} %get-tuple-element.26.sent_ref), channel_id=1, source_target_pairs={{0,12},{4,8},{8,4},{12,0},{1,13},{5,9},{9,5},{13,1},{2,14},{6,10},... | collective-permute-start | bytes 159752 | tf_op jit(solution)/shard_map/ppermute | solution.py:352
  7.2 0.1 collective-permute-start
  7.3 1.5 %collective-permute-start.2 = (f32[13,8,128]{2,1,0:T(8,128)S(1)}, f32[13,8,128]{2,1,0:T(8,128)S(1)}, u32[]{:S(2)}, u32[]{:S(2)}) collective-permute-start(f32[13,8,128]{2,1,0:T(8,128)S(1)} %get-tuple-element.24.same_ref.own_ref.sent_ref), channel_id=1, source_target_pairs={{0,2},{2,0},{1,3},{3,1},{4,6},{6,4},{5,7},{7,5},{8,10},{10,8},{9,1... | collective-permute-start | bytes 159752 | tf_op jit(solution)/shard_map/ppermute | solution.py:355
  8.8 0.0 collective-permute-done.5.same_ref
  8.8 0.5 %collective-permute-start.6 = (f32[13,8,128]{2,1,0:T(8,128)S(1)}, f32[13,8,128]{2,1,0:T(8,128)S(1)}, u32[]{:S(2)}, u32[]{:S(2)}) collective-permute-start(f32[13,8,128]{2,1,0:T(8,128)S(1)} %collective-permute-done.5.same_ref), channel_id=1, source_target_pairs={{0,2},{2,0},{1,3},{3,1},{4,6},{6,4},{5,7},{7,5},{8,10},{10,8},{9,1... | collective-permute-start | bytes 159752 | tf_op jit(solution)/shard_map/ppermute | solution.py:355
  9.3 2.0 %collective-permute-done.3.same_ref = f32[13,8,128]{2,1,0:T(8,128)S(1)} collective-permute-done((f32[13,8,128]{2,1,0:T(8,128)S(1)}, f32[13,8,128]{2,1,0:T(8,128)S(1)}, u32[]{:S(2)}, u32[]{:S(2)}) %collective-permute-start.3) | collective-permute-done | bytes 53280 | tf_op jit(solution)/shard_map/ppermute | solution.py:352
  11.3 1.5 %collective-permute-start.4 = (f32[13,8,128]{2,1,0:T(8,128)S(1)}, f32[13,8,128]{2,1,0:T(8,128)S(1)}, u32[]{:S(2)}, u32[]{:S(2)}) collective-permute-start(f32[13,8,128]{2,1,0:T(8,128)S(1)} %collective-permute-done.3.same_ref), channel_id=1, source_target_pairs={{0,2},{2,0},{1,3},{3,1},{4,6},{6,4},{5,7},{7,5},{8,10},{10,8},{9,1... | collective-permute-start | bytes 159752 | tf_op jit(solution)/shard_map/ppermute | solution.py:355
  12.8 0.0 collective-permute-done.same_ref
  12.8 1.5 %collective-permute-start.1 = (f32[13,8,128]{2,1,0:T(8,128)S(1)}, f32[13,8,128]{2,1,0:T(8,128)S(1)}, u32[]{:S(2)}, u32[]{:S(2)}) collective-permute-start(f32[13,8,128]{2,1,0:T(8,128)S(1)} %collective-permute-done.same_ref), channel_id=1, source_target_pairs={{0,2},{2,0},{1,3},{3,1},{4,6},{6,4},{5,7},{7,5},{8,10},{10,8},{9,1... | collective-permute-start | bytes 159752 | tf_op jit(solution)/shard_map/ppermute | solution.py:355
  14.3 0.0 collective-permute-done.2.other_ref
  14.3 1.1 %shard_map.95 = (f32[8,512]{1,0:T(8,128)S(1)}, f32[8,128]{1,0:T(8,128)S(1)}, f32[8,384]{1,0:T(8,128)S(1)}) custom-call(f32[13,8,128]{2,1,0:T(8,128)S(1)} %get-tuple-element.24.same_ref.own_ref.sent_ref, f32[13,8,128]{2,1,0:T(8,128)S(1)} %collective-permute-done.2.other_ref, f32[13,8,128]{2,1,0:T(8,128)S(1)} %get-tuple-element.24.same_ref.own_ref.sent_ref, ...), custom_call_target="tpu_custom_call" | custom-call | tf_op jit(solution)/shard_map/pallas_call | solution.py:403
  15.4 0.0 collective-permute-done.6.other_ref
  15.4 1.1 %shard_map.97 = (f32[8,512]{1,0:T(8,128)S(1)}, f32[8,128]{1,0:T(8,128)S(1)}, f32[8,384]{1,0:T(8,128)S(1)}) custom-call(f32[13,8,128]{2,1,0:T(8,128)S(1)} %collective-permute-done.5.same_ref, f32[13,8,128]{2,1,0:T(8,128)S(1)} %collective-permute-done.6.other_ref, f32[13,8,128]{2,1,0:T(8,128)S(1)} %get-tuple-element.24.same_ref.own_ref.sent_ref, ...), custom_call_target="tpu_custom_call" | custom-call | tf_op jit(solution)/shard_map/pallas_call | solution.py:403
  16.5 0.0 collective-permute-done.4.other_ref
  16.5 1.1 %shard_map.96 = (f32[8,512]{1,0:T(8,128)S(1)}, f32[8,128]{1,0:T(8,128)S(1)}, f32[8,384]{1,0:T(8,128)S(1)}) custom-call(f32[13,8,128]{2,1,0:T(8,128)S(1)} %collective-permute-done.3.same_ref, f32[13,8,128]{2,1,0:T(8,128)S(1)} %collective-permute-done.4.other_ref, f32[13,8,128]{2,1,0:T(8,128)S(1)} %get-tuple-element.24.same_ref.own_ref.sent_ref, ...), custom_call_target="tpu_custom_call" | custom-call | tf_op jit(solution)/shard_map/pallas_call | solution.py:403
  17.7 0.0 collective-permute-done.1.other_ref
  17.7 0.7 %shard_map.99 = (f32[3,16,128]{2,1,0:T(8,128)S(1)}, f32[16,128]{1,0:T(8,128)S(1)}) custom-call(f32[13,8,128]{2,1,0:T(8,128)S(1)} %collective-permute-done.same_ref, f32[13,8,128]{2,1,0:T(8,128)S(1)} %collective-permute-done.1.other_ref, f32[13,8,128]{2,1,0:T(8,128)S(1)} %get-tuple-element.24.same_ref.own_ref.sent_ref, ...), custom_call_target="tpu_custom_call" | custom-call | tf_op jit(solution)/shard_map/pallas_call | solution.py:403
  18.4 0.0 collective-permute-start.7
  18.4 0.8 %shard_map.98.garm_ref = f32[3,32,128]{2,1,0:T(8,128)S(1)} custom-call(f32[13,8,128]{2,1,0:T(8,128)S(1)} %collective-permute-done.same_ref, f32[13,8,128]{2,1,0:T(8,128)S(1)} %collective-permute-done.1.other_ref, f32[13,8,128]{2,1,0:T(8,128)S(1)} %get-tuple-element.22.sent_ref, f32[4,8,128]{2,1,0:T(8,128)S(1)} %get-tuple-element.23.index_ref, ...), custom_call_target="tpu_custom_call" | custom-call | tf_op jit(solution)/shard_map/pallas_call | solution.py:403
  19.2 0.4 %collective-permute-done.7.other_ref = f32[16,128]{1,0:T(8,128)S(1)} collective-permute-done((f32[16,128]{1,0:T(8,128)S(1)}, f32[16,128]{1,0:T(8,128)S(1)}, u32[]{:S(2)}, u32[]{:S(2)}) %collective-permute-start.7) | collective-permute-done | bytes 8224 | tf_op jit(solution)/shard_map/ppermute | solution.py:387
  19.6 0.6 %shard_map.100 = (f32[3,32,128]{2,1,0:T(8,128)}, f32[3,16,128]{2,1,0:T(8,128)}, f32[16,128]{1,0:T(8,128)}) custom-call(f32[3,32,128]{2,1,0:T(8,128)S(1)} %shard_map.98.garm_ref, f32[3,16,128]{2,1,0:T(8,128)S(1)} %get-tuple-element.36.body_ref, f32[16,128]{1,0:T(8,128)S(1)} %get-tuple-element.37.mine_ref, f32[16,128]{1,0:T(8,128)S(1)} %collective-permute-done.7.other_ref), custom_call_target="tpu_custom_call" | custom-call | tf_op jit(solution)/shard_map/pallas_call | solution.py:403
Async XLA Ops:
  1.6 7.2 %collective-permute-start.5 = (f32[13,8,128]{2,1,0:T(8,128)S(1)}, f32[13,8,128]{2,1,0:T(8,128)S(1)}, u32[]{:S(2)}, u32[]{:S(2)}) collective-permute-start(f32[13,8,128]{2,1,0:T(8,128)S(1)} %get-tuple-element.28.sent_ref), channel_id=1, source_target_pairs={{0,4},{4,0},{8,12},{12,8},{1,5},{5,1},{9,13},{13,9},{2,6},{6,2},{1... | collective-permute-start | bytes 159752 | tf_op jit(solution)/shard_map/ppermute | solution.py:352
  4.7 6.6 %collective-permute-start.3 = (f32[13,8,128]{2,1,0:T(8,128)S(1)}, f32[13,8,128]{2,1,0:T(8,128)S(1)}, u32[]{:S(2)}, u32[]{:S(2)}) collective-permute-start(f32[13,8,128]{2,1,0:T(8,128)S(1)} %get-tuple-element.26.sent_ref), channel_id=1, source_target_pairs={{0,12},{4,8},{8,4},{12,0},{1,13},{5,9},{9,5},{13,1},{2,14},{6,10},... | collective-permute-start | bytes 159752 | tf_op jit(solution)/shard_map/ppermute | solution.py:352
  7.2 5.6 %collective-permute-start = (f32[13,8,128]{2,1,0:T(8,128)S(1)}, f32[13,8,128]{2,1,0:T(8,128)S(1)}, u32[]{:S(2)}, u32[]{:S(2)}) collective-permute-start(f32[13,8,128]{2,1,0:T(8,128)S(1)} %get-tuple-element.22.sent_ref), channel_id=1, source_target_pairs={{0,8},{4,12},{8,0},{12,4},{1,9},{5,13},{9,1},{13,5},{2,10},{6,14},... | collective-permute-start | bytes 159752 | tf_op jit(solution)/shard_map/ppermute | solution.py:352
  7.3 7.0 %collective-permute-start.2 = (f32[13,8,128]{2,1,0:T(8,128)S(1)}, f32[13,8,128]{2,1,0:T(8,128)S(1)}, u32[]{:S(2)}, u32[]{:S(2)}) collective-permute-start(f32[13,8,128]{2,1,0:T(8,128)S(1)} %get-tuple-element.24.same_ref.own_ref.sent_ref), channel_id=1, source_target_pairs={{0,2},{2,0},{1,3},{3,1},{4,6},{6,4},{5,7},{7,5},{8,10},{10,8},{9,1... | collective-permute-start | bytes 159752 | tf_op jit(solution)/shard_map/ppermute | solution.py:355
  8.8 6.6 %collective-permute-start.6 = (f32[13,8,128]{2,1,0:T(8,128)S(1)}, f32[13,8,128]{2,1,0:T(8,128)S(1)}, u32[]{:S(2)}, u32[]{:S(2)}) collective-permute-start(f32[13,8,128]{2,1,0:T(8,128)S(1)} %collective-permute-done.5.same_ref), channel_id=1, source_target_pairs={{0,2},{2,0},{1,3},{3,1},{4,6},{6,4},{5,7},{7,5},{8,10},{10,8},{9,1... | collective-permute-start | bytes 159752 | tf_op jit(solution)/shard_map/ppermute | solution.py:355
  11.3 5.2 %collective-permute-start.4 = (f32[13,8,128]{2,1,0:T(8,128)S(1)}, f32[13,8,128]{2,1,0:T(8,128)S(1)}, u32[]{:S(2)}, u32[]{:S(2)}) collective-permute-start(f32[13,8,128]{2,1,0:T(8,128)S(1)} %collective-permute-done.3.same_ref), channel_id=1, source_target_pairs={{0,2},{2,0},{1,3},{3,1},{4,6},{6,4},{5,7},{7,5},{8,10},{10,8},{9,1... | collective-permute-start | bytes 159752 | tf_op jit(solution)/shard_map/ppermute | solution.py:355
  12.8 4.8 %collective-permute-start.1 = (f32[13,8,128]{2,1,0:T(8,128)S(1)}, f32[13,8,128]{2,1,0:T(8,128)S(1)}, u32[]{:S(2)}, u32[]{:S(2)}) collective-permute-start(f32[13,8,128]{2,1,0:T(8,128)S(1)} %collective-permute-done.same_ref), channel_id=1, source_target_pairs={{0,2},{2,0},{1,3},{3,1},{4,6},{6,4},{5,7},{7,5},{8,10},{10,8},{9,1... | collective-permute-start | bytes 159752 | tf_op jit(solution)/shard_map/ppermute | solution.py:355
  18.4 1.2 %collective-permute-start.7 = (f32[16,128]{1,0:T(8,128)S(1)}, f32[16,128]{1,0:T(8,128)S(1)}, u32[]{:S(2)}, u32[]{:S(2)}) collective-permute-start(f32[16,128]{1,0:T(8,128)S(1)} %get-tuple-element.37.mine_ref), channel_id=1, source_target_pairs={{0,1},{1,0},{2,3},{3,2},{4,5},{5,4},{6,7},{7,6},{8,9},{9,8},{10,11... | collective-permute-start | bytes 24584 | tf_op jit(solution)/shard_map/ppermute | solution.py:387

commit v4 on v3

--- a/solution.py
+++ b/solution.py
@@ -1,4 +1,3 @@
-import functools
 import math
 
 import jax
@@ -52,61 +51,64 @@
     )
 
 
-def pull(left, right):
-    lfeat, rfeat = features(left, right)
-    depth = lfeat.shape[0]
-    weight = left[3]
-    coeff = jnp.concatenate([weight * left[c] for c in range(3)] + [weight], axis=0)
-    chi, clo = pieces(coeff, 2)
-    chi, clo = chi.astype(bf16), clo.astype(bf16)
-    lhs = jnp.concatenate(
-        [
-            jnp.concatenate([chi, chi], axis=1),
-            jnp.concatenate([clo, jnp.zeros_like(clo)], axis=1),
-        ],
-        axis=0,
-    )
-    lfeat_t = lfeat.T
-    row = lax.broadcasted_iota(jnp.int32, (depth, BLOCK), 0) % SUB
+def pull(batches):
+    made = []
+    for left, right in batches:
+        lfeat, rfeat = features(left, right)
+        weight = left[3]
+        coeff = jnp.concatenate([weight * left[c] for c in range(3)] + [weight], axis=0)
+        chi, clo = [part.astype(bf16) for part in pieces(coeff, 2)]
+        lhs = jnp.concatenate(
+            [
+                jnp.concatenate([chi, chi], axis=1),
+                jnp.concatenate([clo, jnp.zeros_like(clo)], axis=1),
+            ],
+            axis=0,
+        )
+        made.append((lfeat.T, rfeat, lhs))
+    row = lax.broadcasted_iota(jnp.int32, made[0][1].shape, 0) % SUB
     sub = lax.broadcasted_iota(jnp.int32, (4 * SUB, BLOCK), 0) % SUB
-    total = jnp.zeros((4 * SUB, BLOCK), f32)
+    totals = [jnp.zeros((4 * SUB, BLOCK), f32) for _ in batches]
     for pair in range(0, SUB, 2):
-        rhs = jnp.concatenate(
-            [rfeat * (row == pair + k).astype(f32).astype(bf16) for k in range(2)], axis=1
-        )
-        exponent = jnp.dot(lfeat_t, rhs, preferred_element_type=f32)
-        kernel = jnp.exp2(exponent)
-        khi = kernel.astype(bf16)
-        klo = (kernel - khi.astype(f32)).astype(bf16)
-        sums = jnp.dot(lhs, jnp.concatenate([khi, klo], axis=0), preferred_element_type=f32)
-        sums = sums[: 4 * SUB] + sums[4 * SUB :]
-        for k in range(2):
-            total = jnp.where(sub == pair + k, sums[:, k * BLOCK : (k + 1) * BLOCK], total)
-    return [total[c * SUB : (c + 1) * SUB] for c in range(4)]
-
-
-def gradients(left, right):
-    total = pull(left, right)
-    out = [FACTOR * right[3] * (right[c] * total[3] - total[c]) for c in range(3)]
-    return out + [amplitude * total[3]]
+        masks = [(row == pair + k).astype(f32).astype(bf16) for k in range(2)]
+        for n, (lfeat_t, rfeat, lhs) in enumerate(made):
+            rhs = jnp.concatenate([rfeat * mask for mask in masks], axis=1)
+            exponent = jnp.dot(lfeat_t, rhs, preferred_element_type=f32)
+            kernel = jnp.exp2(exponent)
+            khi = kernel.astype(bf16)
+            klo = (kernel - khi.astype(f32)).astype(bf16)
+            sums = jnp.dot(lhs, jnp.concatenate([khi, klo], axis=0), preferred_element_type=f32)
+            sums = sums[: 4 * SUB] + sums[4 * SUB :]
+            for k in range(2):
+                part = sums[:, k * BLOCK : (k + 1) * BLOCK]
+                totals[n] = jnp.where(sub == pair + k, part, totals[n])
+    return [[total[c * SUB : (c + 1) * SUB] for c in range(4)] for total in totals]
+
+
+def gradients(batches):
+    out = []
+    for (_, right), total in zip(batches, pull(batches)):
+        rows = [FACTOR * right[3] * (right[c] * total[3] - total[c]) for c in range(3)]
+        out.append(rows + [amplitude * total[3]])
+    return out
 
 
 def run_batches(left_ref, right_ref, grad_ref):
     batches = left_ref.shape[1] // SUB
+    group = math.gcd(batches, 4)
 
     def step(k, carry):
-        rows = pl.ds(pl.multiple_of(k * SUB, SUB), SUB)
-        left = [left_ref[c, rows, :] for c in range(4)]
-        right = [right_ref[c, rows, :] for c in range(4)]
-        for c, value in enumerate(gradients(left, right)):
-            grad_ref[rows, c * BLOCK : (c + 1) * BLOCK] = value
+        places = [pl.ds(pl.multiple_of((k * group + n) * SUB, SUB), SUB) for n in range(group)]
+        work = [
+            tuple([ref[c, rows, :] for c in range(4)] for ref in (left_ref, right_ref))
+            for rows in places
+        ]
+        for rows, values in zip(places, gradients(work)):
+            for c, value in enumerate(values):
+                grad_ref[rows, c * BLOCK : (c + 1) * BLOCK] = value
         return carry
 
-    if batches <= 4:
-        for k in range(batches):
-            step(k, 0)
-    else:
-        lax.fori_loop(0, batches, step, 0)
+    lax.fori_loop(0, batches // group, step, 0)
 
 
 def scatter(index, grads, blocks):
@@ -210,12 +212,23 @@
         out_ref[c] = total[:, c * BLOCK : (c + 1) * BLOCK]
 
 
-def read_table(message_ref):
-    tiles = (message_ref.shape[0] - 5) // 4
-    columns = []
-    for c in range(4):
-        start = 4 + c * tiles
-        columns.append(jnp.concatenate([message_ref[start + q] for q in range(tiles)], axis=0))
+def call(kernel, out_shape, scratch, scalars, arrays):
+    specs = [pl.BlockSpec(memory_space=pltpu.SMEM)] * len(scalars)
+    specs += [pl.BlockSpec(memory_space=pltpu.VMEM)] * len(arrays)
+    return pl.pallas_call(
+        kernel,
+        out_shape=out_shape,
+        in_specs=specs,
+        out_specs=jax.tree.map(lambda _: pl.BlockSpec(memory_space=pltpu.VMEM), out_shape),
+        scratch_shapes=scratch,
+        compiler_params=pltpu.CompilerParams(vmem_limit_bytes=VMEM_LIMIT),
+    )(*scalars, *arrays)
+
+
+def read_table(ref, start, step):
+    columns = [
+        jnp.concatenate([ref[start + c * step + q] for q in range(step)], axis=0) for c in range(4)
+    ]
     return jnp.concatenate(columns, axis=1)
 
 
@@ -230,51 +243,122 @@
     return [rows[:, c * BLOCK : (c + 1) * BLOCK] for c in range(4)]
 
 
-def mix(same_ref, other_ref, tile):
+def halves(top, bottom):
     row = lax.broadcasted_iota(jnp.int32, (SUB, BLOCK), 0)
-    return jnp.where(row < SUB // 2, same_ref[tile], other_ref[tile])
-
-
-def body_batch(same_ref, other_ref, own_ref):
-    left = [mix(same_ref, other_ref, c) for c in range(4)]
-    index = mix(same_ref, other_ref, same_ref.shape[0] - 1)
-    right = choose(index, read_table(own_ref))
-    return jnp.concatenate(gradients(left, right), axis=1), index
-
-
-def garm_batch(same_ref, other_ref, sent_ref):
-    right = [sent_ref[c] for c in range(4)]
-    same, other = read_table(same_ref), read_table(other_ref)
+    return jnp.where(row < SUB // 2, top, bottom)
+
+
+def flip(value):
+    return pltpu.roll(value, SUB // 2, 0)
+
+
+def body_work(tiles, table):
+    return list(tiles[:4]), choose(tiles[4], table)
+
+
+def garm_work(tiles, top, bottom):
     row = lax.broadcasted_iota(jnp.int32, (SUB, BLOCK), 0)
-    index = sent_ref[sent_ref.shape[0] - 1]
-    index = index + jnp.where(row < SUB // 2, 0, same.shape[0]).astype(f32)
-    left = choose(index, jnp.concatenate([same, other], axis=0))
-    return jnp.concatenate(gradients(left, right)[:3], axis=1)
-
-
-def both_kernel(same_ref, other_ref, own_ref, sent_ref, bgrad_ref, bindex_ref, ggrad_ref):
-    bgrad_ref[...], bindex_ref[...] = body_batch(same_ref, other_ref, own_ref)
-    ggrad_ref[...] = garm_batch(same_ref, other_ref, sent_ref)
-
-
-def last_body_kernel(same_ref, other_ref, own_ref, *refs):
-    *earlier, out_ref, stiff_ref = refs
-    grad, index = body_batch(same_ref, other_ref, own_ref)
-    count = len(earlier) // 2
-    grads = jnp.concatenate([ref[...] for ref in earlier[:count]] + [grad], axis=0)
-    index = jnp.concatenate([ref[...] for ref in earlier[count:]] + [index], axis=0)
-    total = scatter(index, grads, out_ref.shape[1])
+    index = tiles[4] + jnp.where(row < SUB // 2, 0, top.shape[0]).astype(f32)
+    return choose(index, jnp.concatenate([top, bottom], axis=0)), list(tiles[:4])
+
+
+def slot_tiles(ref):
+    return [ref[c] for c in range(4)] + [ref[ref.shape[0] - 1]]
+
+
+def message_table(ref):
+    return read_table(ref, 4, (ref.shape[0] - 5) // 4)
+
+
+def near_bundle_kernel(one_ref, two_ref, out_ref):
+    body = one_ref.shape[0] - 5
+    for q in range(body):
+        out_ref[q] = one_ref[4 + q]
+        out_ref[body + q] = two_ref[4 + q]
+    for k, (a, b) in enumerate(zip(slot_tiles(one_ref), slot_tiles(two_ref))):
+        out_ref[2 * body + k] = halves(flip(a), b)
+
+
+def far_bundle_kernel(three_ref, near_ref, out_ref):
+    del near_ref
+    body = three_ref.shape[0] - 5
+    for q in range(body):
+        out_ref[q] = three_ref[4 + q]
+    tiles = slot_tiles(three_ref)
+    out_ref[body] = halves(flip(tiles[0]), tiles[1])
+    out_ref[body + 1] = halves(flip(tiles[2]), tiles[3])
+    out_ref[body + 2] = tiles[4]
+
+
+def far_tiles(three_ref, far_ref):
+    same = slot_tiles(three_ref)
+    body = three_ref.shape[0] - 5
+    a, b, c = [far_ref[body + k] for k in range(3)]
+    other = [flip(a), a, flip(b), b, c]
+    return [halves(x, y) for x, y in zip(same, other)]
+
+
+def near_tiles(one_ref, two_ref):
+    return [halves(a, flip(b)) for a, b in zip(slot_tiles(one_ref), slot_tiles(two_ref))]
+
+
+def cross_tiles(one_ref, two_ref):
+    return [halves(flip(a), b) for a, b in zip(slot_tiles(one_ref), slot_tiles(two_ref))]
+
+
+def early_kernel(
+    m0_ref, m1_ref, m2_ref, x0_ref, z1_ref, z2_ref, far_ref, bgrad_ref, bindex_ref, ggrad_ref
+):
+    del far_ref
+    own = message_table(m0_ref)
+    here = [halves(a, b) for a, b in zip(slot_tiles(m0_ref), slot_tiles(x0_ref))]
+    near = near_tiles(z1_ref, z2_ref)
+    work = [
+        body_work(here, own),
+        body_work(near, own),
+        garm_work(slot_tiles(m0_ref), own, message_table(x0_ref)),
+        garm_work(near_tiles(m1_ref, m2_ref), message_table(z1_ref), message_table(z2_ref)),
+    ]
+    out = gradients(work)
+    for n in range(2):
+        rows = slice(n * SUB, (n + 1) * SUB)
+        bgrad_ref[rows, :] = jnp.concatenate(out[n], axis=1)
+        ggrad_ref[rows, :] = jnp.concatenate(out[2 + n][:3], axis=1)
+    bindex_ref[:SUB, :] = here[4]
+    bindex_ref[SUB:, :] = near[4]
+
+
+def late_body_kernel(
+    m0_ref, z3_ref, near_ref, far_ref, bgrad_ref, bindex_ref, out_ref, stiff_ref
+):
+    own = message_table(m0_ref)
+    body = z3_ref.shape[0] - 5
+    near = [near_ref[2 * body + k] for k in range(5)]
+    far = far_tiles(z3_ref, far_ref)
+    grads = [
+        jnp.concatenate(rows, axis=1)
+        for rows in gradients([body_work(far, own), body_work(near, own)])
+    ]
+    index = jnp.concatenate([bindex_ref[...], far[4], near[4]], axis=0)
+    total = scatter(index, jnp.concatenate([bgrad_ref[...]] + grads, axis=0), out_ref.shape[1])
     for c in range(3):
         out_ref[c] = total[:, c * BLOCK : (c + 1) * BLOCK]
     stiff_ref[...] = total[:, 3 * BLOCK :]
 
 
-def last_garm_kernel(same_ref, other_ref, sent_ref, index_ref, *refs):
-    *earlier, out_ref = refs
-    grad = garm_batch(same_ref, other_ref, sent_ref)
-    grads = jnp.concatenate([ref[...] for ref in earlier] + [grad], axis=0)
+def late_garm_kernel(
+    m1_ref, m2_ref, m3_ref, z3_ref, near_ref, far_ref, ggrad_ref, index_ref, out_ref
+):
+    body = z3_ref.shape[0] - 5
+    step = body // 4
+    tables = [read_table(near_ref, n * body, step) for n in range(2)]
+    work = [
+        garm_work(slot_tiles(m3_ref), message_table(z3_ref), read_table(far_ref, 0, step)),
+        garm_work(cross_tiles(m1_ref, m2_ref), *tables),
+    ]
+    grads = [jnp.concatenate(rows[:3], axis=1) for rows in gradients(work)]
     index = jnp.concatenate([index_ref[k] for k in range(index_ref.shape[0])], axis=0)
-    total = scatter(index, grads, out_ref.shape[1])
+    total = scatter(index, jnp.concatenate([ggrad_ref[...]] + grads, axis=0), out_ref.shape[1])
     for c in range(3):
         out_ref[c] = total[:, c * BLOCK : (c + 1) * BLOCK]
 
@@ -285,7 +369,7 @@
     garm_out[...] = garm_ref[...]
 
 
-def stage_kernel(order, *refs):
+def stage_kernel(*refs):
     hbm, (index_ref, *out_refs), vmem, sems = refs[:7], refs[7:12], refs[12:19], refs[19]
     copies = [
         pltpu.make_async_copy(src, dst, sems.at[k]) for k, (src, dst) in enumerate(zip(hbm, vmem))
@@ -316,7 +400,11 @@
                 out_ref[4 + 4 * tiles, place, :] = jnp.full(
                     (1, BLOCK), pb_ref[s, owner].astype(f32), f32
                 )
-                index_ref[order.index(k), place, :] = jnp.full((1, BLOCK), g.astype(f32), f32)
+                if k in (1, 2):
+                    spot, line = 1 + 2 * x, (k - 1) * cap + s
+                else:
+                    spot, line = (0 if k == 0 else 2), x * cap + s
+                index_ref[spot, line : line + 1, :] = jnp.full((1, BLOCK), g.astype(f32), f32)
 
 
 def staged(garment, cotangent, body_points, stiffness, pg, pb, pc):
@@ -325,7 +413,6 @@
     blocks = points // BLOCK
     tiles = blocks // SUB
     garm_n = lax.axis_size("garm")
-    order = (0, 3, 1, 2)
     message = jax.ShapeDtypeStruct((5 + 4 * tiles, SUB, BLOCK), f32)
     arrays = (
         pg,
@@ -337,7 +424,7 @@
         stiffness.reshape(tiles, SUB, BLOCK),
     )
     index, *sent = pl.pallas_call(
-        functools.partial(stage_kernel, order),
+        stage_kernel,
         out_shape=[jax.ShapeDtypeStruct((garm_n, SUB, BLOCK), f32)] + [message] * garm_n,
         in_specs=[pl.BlockSpec(memory_space=pltpu.HBM)] * len(arrays),
         out_specs=[pl.BlockSpec(memory_space=pltpu.VMEM)] * (garm_n + 1),
@@ -354,39 +441,52 @@
     def along_body(value):
         return lax.ppermute(value, "body", [(0, 1), (1, 0)])
 
-    same = {k: along_garm(k) for k in (3, 2, 1)}
-    same[0] = sent[0]
-    other = {k: along_body(same[k]) for k in (0, 1, 2, 3)}
-    body_grads, body_index, garm_grads = [], [], []
-    for k in order[:-1]:
-        out = call(
-            both_kernel,
-            (
-                jax.ShapeDtypeStruct((SUB, 4 * BLOCK), f32),
-                jax.ShapeDtypeStruct((SUB, BLOCK), f32),
-                jax.ShapeDtypeStruct((SUB, 3 * BLOCK), f32),
-            ),
-            [],
-            (),
-            (same[k], other[k], sent[0], sent[k]),
-        )
-        body_grads.append(out[0])
-        body_index.append(out[1])
-        garm_grads.append(out[2])
-    k = order[-1]
+    z3, z2, z1 = [along_garm(k) for k in (3, 2, 1)]
+    x0 = along_body(sent[0])
+    body = 4 * tiles
+    near = call(
+        near_bundle_kernel,
+        jax.ShapeDtypeStruct((2 * body + 5, SUB, BLOCK), f32),
+        [],
+        (),
+        (z1, z2),
+    )
+    far = call(
+        far_bundle_kernel,
+        jax.ShapeDtypeStruct((body + 3, SUB, BLOCK), f32),
+        [],
+        (),
+        (z3, near),
+    )
+    near_other, far_other = along_body(near), along_body(far)
+    bgrad, bindex, ggrad = call(
+        early_kernel,
+        (
+            jax.ShapeDtypeStruct((2 * SUB, 4 * BLOCK), f32),
+            jax.ShapeDtypeStruct((2 * SUB, BLOCK), f32),
+            jax.ShapeDtypeStruct((2 * SUB, 3 * BLOCK), f32),
+        ),
+        [],
+        (),
+        (sent[0], sent[1], sent[2], x0, z1, z2, far),
+    )
     body_shape = jax.ShapeDtypeStruct((3, blocks, BLOCK), f32)
     stiff_shape = jax.ShapeDtypeStruct((blocks, BLOCK), f32)
     garm_shape = jax.ShapeDtypeStruct((3, verts // BLOCK, BLOCK), f32)
     body_total, stiff = call(
-        last_body_kernel,
+        late_body_kernel,
         (body_shape, stiff_shape),
         [],
         (),
-        (same[k], other[k], sent[0], *body_grads, *body_index),
+        (sent[0], z3, near_other, far_other, bgrad, bindex),
     )
     stiff_other = lax.ppermute(stiff, "frame", [(0, 1), (1, 0)])
     garm_total = call(
-        last_garm_kernel, garm_shape, [], (), (same[k], other[k], sent[k], index, *garm_grads)
+        late_garm_kernel,
+        garm_shape,
+        [],
+        (),
+        (sent[1], sent[2], sent[3], z3, near_other, far_other, ggrad, index),
     )
     return call(
         final_kernel,
@@ -395,19 +495,6 @@
         (),
         (garm_total, body_total, stiff, stiff_other),
     )
-
-
-def call(kernel, out_shape, scratch, scalars, arrays):
-    specs = [pl.BlockSpec(memory_space=pltpu.SMEM)] * len(scalars)
-    specs += [pl.BlockSpec(memory_space=pltpu.VMEM)] * len(arrays)
-    return pl.pallas_call(
-        kernel,
-        out_shape=out_shape,
-        in_specs=specs,
-        out_specs=jax.tree.map(lambda _: pl.BlockSpec(memory_space=pltpu.VMEM), out_shape),
-        scratch_shapes=scratch,
-        compiler_params=pltpu.CompilerParams(vmem_limit_bytes=VMEM_LIMIT),
-    )(*scalars, *arrays)
 
 
 def per_device(garment, cotangent, body_points, stiffness, pair_garment, pair_body, pair_count):

time: 20.4 us -> 20.4 us (level)
  waiting for transfers between devices: 2.42 us -> 5.83 us
  Pallas kernels: 6.42 us -> 4.51 us
  starting transfers between devices: 10.7 us -> 9.27 us
    pallas_call x6, Pallas kernels: 5.43 us -> 3.52 us  [call(): pl.pallas_call(kernel, out_shape=out_shape, in_specs=specs, out_specs=jax...]
    ppermute x3, waiting for transfers between devices: 1.98 us -> 3.82 us  [along_garm(): return lax.ppermute(sent[k], 'garm', [(z, z ^ k) for z in range(garm_n)])]
    ppermute x4 -> x3, waiting for transfers between devices: 0.03 us -> 1.75 us  [along_body(): return lax.ppermute(value, 'body', [(0, 1), (1, 0)])]
    ppermute x4 -> x3, starting transfers between devices: 5.01 us -> 3.58 us  [along_body(): return lax.ppermute(value, 'body', [(0, 1), (1, 0)])]
  transfers between devices with their start and end apart: 8 -> 7, of which waited for: 2 -> 4; matrix products, arithmetic and copies ran while one was open for 0% -> 0% of each run, Pallas kernels for 20% -> 10%
where the time goes in v4:
time: 20.4 us; the launch traced here: 20.3 us
  starting transfers between devices  9.27 us (45%)
  waiting for transfers between devices  5.83 us (29%)
  Pallas kernels  4.51 us (22%)
  between operations  0.67 us (3%)
    ppermute x3, starting transfers between devices, along_garm(): return lax.ppermute(sent[k], 'garm', [(z, z ^ k) for z in range(garm_n)])  5.68 us
    ppermute x3, waiting for transfers between devices, along_garm(): return lax.ppermute(sent[k], 'garm', [(z, z ^ k) for z in range(garm_n)])  3.82 us
    ppermute x3, starting transfers between devices, along_body(): return lax.ppermute(value, 'body', [(0, 1), (1, 0)])  3.58 us
    pallas_call x6, Pallas kernels, call(): pl.pallas_call(kernel, out_shape=out_shape, in_specs=specs, out_specs=jax...  3.52 us
    ppermute x3, waiting for transfers between devices, along_body(): return lax.ppermute(value, 'body', [(0, 1), (1, 0)])  1.75 us
    pallas_call x1, Pallas kernels, staged(): pl.pallas_call(stage_kernel, out_shape=[jax.ShapeDtypeStruct((garm_n, SUB...  0.99 us
  transfers between devices with their start and end apart: 7, of which 4 were waited for; matrix products, arithmetic and copies ran while one was open for 0% of the time, Pallas kernels for 10%

profile of v4, /device:TPU:0, one launch (start us, length us, event | category | flops | bytes accessed | tf_op | source)
XLA Modules:
  0.0 20.3 jit_solution(12939403028641463663)
XLA Ops:
  0.6 1.0 %shard_map.94 = (f32[4,8,128]{2,1,0:T(8,128)S(1)}, f32[13,8,128]{2,1,0:T(8,128)S(1)}, f32[13,8,128]{2,1,0:T(8,128)S(1)}, f32[13,8,128]{2,1,0:T(8,128)S(1)}, f32[13,8,128]{2,1,0:T(8,128)S(1)}) custom-call(s32[4,8]{1,0:T(4,128)} %bitcast.18, s32[4,8]{1,0:T(4,128)} %bitcast.19, s32[1,8]{1,0:T(1,128)} %bitcast.20, f32[3,32,128]{2,1,0:T(8,128)} %bitcast.14, ...), custom_call_target="tpu_custom_call" | custom-call | tf_op jit(solution)/shard_map/pallas_call | solution.py:426
  1.6 3.1 %collective-permute-start.1 = (f32[13,8,128]{2,1,0:T(8,128)S(1)}, f32[13,8,128]{2,1,0:T(8,128)S(1)}, u32[]{:S(2)}, u32[]{:S(2)}) collective-permute-start(f32[13,8,128]{2,1,0:T(8,128)S(1)} %get-tuple-element.16.m1_ref), channel_id=1, source_target_pairs={{0,4},{4,0},{8,12},{12,8},{1,5},{5,1},{9,13},{13,9},{2,6},{6,2},{1... | collective-permute-start | bytes 159752 | tf_op jit(solution)/shard_map/ppermute | solution.py:439
  4.7 2.6 %collective-permute-start.2 = (f32[13,8,128]{2,1,0:T(8,128)S(1)}, f32[13,8,128]{2,1,0:T(8,128)S(1)}, u32[]{:S(2)}, u32[]{:S(2)}) collective-permute-start(f32[13,8,128]{2,1,0:T(8,128)S(1)} %get-tuple-element.17.m2_ref), channel_id=1, source_target_pairs={{0,8},{4,12},{8,0},{12,4},{1,9},{5,13},{9,1},{13,5},{2,10},{6,14},... | collective-permute-start | bytes 159752 | tf_op jit(solution)/shard_map/ppermute | solution.py:439
  7.3 0.0 collective-permute-start
  7.3 0.0 collective-permute-done.1.one_ref.z1_ref
  7.3 3.5 %collective-permute-done.2.two_ref.z2_ref = f32[13,8,128]{2,1,0:T(8,128)S(1)} collective-permute-done((f32[13,8,128]{2,1,0:T(8,128)S(1)}, f32[13,8,128]{2,1,0:T(8,128)S(1)}, u32[]{:S(2)}, u32[]{:S(2)}) %collective-permute-start.2) | collective-permute-done | bytes 53280 | tf_op jit(solution)/shard_map/ppermute | solution.py:439
  10.8 1.6 %collective-permute-start.3 = (f32[21,8,128]{2,1,0:T(8,128)S(1)}, f32[21,8,128]{2,1,0:T(8,128)S(1)}, u32[]{:S(2)}, u32[]{:S(2)}) collective-permute-start(f32[21,8,128]{2,1,0:T(8,128)S(1)} %shard_map.95.near_ref), channel_id=1, source_target_pairs={{0,2},{2,0},{1,3},{3,1},{4,6},{6,4},{5,7},{7,5},{8,10},{10,8},{9,1... | collective-permute-start | bytes 258056 | tf_op jit(solution)/shard_map/ppermute | solution.py:442
  12.3 0.5 %collective-permute-start.5 = (f32[13,8,128]{2,1,0:T(8,128)S(1)}, f32[13,8,128]{2,1,0:T(8,128)S(1)}, u32[]{:S(2)}, u32[]{:S(2)}) collective-permute-start(f32[13,8,128]{2,1,0:T(8,128)S(1)} %get-tuple-element.19.m0_ref), channel_id=1, source_target_pairs={{0,2},{2,0},{1,3},{3,1},{4,6},{6,4},{5,7},{7,5},{8,10},{10,8},{9,1... | collective-permute-start | bytes 159752 | tf_op jit(solution)/shard_map/ppermute | solution.py:442
  12.9 0.4 %collective-permute-done.three_ref.z3_ref = f32[13,8,128]{2,1,0:T(8,128)S(1)} collective-permute-done((f32[13,8,128]{2,1,0:T(8,128)S(1)}, f32[13,8,128]{2,1,0:T(8,128)S(1)}, u32[]{:S(2)}, u32[]{:S(2)}) %collective-permute-start) | collective-permute-done | bytes 53280 | tf_op jit(solution)/shard_map/ppermute | solution.py:439
  13.2 1.5 %collective-permute-start.4 = (f32[11,8,128]{2,1,0:T(8,128)S(1)}, f32[11,8,128]{2,1,0:T(8,128)S(1)}, u32[]{:S(2)}, u32[]{:S(2)}) collective-permute-start(f32[11,8,128]{2,1,0:T(8,128)S(1)} %shard_map.96.far_ref), channel_id=1, source_target_pairs={{0,2},{2,0},{1,3},{3,1},{4,6},{6,4},{5,7},{7,5},{8,10},{10,8},{9,1... | collective-permute-start | bytes 135176 | tf_op jit(solution)/shard_map/ppermute | solution.py:442
  14.7 1.7 %collective-permute-done.5.x0_ref = f32[13,8,128]{2,1,0:T(8,128)S(1)} collective-permute-done((f32[13,8,128]{2,1,0:T(8,128)S(1)}, f32[13,8,128]{2,1,0:T(8,128)S(1)}, u32[]{:S(2)}, u32[]{:S(2)}) %collective-permute-start.5) | collective-permute-done | bytes 53280 | tf_op jit(solution)/shard_map/ppermute | solution.py:442
  16.5 1.1 %shard_map.97 = (f32[16,512]{1,0:T(8,128)S(1)}, f32[16,128]{1,0:T(8,128)S(1)}, f32[16,384]{1,0:T(8,128)S(1)}) custom-call(f32[13,8,128]{2,1,0:T(8,128)S(1)} %get-tuple-element.19.m0_ref, f32[13,8,128]{2,1,0:T(8,128)S(1)} %get-tuple-element.16.m1_ref, f32[13,8,128]{2,1,0:T(8,128)S(1)} %get-tuple-element.17.m2_ref, ...), custom_call_target="tpu_custom_call" | custom-call | tf_op jit(solution)/shard_map/pallas_call | solution.py:218
  17.5 0.0 collective-permute-done.4.far_ref
  17.6 0.0 collective-permute-done.3.near_ref
  17.6 0.9 %shard_map.99 = (f32[3,16,128]{2,1,0:T(8,128)S(1)}, f32[16,128]{1,0:T(8,128)S(1)}) custom-call(f32[13,8,128]{2,1,0:T(8,128)S(1)} %get-tuple-element.19.m0_ref, f32[13,8,128]{2,1,0:T(8,128)S(1)} %collective-permute-done.three_ref.z3_ref, f32[21,8,128]{2,1,0:T(8,128)S(1)} %collective-permute-done.3.near_ref, f32[11,8,128]{2,1,0:T(8,128)S(1)} %collective-permute-done.4.far_ref, ...), custom_call_target="tpu_custom_call" | custom-call | tf_op jit(solution)/shard_map/pallas_call | solution.py:218
  18.4 0.0 collective-permute-start.6
  18.4 0.9 %shard_map.98.garm_ref = f32[3,32,128]{2,1,0:T(8,128)S(1)} custom-call(f32[13,8,128]{2,1,0:T(8,128)S(1)} %get-tuple-element.16.m1_ref, f32[13,8,128]{2,1,0:T(8,128)S(1)} %get-tuple-element.17.m2_ref, f32[13,8,128]{2,1,0:T(8,128)S(1)} %get-tuple-element.18.m3_ref, f32[13,8,128]{2,1,0:T(8,128)S(1)} %collective-permute-done.three_ref.z3_ref, ...), custom_call_target="tpu_custom_call" | custom-call | tf_op jit(solution)/shard_map/pallas_call | solution.py:218
  19.4 0.3 %collective-permute-done.6.other_ref = f32[16,128]{1,0:T(8,128)S(1)} collective-permute-done((f32[16,128]{1,0:T(8,128)S(1)}, f32[16,128]{1,0:T(8,128)S(1)}, u32[]{:S(2)}, u32[]{:S(2)}) %collective-permute-start.6) | collective-permute-done | bytes 8224 | tf_op jit(solution)/shard_map/ppermute | solution.py:483
  19.6 0.6 %shard_map.100 = (f32[3,32,128]{2,1,0:T(8,128)}, f32[3,16,128]{2,1,0:T(8,128)}, f32[16,128]{1,0:T(8,128)}) custom-call(f32[3,32,128]{2,1,0:T(8,128)S(1)} %shard_map.98.garm_ref, f32[3,16,128]{2,1,0:T(8,128)S(1)} %get-tuple-element.24.body_ref, f32[16,128]{1,0:T(8,128)S(1)} %get-tuple-element.25.mine_ref, f32[16,128]{1,0:T(8,128)S(1)} %collective-permute-done.6.other_ref), custom_call_target="tpu_custom_call" | custom-call | tf_op jit(solution)/shard_map/pallas_call | solution.py:218
  (2 shorter events, 0.0 us)
Async XLA Ops:
  1.6 5.7 %collective-permute-start.1 = (f32[13,8,128]{2,1,0:T(8,128)S(1)}, f32[13,8,128]{2,1,0:T(8,128)S(1)}, u32[]{:S(2)}, u32[]{:S(2)}) collective-permute-start(f32[13,8,128]{2,1,0:T(8,128)S(1)} %get-tuple-element.16.m1_ref), channel_id=1, source_target_pairs={{0,4},{4,0},{8,12},{12,8},{1,5},{5,1},{9,13},{13,9},{2,6},{6,2},{1... | collective-permute-start | bytes 159752 | tf_op jit(solution)/shard_map/ppermute | solution.py:439
  4.7 6.1 %collective-permute-start.2 = (f32[13,8,128]{2,1,0:T(8,128)S(1)}, f32[13,8,128]{2,1,0:T(8,128)S(1)}, u32[]{:S(2)}, u32[]{:S(2)}) collective-permute-start(f32[13,8,128]{2,1,0:T(8,128)S(1)} %get-tuple-element.17.m2_ref), channel_id=1, source_target_pairs={{0,8},{4,12},{8,0},{12,4},{1,9},{5,13},{9,1},{13,5},{2,10},{6,14},... | collective-permute-start | bytes 159752 | tf_op jit(solution)/shard_map/ppermute | solution.py:439
  7.3 5.9 %collective-permute-start = (f32[13,8,128]{2,1,0:T(8,128)S(1)}, f32[13,8,128]{2,1,0:T(8,128)S(1)}, u32[]{:S(2)}, u32[]{:S(2)}) collective-permute-start(f32[13,8,128]{2,1,0:T(8,128)S(1)} %get-tuple-element.18.m3_ref), channel_id=1, source_target_pairs={{0,12},{4,8},{8,4},{12,0},{1,13},{5,9},{9,5},{13,1},{2,14},{6,10},... | collective-permute-start | bytes 159752 | tf_op jit(solution)/shard_map/ppermute | solution.py:439
  10.8 6.8 %collective-permute-start.3 = (f32[21,8,128]{2,1,0:T(8,128)S(1)}, f32[21,8,128]{2,1,0:T(8,128)S(1)}, u32[]{:S(2)}, u32[]{:S(2)}) collective-permute-start(f32[21,8,128]{2,1,0:T(8,128)S(1)} %shard_map.95.near_ref), channel_id=1, source_target_pairs={{0,2},{2,0},{1,3},{3,1},{4,6},{6,4},{5,7},{7,5},{8,10},{10,8},{9,1... | collective-permute-start | bytes 258056 | tf_op jit(solution)/shard_map/ppermute | solution.py:442
  12.3 4.1 %collective-permute-start.5 = (f32[13,8,128]{2,1,0:T(8,128)S(1)}, f32[13,8,128]{2,1,0:T(8,128)S(1)}, u32[]{:S(2)}, u32[]{:S(2)}) collective-permute-start(f32[13,8,128]{2,1,0:T(8,128)S(1)} %get-tuple-element.19.m0_ref), channel_id=1, source_target_pairs={{0,2},{2,0},{1,3},{3,1},{4,6},{6,4},{5,7},{7,5},{8,10},{10,8},{9,1... | collective-permute-start | bytes 159752 | tf_op jit(solution)/shard_map/ppermute | solution.py:442
  13.2 4.3 %collective-permute-start.4 = (f32[11,8,128]{2,1,0:T(8,128)S(1)}, f32[11,8,128]{2,1,0:T(8,128)S(1)}, u32[]{:S(2)}, u32[]{:S(2)}) collective-permute-start(f32[11,8,128]{2,1,0:T(8,128)S(1)} %shard_map.96.far_ref), channel_id=1, source_target_pairs={{0,2},{2,0},{1,3},{3,1},{4,6},{6,4},{5,7},{7,5},{8,10},{10,8},{9,1... | collective-permute-start | bytes 135176 | tf_op jit(solution)/shard_map/ppermute | solution.py:442
  18.4 1.2 %collective-permute-start.6 = (f32[16,128]{1,0:T(8,128)S(1)}, f32[16,128]{1,0:T(8,128)S(1)}, u32[]{:S(2)}, u32[]{:S(2)}) collective-permute-start(f32[16,128]{1,0:T(8,128)S(1)} %get-tuple-element.25.mine_ref), channel_id=1, source_target_pairs={{0,1},{1,0},{2,3},{3,2},{4,5},{5,4},{6,7},{7,6},{8,9},{9,8},{10,11... | collective-permute-start | bytes 24584 | tf_op jit(solution)/shard_map/ppermute | solution.py:483

commit v5 on v4

--- a/solution.py
+++ b/solution.py
@@ -9,6 +9,7 @@
 
 BLOCK = 128
 SUB = 8
+DISTANCES = (3, 2, 1)
 VMEM_LIMIT = 32 * 1024 * 1024
 
 amplitude = 0.05
@@ -270,7 +271,8 @@
     return read_table(ref, 4, (ref.shape[0] - 5) // 4)
 
 
-def near_bundle_kernel(one_ref, two_ref, out_ref):
+def near_bundle_kernel(one_ref, two_ref, x0_ref, out_ref):
+    del x0_ref
     body = one_ref.shape[0] - 5
     for q in range(body):
         out_ref[q] = one_ref[4 + q]
@@ -400,8 +402,8 @@
                 out_ref[4 + 4 * tiles, place, :] = jnp.full(
                     (1, BLOCK), pb_ref[s, owner].astype(f32), f32
                 )
-                if k in (1, 2):
-                    spot, line = 1 + 2 * x, (k - 1) * cap + s
+                if k in DISTANCES[:2]:
+                    spot, line = 1 + 2 * x, DISTANCES.index(k) * cap + s
                 else:
                     spot, line = (0 if k == 0 else 2), x * cap + s
                 index_ref[spot, line : line + 1, :] = jnp.full((1, BLOCK), g.astype(f32), f32)
@@ -441,7 +443,8 @@
     def along_body(value):
         return lax.ppermute(value, "body", [(0, 1), (1, 0)])
 
-    z3, z2, z1 = [along_garm(k) for k in (3, 2, 1)]
+    first, second, third = [along_garm(k) for k in DISTANCES]
+    one, two, three = [sent[k] for k in DISTANCES]
     x0 = along_body(sent[0])
     body = 4 * tiles
     near = call(
@@ -449,14 +452,14 @@
         jax.ShapeDtypeStruct((2 * body + 5, SUB, BLOCK), f32),
         [],
         (),
-        (z1, z2),
+        (first, second, x0),
     )
     far = call(
         far_bundle_kernel,
         jax.ShapeDtypeStruct((body + 3, SUB, BLOCK), f32),
         [],
         (),
-        (z3, near),
+        (third, near),
     )
     near_other, far_other = along_body(near), along_body(far)
     bgrad, bindex, ggrad = call(
@@ -468,7 +471,7 @@
         ),
         [],
         (),
-        (sent[0], sent[1], sent[2], x0, z1, z2, far),
+        (sent[0], one, two, x0, first, second, far),
     )
     body_shape = jax.ShapeDtypeStruct((3, blocks, BLOCK), f32)
     stiff_shape = jax.ShapeDtypeStruct((blocks, BLOCK), f32)
@@ -478,7 +481,7 @@
         (body_shape, stiff_shape),
         [],
         (),
-        (sent[0], z3, near_other, far_other, bgrad, bindex),
+        (sent[0], third, near_other, far_other, bgrad, bindex),
     )
     stiff_other = lax.ppermute(stiff, "frame", [(0, 1), (1, 0)])
     garm_total = call(
@@ -486,7 +489,7 @@
         garm_shape,
         [],
         (),
-        (sent[1], sent[2], sent[3], z3, near_other, far_other, ggrad, index),
+        (one, two, three, third, near_other, far_other, ggrad, index),
     )
     return call(
         final_kernel,

time: 20.4 us -> 20.4 us (level)
  waiting for transfers between devices: 5.83 us -> 5.51 us
  starting transfers between devices: 9.27 us -> 9.56 us
    ppermute x3, waiting for transfers between devices: 3.82 us -> 2.76 us  [along_garm(): return lax.ppermute(sent[k], 'garm', [(z, z ^ k) for z in range(garm_n)])]
    ppermute x3, waiting for transfers between devices: 1.75 us -> 2.5 us  [along_body(): return lax.ppermute(value, 'body', [(0, 1), (1, 0)])]
    ppermute x3, starting transfers between devices: 5.68 us -> 5.9 us  [along_garm(): return lax.ppermute(sent[k], 'garm', [(z, z ^ k) for z in range(garm_n)])]
  transfers between devices with their start and end apart: 7 -> 7, of which waited for: 4 -> 3; matrix products, arithmetic and copies ran while one was open for 0% -> 0% of each run, Pallas kernels for 10% -> 10%
where the time goes in v5:
time: 20.4 us; the launch traced here: 20.2 us
  starting transfers between devices  9.56 us (47%)
  waiting for transfers between devices  5.51 us (27%)
  Pallas kernels  4.51 us (22%)
  between operations  0.66 us (3%)
    ppermute x3, starting transfers between devices, along_garm(): return lax.ppermute(sent[k], 'garm', [(z, z ^ k) for z in range(garm_n)])  5.9 us
    ppermute x3, starting transfers between devices, along_body(): return lax.ppermute(value, 'body', [(0, 1), (1, 0)])  3.66 us
    pallas_call x6, Pallas kernels, call(): pl.pallas_call(kernel, out_shape=out_shape, in_specs=specs, out_specs=jax...  3.52 us
    ppermute x3, waiting for transfers between devices, along_garm(): return lax.ppermute(sent[k], 'garm', [(z, z ^ k) for z in range(garm_n)])  2.76 us
    ppermute x3, waiting for transfers between devices, along_body(): return lax.ppermute(value, 'body', [(0, 1), (1, 0)])  2.5 us
    pallas_call x1, Pallas kernels, staged(): pl.pallas_call(stage_kernel, out_shape=[jax.ShapeDtypeStruct((garm_n, SUB...  0.99 us
  transfers between devices with their start and end apart: 7, of which 3 were waited for; matrix products, arithmetic and copies ran while one was open for 0% of the time, Pallas kernels for 10%

profile of v5, /device:TPU:0, one launch (start us, length us, event | category | flops | bytes accessed | tf_op | source)
XLA Modules:
  0.0 20.2 jit_solution(15359350795012842188)
XLA Ops:
  0.6 1.0 %shard_map.94 = (f32[4,8,128]{2,1,0:T(8,128)S(1)}, f32[13,8,128]{2,1,0:T(8,128)S(1)}, f32[13,8,128]{2,1,0:T(8,128)S(1)}, f32[13,8,128]{2,1,0:T(8,128)S(1)}, f32[13,8,128]{2,1,0:T(8,128)S(1)}) custom-call(s32[4,8]{1,0:T(4,128)} %bitcast.18, s32[4,8]{1,0:T(4,128)} %bitcast.19, s32[1,8]{1,0:T(1,128)} %bitcast.20, f32[3,32,128]{2,1,0:T(8,128)} %bitcast.14, ...), custom_call_target="tpu_custom_call" | custom-call | tf_op jit(solution)/shard_map/pallas_call | solution.py:428
  1.6 5.1 %collective-permute-start.1 = (f32[13,8,128]{2,1,0:T(8,128)S(1)}, f32[13,8,128]{2,1,0:T(8,128)S(1)}, u32[]{:S(2)}, u32[]{:S(2)}) collective-permute-start(f32[13,8,128]{2,1,0:T(8,128)S(1)} %get-tuple-element.16.m1_ref), channel_id=1, source_target_pairs={{0,12},{4,8},{8,4},{12,0},{1,13},{5,9},{9,5},{13,1},{2,14},{6,10},... | collective-permute-start | bytes 159752 | tf_op jit(solution)/shard_map/ppermute | solution.py:441
  6.7 0.0 collective-permute-start.2
  6.8 1.5 %collective-permute-start.3 = (f32[13,8,128]{2,1,0:T(8,128)S(1)}, f32[13,8,128]{2,1,0:T(8,128)S(1)}, u32[]{:S(2)}, u32[]{:S(2)}) collective-permute-start(f32[13,8,128]{2,1,0:T(8,128)S(1)} %get-tuple-element.19.m0_ref), channel_id=1, source_target_pairs={{0,2},{2,0},{1,3},{3,1},{4,6},{6,4},{5,7},{7,5},{8,10},{10,8},{9,1... | collective-permute-start | bytes 159752 | tf_op jit(solution)/shard_map/ppermute | solution.py:444
  8.2 0.8 %collective-permute-start = (f32[13,8,128]{2,1,0:T(8,128)S(1)}, f32[13,8,128]{2,1,0:T(8,128)S(1)}, u32[]{:S(2)}, u32[]{:S(2)}) collective-permute-start(f32[13,8,128]{2,1,0:T(8,128)S(1)} %get-tuple-element.18.m3_ref), channel_id=1, source_target_pairs={{0,4},{4,0},{8,12},{12,8},{1,5},{5,1},{9,13},{13,9},{2,6},{6,2},{1... | collective-permute-start | bytes 159752 | tf_op jit(solution)/shard_map/ppermute | solution.py:441
  9.0 0.0 collective-permute-done.1.one_ref.z1_ref
  9.1 2.7 %collective-permute-done.2.two_ref.z2_ref = f32[13,8,128]{2,1,0:T(8,128)S(1)} collective-permute-done((f32[13,8,128]{2,1,0:T(8,128)S(1)}, f32[13,8,128]{2,1,0:T(8,128)S(1)}, u32[]{:S(2)}, u32[]{:S(2)}) %collective-permute-start.2) | collective-permute-done | bytes 53280 | tf_op jit(solution)/shard_map/ppermute | solution.py:441
  11.8 0.0 collective-permute-done.3.x0_ref
  11.8 1.6 %collective-permute-start.4 = (f32[21,8,128]{2,1,0:T(8,128)S(1)}, f32[21,8,128]{2,1,0:T(8,128)S(1)}, u32[]{:S(2)}, u32[]{:S(2)}) collective-permute-start(f32[21,8,128]{2,1,0:T(8,128)S(1)} %shard_map.95.near_ref), channel_id=1, source_target_pairs={{0,2},{2,0},{1,3},{3,1},{4,6},{6,4},{5,7},{7,5},{8,10},{10,8},{9,1... | collective-permute-start | bytes 258056 | tf_op jit(solution)/shard_map/ppermute | solution.py:444
  13.4 0.0 collective-permute-done.three_ref.z3_ref
  13.4 0.6 %collective-permute-start.5 = (f32[11,8,128]{2,1,0:T(8,128)S(1)}, f32[11,8,128]{2,1,0:T(8,128)S(1)}, u32[]{:S(2)}, u32[]{:S(2)}) collective-permute-start(f32[11,8,128]{2,1,0:T(8,128)S(1)} %shard_map.96.far_ref), channel_id=1, source_target_pairs={{0,2},{2,0},{1,3},{3,1},{4,6},{6,4},{5,7},{7,5},{8,10},{10,8},{9,1... | collective-permute-start | bytes 135176 | tf_op jit(solution)/shard_map/ppermute | solution.py:444
  14.0 1.1 %shard_map.97 = (f32[16,512]{1,0:T(8,128)S(1)}, f32[16,128]{1,0:T(8,128)S(1)}, f32[16,384]{1,0:T(8,128)S(1)}) custom-call(f32[13,8,128]{2,1,0:T(8,128)S(1)} %get-tuple-element.19.m0_ref, f32[13,8,128]{2,1,0:T(8,128)S(1)} %get-tuple-element.16.m1_ref, f32[13,8,128]{2,1,0:T(8,128)S(1)} %get-tuple-element.17.m2_ref, ...), custom_call_target="tpu_custom_call" | custom-call | tf_op jit(solution)/shard_map/pallas_call | solution.py:219
  15.0 2.5 %collective-permute-done.5.far_ref = f32[11,8,128]{2,1,0:T(8,128)S(1)} collective-permute-done((f32[11,8,128]{2,1,0:T(8,128)S(1)}, f32[11,8,128]{2,1,0:T(8,128)S(1)}, u32[]{:S(2)}, u32[]{:S(2)}) %collective-permute-start.5) | collective-permute-done | bytes 45088 | tf_op jit(solution)/shard_map/ppermute | solution.py:444
  17.5 0.0 collective-permute-done.4.near_ref
  17.5 0.9 %shard_map.99 = (f32[3,16,128]{2,1,0:T(8,128)S(1)}, f32[16,128]{1,0:T(8,128)S(1)}) custom-call(f32[13,8,128]{2,1,0:T(8,128)S(1)} %get-tuple-element.19.m0_ref, f32[13,8,128]{2,1,0:T(8,128)S(1)} %collective-permute-done.three_ref.z3_ref, f32[21,8,128]{2,1,0:T(8,128)S(1)} %collective-permute-done.4.near_ref, f32[11,8,128]{2,1,0:T(8,128)S(1)} %collective-permute-done.5.far_ref, ...), custom_call_target="tpu_custom_call" | custom-call | tf_op jit(solution)/shard_map/pallas_call | solution.py:219
  18.4 0.0 collective-permute-start.6
  18.4 0.9 %shard_map.98.garm_ref = f32[3,32,128]{2,1,0:T(8,128)S(1)} custom-call(f32[13,8,128]{2,1,0:T(8,128)S(1)} %get-tuple-element.16.m1_ref, f32[13,8,128]{2,1,0:T(8,128)S(1)} %get-tuple-element.17.m2_ref, f32[13,8,128]{2,1,0:T(8,128)S(1)} %get-tuple-element.18.m3_ref, f32[13,8,128]{2,1,0:T(8,128)S(1)} %collective-permute-done.three_ref.z3_ref, ...), custom_call_target="tpu_custom_call" | custom-call | tf_op jit(solution)/shard_map/pallas_call | solution.py:219
  19.3 0.3 %collective-permute-done.6.other_ref = f32[16,128]{1,0:T(8,128)S(1)} collective-permute-done((f32[16,128]{1,0:T(8,128)S(1)}, f32[16,128]{1,0:T(8,128)S(1)}, u32[]{:S(2)}, u32[]{:S(2)}) %collective-permute-start.6) | collective-permute-done | bytes 8224 | tf_op jit(solution)/shard_map/ppermute | solution.py:486
  19.6 0.6 %shard_map.100 = (f32[3,32,128]{2,1,0:T(8,128)}, f32[3,16,128]{2,1,0:T(8,128)}, f32[16,128]{1,0:T(8,128)}) custom-call(f32[3,32,128]{2,1,0:T(8,128)S(1)} %shard_map.98.garm_ref, f32[3,16,128]{2,1,0:T(8,128)S(1)} %get-tuple-element.24.body_ref, f32[16,128]{1,0:T(8,128)S(1)} %get-tuple-element.25.mine_ref, f32[16,128]{1,0:T(8,128)S(1)} %collective-permute-done.6.other_ref), custom_call_target="tpu_custom_call" | custom-call | tf_op jit(solution)/shard_map/pallas_call | solution.py:219
  (2 shorter events, 0.0 us)
Async XLA Ops:
  1.6 7.4 %collective-permute-start.1 = (f32[13,8,128]{2,1,0:T(8,128)S(1)}, f32[13,8,128]{2,1,0:T(8,128)S(1)}, u32[]{:S(2)}, u32[]{:S(2)}) collective-permute-start(f32[13,8,128]{2,1,0:T(8,128)S(1)} %get-tuple-element.16.m1_ref), channel_id=1, source_target_pairs={{0,12},{4,8},{8,4},{12,0},{1,13},{5,9},{9,5},{13,1},{2,14},{6,10},... | collective-permute-start | bytes 159752 | tf_op jit(solution)/shard_map/ppermute | solution.py:441
  6.7 5.0 %collective-permute-start.2 = (f32[13,8,128]{2,1,0:T(8,128)S(1)}, f32[13,8,128]{2,1,0:T(8,128)S(1)}, u32[]{:S(2)}, u32[]{:S(2)}) collective-permute-start(f32[13,8,128]{2,1,0:T(8,128)S(1)} %get-tuple-element.17.m2_ref), channel_id=1, source_target_pairs={{0,8},{4,12},{8,0},{12,4},{1,9},{5,13},{9,1},{13,5},{2,10},{6,14},... | collective-permute-start | bytes 159752 | tf_op jit(solution)/shard_map/ppermute | solution.py:441
  6.8 5.0 %collective-permute-start.3 = (f32[13,8,128]{2,1,0:T(8,128)S(1)}, f32[13,8,128]{2,1,0:T(8,128)S(1)}, u32[]{:S(2)}, u32[]{:S(2)}) collective-permute-start(f32[13,8,128]{2,1,0:T(8,128)S(1)} %get-tuple-element.19.m0_ref), channel_id=1, source_target_pairs={{0,2},{2,0},{1,3},{3,1},{4,6},{6,4},{5,7},{7,5},{8,10},{10,8},{9,1... | collective-permute-start | bytes 159752 | tf_op jit(solution)/shard_map/ppermute | solution.py:444
  8.2 5.2 %collective-permute-start = (f32[13,8,128]{2,1,0:T(8,128)S(1)}, f32[13,8,128]{2,1,0:T(8,128)S(1)}, u32[]{:S(2)}, u32[]{:S(2)}) collective-permute-start(f32[13,8,128]{2,1,0:T(8,128)S(1)} %get-tuple-element.18.m3_ref), channel_id=1, source_target_pairs={{0,4},{4,0},{8,12},{12,8},{1,5},{5,1},{9,13},{13,9},{2,6},{6,2},{1... | collective-permute-start | bytes 159752 | tf_op jit(solution)/shard_map/ppermute | solution.py:441
  11.8 5.7 %collective-permute-start.4 = (f32[21,8,128]{2,1,0:T(8,128)S(1)}, f32[21,8,128]{2,1,0:T(8,128)S(1)}, u32[]{:S(2)}, u32[]{:S(2)}) collective-permute-start(f32[21,8,128]{2,1,0:T(8,128)S(1)} %shard_map.95.near_ref), channel_id=1, source_target_pairs={{0,2},{2,0},{1,3},{3,1},{4,6},{6,4},{5,7},{7,5},{8,10},{10,8},{9,1... | collective-permute-start | bytes 258056 | tf_op jit(solution)/shard_map/ppermute | solution.py:444
  13.4 4.1 %collective-permute-start.5 = (f32[11,8,128]{2,1,0:T(8,128)S(1)}, f32[11,8,128]{2,1,0:T(8,128)S(1)}, u32[]{:S(2)}, u32[]{:S(2)}) collective-permute-start(f32[11,8,128]{2,1,0:T(8,128)S(1)} %shard_map.96.far_ref), channel_id=1, source_target_pairs={{0,2},{2,0},{1,3},{3,1},{4,6},{6,4},{5,7},{7,5},{8,10},{10,8},{9,1... | collective-permute-start | bytes 135176 | tf_op jit(solution)/shard_map/ppermute | solution.py:444
  18.4 1.2 %collective-permute-start.6 = (f32[16,128]{1,0:T(8,128)S(1)}, f32[16,128]{1,0:T(8,128)S(1)}, u32[]{:S(2)}, u32[]{:S(2)}) collective-permute-start(f32[16,128]{1,0:T(8,128)S(1)} %get-tuple-element.25.mine_ref), channel_id=1, source_target_pairs={{0,1},{1,0},{2,3},{3,2},{4,5},{5,4},{6,7},{7,6},{8,9},{9,8},{10,11... | collective-permute-start | bytes 24584 | tf_op jit(solution)/shard_map/ppermute | solution.py:486

commit v6 on v4

--- a/solution.py
+++ b/solution.py
@@ -1,3 +1,4 @@
+import functools
 import math
 
 import jax
@@ -9,6 +10,11 @@
 
 BLOCK = 128
 SUB = 8
+EARLY_COST = 40_000_000_000
+BUNDLE_COST = 1000
+DISTANCES = (1, 2, 3)
+COPIES = (0, 1, 1, 2, 2, 3, 3)
+EXTRA = (0, 0, 1, 0, 2, 0, 3)
 VMEM_LIMIT = 32 * 1024 * 1024
 
 amplitude = 0.05
@@ -212,7 +218,7 @@
         out_ref[c] = total[:, c * BLOCK : (c + 1) * BLOCK]
 
 
-def call(kernel, out_shape, scratch, scalars, arrays):
+def call(kernel, out_shape, scratch, scalars, arrays, cost=None):
     specs = [pl.BlockSpec(memory_space=pltpu.SMEM)] * len(scalars)
     specs += [pl.BlockSpec(memory_space=pltpu.VMEM)] * len(arrays)
     return pl.pallas_call(
@@ -221,6 +227,7 @@
         in_specs=specs,
         out_specs=jax.tree.map(lambda _: pl.BlockSpec(memory_space=pltpu.VMEM), out_shape),
         scratch_shapes=scratch,
+        cost_estimate=cost and pl.CostEstimate(flops=cost, bytes_accessed=1000, transcendentals=0),
         compiler_params=pltpu.CompilerParams(vmem_limit_bytes=VMEM_LIMIT),
     )(*scalars, *arrays)
 
@@ -263,61 +270,85 @@
 
 
 def slot_tiles(ref):
-    return [ref[c] for c in range(4)] + [ref[ref.shape[0] - 1]]
-
-
-def message_table(ref):
-    return read_table(ref, 4, (ref.shape[0] - 5) // 4)
-
-
-def near_bundle_kernel(one_ref, two_ref, out_ref):
-    body = one_ref.shape[0] - 5
+    return [ref[c] for c in range(5)]
+
+
+def message_table(ref, step):
+    return read_table(ref, 5, step)
+
+
+def pack_slots(ref):
+    a, b, c, d, e = slot_tiles(ref)
+    return [halves(flip(a), b), halves(flip(c), d), e]
+
+
+def unpack_top(tiles):
+    a, b, c = tiles
+    return [a, flip(a), b, flip(b), flip(c)]
+
+
+def unpack_bottom(tiles):
+    a, b, c = tiles
+    return [flip(a), a, flip(b), b, c]
+
+
+def near_bundle_kernel(own_ref, first_ref, second_down, second_up, out_ref, second_ref):
+    second_ref[...] = second_down[: second_ref.shape[0]] + second_up[...]
+    body = own_ref.shape[0] - 5
+    for n, ref in enumerate((own_ref, first_ref, second_ref)):
+        for q in range(body):
+            out_ref[n * body + q] = ref[5 + q]
+    for k, (a, b) in enumerate(zip(slot_tiles(first_ref), slot_tiles(second_ref))):
+        out_ref[3 * body + k] = halves(flip(a), b)
+    for k, tile in enumerate(pack_slots(own_ref)):
+        out_ref[3 * body + 5 + k] = tile
+
+
+def far_bundle_kernel(third_down, third_up, near_ref, out_ref, third_ref):
+    del near_ref
+    third_ref[...] = third_down[: third_ref.shape[0]] + third_up[...]
+    body = third_ref.shape[0] - 5
     for q in range(body):
-        out_ref[q] = one_ref[4 + q]
-        out_ref[body + q] = two_ref[4 + q]
-    for k, (a, b) in enumerate(zip(slot_tiles(one_ref), slot_tiles(two_ref))):
-        out_ref[2 * body + k] = halves(flip(a), b)
-
-
-def far_bundle_kernel(three_ref, near_ref, out_ref):
-    del near_ref
-    body = three_ref.shape[0] - 5
-    for q in range(body):
-        out_ref[q] = three_ref[4 + q]
-    tiles = slot_tiles(three_ref)
-    out_ref[body] = halves(flip(tiles[0]), tiles[1])
-    out_ref[body + 1] = halves(flip(tiles[2]), tiles[3])
-    out_ref[body + 2] = tiles[4]
-
-
-def far_tiles(three_ref, far_ref):
-    same = slot_tiles(three_ref)
-    body = three_ref.shape[0] - 5
-    a, b, c = [far_ref[body + k] for k in range(3)]
-    other = [flip(a), a, flip(b), b, c]
-    return [halves(x, y) for x, y in zip(same, other)]
-
-
-def near_tiles(one_ref, two_ref):
+        out_ref[q] = third_ref[5 + q]
+    for k, tile in enumerate(pack_slots(third_ref)):
+        out_ref[body + k] = tile
+
+
+def top_tiles(one_ref, two_ref):
     return [halves(a, flip(b)) for a, b in zip(slot_tiles(one_ref), slot_tiles(two_ref))]
 
 
-def cross_tiles(one_ref, two_ref):
+def bottom_tiles(one_ref, two_ref):
     return [halves(flip(a), b) for a, b in zip(slot_tiles(one_ref), slot_tiles(two_ref))]
 
 
 def early_kernel(
-    m0_ref, m1_ref, m2_ref, x0_ref, z1_ref, z2_ref, far_ref, bgrad_ref, bindex_ref, ggrad_ref
+    m0_ref,
+    m1_ref,
+    m2_ref,
+    m3_ref,
+    first_ref,
+    second_ref,
+    third_ref,
+    far_ref,
+    bgrad_ref,
+    bindex_ref,
+    ggrad_ref,
 ):
     del far_ref
-    own = message_table(m0_ref)
-    here = [halves(a, b) for a, b in zip(slot_tiles(m0_ref), slot_tiles(x0_ref))]
-    near = near_tiles(z1_ref, z2_ref)
+    step = (m0_ref.shape[0] - 5) // 4
+    own = message_table(m0_ref, step)
+    here = top_tiles(m0_ref, third_ref)
+    near = top_tiles(first_ref, second_ref)
     work = [
         body_work(here, own),
         body_work(near, own),
-        garm_work(slot_tiles(m0_ref), own, message_table(x0_ref)),
-        garm_work(near_tiles(m1_ref, m2_ref), message_table(z1_ref), message_table(z2_ref)),
+        garm_work(top_tiles(m0_ref, m3_ref), own, message_table(third_ref, step)),
+        garm_work(
+            top_tiles(m1_ref, m2_ref),
+            message_table(first_ref, step),
+            message_table(second_ref, step),
+        ),
     ]
     out = gradients(work)
     for n in range(2):
@@ -328,18 +359,18 @@
     bindex_ref[SUB:, :] = near[4]
 
 
-def late_body_kernel(
-    m0_ref, z3_ref, near_ref, far_ref, bgrad_ref, bindex_ref, out_ref, stiff_ref
-):
-    own = message_table(m0_ref)
-    body = z3_ref.shape[0] - 5
-    near = [near_ref[2 * body + k] for k in range(5)]
-    far = far_tiles(z3_ref, far_ref)
+def late_body_kernel(m0_ref, near_ref, far_ref, bgrad_ref, bindex_ref, out_ref, stiff_ref):
+    body = m0_ref.shape[0] - 5
+    own = message_table(m0_ref, body // 4)
+    near = [near_ref[3 * body + k] for k in range(5)]
+    top = unpack_top([near_ref[3 * body + 5 + k] for k in range(3)])
+    bottom = unpack_bottom([far_ref[body + k] for k in range(3)])
+    here = [halves(a, b) for a, b in zip(top, bottom)]
     grads = [
         jnp.concatenate(rows, axis=1)
-        for rows in gradients([body_work(far, own), body_work(near, own)])
-    ]
-    index = jnp.concatenate([bindex_ref[...], far[4], near[4]], axis=0)
+        for rows in gradients([body_work(here, own), body_work(near, own)])
+    ]
+    index = jnp.concatenate([bindex_ref[...], here[4], near[4]], axis=0)
     total = scatter(index, jnp.concatenate([bgrad_ref[...]] + grads, axis=0), out_ref.shape[1])
     for c in range(3):
         out_ref[c] = total[:, c * BLOCK : (c + 1) * BLOCK]
@@ -347,14 +378,14 @@
 
 
 def late_garm_kernel(
-    m1_ref, m2_ref, m3_ref, z3_ref, near_ref, far_ref, ggrad_ref, index_ref, out_ref
+    m0_ref, m1_ref, m2_ref, m3_ref, near_ref, far_ref, ggrad_ref, index_ref, out_ref
 ):
-    body = z3_ref.shape[0] - 5
+    body = m0_ref.shape[0] - 5
     step = body // 4
-    tables = [read_table(near_ref, n * body, step) for n in range(2)]
+    own, first, second = [read_table(near_ref, n * body, step) for n in range(3)]
     work = [
-        garm_work(slot_tiles(m3_ref), message_table(z3_ref), read_table(far_ref, 0, step)),
-        garm_work(cross_tiles(m1_ref, m2_ref), *tables),
+        garm_work(bottom_tiles(m0_ref, m3_ref), own, read_table(far_ref, 0, step)),
+        garm_work(bottom_tiles(m1_ref, m2_ref), first, second),
     ]
     grads = [jnp.concatenate(rows[:3], axis=1) for rows in gradients(work)]
     index = jnp.concatenate([index_ref[k] for k in range(index_ref.shape[0])], axis=0)
@@ -369,8 +400,8 @@
     garm_out[...] = garm_ref[...]
 
 
-def stage_kernel(*refs):
-    hbm, (index_ref, *out_refs), vmem, sems = refs[:7], refs[7:12], refs[12:19], refs[19]
+def stage_kernel(count, *refs):
+    hbm, (index_ref, *out_refs), (vmem, sems) = refs[:7], refs[7 : 8 + count], (refs[-8:-1], refs[-1])
     copies = [
         pltpu.make_async_copy(src, dst, sems.at[k]) for k, (src, dst) in enumerate(zip(hbm, vmem))
     ]
@@ -383,27 +414,31 @@
     tiles = stiff_ref.shape[0]
     width = lax.axis_size("body")
     here, column = lax.axis_index("garm"), lax.axis_index("body")
-    for k, out_ref in enumerate(out_refs):
+    for n, out_ref in enumerate(out_refs):
         for q in range(3 * tiles):
-            out_ref[4 + q] = body_ref[q]
+            out_ref[5 + q] = body_ref[q]
         for q in range(tiles):
-            out_ref[4 + 3 * tiles + q] = stiff_ref[q]
+            out_ref[5 + 3 * tiles + q] = stiff_ref[q]
+        for q in range(5 + 4 * tiles, out_ref.shape[0]):
+            out_ref[q] = jnp.zeros((SUB, BLOCK), f32)
+    for k in range(len(DISTANCES) + 1):
+        targets = [ref for n, ref in enumerate(out_refs) if COPIES[n] == k]
         for x in range(2):
             owner = (here ^ k) * width + (column ^ x)
             live = pc_ref[0, owner]
             for s in range(cap):
                 g = pg_ref[s, owner]
                 row, place = pl.ds(g, 1), pl.ds(x * cap + s, 1)
-                for c in range(3):
-                    out_ref[c, place, :] = garm_ref[c, row, :]
-                out_ref[3, place, :] = jnp.where(s < live, cot_ref[row, :], 0.0)
-                out_ref[4 + 4 * tiles, place, :] = jnp.full(
-                    (1, BLOCK), pb_ref[s, owner].astype(f32), f32
-                )
-                if k in (1, 2):
-                    spot, line = 1 + 2 * x, (k - 1) * cap + s
+                values = [garm_ref[c, row, :] for c in range(3)]
+                values.append(jnp.where(s < live, cot_ref[row, :], 0.0))
+                values.append(jnp.full((1, BLOCK), pb_ref[s, owner].astype(f32), f32))
+                for out_ref in targets:
+                    for c, value in enumerate(values):
+                        out_ref[c, place, :] = value
+                if k in DISTANCES[:2]:
+                    spot, line = 2 * x + 1, DISTANCES.index(k) * cap + s
                 else:
-                    spot, line = (0 if k == 0 else 2), x * cap + s
+                    spot, line = 2 * x, (0 if k == 0 else cap) + s
                 index_ref[spot, line : line + 1, :] = jnp.full((1, BLOCK), g.astype(f32), f32)
 
 
@@ -413,7 +448,10 @@
     blocks = points // BLOCK
     tiles = blocks // SUB
     garm_n = lax.axis_size("garm")
-    message = jax.ShapeDtypeStruct((5 + 4 * tiles, SUB, BLOCK), f32)
+    messages = [
+        jax.ShapeDtypeStruct((5 + 4 * tiles + extra, SUB, BLOCK), f32) for extra in EXTRA
+    ]
+    message = messages[0]
     arrays = (
         pg,
         pb,
@@ -423,11 +461,11 @@
         body_points.reshape(3 * tiles, SUB, BLOCK),
         stiffness.reshape(tiles, SUB, BLOCK),
     )
-    index, *sent = pl.pallas_call(
-        stage_kernel,
-        out_shape=[jax.ShapeDtypeStruct((garm_n, SUB, BLOCK), f32)] + [message] * garm_n,
+    index, own, one, one_down, two, two_down, three, three_down = pl.pallas_call(
+        functools.partial(stage_kernel, len(messages)),
+        out_shape=[jax.ShapeDtypeStruct((garm_n, SUB, BLOCK), f32)] + messages,
         in_specs=[pl.BlockSpec(memory_space=pltpu.HBM)] * len(arrays),
-        out_specs=[pl.BlockSpec(memory_space=pltpu.VMEM)] * (garm_n + 1),
+        out_specs=[pl.BlockSpec(memory_space=pltpu.VMEM)] * (len(messages) + 1),
         scratch_shapes=[
             (pltpu.SMEM if k < 3 else pltpu.VMEM)(a.shape, a.dtype) for k, a in enumerate(arrays)
         ]
@@ -435,28 +473,38 @@
         compiler_params=pltpu.CompilerParams(vmem_limit_bytes=VMEM_LIMIT),
     )(*[pltpu.with_memory_space_constraint(a, pltpu.HBM) for a in arrays])
 
-    def along_garm(k):
-        return lax.ppermute(sent[k], "garm", [(z, z ^ k) for z in range(garm_n)])
+    def along_garm(value, k, ways):
+        pairs = [(z, z ^ k) for z in range(garm_n) if (z > z ^ k) in ways]
+        return lax.ppermute(value, "garm", pairs)
 
     def along_body(value):
         return lax.ppermute(value, "body", [(0, 1), (1, 0)])
 
-    z3, z2, z1 = [along_garm(k) for k in (3, 2, 1)]
-    x0 = along_body(sent[0])
+    third = [
+        along_garm(three_down, DISTANCES[2], (True,)),
+        along_garm(three, DISTANCES[2], (False,)),
+    ]
+    second = [
+        along_garm(two_down, DISTANCES[1], (True,)),
+        along_garm(two, DISTANCES[1], (False,)),
+    ]
+    first = along_garm(one_down, DISTANCES[0], (True, False))
     body = 4 * tiles
-    near = call(
+    near, second = call(
         near_bundle_kernel,
-        jax.ShapeDtypeStruct((2 * body + 5, SUB, BLOCK), f32),
+        (jax.ShapeDtypeStruct((3 * body + 8, SUB, BLOCK), f32), message),
         [],
         (),
-        (z1, z2),
-    )
-    far = call(
+        (own, first, *second),
+        BUNDLE_COST,
+    )
+    far, third = call(
         far_bundle_kernel,
-        jax.ShapeDtypeStruct((body + 3, SUB, BLOCK), f32),
+        (jax.ShapeDtypeStruct((body + 3, SUB, BLOCK), f32), message),
         [],
         (),
-        (z3, near),
+        (*third, near),
+        BUNDLE_COST,
     )
     near_other, far_other = along_body(near), along_body(far)
     bgrad, bindex, ggrad = call(
@@ -468,7 +516,8 @@
         ),
         [],
         (),
-        (sent[0], sent[1], sent[2], x0, z1, z2, far),
+        (own, one, two, three, first, second, third, far),
+        EARLY_COST,
     )
     body_shape = jax.ShapeDtypeStruct((3, blocks, BLOCK), f32)
     stiff_shape = jax.ShapeDtypeStruct((blocks, BLOCK), f32)
@@ -478,7 +527,7 @@
         (body_shape, stiff_shape),
         [],
         (),
-        (sent[0], z3, near_other, far_other, bgrad, bindex),
+        (own, near_other, far_other, bgrad, bindex),
     )
     stiff_other = lax.ppermute(stiff, "frame", [(0, 1), (1, 0)])
     garm_total = call(
@@ -486,7 +535,7 @@
         garm_shape,
         [],
         (),
-        (sent[1], sent[2], sent[3], z3, near_other, far_other, ggrad, index),
+        (own, one, two, three, near_other, far_other, ggrad, index),
     )
     return call(
         final_kernel,

time: 20.4 us -> 23.4 us (1.15)
  starting transfers between devices: 9.27 us -> 15.1 us
  waiting for transfers between devices: 5.83 us -> 2.68 us
    ppermute x3 -> x5, starting transfers between devices: 5.68 us -> 12.4 us  [along_garm(): return lax.ppermute(value, 'garm', pairs)]
    ppermute x3 -> x5, waiting for transfers between devices: 3.82 us -> 0.57 us  [along_garm(): return lax.ppermute(value, 'garm', pairs)]
    ppermute x3 -> x2, starting transfers between devices: 3.58 us -> 2.74 us  [along_body(): return lax.ppermute(value, 'body', [(0, 1), (1, 0)])]
    ppermute x3 -> x2, waiting for transfers between devices: 1.75 us -> 1.87 us  [along_body(): return lax.ppermute(value, 'body', [(0, 1), (1, 0)])]
  transfers between devices with their start and end apart: 7 -> 8, of which waited for: 4 -> 3; matrix products, arithmetic and copies ran while one was open for 0% -> 0% of each run, Pallas kernels for 10% -> 9%
where the time goes in v6:
time: 23.4 us; the launch traced here: 23.1 us
  starting transfers between devices  15.1 us (65%)
  Pallas kernels  4.55 us (19%)
  waiting for transfers between devices  2.68 us (11%)
  between operations  0.69 us (3%)
    ppermute x5, starting transfers between devices, along_garm(): return lax.ppermute(value, 'garm', pairs)  12.4 us
    pallas_call x6, Pallas kernels, call(): pl.pallas_call(kernel, out_shape=out_shape, in_specs=specs, out_specs=jax...  3.54 us
    ppermute x2, starting transfers between devices, along_body(): return lax.ppermute(value, 'body', [(0, 1), (1, 0)])  2.74 us
    ppermute x2, waiting for transfers between devices, along_body(): return lax.ppermute(value, 'body', [(0, 1), (1, 0)])  1.87 us
    pallas_call x1, Pallas kernels, staged(): pl.pallas_call(functools.partial(stage_kernel, len(messages)), out_shape=...  1.01 us
    ppermute x5, waiting for transfers between devices, along_garm(): return lax.ppermute(value, 'garm', pairs)  0.57 us
  transfers between devices with their start and end apart: 8, of which 3 were waited for; matrix products, arithmetic and copies ran while one was open for 0% of the time, Pallas kernels for 9%

profile of v6, /device:TPU:0, one launch (start us, length us, event | category | flops | bytes accessed | tf_op | source)
XLA Modules:
  0.0 23.1 jit_solution(10714167472263270133)
XLA Ops:
  0.6 1.0 %shard_map.94 = (f32[4,8,128]{2,1,0:T(8,128)S(1)}, f32[13,8,128]{2,1,0:T(8,128)S(1)}, f32[13,8,128]{2,1,0:T(8,128)S(1)}, f32[14,8,128]{2,1,0:T(8,128)S(1)}, f32[...) custom-call(s32[4,8]{1,0:T(4,128)} %bitcast.18, ...), custom_call_target="tpu_custom_call" | custom-call | tf_op jit(solution)/shard_map/pallas_call | solution.py:464
  1.7 1.3 %collective-permute-start.4 = (f32[16,8,128]{2,1,0:T(8,128)S(1)}, f32[16,8,128]{2,1,0:T(8,128)S(1)}, u32[]{:S(2)}, u32[]{:S(2)}) collective-permute-start(f32[16,8,128]{2,1,0:T(8,128)S(1)} %get-tuple-element.30), channel_id=1, source_target_pairs={{8,4},{12,0},{9,5},{13,1},{10,6},{14,2},{11,7},{15,3},{24,20},{28,... | collective-permute-start | bytes 196616 | tf_op jit(solution)/shard_map/ppermute | solution.py:478
  3.0 1.3 %collective-permute-start.1 = (f32[15,8,128]{2,1,0:T(8,128)S(1)}, f32[15,8,128]{2,1,0:T(8,128)S(1)}, u32[]{:S(2)}, u32[]{:S(2)}) collective-permute-start(f32[15,8,128]{2,1,0:T(8,128)S(1)} %get-tuple-element.28), channel_id=1, source_target_pairs={{8,0},{12,4},{9,1},{13,5},{10,2},{14,6},{11,3},{15,7},{24,16},{28,... | collective-permute-start | bytes 184328 | tf_op jit(solution)/shard_map/ppermute | solution.py:478
  4.3 3.1 %collective-permute-start = (f32[14,8,128]{2,1,0:T(8,128)S(1)}, f32[14,8,128]{2,1,0:T(8,128)S(1)}, u32[]{:S(2)}, u32[]{:S(2)}) collective-permute-start(f32[14,8,128]{2,1,0:T(8,128)S(1)} %get-tuple-element.27), channel_id=1, source_target_pairs={{0,4},{4,0},{8,12},{12,8},{1,5},{5,1},{9,13},{13,9},{2,6},{6,2},{1... | collective-permute-start | bytes 172040 | tf_op jit(solution)/shard_map/ppermute | solution.py:478
  7.3 5.4 %collective-permute-start.2 = (f32[13,8,128]{2,1,0:T(8,128)S(1)}, f32[13,8,128]{2,1,0:T(8,128)S(1)}, u32[]{:S(2)}, u32[]{:S(2)}) collective-permute-start(f32[13,8,128]{2,1,0:T(8,128)S(1)} %get-tuple-element.25.m2_ref), channel_id=1, source_target_pairs={{0,8},{4,12},{1,9},{5,13},{2,10},{6,14},{3,11},{7,15},{16,24},{20,... | collective-permute-start | bytes 159752 | tf_op jit(solution)/shard_map/ppermute | solution.py:478
  12.8 1.3 %collective-permute-start.5 = (f32[13,8,128]{2,1,0:T(8,128)S(1)}, f32[13,8,128]{2,1,0:T(8,128)S(1)}, u32[]{:S(2)}, u32[]{:S(2)}) collective-permute-start(f32[13,8,128]{2,1,0:T(8,128)S(1)} %get-tuple-element.26.m3_ref), channel_id=1, source_target_pairs={{0,12},{4,8},{1,13},{5,9},{2,14},{6,10},{3,15},{7,11},{16,28},{20,... | collective-permute-start | bytes 159752 | tf_op jit(solution)/shard_map/ppermute | solution.py:478
  14.1 0.6 %collective-permute-done.2.second_up = f32[13,8,128]{2,1,0:T(8,128)S(1)} collective-permute-done((f32[13,8,128]{2,1,0:T(8,128)S(1)}, f32[13,8,128]{2,1,0:T(8,128)S(1)}, u32[]{:S(2)}, u32[]{:S(2)}) %collective-permute-start.2) | collective-permute-done | bytes 53280 | tf_op jit(solution)/shard_map/ppermute | solution.py:478
  14.6 0.0 collective-permute-done.first_ref
  14.6 0.0 collective-permute-done.1.second_down
  14.7 1.6 %collective-permute-start.3 = (f32[32,8,128]{2,1,0:T(8,128)S(1)}, f32[32,8,128]{2,1,0:T(8,128)S(1)}, u32[]{:S(2)}, u32[]{:S(2)}) collective-permute-start(f32[32,8,128]{2,1,0:T(8,128)S(1)} %get-tuple-element.29.near_ref), channel_id=1, source_target_pairs={{0,2},{2,0},{1,3},{3,1},{4,6},{6,4},{5,7},{7,5},{8,10},{10,8},{9,1... | collective-permute-start | bytes 393224 | tf_op jit(solution)/shard_map/ppermute | solution.py:481
  16.2 0.0 collective-permute-done.5.third_up
  16.2 0.0 collective-permute-done.4.third_down
  16.3 1.2 %collective-permute-start.6 = (f32[11,8,128]{2,1,0:T(8,128)S(1)}, f32[11,8,128]{2,1,0:T(8,128)S(1)}, u32[]{:S(2)}, u32[]{:S(2)}) collective-permute-start(f32[11,8,128]{2,1,0:T(8,128)S(1)} %get-tuple-element.31.far_ref), channel_id=1, source_target_pairs={{0,2},{2,0},{1,3},{3,1},{4,6},{6,4},{5,7},{7,5},{8,10},{10,8},{9,1... | collective-permute-start | bytes 135176 | tf_op jit(solution)/shard_map/ppermute | solution.py:481
  17.4 1.1 %shard_map.97 = (f32[16,512]{1,0:T(8,128)S(1)}, f32[16,128]{1,0:T(8,128)S(1)}, f32[16,384]{1,0:T(8,128)S(1)}) custom-call(f32[13,8,128]{2,1,0:T(8,128)S(1)} %get-tuple-element.23.own_ref.m0_ref, f32[13,8,128]{2,1,0:T(8,128)S(1)} %get-tuple-element.24.m1_ref, f32[13,8,128]{2,1,0:T(8,128)S(1)} %get-tuple-element.25.m2_ref, ...), custom_call_target="tpu_custom_call" | custom-call | flops 40000000000 | bytes 1000 | tf_op jit(solution)/shard_map/pallas_call | solution.py:224
  18.5 1.9 %collective-permute-done.6.far_ref = f32[11,8,128]{2,1,0:T(8,128)S(1)} collective-permute-done((f32[11,8,128]{2,1,0:T(8,128)S(1)}, f32[11,8,128]{2,1,0:T(8,128)S(1)}, u32[]{:S(2)}, u32[]{:S(2)}) %collective-permute-start.6) | collective-permute-done | bytes 45088 | tf_op jit(solution)/shard_map/ppermute | solution.py:481
  20.4 0.0 collective-permute-done.3.near_ref
  20.4 0.9 %shard_map.99 = (f32[3,16,128]{2,1,0:T(8,128)S(1)}, f32[16,128]{1,0:T(8,128)S(1)}) custom-call(f32[13,8,128]{2,1,0:T(8,128)S(1)} %get-tuple-element.23.own_ref.m0_ref, f32[32,8,128]{2,1,0:T(8,128)S(1)} %collective-permute-done.3.near_ref, f32[11,8,128]{2,1,0:T(8,128)S(1)} %collective-permute-done.6.far_ref, f32[16,512]{1,0:T(8,128)S(1)} %get-tuple-element.36.bgrad_ref, ...), custom_call_target="tpu_custom_call" | custom-call | tf_op jit(solution)/shard_map/pallas_call | solution.py:224
  21.2 0.0 collective-permute-start.7
  21.2 0.9 %shard_map.98.garm_ref = f32[3,32,128]{2,1,0:T(8,128)S(1)} custom-call(f32[13,8,128]{2,1,0:T(8,128)S(1)} %get-tuple-element.23.own_ref.m0_ref, f32[13,8,128]{2,1,0:T(8,128)S(1)} %get-tuple-element.24.m1_ref, f32[13,8,128]{2,1,0:T(8,128)S(1)} %get-tuple-element.25.m2_ref, f32[13,8,128]{2,1,0:T(8,128)S(1)} %get-tuple-element.26.m3_ref, ...), custom_call_target="tpu_custom_call" | custom-call | tf_op jit(solution)/shard_map/pallas_call | solution.py:224
  22.2 0.2 %collective-permute-done.7.other_ref = f32[16,128]{1,0:T(8,128)S(1)} collective-permute-done((f32[16,128]{1,0:T(8,128)S(1)}, f32[16,128]{1,0:T(8,128)S(1)}, u32[]{:S(2)}, u32[]{:S(2)}) %collective-permute-start.7) | collective-permute-done | bytes 8224 | tf_op jit(solution)/shard_map/ppermute | solution.py:532
  22.4 0.6 %shard_map.100 = (f32[3,32,128]{2,1,0:T(8,128)}, f32[3,16,128]{2,1,0:T(8,128)}, f32[16,128]{1,0:T(8,128)}) custom-call(f32[3,32,128]{2,1,0:T(8,128)S(1)} %shard_map.98.garm_ref, f32[3,16,128]{2,1,0:T(8,128)S(1)} %get-tuple-element.38.body_ref, f32[16,128]{1,0:T(8,128)S(1)} %get-tuple-element.39.mine_ref, f32[16,128]{1,0:T(8,128)S(1)} %collective-permute-done.7.other_ref), custom_call_target="tpu_custom_call" | custom-call | tf_op jit(solution)/shard_map/pallas_call | solution.py:224
  (2 shorter events, 0.0 us)
Async XLA Ops:
  1.7 14.6 %collective-permute-start.4 = (f32[16,8,128]{2,1,0:T(8,128)S(1)}, f32[16,8,128]{2,1,0:T(8,128)S(1)}, u32[]{:S(2)}, u32[]{:S(2)}) collective-permute-start(f32[16,8,128]{2,1,0:T(8,128)S(1)} %get-tuple-element.30), channel_id=1, source_target_pairs={{8,4},{12,0},{9,5},{13,1},{10,6},{14,2},{11,7},{15,3},{24,20},{28,... | collective-permute-start | bytes 196616 | tf_op jit(solution)/shard_map/ppermute | solution.py:478
  3.0 11.7 %collective-permute-start.1 = (f32[15,8,128]{2,1,0:T(8,128)S(1)}, f32[15,8,128]{2,1,0:T(8,128)S(1)}, u32[]{:S(2)}, u32[]{:S(2)}) collective-permute-start(f32[15,8,128]{2,1,0:T(8,128)S(1)} %get-tuple-element.28), channel_id=1, source_target_pairs={{8,0},{12,4},{9,1},{13,5},{10,2},{14,6},{11,3},{15,7},{24,16},{28,... | collective-permute-start | bytes 184328 | tf_op jit(solution)/shard_map/ppermute | solution.py:478
  4.3 10.4 %collective-permute-start = (f32[14,8,128]{2,1,0:T(8,128)S(1)}, f32[14,8,128]{2,1,0:T(8,128)S(1)}, u32[]{:S(2)}, u32[]{:S(2)}) collective-permute-start(f32[14,8,128]{2,1,0:T(8,128)S(1)} %get-tuple-element.27), channel_id=1, source_target_pairs={{0,4},{4,0},{8,12},{12,8},{1,5},{5,1},{9,13},{13,9},{2,6},{6,2},{1... | collective-permute-start | bytes 172040 | tf_op jit(solution)/shard_map/ppermute | solution.py:478
  7.3 7.3 %collective-permute-start.2 = (f32[13,8,128]{2,1,0:T(8,128)S(1)}, f32[13,8,128]{2,1,0:T(8,128)S(1)}, u32[]{:S(2)}, u32[]{:S(2)}) collective-permute-start(f32[13,8,128]{2,1,0:T(8,128)S(1)} %get-tuple-element.25.m2_ref), channel_id=1, source_target_pairs={{0,8},{4,12},{1,9},{5,13},{2,10},{6,14},{3,11},{7,15},{16,24},{20,... | collective-permute-start | bytes 159752 | tf_op jit(solution)/shard_map/ppermute | solution.py:478
  12.8 3.4 %collective-permute-start.5 = (f32[13,8,128]{2,1,0:T(8,128)S(1)}, f32[13,8,128]{2,1,0:T(8,128)S(1)}, u32[]{:S(2)}, u32[]{:S(2)}) collective-permute-start(f32[13,8,128]{2,1,0:T(8,128)S(1)} %get-tuple-element.26.m3_ref), channel_id=1, source_target_pairs={{0,12},{4,8},{1,13},{5,9},{2,14},{6,10},{3,15},{7,11},{16,28},{20,... | collective-permute-start | bytes 159752 | tf_op jit(solution)/shard_map/ppermute | solution.py:478
  14.7 5.7 %collective-permute-start.3 = (f32[32,8,128]{2,1,0:T(8,128)S(1)}, f32[32,8,128]{2,1,0:T(8,128)S(1)}, u32[]{:S(2)}, u32[]{:S(2)}) collective-permute-start(f32[32,8,128]{2,1,0:T(8,128)S(1)} %get-tuple-element.29.near_ref), channel_id=1, source_target_pairs={{0,2},{2,0},{1,3},{3,1},{4,6},{6,4},{5,7},{7,5},{8,10},{10,8},{9,1... | collective-permute-start | bytes 393224 | tf_op jit(solution)/shard_map/ppermute | solution.py:481
  16.3 4.1 %collective-permute-start.6 = (f32[11,8,128]{2,1,0:T(8,128)S(1)}, f32[11,8,128]{2,1,0:T(8,128)S(1)}, u32[]{:S(2)}, u32[]{:S(2)}) collective-permute-start(f32[11,8,128]{2,1,0:T(8,128)S(1)} %get-tuple-element.31.far_ref), channel_id=1, source_target_pairs={{0,2},{2,0},{1,3},{3,1},{4,6},{6,4},{5,7},{7,5},{8,10},{10,8},{9,1... | collective-permute-start | bytes 135176 | tf_op jit(solution)/shard_map/ppermute | solution.py:481
  21.2 1.2 %collective-permute-start.7 = (f32[16,128]{1,0:T(8,128)S(1)}, f32[16,128]{1,0:T(8,128)S(1)}, u32[]{:S(2)}, u32[]{:S(2)}) collective-permute-start(f32[16,128]{1,0:T(8,128)S(1)} %get-tuple-element.39.mine_ref), channel_id=1, source_target_pairs={{0,1},{1,0},{2,3},{3,2},{4,5},{5,4},{6,7},{7,6},{8,9},{9,8},{10,11... | collective-permute-start | bytes 24584 | tf_op jit(solution)/shard_map/ppermute | solution.py:532

commit v7 on v4

--- a/solution.py
+++ b/solution.py
@@ -10,6 +10,8 @@
 BLOCK = 128
 SUB = 8
 VMEM_LIMIT = 32 * 1024 * 1024
+EARLY_COST = 40_000_000_000
+BUNDLE_COST = 1000
 
 amplitude = 0.05
 width_sq = 4.0
@@ -212,7 +214,7 @@
         out_ref[c] = total[:, c * BLOCK : (c + 1) * BLOCK]
 
 
-def call(kernel, out_shape, scratch, scalars, arrays):
+def call(kernel, out_shape, scratch, scalars, arrays, cost=None):
     specs = [pl.BlockSpec(memory_space=pltpu.SMEM)] * len(scalars)
     specs += [pl.BlockSpec(memory_space=pltpu.VMEM)] * len(arrays)
     return pl.pallas_call(
@@ -221,6 +223,7 @@
         in_specs=specs,
         out_specs=jax.tree.map(lambda _: pl.BlockSpec(memory_space=pltpu.VMEM), out_shape),
         scratch_shapes=scratch,
+        cost_estimate=cost and pl.CostEstimate(flops=cost, bytes_accessed=1000, transcendentals=0),
         compiler_params=pltpu.CompilerParams(vmem_limit_bytes=VMEM_LIMIT),
     )(*scalars, *arrays)
 
@@ -263,61 +266,45 @@
 
 
 def slot_tiles(ref):
-    return [ref[c] for c in range(4)] + [ref[ref.shape[0] - 1]]
-
-
-def message_table(ref):
-    return read_table(ref, 4, (ref.shape[0] - 5) // 4)
-
-
-def near_bundle_kernel(one_ref, two_ref, out_ref):
+    return [ref[c] for c in range(5)]
+
+
+def message_table(ref, step):
+    return read_table(ref, 5, step)
+
+
+def bundle_kernel(one_ref, two_ref, *refs):
+    out_ref = refs[-1]
     body = one_ref.shape[0] - 5
     for q in range(body):
-        out_ref[q] = one_ref[4 + q]
-        out_ref[body + q] = two_ref[4 + q]
-    for k, (a, b) in enumerate(zip(slot_tiles(one_ref), slot_tiles(two_ref))):
-        out_ref[2 * body + k] = halves(flip(a), b)
-
-
-def far_bundle_kernel(three_ref, near_ref, out_ref):
-    del near_ref
-    body = three_ref.shape[0] - 5
-    for q in range(body):
-        out_ref[q] = three_ref[4 + q]
-    tiles = slot_tiles(three_ref)
-    out_ref[body] = halves(flip(tiles[0]), tiles[1])
-    out_ref[body + 1] = halves(flip(tiles[2]), tiles[3])
-    out_ref[body + 2] = tiles[4]
-
-
-def far_tiles(three_ref, far_ref):
-    same = slot_tiles(three_ref)
-    body = three_ref.shape[0] - 5
-    a, b, c = [far_ref[body + k] for k in range(3)]
-    other = [flip(a), a, flip(b), b, c]
-    return [halves(x, y) for x, y in zip(same, other)]
-
-
-def near_tiles(one_ref, two_ref):
+        out_ref[q] = one_ref[5 + q]
+        out_ref[body + q] = two_ref[5 + q]
+    for k, tile in enumerate(bottom_tiles(one_ref, two_ref)):
+        out_ref[2 * body + k] = tile
+
+
+def top_tiles(one_ref, two_ref):
     return [halves(a, flip(b)) for a, b in zip(slot_tiles(one_ref), slot_tiles(two_ref))]
 
 
-def cross_tiles(one_ref, two_ref):
+def bottom_tiles(one_ref, two_ref):
     return [halves(flip(a), b) for a, b in zip(slot_tiles(one_ref), slot_tiles(two_ref))]
 
 
-def early_kernel(
-    m0_ref, m1_ref, m2_ref, x0_ref, z1_ref, z2_ref, far_ref, bgrad_ref, bindex_ref, ggrad_ref
-):
+def early_kernel(*refs):
+    own_ref, sent_refs, got_refs, far_ref = refs[0], refs[1:4], refs[4:7], refs[7]
     del far_ref
-    own = message_table(m0_ref)
-    here = [halves(a, b) for a, b in zip(slot_tiles(m0_ref), slot_tiles(x0_ref))]
-    near = near_tiles(z1_ref, z2_ref)
+    bgrad_ref, bindex_ref, ggrad_ref = refs[8:]
+    step = (own_ref.shape[0] - 5) // 4
+    own = message_table(own_ref, step)
+    a, b, c = [message_table(ref, step) for ref in got_refs]
+    here = top_tiles(own_ref, got_refs[0])
+    far = top_tiles(got_refs[1], got_refs[2])
     work = [
         body_work(here, own),
-        body_work(near, own),
-        garm_work(slot_tiles(m0_ref), own, message_table(x0_ref)),
-        garm_work(near_tiles(m1_ref, m2_ref), message_table(z1_ref), message_table(z2_ref)),
+        body_work(far, own),
+        garm_work(top_tiles(own_ref, sent_refs[0]), own, a),
+        garm_work(top_tiles(sent_refs[1], sent_refs[2]), b, c),
     ]
     out = gradients(work)
     for n in range(2):
@@ -325,36 +312,35 @@
         bgrad_ref[rows, :] = jnp.concatenate(out[n], axis=1)
         ggrad_ref[rows, :] = jnp.concatenate(out[2 + n][:3], axis=1)
     bindex_ref[:SUB, :] = here[4]
-    bindex_ref[SUB:, :] = near[4]
-
-
-def late_body_kernel(
-    m0_ref, z3_ref, near_ref, far_ref, bgrad_ref, bindex_ref, out_ref, stiff_ref
-):
-    own = message_table(m0_ref)
-    body = z3_ref.shape[0] - 5
-    near = [near_ref[2 * body + k] for k in range(5)]
-    far = far_tiles(z3_ref, far_ref)
-    grads = [
-        jnp.concatenate(rows, axis=1)
-        for rows in gradients([body_work(far, own), body_work(near, own)])
-    ]
-    index = jnp.concatenate([bindex_ref[...], far[4], near[4]], axis=0)
+    bindex_ref[SUB:, :] = far[4]
+
+
+def late_body_kernel(own_ref, near_ref, far_ref, bgrad_ref, bindex_ref, out_ref, stiff_ref):
+    body = own_ref.shape[0] - 5
+    own = message_table(own_ref, body // 4)
+    tiles = [[ref[2 * body + k] for k in range(5)] for ref in (near_ref, far_ref)]
+    out = gradients([body_work(part, own) for part in tiles])
+    grads = [jnp.concatenate(rows, axis=1) for rows in out]
+    index = jnp.concatenate([bindex_ref[...]] + [part[4] for part in tiles], axis=0)
     total = scatter(index, jnp.concatenate([bgrad_ref[...]] + grads, axis=0), out_ref.shape[1])
     for c in range(3):
         out_ref[c] = total[:, c * BLOCK : (c + 1) * BLOCK]
     stiff_ref[...] = total[:, 3 * BLOCK :]
 
 
-def late_garm_kernel(
-    m1_ref, m2_ref, m3_ref, z3_ref, near_ref, far_ref, ggrad_ref, index_ref, out_ref
-):
-    body = z3_ref.shape[0] - 5
-    step = body // 4
-    tables = [read_table(near_ref, n * body, step) for n in range(2)]
+def late_garm_kernel(*refs):
+    own_ref, sent_refs, (near_ref, far_ref, ggrad_ref, index_ref, out_ref) = (
+        refs[0],
+        refs[1:4],
+        refs[4:],
+    )
+    body = own_ref.shape[0] - 5
+    near, far = [
+        [read_table(ref, n * body, body // 4) for n in range(2)] for ref in (near_ref, far_ref)
+    ]
     work = [
-        garm_work(slot_tiles(m3_ref), message_table(z3_ref), read_table(far_ref, 0, step)),
-        garm_work(cross_tiles(m1_ref, m2_ref), *tables),
+        garm_work(bottom_tiles(own_ref, sent_refs[0]), *near),
+        garm_work(bottom_tiles(sent_refs[1], sent_refs[2]), *far),
     ]
     grads = [jnp.concatenate(rows[:3], axis=1) for rows in gradients(work)]
     index = jnp.concatenate([index_ref[k] for k in range(index_ref.shape[0])], axis=0)
@@ -370,7 +356,7 @@
 
 
 def stage_kernel(*refs):
-    hbm, (index_ref, *out_refs), vmem, sems = refs[:7], refs[7:12], refs[12:19], refs[19]
+    hbm, (index_ref, *out_refs), (vmem, sems) = refs[:7], refs[7:12], (refs[12:19], refs[19])
     copies = [
         pltpu.make_async_copy(src, dst, sems.at[k]) for k, (src, dst) in enumerate(zip(hbm, vmem))
     ]
@@ -383,13 +369,16 @@
     tiles = stiff_ref.shape[0]
     width = lax.axis_size("body")
     here, column = lax.axis_index("garm"), lax.axis_index("body")
-    for k, out_ref in enumerate(out_refs):
+    out_distance = 2 + here // 2
+    for n, (out_ref, distance) in enumerate(
+        zip(out_refs, (0, 5 - out_distance, out_distance, 1))
+    ):
         for q in range(3 * tiles):
-            out_ref[4 + q] = body_ref[q]
+            out_ref[5 + q] = body_ref[q]
         for q in range(tiles):
-            out_ref[4 + 3 * tiles + q] = stiff_ref[q]
+            out_ref[5 + 3 * tiles + q] = stiff_ref[q]
         for x in range(2):
-            owner = (here ^ k) * width + (column ^ x)
+            owner = (here ^ distance) * width + (column ^ x)
             live = pc_ref[0, owner]
             for s in range(cap):
                 g = pg_ref[s, owner]
@@ -397,13 +386,8 @@
                 for c in range(3):
                     out_ref[c, place, :] = garm_ref[c, row, :]
                 out_ref[3, place, :] = jnp.where(s < live, cot_ref[row, :], 0.0)
-                out_ref[4 + 4 * tiles, place, :] = jnp.full(
-                    (1, BLOCK), pb_ref[s, owner].astype(f32), f32
-                )
-                if k in (1, 2):
-                    spot, line = 1 + 2 * x, (k - 1) * cap + s
-                else:
-                    spot, line = (0 if k == 0 else 2), x * cap + s
+                out_ref[4, place, :] = jnp.full((1, BLOCK), pb_ref[s, owner].astype(f32), f32)
+                spot, line = 2 * x + n // 2, n % 2 * cap + s
                 index_ref[spot, line : line + 1, :] = jnp.full((1, BLOCK), g.astype(f32), f32)
 
 
@@ -423,7 +407,7 @@
         body_points.reshape(3 * tiles, SUB, BLOCK),
         stiffness.reshape(tiles, SUB, BLOCK),
     )
-    index, *sent = pl.pallas_call(
+    index, own, *sent = pl.pallas_call(
         stage_kernel,
         out_shape=[jax.ShapeDtypeStruct((garm_n, SUB, BLOCK), f32)] + [message] * garm_n,
         in_specs=[pl.BlockSpec(memory_space=pltpu.HBM)] * len(arrays),
@@ -435,29 +419,21 @@
         compiler_params=pltpu.CompilerParams(vmem_limit_bytes=VMEM_LIMIT),
     )(*[pltpu.with_memory_space_constraint(a, pltpu.HBM) for a in arrays])
 
-    def along_garm(k):
-        return lax.ppermute(sent[k], "garm", [(z, z ^ k) for z in range(garm_n)])
+    def along_garm(value, pairs):
+        return lax.ppermute(value, "garm", pairs)
 
     def along_body(value):
         return lax.ppermute(value, "body", [(0, 1), (1, 0)])
 
-    z3, z2, z1 = [along_garm(k) for k in (3, 2, 1)]
-    x0 = along_body(sent[0])
-    body = 4 * tiles
-    near = call(
-        near_bundle_kernel,
-        jax.ShapeDtypeStruct((2 * body + 5, SUB, BLOCK), f32),
-        [],
-        (),
-        (z1, z2),
-    )
-    far = call(
-        far_bundle_kernel,
-        jax.ShapeDtypeStruct((body + 3, SUB, BLOCK), f32),
-        [],
-        (),
-        (z3, near),
-    )
+    cycle = [(0, 2), (2, 1), (1, 3), (3, 0)]
+    got = [
+        along_garm(sent[1], cycle),
+        along_garm(sent[0], [(b, a) for a, b in cycle]),
+        along_garm(sent[2], [(z, z ^ 1) for z in range(garm_n)]),
+    ]
+    bundle = jax.ShapeDtypeStruct((5 + 8 * tiles, SUB, BLOCK), f32)
+    near = call(bundle_kernel, bundle, [], (), (own, got[0]), BUNDLE_COST)
+    far = call(bundle_kernel, bundle, [], (), (got[1], got[2], near), BUNDLE_COST)
     near_other, far_other = along_body(near), along_body(far)
     bgrad, bindex, ggrad = call(
         early_kernel,
@@ -468,7 +444,8 @@
         ),
         [],
         (),
-        (sent[0], sent[1], sent[2], x0, z1, z2, far),
+        (own, *sent, *got, far),
+        EARLY_COST,
     )
     body_shape = jax.ShapeDtypeStruct((3, blocks, BLOCK), f32)
     stiff_shape = jax.ShapeDtypeStruct((blocks, BLOCK), f32)
@@ -478,7 +455,7 @@
         (body_shape, stiff_shape),
         [],
         (),
-        (sent[0], z3, near_other, far_other, bgrad, bindex),
+        (own, near_other, far_other, bgrad, bindex),
     )
     stiff_other = lax.ppermute(stiff, "frame", [(0, 1), (1, 0)])
     garm_total = call(
@@ -486,7 +463,7 @@
         garm_shape,
         [],
         (),
-        (sent[1], sent[2], sent[3], z3, near_other, far_other, ggrad, index),
+        (own, *sent, near_other, far_other, ggrad, index),
     )
     return call(
         final_kernel,

time: 20.4 us -> 18.9 us (0.926)
  waiting for transfers between devices: 5.83 us -> 4.5 us
    ppermute x3, waiting for transfers between devices: 3.82 us -> 2.32 us  [along_garm(): return lax.ppermute(value, 'garm', pairs)]
    ppermute x3 -> x2, waiting for transfers between devices: 1.75 us -> 1.93 us  [along_body(): return lax.ppermute(value, 'body', [(0, 1), (1, 0)])]
    ppermute x3 -> x2, starting transfers between devices: 3.58 us -> 3.41 us  [along_body(): return lax.ppermute(value, 'body', [(0, 1), (1, 0)])]
  transfers between devices with their start and end apart: 7 -> 6, of which waited for: 4 -> 5; matrix products, arithmetic and copies ran while one was open for 0% -> 0% of each run, Pallas kernels for 10% -> 11%
where the time goes in v7:
time: 18.9 us; the launch traced here: 18.8 us
  starting transfers between devices  9.08 us (48%)
  Pallas kernels  4.53 us (24%)
  waiting for transfers between devices  4.5 us (24%)
  between operations  0.65 us (3%)
    ppermute x3, starting transfers between devices, along_garm(): return lax.ppermute(value, 'garm', pairs)  5.67 us
    pallas_call x6, Pallas kernels, call(): pl.pallas_call(kernel, out_shape=out_shape, in_specs=specs, out_specs=jax...  3.53 us
    ppermute x2, starting transfers between devices, along_body(): return lax.ppermute(value, 'body', [(0, 1), (1, 0)])  3.41 us
    ppermute x3, waiting for transfers between devices, along_garm(): return lax.ppermute(value, 'garm', pairs)  2.32 us
    ppermute x2, waiting for transfers between devices, along_body(): return lax.ppermute(value, 'body', [(0, 1), (1, 0)])  1.93 us
    pallas_call x1, Pallas kernels, staged(): pl.pallas_call(stage_kernel, out_shape=[jax.ShapeDtypeStruct((garm_n, SUB...  1 us
  transfers between devices with their start and end apart: 6, of which 5 were waited for; matrix products, arithmetic and copies ran while one was open for 0% of the time, Pallas kernels for 11%

profile of v7, /device:TPU:0, one launch (start us, length us, event | category | flops | bytes accessed | tf_op | source)
XLA Modules:
  0.0 18.8 jit_solution(16877482904402997730)
XLA Ops:
  0.6 1.0 %shard_map.94 = (f32[4,8,128]{2,1,0:T(8,128)S(1)}, f32[13,8,128]{2,1,0:T(8,128)S(1)}, f32[13,8,128]{2,1,0:T(8,128)S(1)}, f32[13,8,128]{2,1,0:T(8,128)S(1)}, f32[13,8,128]{2,1,0:T(8,128)S(1)}) custom-call(s32[4,8]{1,0:T(4,128)} %bitcast.18, s32[4,8]{1,0:T(4,128)} %bitcast.19, s32[1,8]{1,0:T(1,128)} %bitcast.20, f32[3,32,128]{2,1,0:T(8,128)} %bitcast.14, ...), custom_call_target="tpu_custom_call" | custom-call | tf_op jit(solution)/shard_map/pallas_call | solution.py:410
  1.6 4.1 %collective-permute-start = (f32[13,8,128]{2,1,0:T(8,128)S(1)}, f32[13,8,128]{2,1,0:T(8,128)S(1)}, u32[]{:S(2)}, u32[]{:S(2)}) collective-permute-start(f32[13,8,128]{2,1,0:T(8,128)S(1)} %get-tuple-element.18.refs_2_), channel_id=1, source_target_pairs={{0,8},{8,4},{4,12},{12,0},{1,9},{9,5},{5,13},{13,1},{2,10},{10,6},... | collective-permute-start | bytes 159752 | tf_op jit(solution)/shard_map/ppermute | solution.py:423
  5.7 1.1 %collective-permute-start.2 = (f32[13,8,128]{2,1,0:T(8,128)S(1)}, f32[13,8,128]{2,1,0:T(8,128)S(1)}, u32[]{:S(2)}, u32[]{:S(2)}) collective-permute-start(f32[13,8,128]{2,1,0:T(8,128)S(1)} %get-tuple-element.17.refs_1_), channel_id=1, source_target_pairs={{8,0},{4,8},{12,4},{0,12},{9,1},{5,9},{13,5},{1,13},{10,2},{6,10},... | collective-permute-start | bytes 159752 | tf_op jit(solution)/shard_map/ppermute | solution.py:423
  6.8 0.5 %collective-permute-start.3 = (f32[13,8,128]{2,1,0:T(8,128)S(1)}, f32[13,8,128]{2,1,0:T(8,128)S(1)}, u32[]{:S(2)}, u32[]{:S(2)}) collective-permute-start(f32[13,8,128]{2,1,0:T(8,128)S(1)} %get-tuple-element.19.refs_3_), channel_id=1, source_target_pairs={{0,4},{4,0},{8,12},{12,8},{1,5},{5,1},{9,13},{13,9},{2,6},{6,2},{1... | collective-permute-start | bytes 159752 | tf_op jit(solution)/shard_map/ppermute | solution.py:423
  7.3 1.6 %collective-permute-done.two_ref.refs_4_ = f32[13,8,128]{2,1,0:T(8,128)S(1)} collective-permute-done((f32[13,8,128]{2,1,0:T(8,128)S(1)}, f32[13,8,128]{2,1,0:T(8,128)S(1)}, u32[]{:S(2)}, u32[]{:S(2)}) %collective-permute-start) | collective-permute-done | bytes 53280 | tf_op jit(solution)/shard_map/ppermute | solution.py:423
  8.9 1.8 %collective-permute-start.1 = (f32[21,8,128]{2,1,0:T(8,128)S(1)}, f32[21,8,128]{2,1,0:T(8,128)S(1)}, u32[]{:S(2)}, u32[]{:S(2)}) collective-permute-start(f32[21,8,128]{2,1,0:T(8,128)S(1)} %shard_map.95.refs_0_), channel_id=1, source_target_pairs={{0,2},{2,0},{1,3},{3,1},{4,6},{6,4},{5,7},{7,5},{8,10},{10,8},{9,1... | collective-permute-start | bytes 258056 | tf_op jit(solution)/shard_map/ppermute | solution.py:426
  10.8 0.2 %collective-permute-done.2.one_ref.refs_5_ = f32[13,8,128]{2,1,0:T(8,128)S(1)} collective-permute-done((f32[13,8,128]{2,1,0:T(8,128)S(1)}, f32[13,8,128]{2,1,0:T(8,128)S(1)}, u32[]{:S(2)}, u32[]{:S(2)}) %collective-permute-start.2) | collective-permute-done | bytes 53280 | tf_op jit(solution)/shard_map/ppermute | solution.py:423
  11.0 0.5 %collective-permute-done.3.two_ref.refs_6_ = f32[13,8,128]{2,1,0:T(8,128)S(1)} collective-permute-done((f32[13,8,128]{2,1,0:T(8,128)S(1)}, f32[13,8,128]{2,1,0:T(8,128)S(1)}, u32[]{:S(2)}, u32[]{:S(2)}) %collective-permute-start.3) | collective-permute-done | bytes 53280 | tf_op jit(solution)/shard_map/ppermute | solution.py:423
  11.5 1.6 %collective-permute-start.4 = (f32[21,8,128]{2,1,0:T(8,128)S(1)}, f32[21,8,128]{2,1,0:T(8,128)S(1)}, u32[]{:S(2)}, u32[]{:S(2)}) collective-permute-start(f32[21,8,128]{2,1,0:T(8,128)S(1)} %shard_map.96.refs_7_), channel_id=1, source_target_pairs={{0,2},{2,0},{1,3},{3,1},{4,6},{6,4},{5,7},{7,5},{8,10},{10,8},{9,1... | collective-permute-start | bytes 258056 | tf_op jit(solution)/shard_map/ppermute | solution.py:426
  13.1 1.1 %shard_map.97 = (f32[16,512]{1,0:T(8,128)S(1)}, f32[16,128]{1,0:T(8,128)S(1)}, f32[16,384]{1,0:T(8,128)S(1)}) custom-call(f32[13,8,128]{2,1,0:T(8,128)S(1)} %get-tuple-element.16.one_ref.refs_0_.own_ref, f32[13,8,128]{2,1,0:T(8,128)S(1)} %get-tuple-element.17.refs_1_, f32[13,8,128]{2,1,0:T(8,128)S(1)} %get-tuple-element.18.refs_2_, ...), custom_call_target="tpu_custom_call" | custom-call | flops 40000000000 | bytes 1000 | tf_op jit(solution)/shard_map/pallas_call | solution.py:220
  14.1 1.9 %collective-permute-done.4.refs_5_.far_ref = f32[21,8,128]{2,1,0:T(8,128)S(1)} collective-permute-done((f32[21,8,128]{2,1,0:T(8,128)S(1)}, f32[21,8,128]{2,1,0:T(8,128)S(1)}, u32[]{:S(2)}, u32[]{:S(2)}) %collective-permute-start.4) | collective-permute-done | bytes 86048 | tf_op jit(solution)/shard_map/ppermute | solution.py:426
  16.1 0.0 collective-permute-done.1.refs_4_.near_ref
  16.1 0.9 %shard_map.99 = (f32[3,16,128]{2,1,0:T(8,128)S(1)}, f32[16,128]{1,0:T(8,128)S(1)}) custom-call(f32[13,8,128]{2,1,0:T(8,128)S(1)} %get-tuple-element.16.one_ref.refs_0_.own_ref, f32[21,8,128]{2,1,0:T(8,128)S(1)} %collective-permute-done.1.refs_4_.near_ref, f32[21,8,128]{2,1,0:T(8,128)S(1)} %collective-permute-done.4.refs_5_.far_ref, ...), custom_call_target="tpu_custom_call" | custom-call | tf_op jit(solution)/shard_map/pallas_call | solution.py:220
  16.9 0.0 collective-permute-start.5
  16.9 0.9 %shard_map.98.garm_ref = f32[3,32,128]{2,1,0:T(8,128)S(1)} custom-call(f32[13,8,128]{2,1,0:T(8,128)S(1)} %get-tuple-element.16.one_ref.refs_0_.own_ref, f32[13,8,128]{2,1,0:T(8,128)S(1)} %get-tuple-element.17.refs_1_, f32[13,8,128]{2,1,0:T(8,128)S(1)} %get-tuple-element.18.refs_2_, f32[13,8,128]{2,1,0:T(8,128)S(1)} %get-tuple-element.19.refs_3_, ...), custom_call_target="tpu_custom_call" | custom-call | tf_op jit(solution)/shard_map/pallas_call | solution.py:220
  17.9 0.3 %collective-permute-done.5.other_ref = f32[16,128]{1,0:T(8,128)S(1)} collective-permute-done((f32[16,128]{1,0:T(8,128)S(1)}, f32[16,128]{1,0:T(8,128)S(1)}, u32[]{:S(2)}, u32[]{:S(2)}) %collective-permute-start.5) | collective-permute-done | bytes 8224 | tf_op jit(solution)/shard_map/ppermute | solution.py:460
  18.1 0.6 %shard_map.100 = (f32[3,32,128]{2,1,0:T(8,128)}, f32[3,16,128]{2,1,0:T(8,128)}, f32[16,128]{1,0:T(8,128)}) custom-call(f32[3,32,128]{2,1,0:T(8,128)S(1)} %shard_map.98.garm_ref, f32[3,16,128]{2,1,0:T(8,128)S(1)} %get-tuple-element.24.body_ref, f32[16,128]{1,0:T(8,128)S(1)} %get-tuple-element.25.mine_ref, f32[16,128]{1,0:T(8,128)S(1)} %collective-permute-done.5.other_ref), custom_call_target="tpu_custom_call" | custom-call | tf_op jit(solution)/shard_map/pallas_call | solution.py:220
  (2 shorter events, 0.0 us)
Async XLA Ops:
  1.6 7.3 %collective-permute-start = (f32[13,8,128]{2,1,0:T(8,128)S(1)}, f32[13,8,128]{2,1,0:T(8,128)S(1)}, u32[]{:S(2)}, u32[]{:S(2)}) collective-permute-start(f32[13,8,128]{2,1,0:T(8,128)S(1)} %get-tuple-element.18.refs_2_), channel_id=1, source_target_pairs={{0,8},{8,4},{4,12},{12,0},{1,9},{9,5},{5,13},{13,1},{2,10},{10,6},... | collective-permute-start | bytes 159752 | tf_op jit(solution)/shard_map/ppermute | solution.py:423
  5.7 5.3 %collective-permute-start.2 = (f32[13,8,128]{2,1,0:T(8,128)S(1)}, f32[13,8,128]{2,1,0:T(8,128)S(1)}, u32[]{:S(2)}, u32[]{:S(2)}) collective-permute-start(f32[13,8,128]{2,1,0:T(8,128)S(1)} %get-tuple-element.17.refs_1_), channel_id=1, source_target_pairs={{8,0},{4,8},{12,4},{0,12},{9,1},{5,9},{13,5},{1,13},{10,2},{6,10},... | collective-permute-start | bytes 159752 | tf_op jit(solution)/shard_map/ppermute | solution.py:423
  6.8 4.7 %collective-permute-start.3 = (f32[13,8,128]{2,1,0:T(8,128)S(1)}, f32[13,8,128]{2,1,0:T(8,128)S(1)}, u32[]{:S(2)}, u32[]{:S(2)}) collective-permute-start(f32[13,8,128]{2,1,0:T(8,128)S(1)} %get-tuple-element.19.refs_3_), channel_id=1, source_target_pairs={{0,4},{4,0},{8,12},{12,8},{1,5},{5,1},{9,13},{13,9},{2,6},{6,2},{1... | collective-permute-start | bytes 159752 | tf_op jit(solution)/shard_map/ppermute | solution.py:423
  8.9 7.1 %collective-permute-start.1 = (f32[21,8,128]{2,1,0:T(8,128)S(1)}, f32[21,8,128]{2,1,0:T(8,128)S(1)}, u32[]{:S(2)}, u32[]{:S(2)}) collective-permute-start(f32[21,8,128]{2,1,0:T(8,128)S(1)} %shard_map.95.refs_0_), channel_id=1, source_target_pairs={{0,2},{2,0},{1,3},{3,1},{4,6},{6,4},{5,7},{7,5},{8,10},{10,8},{9,1... | collective-permute-start | bytes 258056 | tf_op jit(solution)/shard_map/ppermute | solution.py:426
  11.5 4.5 %collective-permute-start.4 = (f32[21,8,128]{2,1,0:T(8,128)S(1)}, f32[21,8,128]{2,1,0:T(8,128)S(1)}, u32[]{:S(2)}, u32[]{:S(2)}) collective-permute-start(f32[21,8,128]{2,1,0:T(8,128)S(1)} %shard_map.96.refs_7_), channel_id=1, source_target_pairs={{0,2},{2,0},{1,3},{3,1},{4,6},{6,4},{5,7},{7,5},{8,10},{10,8},{9,1... | collective-permute-start | bytes 258056 | tf_op jit(solution)/shard_map/ppermute | solution.py:426
  16.9 1.2 %collective-permute-start.5 = (f32[16,128]{1,0:T(8,128)S(1)}, f32[16,128]{1,0:T(8,128)S(1)}, u32[]{:S(2)}, u32[]{:S(2)}) collective-permute-start(f32[16,128]{1,0:T(8,128)S(1)} %get-tuple-element.25.mine_ref), channel_id=1, source_target_pairs={{0,1},{1,0},{2,3},{3,2},{4,5},{5,4},{6,7},{7,6},{8,9},{9,8},{10,11... | collective-permute-start | bytes 24584 | tf_op jit(solution)/shard_map/ppermute | solution.py:460

commit v8 on v7

--- a/solution.py
+++ b/solution.py
@@ -10,6 +10,7 @@
 BLOCK = 128
 SUB = 8
 VMEM_LIMIT = 32 * 1024 * 1024
+STEPS = (0, 1, 3, 2)
 EARLY_COST = 40_000_000_000
 BUNDLE_COST = 1000
 
@@ -273,14 +274,37 @@
     return read_table(ref, 5, step)
 
 
-def bundle_kernel(one_ref, two_ref, *refs):
-    out_ref = refs[-1]
-    body = one_ref.shape[0] - 5
+def pack_slots(ref):
+    a, b, c, d, e = slot_tiles(ref)
+    return [halves(flip(a), b), halves(flip(c), d), e]
+
+
+def unpack_top(tiles):
+    a, b, c = tiles
+    return [a, flip(a), b, flip(b), flip(c)]
+
+
+def unpack_bottom(tiles):
+    a, b, c = tiles
+    return [flip(a), a, flip(b), b, c]
+
+
+def near_bundle_kernel(own_ref, one_ref, two_ref, out_ref):
+    body = own_ref.shape[0] - 5
+    for n, ref in enumerate((own_ref, one_ref, two_ref)):
+        for q in range(body):
+            out_ref[n * body + q] = ref[5 + q]
+    for k, tile in enumerate(bottom_tiles(one_ref, two_ref) + pack_slots(own_ref)):
+        out_ref[3 * body + k] = tile
+
+
+def far_bundle_kernel(ref, near_ref, out_ref):
+    del near_ref
+    body = ref.shape[0] - 5
     for q in range(body):
-        out_ref[q] = one_ref[5 + q]
-        out_ref[body + q] = two_ref[5 + q]
-    for k, tile in enumerate(bottom_tiles(one_ref, two_ref)):
-        out_ref[2 * body + k] = tile
+        out_ref[q] = ref[5 + q]
+    for k, tile in enumerate(pack_slots(ref)):
+        out_ref[body + k] = tile
 
 
 def top_tiles(one_ref, two_ref):
@@ -298,13 +322,13 @@
     step = (own_ref.shape[0] - 5) // 4
     own = message_table(own_ref, step)
     a, b, c = [message_table(ref, step) for ref in got_refs]
-    here = top_tiles(own_ref, got_refs[0])
-    far = top_tiles(got_refs[1], got_refs[2])
+    here = top_tiles(own_ref, got_refs[2])
+    next_to = top_tiles(got_refs[0], got_refs[1])
     work = [
         body_work(here, own),
-        body_work(far, own),
-        garm_work(top_tiles(own_ref, sent_refs[0]), own, a),
-        garm_work(top_tiles(sent_refs[1], sent_refs[2]), b, c),
+        body_work(next_to, own),
+        garm_work(top_tiles(own_ref, sent_refs[2]), own, c),
+        garm_work(top_tiles(sent_refs[0], sent_refs[1]), a, b),
     ]
     out = gradients(work)
     for n in range(2):
@@ -312,13 +336,18 @@
         bgrad_ref[rows, :] = jnp.concatenate(out[n], axis=1)
         ggrad_ref[rows, :] = jnp.concatenate(out[2 + n][:3], axis=1)
     bindex_ref[:SUB, :] = here[4]
-    bindex_ref[SUB:, :] = far[4]
+    bindex_ref[SUB:, :] = next_to[4]
 
 
 def late_body_kernel(own_ref, near_ref, far_ref, bgrad_ref, bindex_ref, out_ref, stiff_ref):
     body = own_ref.shape[0] - 5
     own = message_table(own_ref, body // 4)
-    tiles = [[ref[2 * body + k] for k in range(5)] for ref in (near_ref, far_ref)]
+    top = unpack_top([near_ref[3 * body + 5 + k] for k in range(3)])
+    bottom = unpack_bottom([far_ref[body + k] for k in range(3)])
+    tiles = [
+        [near_ref[3 * body + k] for k in range(5)],
+        [halves(x, y) for x, y in zip(top, bottom)],
+    ]
     out = gradients([body_work(part, own) for part in tiles])
     grads = [jnp.concatenate(rows, axis=1) for rows in out]
     index = jnp.concatenate([bindex_ref[...]] + [part[4] for part in tiles], axis=0)
@@ -335,12 +364,11 @@
         refs[4:],
     )
     body = own_ref.shape[0] - 5
-    near, far = [
-        [read_table(ref, n * body, body // 4) for n in range(2)] for ref in (near_ref, far_ref)
-    ]
+    own, a, b = [read_table(near_ref, n * body, body // 4) for n in range(3)]
+    c = read_table(far_ref, 0, body // 4)
     work = [
-        garm_work(bottom_tiles(own_ref, sent_refs[0]), *near),
-        garm_work(bottom_tiles(sent_refs[1], sent_refs[2]), *far),
+        garm_work(bottom_tiles(sent_refs[0], sent_refs[1]), a, b),
+        garm_work(bottom_tiles(own_ref, sent_refs[2]), own, c),
     ]
     grads = [jnp.concatenate(rows[:3], axis=1) for rows in gradients(work)]
     index = jnp.concatenate([index_ref[k] for k in range(index_ref.shape[0])], axis=0)
@@ -369,16 +397,15 @@
     tiles = stiff_ref.shape[0]
     width = lax.axis_size("body")
     here, column = lax.axis_index("garm"), lax.axis_index("body")
-    out_distance = 2 + here // 2
-    for n, (out_ref, distance) in enumerate(
-        zip(out_refs, (0, 5 - out_distance, out_distance, 1))
-    ):
+    garm_n = lax.axis_size("garm")
+    for n, out_ref in enumerate(out_refs):
+        place_z = lax.rem(here + STEPS[n], garm_n)
         for q in range(3 * tiles):
             out_ref[5 + q] = body_ref[q]
         for q in range(tiles):
             out_ref[5 + 3 * tiles + q] = stiff_ref[q]
         for x in range(2):
-            owner = (here ^ distance) * width + (column ^ x)
+            owner = place_z * width + (column ^ x)
             live = pc_ref[0, owner]
             for s in range(cap):
                 g = pg_ref[s, owner]
@@ -387,7 +414,8 @@
                     out_ref[c, place, :] = garm_ref[c, row, :]
                 out_ref[3, place, :] = jnp.where(s < live, cot_ref[row, :], 0.0)
                 out_ref[4, place, :] = jnp.full((1, BLOCK), pb_ref[s, owner].astype(f32), f32)
-                spot, line = 2 * x + n // 2, n % 2 * cap + s
+                spot = 2 * x + (x if n in (0, 3) else 1 - x)
+                line = (0 if n < 2 else cap) + s
                 index_ref[spot, line : line + 1, :] = jnp.full((1, BLOCK), g.astype(f32), f32)
 
 
@@ -419,21 +447,29 @@
         compiler_params=pltpu.CompilerParams(vmem_limit_bytes=VMEM_LIMIT),
     )(*[pltpu.with_memory_space_constraint(a, pltpu.HBM) for a in arrays])
 
-    def along_garm(value, pairs):
-        return lax.ppermute(value, "garm", pairs)
+    def along_garm(value, step):
+        return lax.ppermute(value, "garm", [(z, (z + step) % garm_n) for z in range(garm_n)])
 
     def along_body(value):
         return lax.ppermute(value, "body", [(0, 1), (1, 0)])
 
-    cycle = [(0, 2), (2, 1), (1, 3), (3, 0)]
-    got = [
-        along_garm(sent[1], cycle),
-        along_garm(sent[0], [(b, a) for a, b in cycle]),
-        along_garm(sent[2], [(z, z ^ 1) for z in range(garm_n)]),
-    ]
-    bundle = jax.ShapeDtypeStruct((5 + 8 * tiles, SUB, BLOCK), f32)
-    near = call(bundle_kernel, bundle, [], (), (own, got[0]), BUNDLE_COST)
-    far = call(bundle_kernel, bundle, [], (), (got[1], got[2], near), BUNDLE_COST)
+    got = [along_garm(sent[n], STEPS[1 + n]) for n in (1, 0, 2)]
+    near = call(
+        near_bundle_kernel,
+        jax.ShapeDtypeStruct((8 + 12 * tiles, SUB, BLOCK), f32),
+        [],
+        (),
+        (own, got[0], got[1]),
+        BUNDLE_COST,
+    )
+    far = call(
+        far_bundle_kernel,
+        jax.ShapeDtypeStruct((3 + 4 * tiles, SUB, BLOCK), f32),
+        [],
+        (),
+        (got[2], near),
+        BUNDLE_COST,
+    )
     near_other, far_other = along_body(near), along_body(far)
     bgrad, bindex, ggrad = call(
         early_kernel,

time: 18.9 us -> 19.1 us (1.011)
    ppermute x3, waiting for transfers between devices: 2.32 us -> 2.82 us  [along_garm(): lax.ppermute(value, 'garm', [(z, (z + step) % garm_n) for z in range(garm...]
    ppermute x2, waiting for transfers between devices: 1.93 us -> 1.47 us  [along_body(): return lax.ppermute(value, 'body', [(0, 1), (1, 0)])]
    ppermute x3, starting transfers between devices: 5.67 us -> 6.11 us  [along_garm(): lax.ppermute(value, 'garm', [(z, (z + step) % garm_n) for z in range(garm...]
    ppermute x2, starting transfers between devices: 3.41 us -> 3.07 us  [along_body(): return lax.ppermute(value, 'body', [(0, 1), (1, 0)])]
where the time goes in v8:
time: 19.1 us; the launch traced here: 18.9 us
  starting transfers between devices  9.19 us (48%)
  Pallas kernels  4.53 us (24%)
  waiting for transfers between devices  4.53 us (24%)
  between operations  0.65 us (3%)
    ppermute x3, starting transfers between devices, along_garm(): lax.ppermute(value, 'garm', [(z, (z + step) % garm_n) for z in range(garm...  6.11 us
    pallas_call x6, Pallas kernels, call(): pl.pallas_call(kernel, out_shape=out_shape, in_specs=specs, out_specs=jax...  3.53 us
    ppermute x2, starting transfers between devices, along_body(): return lax.ppermute(value, 'body', [(0, 1), (1, 0)])  3.07 us
    ppermute x3, waiting for transfers between devices, along_garm(): lax.ppermute(value, 'garm', [(z, (z + step) % garm_n) for z in range(garm...  2.82 us
    ppermute x2, waiting for transfers between devices, along_body(): return lax.ppermute(value, 'body', [(0, 1), (1, 0)])  1.47 us
    pallas_call x1, Pallas kernels, staged(): pl.pallas_call(stage_kernel, out_shape=[jax.ShapeDtypeStruct((garm_n, SUB...  1 us
  transfers between devices with their start and end apart: 6, of which 5 were waited for; matrix products, arithmetic and copies ran while one was open for 0% of the time, Pallas kernels for 11%

profile of v8, /device:TPU:0, one launch (start us, length us, event | category | flops | bytes accessed | tf_op | source)
XLA Modules:
  0.0 18.9 jit_solution(4830564499171331840)
XLA Ops:
  0.6 1.0 %shard_map.94 = (f32[4,8,128]{2,1,0:T(8,128)S(1)}, f32[13,8,128]{2,1,0:T(8,128)S(1)}, f32[13,8,128]{2,1,0:T(8,128)S(1)}, f32[13,8,128]{2,1,0:T(8,128)S(1)}, f32[13,8,128]{2,1,0:T(8,128)S(1)}) custom-call(s32[4,8]{1,0:T(4,128)} %bitcast.18, s32[4,8]{1,0:T(4,128)} %bitcast.19, s32[1,8]{1,0:T(1,128)} %bitcast.20, f32[3,32,128]{2,1,0:T(8,128)} %bitcast.14, ...), custom_call_target="tpu_custom_call" | custom-call | tf_op jit(solution)/shard_map/pallas_call | solution.py:438
  1.6 3.1 %collective-permute-start.1 = (f32[13,8,128]{2,1,0:T(8,128)S(1)}, f32[13,8,128]{2,1,0:T(8,128)S(1)}, u32[]{:S(2)}, u32[]{:S(2)}) collective-permute-start(f32[13,8,128]{2,1,0:T(8,128)S(1)} %get-tuple-element.17.refs_1_), channel_id=1, source_target_pairs={{0,4},{4,8},{8,12},{12,0},{1,5},{5,9},{9,13},{13,1},{2,6},{6,10},{... | collective-permute-start | bytes 159752 | tf_op jit(solution)/shard_map/ppermute | solution.py:451
  4.7 2.1 %collective-permute-start = (f32[13,8,128]{2,1,0:T(8,128)S(1)}, f32[13,8,128]{2,1,0:T(8,128)S(1)}, u32[]{:S(2)}, u32[]{:S(2)}) collective-permute-start(f32[13,8,128]{2,1,0:T(8,128)S(1)} %get-tuple-element.18.refs_2_), channel_id=1, source_target_pairs={{0,12},{4,0},{8,4},{12,8},{1,13},{5,1},{9,5},{13,9},{2,14},{6,2},{... | collective-permute-start | bytes 159752 | tf_op jit(solution)/shard_map/ppermute | solution.py:451
  6.8 0.9 %collective-permute-start.3 = (f32[13,8,128]{2,1,0:T(8,128)S(1)}, f32[13,8,128]{2,1,0:T(8,128)S(1)}, u32[]{:S(2)}, u32[]{:S(2)}) collective-permute-start(f32[13,8,128]{2,1,0:T(8,128)S(1)} %get-tuple-element.19.refs_3_), channel_id=1, source_target_pairs={{0,8},{4,12},{8,0},{12,4},{1,9},{5,13},{9,1},{13,5},{2,10},{6,14},... | collective-permute-start | bytes 159752 | tf_op jit(solution)/shard_map/ppermute | solution.py:451
  7.8 1.2 %collective-permute-done.1.two_ref.refs_5_ = f32[13,8,128]{2,1,0:T(8,128)S(1)} collective-permute-done((f32[13,8,128]{2,1,0:T(8,128)S(1)}, f32[13,8,128]{2,1,0:T(8,128)S(1)}, u32[]{:S(2)}, u32[]{:S(2)}) %collective-permute-start.1) | collective-permute-done | bytes 53280 | tf_op jit(solution)/shard_map/ppermute | solution.py:451
  8.9 0.5 %collective-permute-done.one_ref.refs_4_ = f32[13,8,128]{2,1,0:T(8,128)S(1)} collective-permute-done((f32[13,8,128]{2,1,0:T(8,128)S(1)}, f32[13,8,128]{2,1,0:T(8,128)S(1)}, u32[]{:S(2)}, u32[]{:S(2)}) %collective-permute-start) | collective-permute-done | bytes 53280 | tf_op jit(solution)/shard_map/ppermute | solution.py:451
  9.4 1.6 %collective-permute-start.2 = (f32[32,8,128]{2,1,0:T(8,128)S(1)}, f32[32,8,128]{2,1,0:T(8,128)S(1)}, u32[]{:S(2)}, u32[]{:S(2)}) collective-permute-start(f32[32,8,128]{2,1,0:T(8,128)S(1)} %shard_map.95.near_ref), channel_id=1, source_target_pairs={{0,2},{2,0},{1,3},{3,1},{4,6},{6,4},{5,7},{7,5},{8,10},{10,8},{9,1... | collective-permute-start | bytes 393224 | tf_op jit(solution)/shard_map/ppermute | solution.py:454
  11.0 1.2 %collective-permute-done.3.ref.refs_6_ = f32[13,8,128]{2,1,0:T(8,128)S(1)} collective-permute-done((f32[13,8,128]{2,1,0:T(8,128)S(1)}, f32[13,8,128]{2,1,0:T(8,128)S(1)}, u32[]{:S(2)}, u32[]{:S(2)}) %collective-permute-start.3) | collective-permute-done | bytes 53280 | tf_op jit(solution)/shard_map/ppermute | solution.py:451
  12.2 1.5 %collective-permute-start.4 = (f32[11,8,128]{2,1,0:T(8,128)S(1)}, f32[11,8,128]{2,1,0:T(8,128)S(1)}, u32[]{:S(2)}, u32[]{:S(2)}) collective-permute-start(f32[11,8,128]{2,1,0:T(8,128)S(1)} %shard_map.96.refs_7_), channel_id=1, source_target_pairs={{0,2},{2,0},{1,3},{3,1},{4,6},{6,4},{5,7},{7,5},{8,10},{10,8},{9,1... | collective-permute-start | bytes 135176 | tf_op jit(solution)/shard_map/ppermute | solution.py:454
  13.7 1.1 %shard_map.97 = (f32[16,512]{1,0:T(8,128)S(1)}, f32[16,128]{1,0:T(8,128)S(1)}, f32[16,384]{1,0:T(8,128)S(1)}) custom-call(f32[13,8,128]{2,1,0:T(8,128)S(1)} %get-tuple-element.16.own_ref.refs_0_, f32[13,8,128]{2,1,0:T(8,128)S(1)} %get-tuple-element.17.refs_1_, f32[13,8,128]{2,1,0:T(8,128)S(1)} %get-tuple-element.18.refs_2_, ...), custom_call_target="tpu_custom_call" | custom-call | flops 40000000000 | bytes 1000 | tf_op jit(solution)/shard_map/pallas_call | solution.py:221
  14.7 1.5 %collective-permute-done.4.refs_5_.far_ref = f32[11,8,128]{2,1,0:T(8,128)S(1)} collective-permute-done((f32[11,8,128]{2,1,0:T(8,128)S(1)}, f32[11,8,128]{2,1,0:T(8,128)S(1)}, u32[]{:S(2)}, u32[]{:S(2)}) %collective-permute-start.4) | collective-permute-done | bytes 45088 | tf_op jit(solution)/shard_map/ppermute | solution.py:454
  16.2 0.0 collective-permute-done.2.refs_4_.near_ref
  16.2 0.9 %shard_map.99 = (f32[3,16,128]{2,1,0:T(8,128)S(1)}, f32[16,128]{1,0:T(8,128)S(1)}) custom-call(f32[13,8,128]{2,1,0:T(8,128)S(1)} %get-tuple-element.16.own_ref.refs_0_, f32[32,8,128]{2,1,0:T(8,128)S(1)} %collective-permute-done.2.refs_4_.near_ref, f32[11,8,128]{2,1,0:T(8,128)S(1)} %collective-permute-done.4.refs_5_.far_ref, ...), custom_call_target="tpu_custom_call" | custom-call | tf_op jit(solution)/shard_map/pallas_call | solution.py:221
  17.1 0.0 collective-permute-start.5
  17.1 0.9 %shard_map.98.garm_ref = f32[3,32,128]{2,1,0:T(8,128)S(1)} custom-call(f32[13,8,128]{2,1,0:T(8,128)S(1)} %get-tuple-element.16.own_ref.refs_0_, f32[13,8,128]{2,1,0:T(8,128)S(1)} %get-tuple-element.17.refs_1_, f32[13,8,128]{2,1,0:T(8,128)S(1)} %get-tuple-element.18.refs_2_, f32[13,8,128]{2,1,0:T(8,128)S(1)} %get-tuple-element.19.refs_3_, ...), custom_call_target="tpu_custom_call" | custom-call | tf_op jit(solution)/shard_map/pallas_call | solution.py:221
  18.0 0.2 %collective-permute-done.5.other_ref = f32[16,128]{1,0:T(8,128)S(1)} collective-permute-done((f32[16,128]{1,0:T(8,128)S(1)}, f32[16,128]{1,0:T(8,128)S(1)}, u32[]{:S(2)}, u32[]{:S(2)}) %collective-permute-start.5) | collective-permute-done | bytes 8224 | tf_op jit(solution)/shard_map/ppermute | solution.py:496
  18.3 0.6 %shard_map.100 = (f32[3,32,128]{2,1,0:T(8,128)}, f32[3,16,128]{2,1,0:T(8,128)}, f32[16,128]{1,0:T(8,128)}) custom-call(f32[3,32,128]{2,1,0:T(8,128)S(1)} %shard_map.98.garm_ref, f32[3,16,128]{2,1,0:T(8,128)S(1)} %get-tuple-element.24.body_ref, f32[16,128]{1,0:T(8,128)S(1)} %get-tuple-element.25.mine_ref, f32[16,128]{1,0:T(8,128)S(1)} %collective-permute-done.5.other_ref), custom_call_target="tpu_custom_call" | custom-call | tf_op jit(solution)/shard_map/pallas_call | solution.py:221
  (2 shorter events, 0.0 us)
Async XLA Ops:
  1.6 7.3 %collective-permute-start.1 = (f32[13,8,128]{2,1,0:T(8,128)S(1)}, f32[13,8,128]{2,1,0:T(8,128)S(1)}, u32[]{:S(2)}, u32[]{:S(2)}) collective-permute-start(f32[13,8,128]{2,1,0:T(8,128)S(1)} %get-tuple-element.17.refs_1_), channel_id=1, source_target_pairs={{0,4},{4,8},{8,12},{12,0},{1,5},{5,9},{9,13},{13,1},{2,6},{6,10},{... | collective-permute-start | bytes 159752 | tf_op jit(solution)/shard_map/ppermute | solution.py:451
  4.7 4.7 %collective-permute-start = (f32[13,8,128]{2,1,0:T(8,128)S(1)}, f32[13,8,128]{2,1,0:T(8,128)S(1)}, u32[]{:S(2)}, u32[]{:S(2)}) collective-permute-start(f32[13,8,128]{2,1,0:T(8,128)S(1)} %get-tuple-element.18.refs_2_), channel_id=1, source_target_pairs={{0,12},{4,0},{8,4},{12,8},{1,13},{5,1},{9,5},{13,9},{2,14},{6,2},{... | collective-permute-start | bytes 159752 | tf_op jit(solution)/shard_map/ppermute | solution.py:451
  6.8 5.3 %collective-permute-start.3 = (f32[13,8,128]{2,1,0:T(8,128)S(1)}, f32[13,8,128]{2,1,0:T(8,128)S(1)}, u32[]{:S(2)}, u32[]{:S(2)}) collective-permute-start(f32[13,8,128]{2,1,0:T(8,128)S(1)} %get-tuple-element.19.refs_3_), channel_id=1, source_target_pairs={{0,8},{4,12},{8,0},{12,4},{1,9},{5,13},{9,1},{13,5},{2,10},{6,14},... | collective-permute-start | bytes 159752 | tf_op jit(solution)/shard_map/ppermute | solution.py:451
  9.4 6.8 %collective-permute-start.2 = (f32[32,8,128]{2,1,0:T(8,128)S(1)}, f32[32,8,128]{2,1,0:T(8,128)S(1)}, u32[]{:S(2)}, u32[]{:S(2)}) collective-permute-start(f32[32,8,128]{2,1,0:T(8,128)S(1)} %shard_map.95.near_ref), channel_id=1, source_target_pairs={{0,2},{2,0},{1,3},{3,1},{4,6},{6,4},{5,7},{7,5},{8,10},{10,8},{9,1... | collective-permute-start | bytes 393224 | tf_op jit(solution)/shard_map/ppermute | solution.py:454
  12.2 4.0 %collective-permute-start.4 = (f32[11,8,128]{2,1,0:T(8,128)S(1)}, f32[11,8,128]{2,1,0:T(8,128)S(1)}, u32[]{:S(2)}, u32[]{:S(2)}) collective-permute-start(f32[11,8,128]{2,1,0:T(8,128)S(1)} %shard_map.96.refs_7_), channel_id=1, source_target_pairs={{0,2},{2,0},{1,3},{3,1},{4,6},{6,4},{5,7},{7,5},{8,10},{10,8},{9,1... | collective-permute-start | bytes 135176 | tf_op jit(solution)/shard_map/ppermute | solution.py:454
  17.1 1.2 %collective-permute-start.5 = (f32[16,128]{1,0:T(8,128)S(1)}, f32[16,128]{1,0:T(8,128)S(1)}, u32[]{:S(2)}, u32[]{:S(2)}) collective-permute-start(f32[16,128]{1,0:T(8,128)S(1)} %get-tuple-element.25.mine_ref), channel_id=1, source_target_pairs={{0,1},{1,0},{2,3},{3,2},{4,5},{5,4},{6,7},{7,6},{8,9},{9,8},{10,11... | collective-permute-start | bytes 24584 | tf_op jit(solution)/shard_map/ppermute | solution.py:496

commit v9 on v8

--- a/solution.py
+++ b/solution.py
@@ -10,8 +10,9 @@
 BLOCK = 128
 SUB = 8
 VMEM_LIMIT = 32 * 1024 * 1024
-STEPS = (0, 1, 3, 2)
-EARLY_COST = 40_000_000_000
+STEPS = (0, 3, 1, 2)
+FIRST_COST = 1_000_000_000
+SECOND_COST = 40_000_000_000
 BUNDLE_COST = 1000
 
 amplitude = 0.05
@@ -289,22 +290,22 @@
     return [flip(a), a, flip(b), b, c]
 
 
-def near_bundle_kernel(own_ref, one_ref, two_ref, out_ref):
-    body = own_ref.shape[0] - 5
-    for n, ref in enumerate((own_ref, one_ref, two_ref)):
+def bundle_tiles(ref):
+    return [ref[5 + q] for q in range(ref.shape[0] - 5)] + pack_slots(ref)
+
+
+def near_bundle_kernel(one_ref, two_ref, out_ref):
+    body = one_ref.shape[0] - 5
+    for n, ref in enumerate((one_ref, two_ref)):
         for q in range(body):
             out_ref[n * body + q] = ref[5 + q]
-    for k, tile in enumerate(bottom_tiles(one_ref, two_ref) + pack_slots(own_ref)):
-        out_ref[3 * body + k] = tile
-
-
-def far_bundle_kernel(ref, near_ref, out_ref):
-    del near_ref
-    body = ref.shape[0] - 5
-    for q in range(body):
-        out_ref[q] = ref[5 + q]
-    for k, tile in enumerate(pack_slots(ref)):
-        out_ref[body + k] = tile
+    for k, tile in enumerate(bottom_tiles(one_ref, two_ref)):
+        out_ref[2 * body + k] = tile
+
+
+def far_bundle_kernel(ref, *refs):
+    for k, tile in enumerate(bundle_tiles(ref)):
+        refs[-1][k] = tile
 
 
 def top_tiles(one_ref, two_ref):
@@ -315,64 +316,65 @@
     return [halves(flip(a), b) for a, b in zip(slot_tiles(one_ref), slot_tiles(two_ref))]
 
 
-def early_kernel(*refs):
-    own_ref, sent_refs, got_refs, far_ref = refs[0], refs[1:4], refs[4:7], refs[7]
-    del far_ref
-    bgrad_ref, bindex_ref, ggrad_ref = refs[8:]
+def store(work, index, bgrad_ref, bindex_ref, ggrad_ref):
+    out = gradients(work)
+    for n, value in enumerate(index):
+        rows = slice(n * SUB, (n + 1) * SUB)
+        bgrad_ref[rows, :] = jnp.concatenate(out[n], axis=1)
+        ggrad_ref[rows, :] = jnp.concatenate(out[len(index) + n][:3], axis=1)
+        bindex_ref[rows, :] = value
+
+
+def first_kernel(own_ref, sent0, sent1, got0, got1, after_ref, *out_refs):
+    del after_ref
     step = (own_ref.shape[0] - 5) // 4
+    tiles = top_tiles(got0, got1)
+    work = [
+        body_work(tiles, message_table(own_ref, step)),
+        garm_work(top_tiles(sent0, sent1), message_table(got0, step), message_table(got1, step)),
+    ]
+    store(work, [tiles[4]], *out_refs)
+
+
+def second_kernel(own_ref, sent0, sent1, sent2, got2, near_ref, after_ref, *out_refs):
+    del after_ref
+    body = own_ref.shape[0] - 5
+    step = body // 4
     own = message_table(own_ref, step)
-    a, b, c = [message_table(ref, step) for ref in got_refs]
-    here = top_tiles(own_ref, got_refs[2])
-    next_to = top_tiles(got_refs[0], got_refs[1])
+    here = top_tiles(own_ref, got2)
+    near = [near_ref[2 * body + k] for k in range(5)]
     work = [
         body_work(here, own),
-        body_work(next_to, own),
-        garm_work(top_tiles(own_ref, sent_refs[2]), own, c),
-        garm_work(top_tiles(sent_refs[0], sent_refs[1]), a, b),
-    ]
-    out = gradients(work)
-    for n in range(2):
-        rows = slice(n * SUB, (n + 1) * SUB)
-        bgrad_ref[rows, :] = jnp.concatenate(out[n], axis=1)
-        ggrad_ref[rows, :] = jnp.concatenate(out[2 + n][:3], axis=1)
-    bindex_ref[:SUB, :] = here[4]
-    bindex_ref[SUB:, :] = next_to[4]
-
-
-def late_body_kernel(own_ref, near_ref, far_ref, bgrad_ref, bindex_ref, out_ref, stiff_ref):
+        body_work(near, own),
+        garm_work(top_tiles(own_ref, sent2), own, message_table(got2, step)),
+        garm_work(
+            bottom_tiles(sent0, sent1), *[read_table(near_ref, n * body, step) for n in range(2)]
+        ),
+    ]
+    store(work, [here[4], near[4]], *out_refs)
+
+
+def late_body_kernel(own_ref, x0_ref, far_ref, bg1, bg2, bi1, bi2, out_ref, stiff_ref):
     body = own_ref.shape[0] - 5
-    own = message_table(own_ref, body // 4)
-    top = unpack_top([near_ref[3 * body + 5 + k] for k in range(3)])
+    top = unpack_top([x0_ref[body + k] for k in range(3)])
     bottom = unpack_bottom([far_ref[body + k] for k in range(3)])
-    tiles = [
-        [near_ref[3 * body + k] for k in range(5)],
-        [halves(x, y) for x, y in zip(top, bottom)],
-    ]
-    out = gradients([body_work(part, own) for part in tiles])
-    grads = [jnp.concatenate(rows, axis=1) for rows in out]
-    index = jnp.concatenate([bindex_ref[...]] + [part[4] for part in tiles], axis=0)
-    total = scatter(index, jnp.concatenate([bgrad_ref[...]] + grads, axis=0), out_ref.shape[1])
+    tiles = [halves(x, y) for x, y in zip(top, bottom)]
+    out = gradients([body_work(tiles, message_table(own_ref, body // 4))])
+    grads = jnp.concatenate([bg1[...], bg2[...], jnp.concatenate(out[0], axis=1)], axis=0)
+    index = jnp.concatenate([bi1[...], bi2[...], tiles[4]], axis=0)
+    total = scatter(index, grads, out_ref.shape[1])
     for c in range(3):
         out_ref[c] = total[:, c * BLOCK : (c + 1) * BLOCK]
     stiff_ref[...] = total[:, 3 * BLOCK :]
 
 
-def late_garm_kernel(*refs):
-    own_ref, sent_refs, (near_ref, far_ref, ggrad_ref, index_ref, out_ref) = (
-        refs[0],
-        refs[1:4],
-        refs[4:],
-    )
-    body = own_ref.shape[0] - 5
-    own, a, b = [read_table(near_ref, n * body, body // 4) for n in range(3)]
-    c = read_table(far_ref, 0, body // 4)
-    work = [
-        garm_work(bottom_tiles(sent_refs[0], sent_refs[1]), a, b),
-        garm_work(bottom_tiles(own_ref, sent_refs[2]), own, c),
-    ]
-    grads = [jnp.concatenate(rows[:3], axis=1) for rows in gradients(work)]
+def late_garm_kernel(own_ref, sent2, x0_ref, far_ref, gg1, gg2, index_ref, out_ref):
+    step = (own_ref.shape[0] - 5) // 4
+    tables = [read_table(ref, 0, step) for ref in (x0_ref, far_ref)]
+    out = gradients([garm_work(bottom_tiles(own_ref, sent2), *tables)])
+    grads = jnp.concatenate([gg1[...], gg2[...], jnp.concatenate(out[0][:3], axis=1)], axis=0)
     index = jnp.concatenate([index_ref[k] for k in range(index_ref.shape[0])], axis=0)
-    total = scatter(index, jnp.concatenate([ggrad_ref[...]] + grads, axis=0), out_ref.shape[1])
+    total = scatter(index, grads, out_ref.shape[1])
     for c in range(3):
         out_ref[c] = total[:, c * BLOCK : (c + 1) * BLOCK]
 
@@ -384,7 +386,8 @@
 
 
 def stage_kernel(*refs):
-    hbm, (index_ref, *out_refs), (vmem, sems) = refs[:7], refs[7:12], (refs[12:19], refs[19])
+    hbm, (index_ref, bundle_ref, *out_refs) = refs[:7], refs[7:13]
+    vmem, sems = refs[13:20], refs[20]
     copies = [
         pltpu.make_async_copy(src, dst, sems.at[k]) for k, (src, dst) in enumerate(zip(hbm, vmem))
     ]
@@ -414,9 +417,11 @@
                     out_ref[c, place, :] = garm_ref[c, row, :]
                 out_ref[3, place, :] = jnp.where(s < live, cot_ref[row, :], 0.0)
                 out_ref[4, place, :] = jnp.full((1, BLOCK), pb_ref[s, owner].astype(f32), f32)
-                spot = 2 * x + (x if n in (0, 3) else 1 - x)
+                spot = 2 * x + (n in (0, 3))
                 line = (0 if n < 2 else cap) + s
                 index_ref[spot, line : line + 1, :] = jnp.full((1, BLOCK), g.astype(f32), f32)
+    for k, tile in enumerate(bundle_tiles(out_refs[0])):
+        bundle_ref[k] = tile
 
 
 def staged(garment, cotangent, body_points, stiffness, pg, pb, pc):
@@ -435,11 +440,12 @@
         body_points.reshape(3 * tiles, SUB, BLOCK),
         stiffness.reshape(tiles, SUB, BLOCK),
     )
-    index, own, *sent = pl.pallas_call(
+    bundle = jax.ShapeDtypeStruct((3 + 4 * tiles, SUB, BLOCK), f32)
+    index, own_bundle, own, *sent = pl.pallas_call(
         stage_kernel,
-        out_shape=[jax.ShapeDtypeStruct((garm_n, SUB, BLOCK), f32)] + [message] * garm_n,
+        out_shape=[jax.ShapeDtypeStruct((garm_n, SUB, BLOCK), f32), bundle] + [message] * garm_n,
         in_specs=[pl.BlockSpec(memory_space=pltpu.HBM)] * len(arrays),
-        out_specs=[pl.BlockSpec(memory_space=pltpu.VMEM)] * (garm_n + 1),
+        out_specs=[pl.BlockSpec(memory_space=pltpu.VMEM)] * (garm_n + 2),
         scratch_shapes=[
             (pltpu.SMEM if k < 3 else pltpu.VMEM)(a.shape, a.dtype) for k, a in enumerate(arrays)
         ]
@@ -454,34 +460,27 @@
         return lax.ppermute(value, "body", [(0, 1), (1, 0)])
 
     got = [along_garm(sent[n], STEPS[1 + n]) for n in (1, 0, 2)]
-    near = call(
-        near_bundle_kernel,
-        jax.ShapeDtypeStruct((8 + 12 * tiles, SUB, BLOCK), f32),
+    x0 = along_body(own_bundle)
+    near_shape = jax.ShapeDtypeStruct((5 + 8 * tiles, SUB, BLOCK), f32)
+    near = call(near_bundle_kernel, near_shape, [], (), (got[0], got[1]), BUNDLE_COST)
+
+    def batch_shapes(count):
+        return tuple(
+            jax.ShapeDtypeStruct((count * SUB, width * BLOCK), f32) for width in (4, 1, 3)
+        )
+
+    bg1, bi1, gg1 = call(
+        first_kernel,
+        batch_shapes(1),
         [],
         (),
-        (own, got[0], got[1]),
-        BUNDLE_COST,
-    )
-    far = call(
-        far_bundle_kernel,
-        jax.ShapeDtypeStruct((3 + 4 * tiles, SUB, BLOCK), f32),
-        [],
-        (),
-        (got[2], near),
-        BUNDLE_COST,
-    )
+        (own, sent[0], sent[1], got[0], got[1], near),
+        FIRST_COST,
+    )
+    far = call(far_bundle_kernel, bundle, [], (), (got[2], x0, bg1), BUNDLE_COST)
     near_other, far_other = along_body(near), along_body(far)
-    bgrad, bindex, ggrad = call(
-        early_kernel,
-        (
-            jax.ShapeDtypeStruct((2 * SUB, 4 * BLOCK), f32),
-            jax.ShapeDtypeStruct((2 * SUB, BLOCK), f32),
-            jax.ShapeDtypeStruct((2 * SUB, 3 * BLOCK), f32),
-        ),
-        [],
-        (),
-        (own, *sent, *got, far),
-        EARLY_COST,
+    bg2, bi2, gg2 = call(
+        second_kernel, batch_shapes(2), [], (), (own, *sent, got[2], near_other, far), SECOND_COST
     )
     body_shape = jax.ShapeDtypeStruct((3, blocks, BLOCK), f32)
     stiff_shape = jax.ShapeDtypeStruct((blocks, BLOCK), f32)
@@ -491,7 +490,7 @@
         (body_shape, stiff_shape),
         [],
         (),
-        (own, near_other, far_other, bgrad, bindex),
+        (own, x0, far_other, bg1, bg2, bi1, bi2),
     )
     stiff_other = lax.ppermute(stiff, "frame", [(0, 1), (1, 0)])
     garm_total = call(
@@ -499,7 +498,7 @@
         garm_shape,
         [],
         (),
-        (own, *sent, near_other, far_other, ggrad, index),
+        (own, sent[2], x0, far_other, gg1, gg2, index),
     )
     return call(
         final_kernel,

time: 19.1 us -> 18.9 us (0.990)
  waiting for transfers between devices: 4.53 us -> 2.46 us
  starting transfers between devices: 9.19 us -> 10.7 us
  Pallas kernels: 4.53 us -> 4.96 us
    ppermute x3, waiting for transfers between devices: 2.82 us -> 0.27 us  [along_garm(): lax.ppermute(value, 'garm', [(z, (z + step) % garm_n) for z in range(garm...]
    ppermute x2 -> x3, starting transfers between devices: 3.07 us -> 4.56 us  [along_body(): return lax.ppermute(value, 'body', [(0, 1), (1, 0)])]
    pallas_call x6 -> x7, Pallas kernels: 3.53 us -> 3.96 us  [call(): pl.pallas_call(kernel, out_shape=out_shape, in_specs=specs, out_specs=jax...]
    ppermute x2 -> x3, waiting for transfers between devices: 1.47 us -> 1.78 us  [along_body(): return lax.ppermute(value, 'body', [(0, 1), (1, 0)])]
  transfers between devices with their start and end apart: 6 -> 7, of which waited for: 5 -> 6; matrix products, arithmetic and copies ran while one was open for 0% -> 0% of each run, Pallas kernels for 11% -> 14%
where the time goes in v9:
time: 18.9 us; the launch traced here: 18.8 us
  starting transfers between devices  10.7 us (57%)
  Pallas kernels  4.96 us (26%)
  waiting for transfers between devices  2.46 us (13%)
  between operations  0.65 us (3%)
    ppermute x3, starting transfers between devices, along_garm(): lax.ppermute(value, 'garm', [(z, (z + step) % garm_n) for z in range(garm...  6.11 us
    ppermute x3, starting transfers between devices, along_body(): return lax.ppermute(value, 'body', [(0, 1), (1, 0)])  4.56 us
    pallas_call x7, Pallas kernels, call(): pl.pallas_call(kernel, out_shape=out_shape, in_specs=specs, out_specs=jax...  3.96 us
    ppermute x3, waiting for transfers between devices, along_body(): return lax.ppermute(value, 'body', [(0, 1), (1, 0)])  1.78 us
    pallas_call x1, Pallas kernels, staged(): pl.pallas_call(stage_kernel, out_shape=[jax.ShapeDtypeStruct((garm_n, SUB...  1 us
    ppermute x1, waiting for transfers between devices, staged(): stiff_other = lax.ppermute(stiff, 'frame', [(0, 1), (1, 0)])  0.41 us
  transfers between devices with their start and end apart: 7, of which 6 were waited for; matrix products, arithmetic and copies ran while one was open for 0% of the time, Pallas kernels for 14%

profile of v9, /device:TPU:0, one launch (start us, length us, event | category | flops | bytes accessed | tf_op | source)
XLA Modules:
  0.0 18.8 jit_solution(7433333511392942689)
XLA Ops:
  0.6 1.0 %shard_map.94 = (f32[4,8,128]{2,1,0:T(8,128)S(1)}, f32[11,8,128]{2,1,0:T(8,128)S(1)}, f32[13,8,128]{2,1,0:T(8,128)S(1)}, f32[13,8,128]{2,1,0:T(8,128)S(1)}, f32[...) custom-call(s32[4,8]{1,0:T(4,128)} %bitcast.18, s32[4,8]{1,0:T(4,128)} %bitcast.19, s32[1,8]{1,0:T(1,128)} %bitcast.20, ...), custom_call_target="tpu_custom_call" | custom-call | tf_op jit(solution)/shard_map/pallas_call | solution.py:444
  1.6 3.1 %collective-permute-start.2 = (f32[13,8,128]{2,1,0:T(8,128)S(1)}, f32[13,8,128]{2,1,0:T(8,128)S(1)}, u32[]{:S(2)}, u32[]{:S(2)}) collective-permute-start(f32[13,8,128]{2,1,0:T(8,128)S(1)} %get-tuple-element.24.sent1), channel_id=1, source_target_pairs={{0,4},{4,8},{8,12},{12,0},{1,5},{5,9},{9,13},{13,1},{2,6},{6,10},{... | collective-permute-start | bytes 159752 | tf_op jit(solution)/shard_map/ppermute | solution.py:457
  4.7 2.1 %collective-permute-start.3 = (f32[13,8,128]{2,1,0:T(8,128)S(1)}, f32[13,8,128]{2,1,0:T(8,128)S(1)}, u32[]{:S(2)}, u32[]{:S(2)}) collective-permute-start(f32[13,8,128]{2,1,0:T(8,128)S(1)} %get-tuple-element.23.sent0), channel_id=1, source_target_pairs={{0,12},{4,0},{8,4},{12,8},{1,13},{5,1},{9,5},{13,9},{2,14},{6,2},{... | collective-permute-start | bytes 159752 | tf_op jit(solution)/shard_map/ppermute | solution.py:457
  6.8 0.9 %collective-permute-start.1 = (f32[13,8,128]{2,1,0:T(8,128)S(1)}, f32[13,8,128]{2,1,0:T(8,128)S(1)}, u32[]{:S(2)}, u32[]{:S(2)}) collective-permute-start(f32[13,8,128]{2,1,0:T(8,128)S(1)} %get-tuple-element.21.sent2), channel_id=1, source_target_pairs={{0,8},{4,12},{8,0},{12,4},{1,9},{5,13},{9,1},{13,5},{2,10},{6,14},... | collective-permute-start | bytes 159752 | tf_op jit(solution)/shard_map/ppermute | solution.py:457
  7.8 1.5 %collective-permute-start = (f32[11,8,128]{2,1,0:T(8,128)S(1)}, f32[11,8,128]{2,1,0:T(8,128)S(1)}, u32[]{:S(2)}, u32[]{:S(2)}) collective-permute-start(f32[11,8,128]{2,1,0:T(8,128)S(1)} %get-tuple-element.22), channel_id=1, source_target_pairs={{0,2},{2,0},{1,3},{3,1},{4,6},{6,4},{5,7},{7,5},{8,10},{10,8},{9,1... | collective-permute-start | bytes 135176 | tf_op jit(solution)/shard_map/ppermute | solution.py:460
  9.3 0.0 collective-permute-done.2.one_ref.got0
  9.3 0.2 collective-permute-done.3.two_ref.got1
  9.4 1.6 %collective-permute-start.5 = (f32[21,8,128]{2,1,0:T(8,128)S(1)}, f32[21,8,128]{2,1,0:T(8,128)S(1)}, u32[]{:S(2)}, u32[]{:S(2)}) collective-permute-start(f32[21,8,128]{2,1,0:T(8,128)S(1)} %shard_map.95.after_ref), channel_id=1, source_target_pairs={{0,2},{2,0},{1,3},{3,1},{4,6},{6,4},{5,7},{7,5},{8,10},{10,8},{9,1... | collective-permute-start | bytes 258056 | tf_op jit(solution)/shard_map/ppermute | solution.py:460
  11.0 0.8 %shard_map.96 = (f32[8,512]{1,0:T(8,128)S(1)}, f32[8,128]{1,0:T(8,128)S(1)}, f32[8,384]{1,0:T(8,128)S(1)}) custom-call(f32[13,8,128]{2,1,0:T(8,128)S(1)} %get-tuple-element.20.own_ref, f32[13,8,128]{2,1,0:T(8,128)S(1)} %get-tuple-element.23.sent0, f32[13,8,128]{2,1,0:T(8,128)S(1)} %get-tuple-element.24.sent1, ...), custom_call_target="tpu_custom_call" | custom-call | flops 1000000000 | bytes 1000 | tf_op jit(solution)/shard_map/pallas_call | solution.py:222
  11.7 0.3 %collective-permute-done.refs_0_.x0_ref = f32[11,8,128]{2,1,0:T(8,128)S(1)} collective-permute-done((f32[11,8,128]{2,1,0:T(8,128)S(1)}, f32[11,8,128]{2,1,0:T(8,128)S(1)}, u32[]{:S(2)}, u32[]{:S(2)}) %collective-permute-start) | collective-permute-done | bytes 45088 | tf_op jit(solution)/shard_map/ppermute | solution.py:460
  12.1 0.1 collective-permute-done.1.ref.got2
  12.2 1.5 %collective-permute-start.4 = (f32[11,8,128]{2,1,0:T(8,128)S(1)}, f32[11,8,128]{2,1,0:T(8,128)S(1)}, u32[]{:S(2)}, u32[]{:S(2)}) collective-permute-start(f32[11,8,128]{2,1,0:T(8,128)S(1)} %shard_map.97.after_ref), channel_id=1, source_target_pairs={{0,2},{2,0},{1,3},{3,1},{4,6},{6,4},{5,7},{7,5},{8,10},{10,8},{9,1... | collective-permute-start | bytes 135176 | tf_op jit(solution)/shard_map/ppermute | solution.py:460
  13.7 0.3 %collective-permute-done.5.near_ref = f32[21,8,128]{2,1,0:T(8,128)S(1)} collective-permute-done((f32[21,8,128]{2,1,0:T(8,128)S(1)}, f32[21,8,128]{2,1,0:T(8,128)S(1)}, u32[]{:S(2)}, u32[]{:S(2)}) %collective-permute-start.5) | collective-permute-done | bytes 86048 | tf_op jit(solution)/shard_map/ppermute | solution.py:460
  14.0 1.1 %shard_map.98 = (f32[16,512]{1,0:T(8,128)S(1)}, f32[16,128]{1,0:T(8,128)S(1)}, f32[16,384]{1,0:T(8,128)S(1)}) custom-call(f32[13,8,128]{2,1,0:T(8,128)S(1)} %get-tuple-element.20.own_ref, f32[13,8,128]{2,1,0:T(8,128)S(1)} %get-tuple-element.23.sent0, f32[13,8,128]{2,1,0:T(8,128)S(1)} %get-tuple-element.24.sent1, f32[13,8,128]{2,1,0:T(8,128)S(1)} %get-tuple-element.21.sent2, ...), custom_call_target="tpu_custom_call" | custom-call | flops 40000000000 | bytes 1000 | tf_op jit(solution)/shard_map/pallas_call | solution.py:222
  15.1 1.2 %collective-permute-done.4.far_ref = f32[11,8,128]{2,1,0:T(8,128)S(1)} collective-permute-done((f32[11,8,128]{2,1,0:T(8,128)S(1)}, f32[11,8,128]{2,1,0:T(8,128)S(1)}, u32[]{:S(2)}, u32[]{:S(2)}) %collective-permute-start.4) | collective-permute-done | bytes 45088 | tf_op jit(solution)/shard_map/ppermute | solution.py:460
  16.2 0.7 %shard_map.100 = (f32[3,16,128]{2,1,0:T(8,128)S(1)}, f32[16,128]{1,0:T(8,128)S(1)}) custom-call(f32[13,8,128]{2,1,0:T(8,128)S(1)} %get-tuple-element.20.own_ref, f32[11,8,128]{2,1,0:T(8,128)S(1)} %collective-permute-done.refs_0_.x0_ref, f32[11,8,128]{2,1,0:T(8,128)S(1)} %collective-permute-done.4.far_ref, f32[8,512]{1,0:T(8,128)S(1)} %get-tuple-element.25.refs_1_.bg1, ...), custom_call_target="tpu_custom_call" | custom-call | tf_op jit(solution)/shard_map/pallas_call | solution.py:222
  16.9 0.0 collective-permute-start.6
  16.9 0.8 %shard_map.99.garm_ref = f32[3,32,128]{2,1,0:T(8,128)S(1)} custom-call(f32[13,8,128]{2,1,0:T(8,128)S(1)} %get-tuple-element.20.own_ref, f32[13,8,128]{2,1,0:T(8,128)S(1)} %get-tuple-element.21.sent2, f32[11,8,128]{2,1,0:T(8,128)S(1)} %collective-permute-done.refs_0_.x0_ref, f32[11,8,128]{2,1,0:T(8,128)S(1)} %collective-permute-done.4.far_ref, ...), custom_call_target="tpu_custom_call" | custom-call | tf_op jit(solution)/shard_map/pallas_call | solution.py:222
  17.7 0.4 %collective-permute-done.6.other_ref = f32[16,128]{1,0:T(8,128)S(1)} collective-permute-done((f32[16,128]{1,0:T(8,128)S(1)}, f32[16,128]{1,0:T(8,128)S(1)}, u32[]{:S(2)}, u32[]{:S(2)}) %collective-permute-start.6) | collective-permute-done | bytes 8224 | tf_op jit(solution)/shard_map/ppermute | solution.py:495
  18.1 0.6 %shard_map.101 = (f32[3,32,128]{2,1,0:T(8,128)}, f32[3,16,128]{2,1,0:T(8,128)}, f32[16,128]{1,0:T(8,128)}) custom-call(f32[3,32,128]{2,1,0:T(8,128)S(1)} %shard_map.99.garm_ref, f32[3,16,128]{2,1,0:T(8,128)S(1)} %get-tuple-element.32.body_ref, f32[16,128]{1,0:T(8,128)S(1)} %get-tuple-element.33.mine_ref, f32[16,128]{1,0:T(8,128)S(1)} %collective-permute-done.6.other_ref), custom_call_target="tpu_custom_call" | custom-call | tf_op jit(solution)/shard_map/pallas_call | solution.py:222
  (2 shorter events, 0.0 us)
Async XLA Ops:
  1.6 7.6 %collective-permute-start.2 = (f32[13,8,128]{2,1,0:T(8,128)S(1)}, f32[13,8,128]{2,1,0:T(8,128)S(1)}, u32[]{:S(2)}, u32[]{:S(2)}) collective-permute-start(f32[13,8,128]{2,1,0:T(8,128)S(1)} %get-tuple-element.24.sent1), channel_id=1, source_target_pairs={{0,4},{4,8},{8,12},{12,0},{1,5},{5,9},{9,13},{13,1},{2,6},{6,10},{... | collective-permute-start | bytes 159752 | tf_op jit(solution)/shard_map/ppermute | solution.py:457
  4.7 4.7 %collective-permute-start.3 = (f32[13,8,128]{2,1,0:T(8,128)S(1)}, f32[13,8,128]{2,1,0:T(8,128)S(1)}, u32[]{:S(2)}, u32[]{:S(2)}) collective-permute-start(f32[13,8,128]{2,1,0:T(8,128)S(1)} %get-tuple-element.23.sent0), channel_id=1, source_target_pairs={{0,12},{4,0},{8,4},{12,8},{1,13},{5,1},{9,5},{13,9},{2,14},{6,2},{... | collective-permute-start | bytes 159752 | tf_op jit(solution)/shard_map/ppermute | solution.py:457
  6.8 5.3 %collective-permute-start.1 = (f32[13,8,128]{2,1,0:T(8,128)S(1)}, f32[13,8,128]{2,1,0:T(8,128)S(1)}, u32[]{:S(2)}, u32[]{:S(2)}) collective-permute-start(f32[13,8,128]{2,1,0:T(8,128)S(1)} %get-tuple-element.21.sent2), channel_id=1, source_target_pairs={{0,8},{4,12},{8,0},{12,4},{1,9},{5,13},{9,1},{13,5},{2,10},{6,14},... | collective-permute-start | bytes 159752 | tf_op jit(solution)/shard_map/ppermute | solution.py:457
  7.8 4.3 %collective-permute-start = (f32[11,8,128]{2,1,0:T(8,128)S(1)}, f32[11,8,128]{2,1,0:T(8,128)S(1)}, u32[]{:S(2)}, u32[]{:S(2)}) collective-permute-start(f32[11,8,128]{2,1,0:T(8,128)S(1)} %get-tuple-element.22), channel_id=1, source_target_pairs={{0,2},{2,0},{1,3},{3,1},{4,6},{6,4},{5,7},{7,5},{8,10},{10,8},{9,1... | collective-permute-start | bytes 135176 | tf_op jit(solution)/shard_map/ppermute | solution.py:460
  9.4 4.6 %collective-permute-start.5 = (f32[21,8,128]{2,1,0:T(8,128)S(1)}, f32[21,8,128]{2,1,0:T(8,128)S(1)}, u32[]{:S(2)}, u32[]{:S(2)}) collective-permute-start(f32[21,8,128]{2,1,0:T(8,128)S(1)} %shard_map.95.after_ref), channel_id=1, source_target_pairs={{0,2},{2,0},{1,3},{3,1},{4,6},{6,4},{5,7},{7,5},{8,10},{10,8},{9,1... | collective-permute-start | bytes 258056 | tf_op jit(solution)/shard_map/ppermute | solution.py:460
  12.2 4.1 %collective-permute-start.4 = (f32[11,8,128]{2,1,0:T(8,128)S(1)}, f32[11,8,128]{2,1,0:T(8,128)S(1)}, u32[]{:S(2)}, u32[]{:S(2)}) collective-permute-start(f32[11,8,128]{2,1,0:T(8,128)S(1)} %shard_map.97.after_ref), channel_id=1, source_target_pairs={{0,2},{2,0},{1,3},{3,1},{4,6},{6,4},{5,7},{7,5},{8,10},{10,8},{9,1... | collective-permute-start | bytes 135176 | tf_op jit(solution)/shard_map/ppermute | solution.py:460
  16.9 1.2 %collective-permute-start.6 = (f32[16,128]{1,0:T(8,128)S(1)}, f32[16,128]{1,0:T(8,128)S(1)}, u32[]{:S(2)}, u32[]{:S(2)}) collective-permute-start(f32[16,128]{1,0:T(8,128)S(1)} %get-tuple-element.33.mine_ref), channel_id=1, source_target_pairs={{0,1},{1,0},{2,3},{3,2},{4,5},{5,4},{6,7},{7,6},{8,9},{9,8},{10,11... | collective-permute-start | bytes 24584 | tf_op jit(solution)/shard_map/ppermute | solution.py:495

commit v10 on v9

--- a/solution.py
+++ b/solution.py
@@ -10,9 +10,8 @@
 BLOCK = 128
 SUB = 8
 VMEM_LIMIT = 32 * 1024 * 1024
-STEPS = (0, 3, 1, 2)
-FIRST_COST = 1_000_000_000
-SECOND_COST = 40_000_000_000
+STEPS = (0, 1, 3, 2)
+SAME_COST = 40_000_000_000
 BUNDLE_COST = 1000
 
 amplitude = 0.05
@@ -275,37 +274,37 @@
     return read_table(ref, 5, step)
 
 
-def pack_slots(ref):
-    a, b, c, d, e = slot_tiles(ref)
-    return [halves(flip(a), b), halves(flip(c), d), e]
+def pack(tiles):
+    a, b, c, d, e = tiles
+    return [halves(a, flip(b)), halves(c, flip(d)), e]
 
 
 def unpack_top(tiles):
     a, b, c = tiles
-    return [a, flip(a), b, flip(b), flip(c)]
+    return [a, flip(a), b, flip(b), c]
 
 
 def unpack_bottom(tiles):
     a, b, c = tiles
-    return [flip(a), a, flip(b), b, c]
-
-
-def bundle_tiles(ref):
-    return [ref[5 + q] for q in range(ref.shape[0] - 5)] + pack_slots(ref)
-
-
-def near_bundle_kernel(one_ref, two_ref, out_ref):
+    return [flip(a), a, flip(b), b, flip(c)]
+
+
+def half_message(ref, other):
+    slots = slot_tiles(ref)
+    if other:
+        slots = [flip(tile) for tile in slots]
+    return [ref[5 + q] for q in range(ref.shape[0] - 5)] + pack(slots)
+
+
+def forward_kernel(one_ref, two_ref, own_ref, out_ref, own_out_ref):
     body = one_ref.shape[0] - 5
     for n, ref in enumerate((one_ref, two_ref)):
         for q in range(body):
             out_ref[n * body + q] = ref[5 + q]
     for k, tile in enumerate(bottom_tiles(one_ref, two_ref)):
         out_ref[2 * body + k] = tile
-
-
-def far_bundle_kernel(ref, *refs):
-    for k, tile in enumerate(bundle_tiles(ref)):
-        refs[-1][k] = tile
+    for k, tile in enumerate(half_message(own_ref, True)):
+        own_out_ref[k] = tile
 
 
 def top_tiles(one_ref, two_ref):
@@ -325,56 +324,54 @@
         bindex_ref[rows, :] = value
 
 
-def first_kernel(own_ref, sent0, sent1, got0, got1, after_ref, *out_refs):
-    del after_ref
-    step = (own_ref.shape[0] - 5) // 4
-    tiles = top_tiles(got0, got1)
-    work = [
-        body_work(tiles, message_table(own_ref, step)),
-        garm_work(top_tiles(sent0, sent1), message_table(got0, step), message_table(got1, step)),
-    ]
-    store(work, [tiles[4]], *out_refs)
-
-
-def second_kernel(own_ref, sent0, sent1, sent2, got2, near_ref, after_ref, *out_refs):
+def same_kernel(own_ref, sent0, sent1, sent2, got0, got1, got2, after_ref, *out_refs):
     del after_ref
     body = own_ref.shape[0] - 5
     step = body // 4
     own = message_table(own_ref, step)
-    here = top_tiles(own_ref, got2)
+    next_to = top_tiles(got0, got1)
+    last = unpack_bottom([got2[body + k] for k in range(3)])
+    here = [halves(x, y) for x, y in zip(slot_tiles(own_ref), last)]
+    work = [
+        body_work(next_to, own),
+        body_work(here, own),
+        garm_work(top_tiles(sent0, sent1), message_table(got0, step), message_table(got1, step)),
+        garm_work(top_tiles(own_ref, sent2), own, read_table(got2, 0, step)),
+    ]
+    store(work, [next_to[4], here[4]], *out_refs)
+
+
+def late_body_kernel(own_ref, near_ref, x0_ref, far_ref, bgrad_ref, bindex_ref, out_ref, stiff_ref):
+    body = own_ref.shape[0] - 5
+    own = message_table(own_ref, body // 4)
     near = [near_ref[2 * body + k] for k in range(5)]
-    work = [
-        body_work(here, own),
-        body_work(near, own),
-        garm_work(top_tiles(own_ref, sent2), own, message_table(got2, step)),
-        garm_work(
-            bottom_tiles(sent0, sent1), *[read_table(near_ref, n * body, step) for n in range(2)]
-        ),
-    ]
-    store(work, [here[4], near[4]], *out_refs)
-
-
-def late_body_kernel(own_ref, x0_ref, far_ref, bg1, bg2, bi1, bi2, out_ref, stiff_ref):
-    body = own_ref.shape[0] - 5
     top = unpack_top([x0_ref[body + k] for k in range(3)])
     bottom = unpack_bottom([far_ref[body + k] for k in range(3)])
-    tiles = [halves(x, y) for x, y in zip(top, bottom)]
-    out = gradients([body_work(tiles, message_table(own_ref, body // 4))])
-    grads = jnp.concatenate([bg1[...], bg2[...], jnp.concatenate(out[0], axis=1)], axis=0)
-    index = jnp.concatenate([bi1[...], bi2[...], tiles[4]], axis=0)
-    total = scatter(index, grads, out_ref.shape[1])
+    tiles = [near, [halves(x, y) for x, y in zip(top, bottom)]]
+    out = gradients([body_work(part, own) for part in tiles])
+    grads = [bgrad_ref[...]] + [jnp.concatenate(rows, axis=1) for rows in out]
+    index = jnp.concatenate([bindex_ref[...]] + [part[4] for part in tiles], axis=0)
+    total = scatter(index, jnp.concatenate(grads, axis=0), out_ref.shape[1])
     for c in range(3):
         out_ref[c] = total[:, c * BLOCK : (c + 1) * BLOCK]
     stiff_ref[...] = total[:, 3 * BLOCK :]
 
 
-def late_garm_kernel(own_ref, sent2, x0_ref, far_ref, gg1, gg2, index_ref, out_ref):
-    step = (own_ref.shape[0] - 5) // 4
-    tables = [read_table(ref, 0, step) for ref in (x0_ref, far_ref)]
-    out = gradients([garm_work(bottom_tiles(own_ref, sent2), *tables)])
-    grads = jnp.concatenate([gg1[...], gg2[...], jnp.concatenate(out[0][:3], axis=1)], axis=0)
+def late_garm_kernel(
+    own_ref, sent0, sent1, sent2, near_ref, x0_ref, far_ref, ggrad_ref, index_ref, out_ref
+):
+    body = own_ref.shape[0] - 5
+    step = body // 4
+    near = [read_table(near_ref, n * body, step) for n in range(2)]
+    far = [read_table(ref, 0, step) for ref in (x0_ref, far_ref)]
+    work = [
+        garm_work(bottom_tiles(sent0, sent1), *near),
+        garm_work(bottom_tiles(own_ref, sent2), *far),
+    ]
+    out = gradients(work)
+    grads = [ggrad_ref[...]] + [jnp.concatenate(rows[:3], axis=1) for rows in out]
     index = jnp.concatenate([index_ref[k] for k in range(index_ref.shape[0])], axis=0)
-    total = scatter(index, grads, out_ref.shape[1])
+    total = scatter(index, jnp.concatenate(grads, axis=0), out_ref.shape[1])
     for c in range(3):
         out_ref[c] = total[:, c * BLOCK : (c + 1) * BLOCK]
 
@@ -386,8 +383,8 @@
 
 
 def stage_kernel(*refs):
-    hbm, (index_ref, bundle_ref, *out_refs) = refs[:7], refs[7:13]
-    vmem, sems = refs[13:20], refs[20]
+    hbm, (index_ref, same_ref, other_ref, *out_refs) = refs[:7], refs[7:14]
+    vmem, sems = refs[14:21], refs[21]
     copies = [
         pltpu.make_async_copy(src, dst, sems.at[k]) for k, (src, dst) in enumerate(zip(hbm, vmem))
     ]
@@ -420,8 +417,9 @@
                 spot = 2 * x + (n in (0, 3))
                 line = (0 if n < 2 else cap) + s
                 index_ref[spot, line : line + 1, :] = jnp.full((1, BLOCK), g.astype(f32), f32)
-    for k, tile in enumerate(bundle_tiles(out_refs[0])):
-        bundle_ref[k] = tile
+    for ref, other in ((same_ref, False), (other_ref, True)):
+        for k, tile in enumerate(half_message(out_refs[3], other)):
+            ref[k] = tile
 
 
 def staged(garment, cotangent, body_points, stiffness, pg, pb, pc):
@@ -440,12 +438,12 @@
         body_points.reshape(3 * tiles, SUB, BLOCK),
         stiffness.reshape(tiles, SUB, BLOCK),
     )
-    bundle = jax.ShapeDtypeStruct((3 + 4 * tiles, SUB, BLOCK), f32)
-    index, own_bundle, own, *sent = pl.pallas_call(
+    half = jax.ShapeDtypeStruct((3 + 4 * tiles, SUB, BLOCK), f32)
+    index, last_same, last_other, own, *sent = pl.pallas_call(
         stage_kernel,
-        out_shape=[jax.ShapeDtypeStruct((garm_n, SUB, BLOCK), f32), bundle] + [message] * garm_n,
+        out_shape=[jax.ShapeDtypeStruct((garm_n, SUB, BLOCK), f32), half, half] + [message] * garm_n,
         in_specs=[pl.BlockSpec(memory_space=pltpu.HBM)] * len(arrays),
-        out_specs=[pl.BlockSpec(memory_space=pltpu.VMEM)] * (garm_n + 2),
+        out_specs=[pl.BlockSpec(memory_space=pltpu.VMEM)] * (garm_n + 3),
         scratch_shapes=[
             (pltpu.SMEM if k < 3 else pltpu.VMEM)(a.shape, a.dtype) for k, a in enumerate(arrays)
         ]
@@ -459,28 +457,25 @@
     def along_body(value):
         return lax.ppermute(value, "body", [(0, 1), (1, 0)])
 
-    got = [along_garm(sent[n], STEPS[1 + n]) for n in (1, 0, 2)]
-    x0 = along_body(own_bundle)
+    got = [along_garm(sent[1], STEPS[2]), along_garm(sent[0], STEPS[1]), along_garm(last_same, STEPS[3])]
+    far = lax.ppermute(
+        last_other,
+        ("garm", "body"),
+        [(2 * z + x, 2 * ((z + STEPS[3]) % garm_n) + 1 - x) for z in range(garm_n) for x in range(2)],
+    )
     near_shape = jax.ShapeDtypeStruct((5 + 8 * tiles, SUB, BLOCK), f32)
-    near = call(near_bundle_kernel, near_shape, [], (), (got[0], got[1]), BUNDLE_COST)
+    near, own_half = call(
+        forward_kernel, (near_shape, half), [], (), (got[0], got[1], own), BUNDLE_COST
+    )
+    near_other, x0 = along_body(near), along_body(own_half)
 
     def batch_shapes(count):
         return tuple(
             jax.ShapeDtypeStruct((count * SUB, width * BLOCK), f32) for width in (4, 1, 3)
         )
 
-    bg1, bi1, gg1 = call(
-        first_kernel,
-        batch_shapes(1),
-        [],
-        (),
-        (own, sent[0], sent[1], got[0], got[1], near),
-        FIRST_COST,
-    )
-    far = call(far_bundle_kernel, bundle, [], (), (got[2], x0, bg1), BUNDLE_COST)
-    near_other, far_other = along_body(near), along_body(far)
-    bg2, bi2, gg2 = call(
-        second_kernel, batch_shapes(2), [], (), (own, *sent, got[2], near_other, far), SECOND_COST
+    bgrad, bindex, ggrad = call(
+        same_kernel, batch_shapes(2), [], (), (own, *sent, *got, near), SAME_COST
     )
     body_shape = jax.ShapeDtypeStruct((3, blocks, BLOCK), f32)
     stiff_shape = jax.ShapeDtypeStruct((blocks, BLOCK), f32)
@@ -490,7 +485,7 @@
         (body_shape, stiff_shape),
         [],
         (),
-        (own, x0, far_other, bg1, bg2, bi1, bi2),
+        (own, near_other, x0, far, bgrad, bindex),
     )
     stiff_other = lax.ppermute(stiff, "frame", [(0, 1), (1, 0)])
     garm_total = call(
@@ -498,7 +493,7 @@
         garm_shape,
         [],
         (),
-        (own, sent[2], x0, far_other, gg1, gg2, index),
+        (own, *sent, near_other, x0, far, ggrad, index),
     )
     return call(
         final_kernel,

time: 18.9 us -> 18.9 us (level)
  starting transfers between devices: 10.7 us -> 11.3 us
  Pallas kernels: 4.96 us -> 4.53 us
  waiting for transfers between devices: 2.46 us -> 2.25 us
    ppermute x0 -> x1, starting transfers between devices: none -> 3.06 us  [staged(): lax.ppermute(last_other, ('garm', 'body'), [(2 * z + x, 2 * ((z + STEPS[3...]
    ppermute x3 -> x2, starting transfers between devices: 4.56 us -> 2.09 us  [along_body(): return lax.ppermute(value, 'body', [(0, 1), (1, 0)])]
    pallas_call x7 -> x5, Pallas kernels: 3.96 us -> 3.52 us  [call(): pl.pallas_call(kernel, out_shape=out_shape, in_specs=specs, out_specs=jax...]
    ppermute x3, waiting for transfers between devices: 0.27 us -> 0.01 us  [along_garm(): lax.ppermute(value, 'garm', [(z, (z + step) % garm_n) for z in range(garm...]
    ppermute x0 -> x1, waiting for transfers between devices: none -> 0.25 us  [staged(): lax.ppermute(last_other, ('garm', 'body'), [(2 * z + x, 2 * ((z + STEPS[3...]
    ppermute x3 -> x2, waiting for transfers between devices: 1.78 us -> 1.74 us  [along_body(): return lax.ppermute(value, 'body', [(0, 1), (1, 0)])]
  transfers between devices with their start and end apart: 7 -> 7, of which waited for: 6 -> 4; matrix products, arithmetic and copies ran while one was open for 0% -> 0% of each run, Pallas kernels for 14% -> 11%
where the time goes in v10:
time: 18.9 us; the launch traced here: 18.7 us
  starting transfers between devices  11.3 us (60%)
  Pallas kernels  4.53 us (24%)
  waiting for transfers between devices  2.25 us (12%)
  between operations  0.65 us (3%)
    ppermute x3, starting transfers between devices, along_garm(): lax.ppermute(value, 'garm', [(z, (z + step) % garm_n) for z in range(garm...  6.11 us
    pallas_call x5, Pallas kernels, call(): pl.pallas_call(kernel, out_shape=out_shape, in_specs=specs, out_specs=jax...  3.52 us
    ppermute x1, starting transfers between devices, staged(): lax.ppermute(last_other, ('garm', 'body'), [(2 * z + x, 2 * ((z + STEPS[3...  3.06 us
    ppermute x2, starting transfers between devices, along_body(): return lax.ppermute(value, 'body', [(0, 1), (1, 0)])  2.09 us
    ppermute x2, waiting for transfers between devices, along_body(): return lax.ppermute(value, 'body', [(0, 1), (1, 0)])  1.74 us
    pallas_call x1, Pallas kernels, staged(): pl.pallas_call(stage_kernel, out_shape=[jax.ShapeDtypeStruct((garm_n, SUB...  1.01 us
  transfers between devices with their start and end apart: 7, of which 4 were waited for; matrix products, arithmetic and copies ran while one was open for 0% of the time, Pallas kernels for 11%

profile of v10, /device:TPU:0, one launch (start us, length us, event | category | flops | bytes accessed | tf_op | source)
XLA Modules:
  0.0 18.7 jit_solution(6595058566042121500)
XLA Ops:
  0.6 1.0 %shard_map.94 = (f32[4,8,128]{2,1,0:T(8,128)S(1)}, f32[11,8,128]{2,1,0:T(8,128)S(1)}, f32[11,8,128]{2,1,0:T(8,128)S(1)}, f32[13,8,128]{2,1,0:T(8,128)S(1)}, f32[...) custom-call(s32[4,8]{1,0:T(4,128)} %bitcast.18, s32[4,8]{1,0:T(4,128)} %bitcast.19, ...), custom_call_target="tpu_custom_call" | custom-call | tf_op jit(solution)/shard_map/pallas_call | solution.py:442
  1.7 3.1 %collective-permute-start.1 = (f32[13,8,128]{2,1,0:T(8,128)S(1)}, f32[13,8,128]{2,1,0:T(8,128)S(1)}, u32[]{:S(2)}, u32[]{:S(2)}) collective-permute-start(f32[13,8,128]{2,1,0:T(8,128)S(1)} %get-tuple-element.21.sent0), channel_id=1, source_target_pairs={{0,4},{4,8},{8,12},{12,0},{1,5},{5,9},{9,13},{13,1},{2,6},{6,10},{... | collective-permute-start | bytes 159752 | tf_op jit(solution)/shard_map/ppermute | solution.py:455
  4.7 2.1 %collective-permute-start = (f32[13,8,128]{2,1,0:T(8,128)S(1)}, f32[13,8,128]{2,1,0:T(8,128)S(1)}, u32[]{:S(2)}, u32[]{:S(2)}) collective-permute-start(f32[13,8,128]{2,1,0:T(8,128)S(1)} %get-tuple-element.22.sent1), channel_id=1, source_target_pairs={{0,12},{4,0},{8,4},{12,8},{1,13},{5,1},{9,5},{13,9},{2,14},{6,2},{... | collective-permute-start | bytes 159752 | tf_op jit(solution)/shard_map/ppermute | solution.py:455
  6.8 0.9 %collective-permute-start.5 = (f32[11,8,128]{2,1,0:T(8,128)S(1)}, f32[11,8,128]{2,1,0:T(8,128)S(1)}, u32[]{:S(2)}, u32[]{:S(2)}) collective-permute-start(f32[11,8,128]{2,1,0:T(8,128)S(1)} %get-tuple-element.27), channel_id=1, source_target_pairs={{0,8},{4,12},{8,0},{12,4},{1,9},{5,13},{9,1},{13,5},{2,10},{6,14},... | collective-permute-start | bytes 135176 | tf_op jit(solution)/shard_map/ppermute | solution.py:455
  7.8 3.1 %collective-permute-start.4 = (f32[11,8,128]{2,1,0:T(8,128)S(1)}, f32[11,8,128]{2,1,0:T(8,128)S(1)}, u32[]{:S(2)}, u32[]{:S(2)}) collective-permute-start(f32[11,8,128]{2,1,0:T(8,128)S(1)} %get-tuple-element.26), channel_id=1, source_target_pairs={{0,10},{2,8},{4,14},{6,12},{8,2},{10,0},{12,6},{14,4},{1,11},{3,9}... | collective-permute-start | bytes 135176 | tf_op jit(solution)/shard_map/ppermute | solution.py:461
  10.8 0.0 collective-permute-done.1.two_ref.got1
  10.8 0.0 collective-permute-done.one_ref.got0
  10.9 0.4 %collective-permute-start.3 = (f32[11,8,128]{2,1,0:T(8,128)S(1)}, f32[11,8,128]{2,1,0:T(8,128)S(1)}, u32[]{:S(2)}, u32[]{:S(2)}) collective-permute-start(f32[11,8,128]{2,1,0:T(8,128)S(1)} %get-tuple-element.25), channel_id=1, source_target_pairs={{0,2},{2,0},{1,3},{3,1},{4,6},{6,4},{5,7},{7,5},{8,10},{10,8},{9,1... | collective-permute-start | bytes 135176 | tf_op jit(solution)/shard_map/ppermute | solution.py:458
  11.3 1.6 %collective-permute-start.2 = (f32[21,8,128]{2,1,0:T(8,128)S(1)}, f32[21,8,128]{2,1,0:T(8,128)S(1)}, u32[]{:S(2)}, u32[]{:S(2)}) collective-permute-start(f32[21,8,128]{2,1,0:T(8,128)S(1)} %get-tuple-element.24.after_ref), channel_id=1, source_target_pairs={{0,2},{2,0},{1,3},{3,1},{4,6},{6,4},{5,7},{7,5},{8,10},{10,8},{9,1... | collective-permute-start | bytes 258056 | tf_op jit(solution)/shard_map/ppermute | solution.py:458
  12.9 0.0 collective-permute-done.5.got2
  12.9 1.1 %shard_map.96 = (f32[16,512]{1,0:T(8,128)S(1)}, f32[16,128]{1,0:T(8,128)S(1)}, f32[16,384]{1,0:T(8,128)S(1)}) custom-call(f32[13,8,128]{2,1,0:T(8,128)S(1)} %get-tuple-element.20.own_ref, f32[13,8,128]{2,1,0:T(8,128)S(1)} %get-tuple-element.21.sent0, f32[13,8,128]{2,1,0:T(8,128)S(1)} %get-tuple-element.22.sent1, f32[13,8,128]{2,1,0:T(8,128)S(1)} %get-tuple-element.23.sent2, ...), custom_call_target="tpu_custom_call" | custom-call | flops 40000000000 | bytes 1000 | tf_op jit(solution)/shard_map/pallas_call | solution.py:221
  14.0 0.2 %collective-permute-done.4.far_ref = f32[11,8,128]{2,1,0:T(8,128)S(1)} collective-permute-done((f32[11,8,128]{2,1,0:T(8,128)S(1)}, f32[11,8,128]{2,1,0:T(8,128)S(1)}, u32[]{:S(2)}, u32[]{:S(2)}) %collective-permute-start.4) | collective-permute-done | bytes 45088 | tf_op jit(solution)/shard_map/ppermute | solution.py:461
  14.3 0.8 %collective-permute-done.3.x0_ref = f32[11,8,128]{2,1,0:T(8,128)S(1)} collective-permute-done((f32[11,8,128]{2,1,0:T(8,128)S(1)}, f32[11,8,128]{2,1,0:T(8,128)S(1)}, u32[]{:S(2)}, u32[]{:S(2)}) %collective-permute-start.3) | collective-permute-done | bytes 45088 | tf_op jit(solution)/shard_map/ppermute | solution.py:458
  15.1 0.9 %collective-permute-done.2.near_ref = f32[21,8,128]{2,1,0:T(8,128)S(1)} collective-permute-done((f32[21,8,128]{2,1,0:T(8,128)S(1)}, f32[21,8,128]{2,1,0:T(8,128)S(1)}, u32[]{:S(2)}, u32[]{:S(2)}) %collective-permute-start.2) | collective-permute-done | bytes 86048 | tf_op jit(solution)/shard_map/ppermute | solution.py:458
  16.0 0.9 %shard_map.98 = (f32[3,16,128]{2,1,0:T(8,128)S(1)}, f32[16,128]{1,0:T(8,128)S(1)}) custom-call(f32[13,8,128]{2,1,0:T(8,128)S(1)} %get-tuple-element.20.own_ref, f32[21,8,128]{2,1,0:T(8,128)S(1)} %collective-permute-done.2.near_ref, f32[11,8,128]{2,1,0:T(8,128)S(1)} %collective-permute-done.3.x0_ref, f32[11,8,128]{2,1,0:T(8,128)S(1)} %collective-permute-done.4.far_ref, ...), custom_call_target="tpu_custom_call" | custom-call | tf_op jit(solution)/shard_map/pallas_call | solution.py:221
  16.9 0.0 collective-permute-start.6
  16.9 0.9 %shard_map.97.garm_ref = f32[3,32,128]{2,1,0:T(8,128)S(1)} custom-call(f32[13,8,128]{2,1,0:T(8,128)S(1)} %get-tuple-element.20.own_ref, f32[13,8,128]{2,1,0:T(8,128)S(1)} %get-tuple-element.21.sent0, f32[13,8,128]{2,1,0:T(8,128)S(1)} %get-tuple-element.22.sent1, f32[13,8,128]{2,1,0:T(8,128)S(1)} %get-tuple-element.23.sent2, ...), custom_call_target="tpu_custom_call" | custom-call | tf_op jit(solution)/shard_map/pallas_call | solution.py:221
  17.8 0.2 %collective-permute-done.6.other_ref = f32[16,128]{1,0:T(8,128)S(1)} collective-permute-done((f32[16,128]{1,0:T(8,128)S(1)}, f32[16,128]{1,0:T(8,128)S(1)}, u32[]{:S(2)}, u32[]{:S(2)}) %collective-permute-start.6) | collective-permute-done | bytes 8224 | tf_op jit(solution)/shard_map/ppermute | solution.py:490
  18.1 0.6 %shard_map.99 = (f32[3,32,128]{2,1,0:T(8,128)}, f32[3,16,128]{2,1,0:T(8,128)}, f32[16,128]{1,0:T(8,128)}) custom-call(f32[3,32,128]{2,1,0:T(8,128)S(1)} %shard_map.97.garm_ref, f32[3,16,128]{2,1,0:T(8,128)S(1)} %get-tuple-element.32.body_ref, f32[16,128]{1,0:T(8,128)S(1)} %get-tuple-element.33.mine_ref, f32[16,128]{1,0:T(8,128)S(1)} %collective-permute-done.6.other_ref), custom_call_target="tpu_custom_call" | custom-call | tf_op jit(solution)/shard_map/pallas_call | solution.py:221
  (1 shorter events, 0.0 us)
Async XLA Ops:
  1.7 9.2 %collective-permute-start.1 = (f32[13,8,128]{2,1,0:T(8,128)S(1)}, f32[13,8,128]{2,1,0:T(8,128)S(1)}, u32[]{:S(2)}, u32[]{:S(2)}) collective-permute-start(f32[13,8,128]{2,1,0:T(8,128)S(1)} %get-tuple-element.21.sent0), channel_id=1, source_target_pairs={{0,4},{4,8},{8,12},{12,0},{1,5},{5,9},{9,13},{13,1},{2,6},{6,10},{... | collective-permute-start | bytes 159752 | tf_op jit(solution)/shard_map/ppermute | solution.py:455
  4.7 6.1 %collective-permute-start = (f32[13,8,128]{2,1,0:T(8,128)S(1)}, f32[13,8,128]{2,1,0:T(8,128)S(1)}, u32[]{:S(2)}, u32[]{:S(2)}) collective-permute-start(f32[13,8,128]{2,1,0:T(8,128)S(1)} %get-tuple-element.22.sent1), channel_id=1, source_target_pairs={{0,12},{4,0},{8,4},{12,8},{1,13},{5,1},{9,5},{13,9},{2,14},{6,2},{... | collective-permute-start | bytes 159752 | tf_op jit(solution)/shard_map/ppermute | solution.py:455
  6.8 6.1 %collective-permute-start.5 = (f32[11,8,128]{2,1,0:T(8,128)S(1)}, f32[11,8,128]{2,1,0:T(8,128)S(1)}, u32[]{:S(2)}, u32[]{:S(2)}) collective-permute-start(f32[11,8,128]{2,1,0:T(8,128)S(1)} %get-tuple-element.27), channel_id=1, source_target_pairs={{0,8},{4,12},{8,0},{12,4},{1,9},{5,13},{9,1},{13,5},{2,10},{6,14},... | collective-permute-start | bytes 135176 | tf_op jit(solution)/shard_map/ppermute | solution.py:455
  7.8 6.5 %collective-permute-start.4 = (f32[11,8,128]{2,1,0:T(8,128)S(1)}, f32[11,8,128]{2,1,0:T(8,128)S(1)}, u32[]{:S(2)}, u32[]{:S(2)}) collective-permute-start(f32[11,8,128]{2,1,0:T(8,128)S(1)} %get-tuple-element.26), channel_id=1, source_target_pairs={{0,10},{2,8},{4,14},{6,12},{8,2},{10,0},{12,6},{14,4},{1,11},{3,9}... | collective-permute-start | bytes 135176 | tf_op jit(solution)/shard_map/ppermute | solution.py:461
  10.9 4.2 %collective-permute-start.3 = (f32[11,8,128]{2,1,0:T(8,128)S(1)}, f32[11,8,128]{2,1,0:T(8,128)S(1)}, u32[]{:S(2)}, u32[]{:S(2)}) collective-permute-start(f32[11,8,128]{2,1,0:T(8,128)S(1)} %get-tuple-element.25), channel_id=1, source_target_pairs={{0,2},{2,0},{1,3},{3,1},{4,6},{6,4},{5,7},{7,5},{8,10},{10,8},{9,1... | collective-permute-start | bytes 135176 | tf_op jit(solution)/shard_map/ppermute | solution.py:458
  11.3 4.7 %collective-permute-start.2 = (f32[21,8,128]{2,1,0:T(8,128)S(1)}, f32[21,8,128]{2,1,0:T(8,128)S(1)}, u32[]{:S(2)}, u32[]{:S(2)}) collective-permute-start(f32[21,8,128]{2,1,0:T(8,128)S(1)} %get-tuple-element.24.after_ref), channel_id=1, source_target_pairs={{0,2},{2,0},{1,3},{3,1},{4,6},{6,4},{5,7},{7,5},{8,10},{10,8},{9,1... | collective-permute-start | bytes 258056 | tf_op jit(solution)/shard_map/ppermute | solution.py:458
  16.9 1.2 %collective-permute-start.6 = (f32[16,128]{1,0:T(8,128)S(1)}, f32[16,128]{1,0:T(8,128)S(1)}, u32[]{:S(2)}, u32[]{:S(2)}) collective-permute-start(f32[16,128]{1,0:T(8,128)S(1)} %get-tuple-element.33.mine_ref), channel_id=1, source_target_pairs={{0,1},{1,0},{2,3},{3,2},{4,5},{5,4},{6,7},{7,6},{8,9},{9,8},{10,11... | collective-permute-start | bytes 24584 | tf_op jit(solution)/shard_map/ppermute | solution.py:490

commit v11 on v10

--- a/solution.py
+++ b/solution.py
@@ -10,8 +10,8 @@
 BLOCK = 128
 SUB = 8
 VMEM_LIMIT = 32 * 1024 * 1024
-STEPS = (0, 1, 3, 2)
 SAME_COST = 40_000_000_000
+NEAR_COST = 1_000_000_000
 BUNDLE_COST = 1000
 
 amplitude = 0.05
@@ -296,15 +296,19 @@
     return [ref[5 + q] for q in range(ref.shape[0] - 5)] + pack(slots)
 
 
-def forward_kernel(one_ref, two_ref, own_ref, out_ref, own_out_ref):
+def forward_kernel(one_ref, two_ref, out_ref):
     body = one_ref.shape[0] - 5
     for n, ref in enumerate((one_ref, two_ref)):
         for q in range(body):
             out_ref[n * body + q] = ref[5 + q]
     for k, tile in enumerate(bottom_tiles(one_ref, two_ref)):
         out_ref[2 * body + k] = tile
-    for k, tile in enumerate(half_message(own_ref, True)):
-        own_out_ref[k] = tile
+
+
+def half_kernel(ref, after_ref, out_ref):
+    del after_ref
+    for k, tile in enumerate(half_message(ref, True)):
+        out_ref[k] = tile
 
 
 def top_tiles(one_ref, two_ref):
@@ -329,49 +333,52 @@
     body = own_ref.shape[0] - 5
     step = body // 4
     own = message_table(own_ref, step)
-    next_to = top_tiles(got0, got1)
+    here = top_tiles(own_ref, got0)
     last = unpack_bottom([got2[body + k] for k in range(3)])
-    here = [halves(x, y) for x, y in zip(slot_tiles(own_ref), last)]
+    there = [halves(x, y) for x, y in zip(slot_tiles(got1), last)]
     work = [
-        body_work(next_to, own),
         body_work(here, own),
-        garm_work(top_tiles(sent0, sent1), message_table(got0, step), message_table(got1, step)),
-        garm_work(top_tiles(own_ref, sent2), own, read_table(got2, 0, step)),
-    ]
-    store(work, [next_to[4], here[4]], *out_refs)
-
-
-def late_body_kernel(own_ref, near_ref, x0_ref, far_ref, bgrad_ref, bindex_ref, out_ref, stiff_ref):
+        body_work(there, own),
+        garm_work(top_tiles(own_ref, sent0), own, message_table(got0, step)),
+        garm_work(top_tiles(sent1, sent2), message_table(got1, step), read_table(got2, 0, step)),
+    ]
+    store(work, [here[4], there[4]], *out_refs)
+
+
+def near_kernel(own_ref, sent0, near_ref, after_ref, *out_refs):
+    del after_ref
     body = own_ref.shape[0] - 5
-    own = message_table(own_ref, body // 4)
+    step = body // 4
     near = [near_ref[2 * body + k] for k in range(5)]
-    top = unpack_top([x0_ref[body + k] for k in range(3)])
-    bottom = unpack_bottom([far_ref[body + k] for k in range(3)])
-    tiles = [near, [halves(x, y) for x, y in zip(top, bottom)]]
-    out = gradients([body_work(part, own) for part in tiles])
-    grads = [bgrad_ref[...]] + [jnp.concatenate(rows, axis=1) for rows in out]
-    index = jnp.concatenate([bindex_ref[...]] + [part[4] for part in tiles], axis=0)
-    total = scatter(index, jnp.concatenate(grads, axis=0), out_ref.shape[1])
+    tables = [read_table(near_ref, n * body, step) for n in range(2)]
+    work = [
+        body_work(near, message_table(own_ref, step)),
+        garm_work(bottom_tiles(own_ref, sent0), *tables),
+    ]
+    store(work, [near[4]], *out_refs)
+
+
+def late_body_kernel(own_ref, one_ref, two_ref, bg1, bg2, bi1, bi2, out_ref, stiff_ref):
+    body = own_ref.shape[0] - 5
+    top = unpack_top([one_ref[body + k] for k in range(3)])
+    bottom = unpack_bottom([two_ref[body + k] for k in range(3)])
+    tiles = [halves(x, y) for x, y in zip(top, bottom)]
+    out = gradients([body_work(tiles, message_table(own_ref, body // 4))])
+    grads = jnp.concatenate([bg1[...], bg2[...], jnp.concatenate(out[0], axis=1)], axis=0)
+    index = jnp.concatenate([bi1[...], bi2[...], tiles[4]], axis=0)
+    total = scatter(index, grads, out_ref.shape[1])
     for c in range(3):
         out_ref[c] = total[:, c * BLOCK : (c + 1) * BLOCK]
     stiff_ref[...] = total[:, 3 * BLOCK :]
 
 
-def late_garm_kernel(
-    own_ref, sent0, sent1, sent2, near_ref, x0_ref, far_ref, ggrad_ref, index_ref, out_ref
-):
-    body = own_ref.shape[0] - 5
-    step = body // 4
-    near = [read_table(near_ref, n * body, step) for n in range(2)]
-    far = [read_table(ref, 0, step) for ref in (x0_ref, far_ref)]
-    work = [
-        garm_work(bottom_tiles(sent0, sent1), *near),
-        garm_work(bottom_tiles(own_ref, sent2), *far),
-    ]
-    out = gradients(work)
-    grads = [ggrad_ref[...]] + [jnp.concatenate(rows[:3], axis=1) for rows in out]
+def late_garm_kernel(sent1, sent2, one_ref, two_ref, gg1, gg2, index_ref, out_ref):
+    step = (sent1.shape[0] - 5) // 4
+    tables = [read_table(ref, 0, step) for ref in (one_ref, two_ref)]
+    out = gradients([garm_work(bottom_tiles(sent1, sent2), *tables)])
+    grads = jnp.concatenate([gg1[...], gg2[...], jnp.concatenate(out[0][:3], axis=1)], axis=0)
     index = jnp.concatenate([index_ref[k] for k in range(index_ref.shape[0])], axis=0)
-    total = scatter(index, jnp.concatenate(grads, axis=0), out_ref.shape[1])
+    total = scatter(index, grads, out_ref.shape[1])
     for c in range(3):
         out_ref[c] = total[:, c * BLOCK : (c + 1) * BLOCK]
 
@@ -397,9 +404,9 @@
     tiles = stiff_ref.shape[0]
     width = lax.axis_size("body")
     here, column = lax.axis_index("garm"), lax.axis_index("body")
-    garm_n = lax.axis_size("garm")
+    flips = (0, 3 - here // 2, 2 + here // 2, 1)
     for n, out_ref in enumerate(out_refs):
-        place_z = lax.rem(here + STEPS[n], garm_n)
+        place_z = here ^ flips[n]
         for q in range(3 * tiles):
             out_ref[5 + q] = body_ref[q]
         for q in range(tiles):
@@ -414,8 +421,7 @@
                     out_ref[c, place, :] = garm_ref[c, row, :]
                 out_ref[3, place, :] = jnp.where(s < live, cot_ref[row, :], 0.0)
                 out_ref[4, place, :] = jnp.full((1, BLOCK), pb_ref[s, owner].astype(f32), f32)
-                spot = 2 * x + (n in (0, 3))
-                line = (0 if n < 2 else cap) + s
+                spot, line = 2 * x + n // 2, n % 2 * cap + s
                 index_ref[spot, line : line + 1, :] = jnp.full((1, BLOCK), g.astype(f32), f32)
     for ref, other in ((same_ref, False), (other_ref, True)):
         for k, tile in enumerate(half_message(out_refs[3], other)):
@@ -451,31 +457,34 @@
         compiler_params=pltpu.CompilerParams(vmem_limit_bytes=VMEM_LIMIT),
     )(*[pltpu.with_memory_space_constraint(a, pltpu.HBM) for a in arrays])
 
-    def along_garm(value, step):
-        return lax.ppermute(value, "garm", [(z, (z + step) % garm_n) for z in range(garm_n)])
+    def along_garm(value, pairs):
+        return lax.ppermute(value, "garm", pairs)
 
     def along_body(value):
         return lax.ppermute(value, "body", [(0, 1), (1, 0)])
 
-    got = [along_garm(sent[1], STEPS[2]), along_garm(sent[0], STEPS[1]), along_garm(last_same, STEPS[3])]
-    far = lax.ppermute(
-        last_other,
-        ("garm", "body"),
-        [(2 * z + x, 2 * ((z + STEPS[3]) % garm_n) + 1 - x) for z in range(garm_n) for x in range(2)],
-    )
+    cycle = [(0, 2), (2, 1), (1, 3), (3, 0)]
+    got = [
+        along_garm(sent[1], cycle),
+        along_garm(sent[0], [(b, a) for a, b in cycle]),
+        along_garm(last_same, [(z, z ^ 1) for z in range(garm_n)]),
+    ]
+    direct = lax.ppermute(last_other, ("garm", "body"), [(n, n ^ 3) for n in range(2 * garm_n)])
     near_shape = jax.ShapeDtypeStruct((5 + 8 * tiles, SUB, BLOCK), f32)
-    near, own_half = call(
-        forward_kernel, (near_shape, half), [], (), (got[0], got[1], own), BUNDLE_COST
-    )
-    near_other, x0 = along_body(near), along_body(own_half)
+    near = call(forward_kernel, near_shape, [], (), (own, got[0]), BUNDLE_COST)
+    second = call(half_kernel, half, [], (), (got[1], near), BUNDLE_COST)
+    near_other, second_other = along_body(near), along_body(second)
 
     def batch_shapes(count):
         return tuple(
             jax.ShapeDtypeStruct((count * SUB, width * BLOCK), f32) for width in (4, 1, 3)
         )
 
-    bgrad, bindex, ggrad = call(
-        same_kernel, batch_shapes(2), [], (), (own, *sent, *got, near), SAME_COST
+    bg1, bi1, gg1 = call(
+        same_kernel, batch_shapes(2), [], (), (own, *sent, *got, second), SAME_COST
+    )
+    bg2, bi2, gg2 = call(
+        near_kernel, batch_shapes(1), [], (), (own, sent[0], near_other, bg1), NEAR_COST
     )
     body_shape = jax.ShapeDtypeStruct((3, blocks, BLOCK), f32)
     stiff_shape = jax.ShapeDtypeStruct((blocks, BLOCK), f32)
@@ -485,7 +494,7 @@
         (body_shape, stiff_shape),
         [],
         (),
-        (own, near_other, x0, far, bgrad, bindex),
+        (own, second_other, direct, bg1, bg2, bi1, bi2),
     )
     stiff_other = lax.ppermute(stiff, "frame", [(0, 1), (1, 0)])
     garm_total = call(
@@ -493,7 +502,7 @@
         garm_shape,
         [],
         (),
-        (own, *sent, near_other, x0, far, ggrad, index),
+        (sent[1], sent[2], second_other, direct, gg1, gg2, index),
     )
     return call(
         final_kernel,

time: 18.9 us -> 18 us (0.952)
  waiting for transfers between devices: 2.25 us -> 1.48 us
  starting transfers between devices: 11.3 us -> 10.7 us
  Pallas kernels: 4.53 us -> 4.96 us
    ppermute x4, starting transfers between devices: 9.18 us -> 8.28 us  [the longest x3 5.67 us: along_garm(): return lax.ppermute(value, 'garm', pairs)]
    ppermute x2, waiting for transfers between devices: 1.74 us -> 0.89 us  [along_body(): return lax.ppermute(value, 'body', [(0, 1), (1, 0)])]
    pallas_call x5 -> x7, Pallas kernels: 3.52 us -> 3.96 us  [call(): pl.pallas_call(kernel, out_shape=out_shape, in_specs=specs, out_specs=jax...]
    ppermute x2, starting transfers between devices: 2.09 us -> 2.42 us  [along_body(): return lax.ppermute(value, 'body', [(0, 1), (1, 0)])]
  transfers between devices with their start and end apart: 7 -> 7, of which waited for: 4 -> 3; matrix products, arithmetic and copies ran while one was open for 0% -> 0% of each run, Pallas kernels for 11% -> 15%
where the time goes in v11:
time: 18 us; the launch traced here: 17.8 us
  starting transfers between devices  10.7 us (59%)
  Pallas kernels  4.96 us (28%)
  waiting for transfers between devices  1.48 us (8%)
  between operations  0.67 us (4%)
    ppermute x3, starting transfers between devices, along_garm(): return lax.ppermute(value, 'garm', pairs)  5.67 us
    pallas_call x7, Pallas kernels, call(): pl.pallas_call(kernel, out_shape=out_shape, in_specs=specs, out_specs=jax...  3.96 us
    ppermute x1, starting transfers between devices, staged(): lax.ppermute(last_other, ('garm', 'body'), [(n, n ^ 3) for n in range(2 *...  2.61 us
    ppermute x2, starting transfers between devices, along_body(): return lax.ppermute(value, 'body', [(0, 1), (1, 0)])  2.42 us
    pallas_call x1, Pallas kernels, staged(): pl.pallas_call(stage_kernel, out_shape=[jax.ShapeDtypeStruct((garm_n, SUB...  1.01 us
    ppermute x2, waiting for transfers between devices, along_body(): return lax.ppermute(value, 'body', [(0, 1), (1, 0)])  0.89 us
    ppermute x1, waiting for transfers between devices, staged(): stiff_other = lax.ppermute(stiff, 'frame', [(0, 1), (1, 0)])  0.41 us
  transfers between devices with their start and end apart: 7, of which 3 were waited for; matrix products, arithmetic and copies ran while one was open for 0% of the time, Pallas kernels for 15%

profile of v11, /device:TPU:0, one launch (start us, length us, event | category | flops | bytes accessed | tf_op | source)
XLA Modules:
  0.0 17.8 jit_solution(486459420899734270)
XLA Ops:
  0.6 1.0 %shard_map.94 = (f32[4,8,128]{2,1,0:T(8,128)S(1)}, f32[11,8,128]{2,1,0:T(8,128)S(1)}, f32[11,8,128]{2,1,0:T(8,128)S(1)}, f32[13,8,128]{2,1,0:T(8,128)S(1)}, f32[...) custom-call(s32[4,8]{1,0:T(4,128)} %bitcast.18, s32[4,8]{1,0:T(4,128)} %bitcast.19, ...), custom_call_target="tpu_custom_call" | custom-call | tf_op jit(solution)/shard_map/pallas_call | solution.py:448
  1.6 4.1 %collective-permute-start.1 = (f32[13,8,128]{2,1,0:T(8,128)S(1)}, f32[13,8,128]{2,1,0:T(8,128)S(1)}, u32[]{:S(2)}, u32[]{:S(2)}) collective-permute-start(f32[13,8,128]{2,1,0:T(8,128)S(1)} %get-tuple-element.21.sent1), channel_id=1, source_target_pairs={{0,8},{8,4},{4,12},{12,0},{1,9},{9,5},{5,13},{13,1},{2,10},{10,6},... | collective-permute-start | bytes 159752 | tf_op jit(solution)/shard_map/ppermute | solution.py:461
  5.7 1.1 %collective-permute-start = (f32[13,8,128]{2,1,0:T(8,128)S(1)}, f32[13,8,128]{2,1,0:T(8,128)S(1)}, u32[]{:S(2)}, u32[]{:S(2)}) collective-permute-start(f32[13,8,128]{2,1,0:T(8,128)S(1)} %get-tuple-element.23.sent0), channel_id=1, source_target_pairs={{8,0},{4,8},{12,4},{0,12},{9,1},{5,9},{13,5},{1,13},{10,2},{6,10},... | collective-permute-start | bytes 159752 | tf_op jit(solution)/shard_map/ppermute | solution.py:461
  6.8 0.5 %collective-permute-start.4 = (f32[11,8,128]{2,1,0:T(8,128)S(1)}, f32[11,8,128]{2,1,0:T(8,128)S(1)}, u32[]{:S(2)}, u32[]{:S(2)}) collective-permute-start(f32[11,8,128]{2,1,0:T(8,128)S(1)} %get-tuple-element.26), channel_id=1, source_target_pairs={{0,4},{4,0},{8,12},{12,8},{1,5},{5,1},{9,13},{13,9},{2,6},{6,2},{1... | collective-permute-start | bytes 135176 | tf_op jit(solution)/shard_map/ppermute | solution.py:461
  7.3 2.6 %collective-permute-start.3 = (f32[11,8,128]{2,1,0:T(8,128)S(1)}, f32[11,8,128]{2,1,0:T(8,128)S(1)}, u32[]{:S(2)}, u32[]{:S(2)}) collective-permute-start(f32[11,8,128]{2,1,0:T(8,128)S(1)} %get-tuple-element.25), channel_id=1, source_target_pairs={{0,6},{2,4},{4,2},{6,0},{8,14},{10,12},{12,10},{14,8},{1,7},{3,5},... | collective-permute-start | bytes 135176 | tf_op jit(solution)/shard_map/ppermute | solution.py:472
  9.9 0.0 collective-permute-done.1.two_ref.got0
  9.9 0.8 %collective-permute-start.5 = (f32[21,8,128]{2,1,0:T(8,128)S(1)}, f32[21,8,128]{2,1,0:T(8,128)S(1)}, u32[]{:S(2)}, u32[]{:S(2)}) collective-permute-start(f32[21,8,128]{2,1,0:T(8,128)S(1)} %shard_map.95.after_ref), channel_id=1, source_target_pairs={{0,2},{2,0},{1,3},{3,1},{4,6},{6,4},{5,7},{7,5},{8,10},{10,8},{9,1... | collective-permute-start | bytes 258056 | tf_op jit(solution)/shard_map/ppermute | solution.py:464
  10.8 0.2 collective-permute-done.ref.got1
  10.9 1.6 %collective-permute-start.2 = (f32[11,8,128]{2,1,0:T(8,128)S(1)}, f32[11,8,128]{2,1,0:T(8,128)S(1)}, u32[]{:S(2)}, u32[]{:S(2)}) collective-permute-start(f32[11,8,128]{2,1,0:T(8,128)S(1)} %shard_map.96.after_ref), channel_id=1, source_target_pairs={{0,2},{2,0},{1,3},{3,1},{4,6},{6,4},{5,7},{7,5},{8,10},{10,8},{9,1... | collective-permute-start | bytes 135176 | tf_op jit(solution)/shard_map/ppermute | solution.py:464
  12.5 0.0 collective-permute-done.4.got2
  12.5 1.1 %shard_map.97 = (f32[16,512]{1,0:T(8,128)S(1)}, f32[16,128]{1,0:T(8,128)S(1)}, f32[16,384]{1,0:T(8,128)S(1)}) custom-call(f32[13,8,128]{2,1,0:T(8,128)S(1)} %get-tuple-element.24.one_ref.own_ref, f32[13,8,128]{2,1,0:T(8,128)S(1)} %get-tuple-element.23.sent0, f32[13,8,128]{2,1,0:T(8,128)S(1)} %get-tuple-element.21.sent1, ...), custom_call_target="tpu_custom_call" | custom-call | flops 40000000000 | bytes 1000 | tf_op jit(solution)/shard_map/pallas_call | solution.py:221
  13.6 0.9 %collective-permute-done.5.near_ref = f32[21,8,128]{2,1,0:T(8,128)S(1)} collective-permute-done((f32[21,8,128]{2,1,0:T(8,128)S(1)}, f32[21,8,128]{2,1,0:T(8,128)S(1)}, u32[]{:S(2)}, u32[]{:S(2)}) %collective-permute-start.5) | collective-permute-done | bytes 86048 | tf_op jit(solution)/shard_map/ppermute | solution.py:464
  14.5 0.8 %shard_map.98 = (f32[8,512]{1,0:T(8,128)S(1)}, f32[8,128]{1,0:T(8,128)S(1)}, f32[8,384]{1,0:T(8,128)S(1)}) custom-call(f32[13,8,128]{2,1,0:T(8,128)S(1)} %get-tuple-element.24.one_ref.own_ref, f32[13,8,128]{2,1,0:T(8,128)S(1)} %get-tuple-element.23.sent0, f32[21,8,128]{2,1,0:T(8,128)S(1)} %collective-permute-done.5.near_ref, ...), custom_call_target="tpu_custom_call" | custom-call | flops 1000000000 | bytes 1000 | tf_op jit(solution)/shard_map/pallas_call | solution.py:221
  15.2 0.0 collective-permute-done.3.two_ref
  15.3 0.0 collective-permute-done.2.one_ref
  15.3 0.7 %shard_map.100 = (f32[3,16,128]{2,1,0:T(8,128)S(1)}, f32[16,128]{1,0:T(8,128)S(1)}) custom-call(f32[13,8,128]{2,1,0:T(8,128)S(1)} %get-tuple-element.24.one_ref.own_ref, f32[11,8,128]{2,1,0:T(8,128)S(1)} %collective-permute-done.2.one_ref, f32[11,8,128]{2,1,0:T(8,128)S(1)} %collective-permute-done.3.two_ref, f32[16,512]{1,0:T(8,128)S(1)} %get-tuple-element.28.after_ref.bg1, ...), custom_call_target="tpu_custom_call" | custom-call | tf_op jit(solution)/shard_map/pallas_call | solution.py:221
  16.0 0.0 collective-permute-start.6
  16.0 0.8 %shard_map.99.garm_ref = f32[3,32,128]{2,1,0:T(8,128)S(1)} custom-call(f32[13,8,128]{2,1,0:T(8,128)S(1)} %get-tuple-element.21.sent1, f32[13,8,128]{2,1,0:T(8,128)S(1)} %get-tuple-element.22.sent2, f32[11,8,128]{2,1,0:T(8,128)S(1)} %collective-permute-done.2.one_ref, f32[11,8,128]{2,1,0:T(8,128)S(1)} %collective-permute-done.3.two_ref, ...), custom_call_target="tpu_custom_call" | custom-call | tf_op jit(solution)/shard_map/pallas_call | solution.py:221
  16.8 0.4 %collective-permute-done.6.other_ref = f32[16,128]{1,0:T(8,128)S(1)} collective-permute-done((f32[16,128]{1,0:T(8,128)S(1)}, f32[16,128]{1,0:T(8,128)S(1)}, u32[]{:S(2)}, u32[]{:S(2)}) %collective-permute-start.6) | collective-permute-done | bytes 8224 | tf_op jit(solution)/shard_map/ppermute | solution.py:499
  17.2 0.6 %shard_map.101 = (f32[3,32,128]{2,1,0:T(8,128)}, f32[3,16,128]{2,1,0:T(8,128)}, f32[16,128]{1,0:T(8,128)}) custom-call(f32[3,32,128]{2,1,0:T(8,128)S(1)} %shard_map.99.garm_ref, f32[3,16,128]{2,1,0:T(8,128)S(1)} %get-tuple-element.34.body_ref, f32[16,128]{1,0:T(8,128)S(1)} %get-tuple-element.35.mine_ref, f32[16,128]{1,0:T(8,128)S(1)} %collective-permute-done.6.other_ref), custom_call_target="tpu_custom_call" | custom-call | tf_op jit(solution)/shard_map/pallas_call | solution.py:221
  (2 shorter events, 0.0 us)
Async XLA Ops:
  1.6 8.3 %collective-permute-start.1 = (f32[13,8,128]{2,1,0:T(8,128)S(1)}, f32[13,8,128]{2,1,0:T(8,128)S(1)}, u32[]{:S(2)}, u32[]{:S(2)}) collective-permute-start(f32[13,8,128]{2,1,0:T(8,128)S(1)} %get-tuple-element.21.sent1), channel_id=1, source_target_pairs={{0,8},{8,4},{4,12},{12,0},{1,9},{9,5},{5,13},{13,1},{2,10},{10,6},... | collective-permute-start | bytes 159752 | tf_op jit(solution)/shard_map/ppermute | solution.py:461
  5.7 5.2 %collective-permute-start = (f32[13,8,128]{2,1,0:T(8,128)S(1)}, f32[13,8,128]{2,1,0:T(8,128)S(1)}, u32[]{:S(2)}, u32[]{:S(2)}) collective-permute-start(f32[13,8,128]{2,1,0:T(8,128)S(1)} %get-tuple-element.23.sent0), channel_id=1, source_target_pairs={{8,0},{4,8},{12,4},{0,12},{9,1},{5,9},{13,5},{1,13},{10,2},{6,10},... | collective-permute-start | bytes 159752 | tf_op jit(solution)/shard_map/ppermute | solution.py:461
  6.8 5.7 %collective-permute-start.4 = (f32[11,8,128]{2,1,0:T(8,128)S(1)}, f32[11,8,128]{2,1,0:T(8,128)S(1)}, u32[]{:S(2)}, u32[]{:S(2)}) collective-permute-start(f32[11,8,128]{2,1,0:T(8,128)S(1)} %get-tuple-element.26), channel_id=1, source_target_pairs={{0,4},{4,0},{8,12},{12,8},{1,5},{5,1},{9,13},{13,9},{2,6},{6,2},{1... | collective-permute-start | bytes 135176 | tf_op jit(solution)/shard_map/ppermute | solution.py:461
  7.3 7.9 %collective-permute-start.3 = (f32[11,8,128]{2,1,0:T(8,128)S(1)}, f32[11,8,128]{2,1,0:T(8,128)S(1)}, u32[]{:S(2)}, u32[]{:S(2)}) collective-permute-start(f32[11,8,128]{2,1,0:T(8,128)S(1)} %get-tuple-element.25), channel_id=1, source_target_pairs={{0,6},{2,4},{4,2},{6,0},{8,14},{10,12},{12,10},{14,8},{1,7},{3,5},... | collective-permute-start | bytes 135176 | tf_op jit(solution)/shard_map/ppermute | solution.py:472
  9.9 4.6 %collective-permute-start.5 = (f32[21,8,128]{2,1,0:T(8,128)S(1)}, f32[21,8,128]{2,1,0:T(8,128)S(1)}, u32[]{:S(2)}, u32[]{:S(2)}) collective-permute-start(f32[21,8,128]{2,1,0:T(8,128)S(1)} %shard_map.95.after_ref), channel_id=1, source_target_pairs={{0,2},{2,0},{1,3},{3,1},{4,6},{6,4},{5,7},{7,5},{8,10},{10,8},{9,1... | collective-permute-start | bytes 258056 | tf_op jit(solution)/shard_map/ppermute | solution.py:464
  10.9 4.3 %collective-permute-start.2 = (f32[11,8,128]{2,1,0:T(8,128)S(1)}, f32[11,8,128]{2,1,0:T(8,128)S(1)}, u32[]{:S(2)}, u32[]{:S(2)}) collective-permute-start(f32[11,8,128]{2,1,0:T(8,128)S(1)} %shard_map.96.after_ref), channel_id=1, source_target_pairs={{0,2},{2,0},{1,3},{3,1},{4,6},{6,4},{5,7},{7,5},{8,10},{10,8},{9,1... | collective-permute-start | bytes 135176 | tf_op jit(solution)/shard_map/ppermute | solution.py:464
  16.0 1.2 %collective-permute-start.6 = (f32[16,128]{1,0:T(8,128)S(1)}, f32[16,128]{1,0:T(8,128)S(1)}, u32[]{:S(2)}, u32[]{:S(2)}) collective-permute-start(f32[16,128]{1,0:T(8,128)S(1)} %get-tuple-element.35.mine_ref), channel_id=1, source_target_pairs={{0,1},{1,0},{2,3},{3,2},{4,5},{5,4},{6,7},{7,6},{8,9},{9,8},{10,11... | collective-permute-start | bytes 24584 | tf_op jit(solution)/shard_map/ppermute | solution.py:499

commit v12 on v11

--- a/solution.py
+++ b/solution.py
@@ -72,19 +72,28 @@
     row = lax.broadcasted_iota(jnp.int32, made[0][1].shape, 0) % SUB
     sub = lax.broadcasted_iota(jnp.int32, (4 * SUB, BLOCK), 0) % SUB
     totals = [jnp.zeros((4 * SUB, BLOCK), f32) for _ in batches]
+
+    def sums_of(pair, n, exponent):
+        kernel = jnp.exp2(exponent)
+        khi = kernel.astype(bf16)
+        klo = (kernel - khi.astype(f32)).astype(bf16)
+        sums = jnp.dot(made[n][2], jnp.concatenate([khi, klo], axis=0), preferred_element_type=f32)
+        sums = sums[: 4 * SUB] + sums[4 * SUB :]
+        for k in range(2):
+            part = sums[:, k * BLOCK : (k + 1) * BLOCK]
+            totals[n] = jnp.where(sub == pair + k, part, totals[n])
+
+    ahead = SUB // 2 if len(batches) == 1 else 0
+    waiting = []
     for pair in range(0, SUB, 2):
         masks = [(row == pair + k).astype(f32).astype(bf16) for k in range(2)]
-        for n, (lfeat_t, rfeat, lhs) in enumerate(made):
+        for n, (lfeat_t, rfeat, _) in enumerate(made):
             rhs = jnp.concatenate([rfeat * mask for mask in masks], axis=1)
-            exponent = jnp.dot(lfeat_t, rhs, preferred_element_type=f32)
-            kernel = jnp.exp2(exponent)
-            khi = kernel.astype(bf16)
-            klo = (kernel - khi.astype(f32)).astype(bf16)
-            sums = jnp.dot(lhs, jnp.concatenate([khi, klo], axis=0), preferred_element_type=f32)
-            sums = sums[: 4 * SUB] + sums[4 * SUB :]
-            for k in range(2):
-                part = sums[:, k * BLOCK : (k + 1) * BLOCK]
-                totals[n] = jnp.where(sub == pair + k, part, totals[n])
+            waiting.append((pair, n, jnp.dot(lfeat_t, rhs, preferred_element_type=f32)))
+            if len(waiting) > ahead:
+                sums_of(*waiting.pop(0))
+    for work in waiting:
+        sums_of(*work)
     return [[total[c * SUB : (c + 1) * SUB] for c in range(4)] for total in totals]
 
 
@@ -115,13 +124,11 @@
 
 
 def scatter(index, grads, blocks):
+    index = jnp.concatenate([index] * 3, axis=0)
     lane = lax.broadcasted_iota(jnp.int32, index.shape, 1).astype(f32)
     onehot_t = (index == lane).astype(f32).T[:blocks].astype(bf16)
-    parts = [
-        jnp.dot(onehot_t, part.astype(bf16), preferred_element_type=f32)
-        for part in pieces(grads, 3)
-    ]
-    return parts[0] + parts[1] + parts[2]
+    stack = jnp.concatenate(pieces(grads, 3), axis=0).astype(bf16)
+    return jnp.dot(onehot_t, stack, preferred_element_type=f32)
 
 
 def pack_kernel(pg_ref, pb_ref, pc_ref, garm_ref, cot_ref, body_ref, stiff_ref, out_ref):
@@ -237,13 +244,12 @@
 
 
 def choose(index, table):
-    lane = lax.broadcasted_iota(jnp.int32, index.shape, 1).astype(f32)
-    onehot = (index == lane).astype(f32)[:, : table.shape[0]].astype(bf16)
-    parts = [
-        jnp.dot(onehot, part.astype(bf16), preferred_element_type=f32)
-        for part in pieces(table, 3)
-    ]
-    rows = parts[0] + parts[1] + parts[2]
+    blocks = table.shape[0]
+    lane = lax.broadcasted_iota(jnp.int32, index.shape, 1)
+    onehot = (index == (lane % blocks).astype(f32)) & (lane < 3 * blocks)
+    onehot = onehot.astype(f32)[:, : 3 * blocks].astype(bf16)
+    stack = jnp.concatenate(pieces(table, 3), axis=0).astype(bf16)
+    rows = jnp.dot(onehot, stack, preferred_element_type=f32)
     return [rows[:, c * BLOCK : (c + 1) * BLOCK] for c in range(4)]
 
 

time: 18 us -> 17.9 us (level)
  transfers between devices with their start and end apart: 7 -> 7, of which waited for: 3 -> 3; matrix products, arithmetic and copies ran while one was open for 0% -> 0% of each run, Pallas kernels for 15% -> 14%
where the time goes in v12:
time: 17.9 us; the launch traced here: 17.7 us
  starting transfers between devices  10.7 us (60%)
  Pallas kernels  4.79 us (27%)
  waiting for transfers between devices  1.57 us (9%)
  between operations  0.67 us (4%)
    ppermute x3, starting transfers between devices, along_garm(): return lax.ppermute(value, 'garm', pairs)  5.67 us
    pallas_call x7, Pallas kernels, call(): pl.pallas_call(kernel, out_shape=out_shape, in_specs=specs, out_specs=jax...  3.79 us
    ppermute x1, starting transfers between devices, staged(): lax.ppermute(last_other, ('garm', 'body'), [(n, n ^ 3) for n in range(2 *...  2.61 us
    ppermute x2, starting transfers between devices, along_body(): return lax.ppermute(value, 'body', [(0, 1), (1, 0)])  2.42 us
    pallas_call x1, Pallas kernels, staged(): pl.pallas_call(stage_kernel, out_shape=[jax.ShapeDtypeStruct((garm_n, SUB...  1.01 us
    ppermute x2, waiting for transfers between devices, along_body(): return lax.ppermute(value, 'body', [(0, 1), (1, 0)])  0.9 us
    ppermute x1, waiting for transfers between devices, staged(): stiff_other = lax.ppermute(stiff, 'frame', [(0, 1), (1, 0)])  0.48 us
  transfers between devices with their start and end apart: 7, of which 3 were waited for; matrix products, arithmetic and copies ran while one was open for 0% of the time, Pallas kernels for 14%

profile of v12, /device:TPU:0, one launch (start us, length us, event | category | flops | bytes accessed | tf_op | source)
XLA Modules:
  0.0 17.7 jit_solution(4935715673249945582)
XLA Ops:
  0.6 1.0 %shard_map.94 = (f32[4,8,128]{2,1,0:T(8,128)S(1)}, f32[11,8,128]{2,1,0:T(8,128)S(1)}, f32[11,8,128]{2,1,0:T(8,128)S(1)}, f32[13,8,128]{2,1,0:T(8,128)S(1)}, f32[...) custom-call(s32[4,8]{1,0:T(4,128)} %bitcast.18, s32[4,8]{1,0:T(4,128)} %bitcast.19, ...), custom_call_target="tpu_custom_call" | custom-call | tf_op jit(solution)/shard_map/pallas_call | solution.py:454
  1.6 4.1 %collective-permute-start.1 = (f32[13,8,128]{2,1,0:T(8,128)S(1)}, f32[13,8,128]{2,1,0:T(8,128)S(1)}, u32[]{:S(2)}, u32[]{:S(2)}) collective-permute-start(f32[13,8,128]{2,1,0:T(8,128)S(1)} %get-tuple-element.21.sent1), channel_id=1, source_target_pairs={{0,8},{8,4},{4,12},{12,0},{1,9},{9,5},{5,13},{13,1},{2,10},{10,6},... | collective-permute-start | bytes 159752 | tf_op jit(solution)/shard_map/ppermute | solution.py:467
  5.7 1.1 %collective-permute-start = (f32[13,8,128]{2,1,0:T(8,128)S(1)}, f32[13,8,128]{2,1,0:T(8,128)S(1)}, u32[]{:S(2)}, u32[]{:S(2)}) collective-permute-start(f32[13,8,128]{2,1,0:T(8,128)S(1)} %get-tuple-element.23.sent0), channel_id=1, source_target_pairs={{8,0},{4,8},{12,4},{0,12},{9,1},{5,9},{13,5},{1,13},{10,2},{6,10},... | collective-permute-start | bytes 159752 | tf_op jit(solution)/shard_map/ppermute | solution.py:467
  6.8 0.5 %collective-permute-start.4 = (f32[11,8,128]{2,1,0:T(8,128)S(1)}, f32[11,8,128]{2,1,0:T(8,128)S(1)}, u32[]{:S(2)}, u32[]{:S(2)}) collective-permute-start(f32[11,8,128]{2,1,0:T(8,128)S(1)} %get-tuple-element.26), channel_id=1, source_target_pairs={{0,4},{4,0},{8,12},{12,8},{1,5},{5,1},{9,13},{13,9},{2,6},{6,2},{1... | collective-permute-start | bytes 135176 | tf_op jit(solution)/shard_map/ppermute | solution.py:467
  7.3 2.6 %collective-permute-start.3 = (f32[11,8,128]{2,1,0:T(8,128)S(1)}, f32[11,8,128]{2,1,0:T(8,128)S(1)}, u32[]{:S(2)}, u32[]{:S(2)}) collective-permute-start(f32[11,8,128]{2,1,0:T(8,128)S(1)} %get-tuple-element.25), channel_id=1, source_target_pairs={{0,6},{2,4},{4,2},{6,0},{8,14},{10,12},{12,10},{14,8},{1,7},{3,5},... | collective-permute-start | bytes 135176 | tf_op jit(solution)/shard_map/ppermute | solution.py:478
  9.9 0.0 collective-permute-done.1.two_ref.got0
  9.9 0.8 %collective-permute-start.5 = (f32[21,8,128]{2,1,0:T(8,128)S(1)}, f32[21,8,128]{2,1,0:T(8,128)S(1)}, u32[]{:S(2)}, u32[]{:S(2)}) collective-permute-start(f32[21,8,128]{2,1,0:T(8,128)S(1)} %shard_map.95.after_ref), channel_id=1, source_target_pairs={{0,2},{2,0},{1,3},{3,1},{4,6},{6,4},{5,7},{7,5},{8,10},{10,8},{9,1... | collective-permute-start | bytes 258056 | tf_op jit(solution)/shard_map/ppermute | solution.py:470
  10.8 0.2 collective-permute-done.ref.got1
  10.9 1.6 %collective-permute-start.2 = (f32[11,8,128]{2,1,0:T(8,128)S(1)}, f32[11,8,128]{2,1,0:T(8,128)S(1)}, u32[]{:S(2)}, u32[]{:S(2)}) collective-permute-start(f32[11,8,128]{2,1,0:T(8,128)S(1)} %shard_map.96.after_ref), channel_id=1, source_target_pairs={{0,2},{2,0},{1,3},{3,1},{4,6},{6,4},{5,7},{7,5},{8,10},{10,8},{9,1... | collective-permute-start | bytes 135176 | tf_op jit(solution)/shard_map/ppermute | solution.py:470
  12.5 0.0 collective-permute-done.4.got2
  12.5 1.0 %shard_map.97 = (f32[16,512]{1,0:T(8,128)S(1)}, f32[16,128]{1,0:T(8,128)S(1)}, f32[16,384]{1,0:T(8,128)S(1)}) custom-call(f32[13,8,128]{2,1,0:T(8,128)S(1)} %get-tuple-element.24.one_ref.own_ref, f32[13,8,128]{2,1,0:T(8,128)S(1)} %get-tuple-element.23.sent0, f32[13,8,128]{2,1,0:T(8,128)S(1)} %get-tuple-element.21.sent1, ...), custom_call_target="tpu_custom_call" | custom-call | flops 40000000000 | bytes 1000 | tf_op jit(solution)/shard_map/pallas_call | solution.py:228
  13.6 0.9 %collective-permute-done.5.near_ref = f32[21,8,128]{2,1,0:T(8,128)S(1)} collective-permute-done((f32[21,8,128]{2,1,0:T(8,128)S(1)}, f32[21,8,128]{2,1,0:T(8,128)S(1)}, u32[]{:S(2)}, u32[]{:S(2)}) %collective-permute-start.5) | collective-permute-done | bytes 86048 | tf_op jit(solution)/shard_map/ppermute | solution.py:470
  14.5 0.7 %shard_map.98 = (f32[8,512]{1,0:T(8,128)S(1)}, f32[8,128]{1,0:T(8,128)S(1)}, f32[8,384]{1,0:T(8,128)S(1)}) custom-call(f32[13,8,128]{2,1,0:T(8,128)S(1)} %get-tuple-element.24.one_ref.own_ref, f32[13,8,128]{2,1,0:T(8,128)S(1)} %get-tuple-element.23.sent0, f32[21,8,128]{2,1,0:T(8,128)S(1)} %collective-permute-done.5.near_ref, ...), custom_call_target="tpu_custom_call" | custom-call | flops 1000000000 | bytes 1000 | tf_op jit(solution)/shard_map/pallas_call | solution.py:228
  15.2 0.0 collective-permute-done.3.two_ref
  15.2 0.0 collective-permute-done.2.one_ref
  15.3 0.7 %shard_map.100 = (f32[3,16,128]{2,1,0:T(8,128)S(1)}, f32[16,128]{1,0:T(8,128)S(1)}) custom-call(f32[13,8,128]{2,1,0:T(8,128)S(1)} %get-tuple-element.24.one_ref.own_ref, f32[11,8,128]{2,1,0:T(8,128)S(1)} %collective-permute-done.2.one_ref, f32[11,8,128]{2,1,0:T(8,128)S(1)} %collective-permute-done.3.two_ref, f32[16,512]{1,0:T(8,128)S(1)} %get-tuple-element.28.after_ref.bg1, ...), custom_call_target="tpu_custom_call" | custom-call | tf_op jit(solution)/shard_map/pallas_call | solution.py:228
  15.9 0.0 collective-permute-start.6
  15.9 0.7 %shard_map.99.garm_ref = f32[3,32,128]{2,1,0:T(8,128)S(1)} custom-call(f32[13,8,128]{2,1,0:T(8,128)S(1)} %get-tuple-element.21.sent1, f32[13,8,128]{2,1,0:T(8,128)S(1)} %get-tuple-element.22.sent2, f32[11,8,128]{2,1,0:T(8,128)S(1)} %collective-permute-done.2.one_ref, f32[11,8,128]{2,1,0:T(8,128)S(1)} %collective-permute-done.3.two_ref, ...), custom_call_target="tpu_custom_call" | custom-call | tf_op jit(solution)/shard_map/pallas_call | solution.py:228
  16.6 0.5 %collective-permute-done.6.other_ref = f32[16,128]{1,0:T(8,128)S(1)} collective-permute-done((f32[16,128]{1,0:T(8,128)S(1)}, f32[16,128]{1,0:T(8,128)S(1)}, u32[]{:S(2)}, u32[]{:S(2)}) %collective-permute-start.6) | collective-permute-done | bytes 8224 | tf_op jit(solution)/shard_map/ppermute | solution.py:505
  17.1 0.6 %shard_map.101 = (f32[3,32,128]{2,1,0:T(8,128)}, f32[3,16,128]{2,1,0:T(8,128)}, f32[16,128]{1,0:T(8,128)}) custom-call(f32[3,32,128]{2,1,0:T(8,128)S(1)} %shard_map.99.garm_ref, f32[3,16,128]{2,1,0:T(8,128)S(1)} %get-tuple-element.34.body_ref, f32[16,128]{1,0:T(8,128)S(1)} %get-tuple-element.35.mine_ref, f32[16,128]{1,0:T(8,128)S(1)} %collective-permute-done.6.other_ref), custom_call_target="tpu_custom_call" | custom-call | tf_op jit(solution)/shard_map/pallas_call | solution.py:228
  (2 shorter events, 0.0 us)
Async XLA Ops:
  1.6 8.3 %collective-permute-start.1 = (f32[13,8,128]{2,1,0:T(8,128)S(1)}, f32[13,8,128]{2,1,0:T(8,128)S(1)}, u32[]{:S(2)}, u32[]{:S(2)}) collective-permute-start(f32[13,8,128]{2,1,0:T(8,128)S(1)} %get-tuple-element.21.sent1), channel_id=1, source_target_pairs={{0,8},{8,4},{4,12},{12,0},{1,9},{9,5},{5,13},{13,1},{2,10},{10,6},... | collective-permute-start | bytes 159752 | tf_op jit(solution)/shard_map/ppermute | solution.py:467
  5.7 5.2 %collective-permute-start = (f32[13,8,128]{2,1,0:T(8,128)S(1)}, f32[13,8,128]{2,1,0:T(8,128)S(1)}, u32[]{:S(2)}, u32[]{:S(2)}) collective-permute-start(f32[13,8,128]{2,1,0:T(8,128)S(1)} %get-tuple-element.23.sent0), channel_id=1, source_target_pairs={{8,0},{4,8},{12,4},{0,12},{9,1},{5,9},{13,5},{1,13},{10,2},{6,10},... | collective-permute-start | bytes 159752 | tf_op jit(solution)/shard_map/ppermute | solution.py:467
  6.8 5.7 %collective-permute-start.4 = (f32[11,8,128]{2,1,0:T(8,128)S(1)}, f32[11,8,128]{2,1,0:T(8,128)S(1)}, u32[]{:S(2)}, u32[]{:S(2)}) collective-permute-start(f32[11,8,128]{2,1,0:T(8,128)S(1)} %get-tuple-element.26), channel_id=1, source_target_pairs={{0,4},{4,0},{8,12},{12,8},{1,5},{5,1},{9,13},{13,9},{2,6},{6,2},{1... | collective-permute-start | bytes 135176 | tf_op jit(solution)/shard_map/ppermute | solution.py:467
  7.3 7.9 %collective-permute-start.3 = (f32[11,8,128]{2,1,0:T(8,128)S(1)}, f32[11,8,128]{2,1,0:T(8,128)S(1)}, u32[]{:S(2)}, u32[]{:S(2)}) collective-permute-start(f32[11,8,128]{2,1,0:T(8,128)S(1)} %get-tuple-element.25), channel_id=1, source_target_pairs={{0,6},{2,4},{4,2},{6,0},{8,14},{10,12},{12,10},{14,8},{1,7},{3,5},... | collective-permute-start | bytes 135176 | tf_op jit(solution)/shard_map/ppermute | solution.py:478
  9.9 4.6 %collective-permute-start.5 = (f32[21,8,128]{2,1,0:T(8,128)S(1)}, f32[21,8,128]{2,1,0:T(8,128)S(1)}, u32[]{:S(2)}, u32[]{:S(2)}) collective-permute-start(f32[21,8,128]{2,1,0:T(8,128)S(1)} %shard_map.95.after_ref), channel_id=1, source_target_pairs={{0,2},{2,0},{1,3},{3,1},{4,6},{6,4},{5,7},{7,5},{8,10},{10,8},{9,1... | collective-permute-start | bytes 258056 | tf_op jit(solution)/shard_map/ppermute | solution.py:470
  10.9 4.3 %collective-permute-start.2 = (f32[11,8,128]{2,1,0:T(8,128)S(1)}, f32[11,8,128]{2,1,0:T(8,128)S(1)}, u32[]{:S(2)}, u32[]{:S(2)}) collective-permute-start(f32[11,8,128]{2,1,0:T(8,128)S(1)} %shard_map.96.after_ref), channel_id=1, source_target_pairs={{0,2},{2,0},{1,3},{3,1},{4,6},{6,4},{5,7},{7,5},{8,10},{10,8},{9,1... | collective-permute-start | bytes 135176 | tf_op jit(solution)/shard_map/ppermute | solution.py:470
  15.9 1.2 %collective-permute-start.6 = (f32[16,128]{1,0:T(8,128)S(1)}, f32[16,128]{1,0:T(8,128)S(1)}, u32[]{:S(2)}, u32[]{:S(2)}) collective-permute-start(f32[16,128]{1,0:T(8,128)S(1)} %get-tuple-element.35.mine_ref), channel_id=1, source_target_pairs={{0,1},{1,0},{2,3},{3,2},{4,5},{5,4},{6,7},{7,6},{8,9},{9,8},{10,11... | collective-permute-start | bytes 24584 | tf_op jit(solution)/shard_map/ppermute | solution.py:505

commit v13 on v12

--- a/solution.py
+++ b/solution.py
@@ -54,31 +54,32 @@
     )
 
 
-def pull(batches):
+def pull(batches, weights_only=False):
     made = []
     for left, right in batches:
         lfeat, rfeat = features(left, right)
         weight = left[3]
-        coeff = jnp.concatenate([weight * left[c] for c in range(3)] + [weight], axis=0)
-        chi, clo = [part.astype(bf16) for part in pieces(coeff, 2)]
+        coeff = [weight] if weights_only else [weight * left[c] for c in range(3)] + [weight]
+        chi, clo = pieces(jnp.concatenate(coeff, axis=0), 2)
         lhs = jnp.concatenate(
             [
                 jnp.concatenate([chi, chi], axis=1),
                 jnp.concatenate([clo, jnp.zeros_like(clo)], axis=1),
             ],
             axis=0,
-        )
+        ).astype(bf16)
         made.append((lfeat.T, rfeat, lhs))
     row = lax.broadcasted_iota(jnp.int32, made[0][1].shape, 0) % SUB
-    sub = lax.broadcasted_iota(jnp.int32, (4 * SUB, BLOCK), 0) % SUB
-    totals = [jnp.zeros((4 * SUB, BLOCK), f32) for _ in batches]
+    count = made[0][2].shape[0] // 2
+    sub = lax.broadcasted_iota(jnp.int32, (count, BLOCK), 0) % SUB
+    totals = [jnp.zeros((count, BLOCK), f32) for _ in batches]
 
     def sums_of(pair, n, exponent):
         kernel = jnp.exp2(exponent)
         khi = kernel.astype(bf16)
         klo = (kernel - khi.astype(f32)).astype(bf16)
         sums = jnp.dot(made[n][2], jnp.concatenate([khi, klo], axis=0), preferred_element_type=f32)
-        sums = sums[: 4 * SUB] + sums[4 * SUB :]
+        sums = sums[:count] + sums[count:]
         for k in range(2):
             part = sums[:, k * BLOCK : (k + 1) * BLOCK]
             totals[n] = jnp.where(sub == pair + k, part, totals[n])
@@ -94,7 +95,7 @@
                 sums_of(*waiting.pop(0))
     for work in waiting:
         sums_of(*work)
-    return [[total[c * SUB : (c + 1) * SUB] for c in range(4)] for total in totals]
+    return [[total[c * SUB : (c + 1) * SUB] for c in range(count // SUB)] for total in totals]
 
 
 def gradients(batches):
@@ -351,42 +352,76 @@
     store(work, [here[4], there[4]], *out_refs)
 
 
-def near_kernel(own_ref, sent0, near_ref, after_ref, *out_refs):
-    del after_ref
+def near_tiles(own_ref, near_ref):
     body = own_ref.shape[0] - 5
-    step = body // 4
-    near = [near_ref[2 * body + k] for k in range(5)]
-    tables = [read_table(near_ref, n * body, step) for n in range(2)]
-    work = [
-        body_work(near, message_table(own_ref, step)),
-        garm_work(bottom_tiles(own_ref, sent0), *tables),
-    ]
-    store(work, [near[4]], *out_refs)
-
-
-def late_body_kernel(own_ref, one_ref, two_ref, bg1, bg2, bi1, bi2, out_ref, stiff_ref):
+    return [near_ref[2 * body + k] for k in range(5)]
+
+
+def late_tiles(own_ref, one_ref, two_ref):
     body = own_ref.shape[0] - 5
     top = unpack_top([one_ref[body + k] for k in range(3)])
     bottom = unpack_bottom([two_ref[body + k] for k in range(3)])
-    tiles = [halves(x, y) for x, y in zip(top, bottom)]
-    out = gradients([body_work(tiles, message_table(own_ref, body // 4))])
-    grads = jnp.concatenate([bg1[...], bg2[...], jnp.concatenate(out[0], axis=1)], axis=0)
+    return [halves(x, y) for x, y in zip(top, bottom)]
+
+
+def near_kernel(own_ref, near_ref, after_ref, bgrad_ref, bindex_ref):
+    del after_ref
+    tiles = near_tiles(own_ref, near_ref)
+    own = message_table(own_ref, (own_ref.shape[0] - 5) // 4)
+    bgrad_ref[...] = jnp.concatenate(gradients([body_work(tiles, own)])[0], axis=1)
+    bindex_ref[...] = tiles[4]
+
+
+def stiff_kernel(own_ref, one_ref, two_ref, bg1, bg2, bi1, bi2, out_ref):
+    tiles = late_tiles(own_ref, one_ref, two_ref)
+    own = message_table(own_ref, (own_ref.shape[0] - 5) // 4)
+    [[last]] = pull([body_work(tiles, own)], weights_only=True)
+    grads = [bg1[:, 3 * BLOCK :], bg2[:, 3 * BLOCK :], amplitude * last]
     index = jnp.concatenate([bi1[...], bi2[...], tiles[4]], axis=0)
-    total = scatter(index, grads, out_ref.shape[1])
+    out_ref[...] = scatter(index, jnp.concatenate(grads, axis=0), out_ref.shape[0])
+
+
+def late_kernel(
+    own_ref,
+    sent0,
+    sent1,
+    sent2,
+    near_ref,
+    one_ref,
+    two_ref,
+    bg1,
+    bg2,
+    bi1,
+    bi2,
+    gg1,
+    index_ref,
+    body_out,
+    garm_out,
+):
+    body = own_ref.shape[0] - 5
+    step = body // 4
+    tiles = late_tiles(own_ref, one_ref, two_ref)
+    near = [read_table(near_ref, n * body, step) for n in range(2)]
+    far = [read_table(ref, 0, step) for ref in (one_ref, two_ref)]
+    out = gradients(
+        [
+            body_work(tiles, message_table(own_ref, step)),
+            garm_work(bottom_tiles(own_ref, sent0), *near),
+            garm_work(bottom_tiles(sent1, sent2), *far),
+        ]
+    )
+    rows = [jnp.concatenate(values[:3], axis=1) for values in out]
+    width = 3 * BLOCK
+    index = jnp.concatenate([bi1[...], bi2[...], tiles[4]], axis=0)
+    grads = jnp.concatenate([bg1[:, :width], bg2[:, :width], rows[0]], axis=0)
+    total = scatter(index, grads, body_out.shape[1])
     for c in range(3):
-        out_ref[c] = total[:, c * BLOCK : (c + 1) * BLOCK]
-    stiff_ref[...] = total[:, 3 * BLOCK :]
-
-
-def late_garm_kernel(sent1, sent2, one_ref, two_ref, gg1, gg2, index_ref, out_ref):
-    step = (sent1.shape[0] - 5) // 4
-    tables = [read_table(ref, 0, step) for ref in (one_ref, two_ref)]
-    out = gradients([garm_work(bottom_tiles(sent1, sent2), *tables)])
-    grads = jnp.concatenate([gg1[...], gg2[...], jnp.concatenate(out[0][:3], axis=1)], axis=0)
+        body_out[c] = total[:, c * BLOCK : (c + 1) * BLOCK]
     index = jnp.concatenate([index_ref[k] for k in range(index_ref.shape[0])], axis=0)
-    total = scatter(index, grads, out_ref.shape[1])
+    grads = jnp.concatenate([gg1[...], rows[1], rows[2]], axis=0)
+    total = scatter(index, grads, garm_out.shape[1])
     for c in range(3):
-        out_ref[c] = total[:, c * BLOCK : (c + 1) * BLOCK]
+        garm_out[c] = total[:, c * BLOCK : (c + 1) * BLOCK]
 
 
 def final_kernel(garm_ref, body_ref, mine_ref, other_ref, garm_out, body_out, stiff_out):
@@ -489,26 +524,22 @@
     bg1, bi1, gg1 = call(
         same_kernel, batch_shapes(2), [], (), (own, *sent, *got, second), SAME_COST
     )
-    bg2, bi2, gg2 = call(
-        near_kernel, batch_shapes(1), [], (), (own, sent[0], near_other, bg1), NEAR_COST
+    bg2, bi2 = call(
+        near_kernel, batch_shapes(1)[:2], [], (), (own, near_other, bg1), NEAR_COST
     )
     body_shape = jax.ShapeDtypeStruct((3, blocks, BLOCK), f32)
     stiff_shape = jax.ShapeDtypeStruct((blocks, BLOCK), f32)
     garm_shape = jax.ShapeDtypeStruct((3, verts // BLOCK, BLOCK), f32)
-    body_total, stiff = call(
-        late_body_kernel,
-        (body_shape, stiff_shape),
+    stiff = call(
+        stiff_kernel, stiff_shape, [], (), (own, second_other, direct, bg1, bg2, bi1, bi2)
+    )
+    stiff_other = lax.ppermute(stiff, "frame", [(0, 1), (1, 0)])
+    body_total, garm_total = call(
+        late_kernel,
+        (body_shape, garm_shape),
         [],
         (),
-        (own, second_other, direct, bg1, bg2, bi1, bi2),
-    )
-    stiff_other = lax.ppermute(stiff, "frame", [(0, 1), (1, 0)])
-    garm_total = call(
-        late_garm_kernel,
-        garm_shape,
-        [],
-        (),
-        (sent[1], sent[2], second_other, direct, gg1, gg2, index),
+        (own, *sent, near_other, second_other, direct, bg1, bg2, bi1, bi2, gg1, index),
     )
     return call(
         final_kernel,

time: 17.9 us -> 17.8 us (level)
  waiting for transfers between devices: 1.57 us -> 1.23 us
    ppermute x1, waiting for transfers between devices: 0.48 us -> 0.15 us  [staged(): stiff_other = lax.ppermute(stiff, 'frame', [(0, 1), (1, 0)])]
  transfers between devices with their start and end apart: 7 -> 7, of which waited for: 3 -> 3; matrix products, arithmetic and copies ran while one was open for 0% -> 0% of each run, Pallas kernels for 14% -> 15%
where the time goes in v13:
time: 17.8 us; the launch traced here: 17.5 us
  starting transfers between devices  10.7 us (60%)
  Pallas kernels  4.89 us (27%)
  waiting for transfers between devices  1.23 us (7%)
  between operations  0.68 us (4%)
    ppermute x3, starting transfers between devices, along_garm(): return lax.ppermute(value, 'garm', pairs)  5.67 us
    pallas_call x7, Pallas kernels, call(): pl.pallas_call(kernel, out_shape=out_shape, in_specs=specs, out_specs=jax...  3.89 us
    ppermute x1, starting transfers between devices, staged(): lax.ppermute(last_other, ('garm', 'body'), [(n, n ^ 3) for n in range(2 *...  2.61 us
    ppermute x2, starting transfers between devices, along_body(): return lax.ppermute(value, 'body', [(0, 1), (1, 0)])  2.42 us
    pallas_call x1, Pallas kernels, staged(): pl.pallas_call(stage_kernel, out_shape=[jax.ShapeDtypeStruct((garm_n, SUB...  1.01 us
    ppermute x2, waiting for transfers between devices, along_body(): return lax.ppermute(value, 'body', [(0, 1), (1, 0)])  0.9 us
  transfers between devices with their start and end apart: 7, of which 3 were waited for; matrix products, arithmetic and copies ran while one was open for 0% of the time, Pallas kernels for 15%

profile of v13, /device:TPU:0, one launch (start us, length us, event | category | flops | bytes accessed | tf_op | source)
XLA Modules:
  0.0 17.5 jit_solution(12813320667846188756)
XLA Ops:
  0.6 1.0 %shard_map.94 = (f32[4,8,128]{2,1,0:T(8,128)S(1)}, f32[11,8,128]{2,1,0:T(8,128)S(1)}, f32[11,8,128]{2,1,0:T(8,128)S(1)}, f32[13,8,128]{2,1,0:T(8,128)S(1)}, f32[...) custom-call(s32[4,8]{1,0:T(4,128)} %bitcast.18, s32[4,8]{1,0:T(4,128)} %bitcast.19, ...), custom_call_target="tpu_custom_call" | custom-call | tf_op jit(solution)/shard_map/pallas_call | solution.py:489
  1.6 4.1 %collective-permute-start = (f32[13,8,128]{2,1,0:T(8,128)S(1)}, f32[13,8,128]{2,1,0:T(8,128)S(1)}, u32[]{:S(2)}, u32[]{:S(2)}) collective-permute-start(f32[13,8,128]{2,1,0:T(8,128)S(1)} %get-tuple-element.22.sent1), channel_id=1, source_target_pairs={{0,8},{8,4},{4,12},{12,0},{1,9},{9,5},{5,13},{13,1},{2,10},{10,6},... | collective-permute-start | bytes 159752 | tf_op jit(solution)/shard_map/ppermute | solution.py:502
  5.7 1.1 %collective-permute-start.2 = (f32[13,8,128]{2,1,0:T(8,128)S(1)}, f32[13,8,128]{2,1,0:T(8,128)S(1)}, u32[]{:S(2)}, u32[]{:S(2)}) collective-permute-start(f32[13,8,128]{2,1,0:T(8,128)S(1)} %get-tuple-element.21.sent0), channel_id=1, source_target_pairs={{8,0},{4,8},{12,4},{0,12},{9,1},{5,9},{13,5},{1,13},{10,2},{6,10},... | collective-permute-start | bytes 159752 | tf_op jit(solution)/shard_map/ppermute | solution.py:502
  6.8 0.5 %collective-permute-start.5 = (f32[11,8,128]{2,1,0:T(8,128)S(1)}, f32[11,8,128]{2,1,0:T(8,128)S(1)}, u32[]{:S(2)}, u32[]{:S(2)}) collective-permute-start(f32[11,8,128]{2,1,0:T(8,128)S(1)} %get-tuple-element.25), channel_id=1, source_target_pairs={{0,4},{4,0},{8,12},{12,8},{1,5},{5,1},{9,13},{13,9},{2,6},{6,2},{1... | collective-permute-start | bytes 135176 | tf_op jit(solution)/shard_map/ppermute | solution.py:502
  7.3 2.6 %collective-permute-start.4 = (f32[11,8,128]{2,1,0:T(8,128)S(1)}, f32[11,8,128]{2,1,0:T(8,128)S(1)}, u32[]{:S(2)}, u32[]{:S(2)}) collective-permute-start(f32[11,8,128]{2,1,0:T(8,128)S(1)} %get-tuple-element.24), channel_id=1, source_target_pairs={{0,6},{2,4},{4,2},{6,0},{8,14},{10,12},{12,10},{14,8},{1,7},{3,5},... | collective-permute-start | bytes 135176 | tf_op jit(solution)/shard_map/ppermute | solution.py:513
  9.9 0.0 collective-permute-done.two_ref.got0
  9.9 0.8 %collective-permute-start.1 = (f32[21,8,128]{2,1,0:T(8,128)S(1)}, f32[21,8,128]{2,1,0:T(8,128)S(1)}, u32[]{:S(2)}, u32[]{:S(2)}) collective-permute-start(f32[21,8,128]{2,1,0:T(8,128)S(1)} %shard_map.95.after_ref), channel_id=1, source_target_pairs={{0,2},{2,0},{1,3},{3,1},{4,6},{6,4},{5,7},{7,5},{8,10},{10,8},{9,1... | collective-permute-start | bytes 258056 | tf_op jit(solution)/shard_map/ppermute | solution.py:505
  10.8 0.2 collective-permute-done.2.ref.got1
  10.9 1.6 %collective-permute-start.3 = (f32[11,8,128]{2,1,0:T(8,128)S(1)}, f32[11,8,128]{2,1,0:T(8,128)S(1)}, u32[]{:S(2)}, u32[]{:S(2)}) collective-permute-start(f32[11,8,128]{2,1,0:T(8,128)S(1)} %shard_map.96.after_ref), channel_id=1, source_target_pairs={{0,2},{2,0},{1,3},{3,1},{4,6},{6,4},{5,7},{7,5},{8,10},{10,8},{9,1... | collective-permute-start | bytes 135176 | tf_op jit(solution)/shard_map/ppermute | solution.py:505
  12.5 0.0 collective-permute-done.5.got2
  12.5 1.0 %shard_map.97 = (f32[16,512]{1,0:T(8,128)S(1)}, f32[16,128]{1,0:T(8,128)S(1)}, f32[16,384]{1,0:T(8,128)S(1)}) custom-call(f32[13,8,128]{2,1,0:T(8,128)S(1)} %get-tuple-element.20.one_ref.own_ref, f32[13,8,128]{2,1,0:T(8,128)S(1)} %get-tuple-element.21.sent0, f32[13,8,128]{2,1,0:T(8,128)S(1)} %get-tuple-element.22.sent1, ...), custom_call_target="tpu_custom_call" | custom-call | flops 40000000000 | bytes 1000 | tf_op jit(solution)/shard_map/pallas_call | solution.py:229
  13.6 0.9 %collective-permute-done.1.near_ref = f32[21,8,128]{2,1,0:T(8,128)S(1)} collective-permute-done((f32[21,8,128]{2,1,0:T(8,128)S(1)}, f32[21,8,128]{2,1,0:T(8,128)S(1)}, u32[]{:S(2)}, u32[]{:S(2)}) %collective-permute-start.1) | collective-permute-done | bytes 86048 | tf_op jit(solution)/shard_map/ppermute | solution.py:505
  14.5 0.5 %shard_map.98 = (f32[8,512]{1,0:T(8,128)S(1)}, f32[8,128]{1,0:T(8,128)S(1)}) custom-call(f32[13,8,128]{2,1,0:T(8,128)S(1)} %get-tuple-element.20.one_ref.own_ref, f32[21,8,128]{2,1,0:T(8,128)S(1)} %collective-permute-done.1.near_ref, f32[16,512]{1,0:T(8,128)S(1)} %get-tuple-element.26.after_ref.bg1), custom_call_target="tpu_custom_call" | custom-call | flops 1000000000 | bytes 1000 | tf_op jit(solution)/shard_map/pallas_call | solution.py:229
  15.0 0.0 collective-permute-done.4.two_ref
  15.0 0.0 collective-permute-done.3.one_ref
  15.0 0.6 %shard_map.100.mine_ref = f32[16,128]{1,0:T(8,128)S(1)} custom-call(f32[13,8,128]{2,1,0:T(8,128)S(1)} %get-tuple-element.20.one_ref.own_ref, f32[11,8,128]{2,1,0:T(8,128)S(1)} %collective-permute-done.3.one_ref, f32[11,8,128]{2,1,0:T(8,128)S(1)} %collective-permute-done.4.two_ref, f32[16,512]{1,0:T(8,128)S(1)} %get-tuple-element.26.after_ref.bg1, ...), custom_call_target="tpu_custom_call" | custom-call | tf_op jit(solution)/shard_map/pallas_call | solution.py:229
  15.7 0.0 collective-permute-start.6
  15.7 1.0 %shard_map.99 = (f32[3,16,128]{2,1,0:T(8,128)S(1)}, f32[3,32,128]{2,1,0:T(8,128)S(1)}) custom-call(f32[13,8,128]{2,1,0:T(8,128)S(1)} %get-tuple-element.20.one_ref.own_ref, f32[13,8,128]{2,1,0:T(8,128)S(1)} %get-tuple-element.21.sent0, f32[13,8,128]{2,1,0:T(8,128)S(1)} %get-tuple-element.22.sent1, f32[13,8,128]{2,1,0:T(8,128)S(1)} %get-tuple-element.23.sent2, ...), custom_call_target="tpu_custom_call" | custom-call | tf_op jit(solution)/shard_map/pallas_call | solution.py:229
  16.7 0.1 collective-permute-done.6.other_ref
  16.9 0.6 %shard_map.101 = (f32[3,32,128]{2,1,0:T(8,128)}, f32[3,16,128]{2,1,0:T(8,128)}, f32[16,128]{1,0:T(8,128)}) custom-call(f32[3,32,128]{2,1,0:T(8,128)S(1)} %get-tuple-element.32.garm_ref, f32[3,16,128]{2,1,0:T(8,128)S(1)} %get-tuple-element.33.body_ref, f32[16,128]{1,0:T(8,128)S(1)} %shard_map.100.mine_ref, f32[16,128]{1,0:T(8,128)S(1)} %collective-permute-done.6.other_ref), custom_call_target="tpu_custom_call" | custom-call | tf_op jit(solution)/shard_map/pallas_call | solution.py:229
  (2 shorter events, 0.0 us)
Async XLA Ops:
  1.6 8.3 %collective-permute-start = (f32[13,8,128]{2,1,0:T(8,128)S(1)}, f32[13,8,128]{2,1,0:T(8,128)S(1)}, u32[]{:S(2)}, u32[]{:S(2)}) collective-permute-start(f32[13,8,128]{2,1,0:T(8,128)S(1)} %get-tuple-element.22.sent1), channel_id=1, source_target_pairs={{0,8},{8,4},{4,12},{12,0},{1,9},{9,5},{5,13},{13,1},{2,10},{10,6},... | collective-permute-start | bytes 159752 | tf_op jit(solution)/shard_map/ppermute | solution.py:502
  5.7 5.2 %collective-permute-start.2 = (f32[13,8,128]{2,1,0:T(8,128)S(1)}, f32[13,8,128]{2,1,0:T(8,128)S(1)}, u32[]{:S(2)}, u32[]{:S(2)}) collective-permute-start(f32[13,8,128]{2,1,0:T(8,128)S(1)} %get-tuple-element.21.sent0), channel_id=1, source_target_pairs={{8,0},{4,8},{12,4},{0,12},{9,1},{5,9},{13,5},{1,13},{10,2},{6,10},... | collective-permute-start | bytes 159752 | tf_op jit(solution)/shard_map/ppermute | solution.py:502
  6.8 5.7 %collective-permute-start.5 = (f32[11,8,128]{2,1,0:T(8,128)S(1)}, f32[11,8,128]{2,1,0:T(8,128)S(1)}, u32[]{:S(2)}, u32[]{:S(2)}) collective-permute-start(f32[11,8,128]{2,1,0:T(8,128)S(1)} %get-tuple-element.25), channel_id=1, source_target_pairs={{0,4},{4,0},{8,12},{12,8},{1,5},{5,1},{9,13},{13,9},{2,6},{6,2},{1... | collective-permute-start | bytes 135176 | tf_op jit(solution)/shard_map/ppermute | solution.py:502
  7.3 7.7 %collective-permute-start.4 = (f32[11,8,128]{2,1,0:T(8,128)S(1)}, f32[11,8,128]{2,1,0:T(8,128)S(1)}, u32[]{:S(2)}, u32[]{:S(2)}) collective-permute-start(f32[11,8,128]{2,1,0:T(8,128)S(1)} %get-tuple-element.24), channel_id=1, source_target_pairs={{0,6},{2,4},{4,2},{6,0},{8,14},{10,12},{12,10},{14,8},{1,7},{3,5},... | collective-permute-start | bytes 135176 | tf_op jit(solution)/shard_map/ppermute | solution.py:513
  9.9 4.6 %collective-permute-start.1 = (f32[21,8,128]{2,1,0:T(8,128)S(1)}, f32[21,8,128]{2,1,0:T(8,128)S(1)}, u32[]{:S(2)}, u32[]{:S(2)}) collective-permute-start(f32[21,8,128]{2,1,0:T(8,128)S(1)} %shard_map.95.after_ref), channel_id=1, source_target_pairs={{0,2},{2,0},{1,3},{3,1},{4,6},{6,4},{5,7},{7,5},{8,10},{10,8},{9,1... | collective-permute-start | bytes 258056 | tf_op jit(solution)/shard_map/ppermute | solution.py:505
  10.9 4.1 %collective-permute-start.3 = (f32[11,8,128]{2,1,0:T(8,128)S(1)}, f32[11,8,128]{2,1,0:T(8,128)S(1)}, u32[]{:S(2)}, u32[]{:S(2)}) collective-permute-start(f32[11,8,128]{2,1,0:T(8,128)S(1)} %shard_map.96.after_ref), channel_id=1, source_target_pairs={{0,2},{2,0},{1,3},{3,1},{4,6},{6,4},{5,7},{7,5},{8,10},{10,8},{9,1... | collective-permute-start | bytes 135176 | tf_op jit(solution)/shard_map/ppermute | solution.py:505
  15.7 1.2 %collective-permute-start.6 = (f32[16,128]{1,0:T(8,128)S(1)}, f32[16,128]{1,0:T(8,128)S(1)}, u32[]{:S(2)}, u32[]{:S(2)}) collective-permute-start(f32[16,128]{1,0:T(8,128)S(1)} %shard_map.100.mine_ref), channel_id=1, source_target_pairs={{0,1},{1,0},{2,3},{3,2},{4,5},{5,4},{6,7},{7,6},{8,9},{9,8},{10,11... | collective-permute-start | bytes 24584 | tf_op jit(solution)/shard_map/ppermute | solution.py:536

commit v14 on v13

--- a/solution.py
+++ b/solution.py
@@ -303,18 +303,16 @@
     return [ref[5 + q] for q in range(ref.shape[0] - 5)] + pack(slots)
 
 
-def forward_kernel(one_ref, two_ref, out_ref):
-    body = one_ref.shape[0] - 5
-    for n, ref in enumerate((one_ref, two_ref)):
-        for q in range(body):
-            out_ref[n * body + q] = ref[5 + q]
-    for k, tile in enumerate(bottom_tiles(one_ref, two_ref)):
-        out_ref[2 * body + k] = tile
-
-
-def half_kernel(ref, after_ref, out_ref):
+def forward_kernel(own_ref, ref, out_ref):
+    body = ref.shape[0] - 5
+    for k, tile in enumerate([ref[5 + q] for q in range(body)] + bottom_tiles(own_ref, ref)):
+        out_ref[k] = tile
+
+
+def second_kernel(own_ref, ref, after_ref, out_ref):
     del after_ref
-    for k, tile in enumerate(half_message(ref, True)):
+    own = [own_ref[5 + q] for q in range(own_ref.shape[0] - 5)]
+    for k, tile in enumerate(half_message(ref, True) + own):
         out_ref[k] = tile
 
 
@@ -354,7 +352,7 @@
 
 def near_tiles(own_ref, near_ref):
     body = own_ref.shape[0] - 5
-    return [near_ref[2 * body + k] for k in range(5)]
+    return [near_ref[body + k] for k in range(5)]
 
 
 def late_tiles(own_ref, one_ref, two_ref):
@@ -401,7 +399,7 @@
     body = own_ref.shape[0] - 5
     step = body // 4
     tiles = late_tiles(own_ref, one_ref, two_ref)
-    near = [read_table(near_ref, n * body, step) for n in range(2)]
+    near = [read_table(one_ref, body + 3, step), read_table(near_ref, 0, step)]
     far = [read_table(ref, 0, step) for ref in (one_ref, two_ref)]
     out = gradients(
         [
@@ -511,9 +509,10 @@
         along_garm(last_same, [(z, z ^ 1) for z in range(garm_n)]),
     ]
     direct = lax.ppermute(last_other, ("garm", "body"), [(n, n ^ 3) for n in range(2 * garm_n)])
-    near_shape = jax.ShapeDtypeStruct((5 + 8 * tiles, SUB, BLOCK), f32)
+    near_shape = jax.ShapeDtypeStruct((5 + 4 * tiles, SUB, BLOCK), f32)
+    second_shape = jax.ShapeDtypeStruct((3 + 8 * tiles, SUB, BLOCK), f32)
     near = call(forward_kernel, near_shape, [], (), (own, got[0]), BUNDLE_COST)
-    second = call(half_kernel, half, [], (), (got[1], near), BUNDLE_COST)
+    second = call(second_kernel, second_shape, [], (), (own, got[1], near), BUNDLE_COST)
     near_other, second_other = along_body(near), along_body(second)
 
     def batch_shapes(count):

time: 17.8 us -> 18.1 us (1.017)
  waiting for transfers between devices: 1.23 us -> 1.54 us
    ppermute x2, waiting for transfers between devices: 0.9 us -> 1.21 us  [along_body(): return lax.ppermute(value, 'body', [(0, 1), (1, 0)])]
  transfers between devices with their start and end apart: 7 -> 7, of which waited for: 3 -> 4; matrix products, arithmetic and copies ran while one was open for 0% -> 0% of each run, Pallas kernels for 15% -> 15%
where the time goes in v14:
time: 18.1 us; the launch traced here: 17.9 us
  starting transfers between devices  10.8 us (60%)
  Pallas kernels  4.89 us (27%)
  waiting for transfers between devices  1.54 us (9%)
  between operations  0.67 us (4%)
    ppermute x3, starting transfers between devices, along_garm(): return lax.ppermute(value, 'garm', pairs)  5.67 us
    pallas_call x7, Pallas kernels, call(): pl.pallas_call(kernel, out_shape=out_shape, in_specs=specs, out_specs=jax...  3.88 us
    ppermute x1, starting transfers between devices, staged(): lax.ppermute(last_other, ('garm', 'body'), [(n, n ^ 3) for n in range(2 *...  2.61 us
    ppermute x2, starting transfers between devices, along_body(): return lax.ppermute(value, 'body', [(0, 1), (1, 0)])  2.48 us
    ppermute x2, waiting for transfers between devices, along_body(): return lax.ppermute(value, 'body', [(0, 1), (1, 0)])  1.21 us
    pallas_call x1, Pallas kernels, staged(): pl.pallas_call(stage_kernel, out_shape=[jax.ShapeDtypeStruct((garm_n, SUB...  1.01 us
  transfers between devices with their start and end apart: 7, of which 4 were waited for; matrix products, arithmetic and copies ran while one was open for 0% of the time, Pallas kernels for 15%

profile of v14, /device:TPU:0, one launch (start us, length us, event | category | flops | bytes accessed | tf_op | source)
XLA Modules:
  0.0 17.9 jit_solution(12492960861735922468)
XLA Ops:
  0.6 1.0 %shard_map.94 = (f32[4,8,128]{2,1,0:T(8,128)S(1)}, f32[11,8,128]{2,1,0:T(8,128)S(1)}, f32[11,8,128]{2,1,0:T(8,128)S(1)}, f32[13,8,128]{2,1,0:T(8,128)S(1)}, f32[...) custom-call(s32[4,8]{1,0:T(4,128)} %bitcast.18, s32[4,8]{1,0:T(4,128)} %bitcast.19, ...), custom_call_target="tpu_custom_call" | custom-call | tf_op jit(solution)/shard_map/pallas_call | solution.py:487
  1.6 4.1 %collective-permute-start = (f32[13,8,128]{2,1,0:T(8,128)S(1)}, f32[13,8,128]{2,1,0:T(8,128)S(1)}, u32[]{:S(2)}, u32[]{:S(2)}) collective-permute-start(f32[13,8,128]{2,1,0:T(8,128)S(1)} %get-tuple-element.22.sent1), channel_id=1, source_target_pairs={{0,8},{8,4},{4,12},{12,0},{1,9},{9,5},{5,13},{13,1},{2,10},{10,6},... | collective-permute-start | bytes 159752 | tf_op jit(solution)/shard_map/ppermute | solution.py:500
  5.7 1.1 %collective-permute-start.2 = (f32[13,8,128]{2,1,0:T(8,128)S(1)}, f32[13,8,128]{2,1,0:T(8,128)S(1)}, u32[]{:S(2)}, u32[]{:S(2)}) collective-permute-start(f32[13,8,128]{2,1,0:T(8,128)S(1)} %get-tuple-element.21.sent0), channel_id=1, source_target_pairs={{8,0},{4,8},{12,4},{0,12},{9,1},{5,9},{13,5},{1,13},{10,2},{6,10},... | collective-permute-start | bytes 159752 | tf_op jit(solution)/shard_map/ppermute | solution.py:500
  6.8 0.5 %collective-permute-start.5 = (f32[11,8,128]{2,1,0:T(8,128)S(1)}, f32[11,8,128]{2,1,0:T(8,128)S(1)}, u32[]{:S(2)}, u32[]{:S(2)}) collective-permute-start(f32[11,8,128]{2,1,0:T(8,128)S(1)} %get-tuple-element.25), channel_id=1, source_target_pairs={{0,4},{4,0},{8,12},{12,8},{1,5},{5,1},{9,13},{13,9},{2,6},{6,2},{1... | collective-permute-start | bytes 135176 | tf_op jit(solution)/shard_map/ppermute | solution.py:500
  7.3 2.6 %collective-permute-start.4 = (f32[11,8,128]{2,1,0:T(8,128)S(1)}, f32[11,8,128]{2,1,0:T(8,128)S(1)}, u32[]{:S(2)}, u32[]{:S(2)}) collective-permute-start(f32[11,8,128]{2,1,0:T(8,128)S(1)} %get-tuple-element.24), channel_id=1, source_target_pairs={{0,6},{2,4},{4,2},{6,0},{8,14},{10,12},{12,10},{14,8},{1,7},{3,5},... | collective-permute-start | bytes 135176 | tf_op jit(solution)/shard_map/ppermute | solution.py:511
  9.9 0.0 collective-permute-done.ref.got0
  9.9 0.8 %collective-permute-start.1 = (f32[13,8,128]{2,1,0:T(8,128)S(1)}, f32[13,8,128]{2,1,0:T(8,128)S(1)}, u32[]{:S(2)}, u32[]{:S(2)}) collective-permute-start(f32[13,8,128]{2,1,0:T(8,128)S(1)} %shard_map.95.after_ref), channel_id=1, source_target_pairs={{0,2},{2,0},{1,3},{3,1},{4,6},{6,4},{5,7},{7,5},{8,10},{10,8},{9,1... | collective-permute-start | bytes 159752 | tf_op jit(solution)/shard_map/ppermute | solution.py:503
  10.8 0.2 collective-permute-done.2.ref.got1
  10.9 1.7 %collective-permute-start.3 = (f32[19,8,128]{2,1,0:T(8,128)S(1)}, f32[19,8,128]{2,1,0:T(8,128)S(1)}, u32[]{:S(2)}, u32[]{:S(2)}) collective-permute-start(f32[19,8,128]{2,1,0:T(8,128)S(1)} %shard_map.96.after_ref), channel_id=1, source_target_pairs={{0,2},{2,0},{1,3},{3,1},{4,6},{6,4},{5,7},{7,5},{8,10},{10,8},{9,1... | collective-permute-start | bytes 233480 | tf_op jit(solution)/shard_map/ppermute | solution.py:503
  12.6 0.0 collective-permute-done.5.got2
  12.6 1.0 %shard_map.97 = (f32[16,512]{1,0:T(8,128)S(1)}, f32[16,128]{1,0:T(8,128)S(1)}, f32[16,384]{1,0:T(8,128)S(1)}) custom-call(f32[13,8,128]{2,1,0:T(8,128)S(1)} %get-tuple-element.20.own_ref, f32[13,8,128]{2,1,0:T(8,128)S(1)} %get-tuple-element.21.sent0, f32[13,8,128]{2,1,0:T(8,128)S(1)} %get-tuple-element.22.sent1, f32[13,8,128]{2,1,0:T(8,128)S(1)} %get-tuple-element.23.sent2, ...), custom_call_target="tpu_custom_call" | custom-call | flops 40000000000 | bytes 1000 | tf_op jit(solution)/shard_map/pallas_call | solution.py:229
  13.7 0.6 %collective-permute-done.1.near_ref = f32[13,8,128]{2,1,0:T(8,128)S(1)} collective-permute-done((f32[13,8,128]{2,1,0:T(8,128)S(1)}, f32[13,8,128]{2,1,0:T(8,128)S(1)}, u32[]{:S(2)}, u32[]{:S(2)}) %collective-permute-start.1) | collective-permute-done | bytes 53280 | tf_op jit(solution)/shard_map/ppermute | solution.py:503
  14.2 0.5 %shard_map.98 = (f32[8,512]{1,0:T(8,128)S(1)}, f32[8,128]{1,0:T(8,128)S(1)}) custom-call(f32[13,8,128]{2,1,0:T(8,128)S(1)} %get-tuple-element.20.own_ref, f32[13,8,128]{2,1,0:T(8,128)S(1)} %collective-permute-done.1.near_ref, f32[16,512]{1,0:T(8,128)S(1)} %get-tuple-element.26.after_ref.bg1), custom_call_target="tpu_custom_call" | custom-call | flops 1000000000 | bytes 1000 | tf_op jit(solution)/shard_map/pallas_call | solution.py:229
  14.7 0.0 collective-permute-done.4.two_ref
  14.8 0.7 %collective-permute-done.3.one_ref = f32[19,8,128]{2,1,0:T(8,128)S(1)} collective-permute-done((f32[19,8,128]{2,1,0:T(8,128)S(1)}, f32[19,8,128]{2,1,0:T(8,128)S(1)}, u32[]{:S(2)}, u32[]{:S(2)}) %collective-permute-start.3) | collective-permute-done | bytes 77856 | tf_op jit(solution)/shard_map/ppermute | solution.py:503
  15.4 0.6 %shard_map.100.mine_ref = f32[16,128]{1,0:T(8,128)S(1)} custom-call(f32[13,8,128]{2,1,0:T(8,128)S(1)} %get-tuple-element.20.own_ref, f32[19,8,128]{2,1,0:T(8,128)S(1)} %collective-permute-done.3.one_ref, f32[11,8,128]{2,1,0:T(8,128)S(1)} %collective-permute-done.4.two_ref, f32[16,512]{1,0:T(8,128)S(1)} %get-tuple-element.26.after_ref.bg1, ...), custom_call_target="tpu_custom_call" | custom-call | tf_op jit(solution)/shard_map/pallas_call | solution.py:229
  16.0 0.0 collective-permute-start.6
  16.0 1.0 %shard_map.99 = (f32[3,16,128]{2,1,0:T(8,128)S(1)}, f32[3,32,128]{2,1,0:T(8,128)S(1)}) custom-call(f32[13,8,128]{2,1,0:T(8,128)S(1)} %get-tuple-element.20.own_ref, f32[13,8,128]{2,1,0:T(8,128)S(1)} %get-tuple-element.21.sent0, f32[13,8,128]{2,1,0:T(8,128)S(1)} %get-tuple-element.22.sent1, f32[13,8,128]{2,1,0:T(8,128)S(1)} %get-tuple-element.23.sent2, ...), custom_call_target="tpu_custom_call" | custom-call | tf_op jit(solution)/shard_map/pallas_call | solution.py:229
  17.1 0.1 collective-permute-done.6.other_ref
  17.2 0.6 %shard_map.101 = (f32[3,32,128]{2,1,0:T(8,128)}, f32[3,16,128]{2,1,0:T(8,128)}, f32[16,128]{1,0:T(8,128)}) custom-call(f32[3,32,128]{2,1,0:T(8,128)S(1)} %get-tuple-element.32.garm_ref, f32[3,16,128]{2,1,0:T(8,128)S(1)} %get-tuple-element.33.body_ref, f32[16,128]{1,0:T(8,128)S(1)} %shard_map.100.mine_ref, f32[16,128]{1,0:T(8,128)S(1)} %collective-permute-done.6.other_ref), custom_call_target="tpu_custom_call" | custom-call | tf_op jit(solution)/shard_map/pallas_call | solution.py:229
  (2 shorter events, 0.0 us)
Async XLA Ops:
  1.6 8.3 %collective-permute-start = (f32[13,8,128]{2,1,0:T(8,128)S(1)}, f32[13,8,128]{2,1,0:T(8,128)S(1)}, u32[]{:S(2)}, u32[]{:S(2)}) collective-permute-start(f32[13,8,128]{2,1,0:T(8,128)S(1)} %get-tuple-element.22.sent1), channel_id=1, source_target_pairs={{0,8},{8,4},{4,12},{12,0},{1,9},{9,5},{5,13},{13,1},{2,10},{10,6},... | collective-permute-start | bytes 159752 | tf_op jit(solution)/shard_map/ppermute | solution.py:500
  5.7 5.2 %collective-permute-start.2 = (f32[13,8,128]{2,1,0:T(8,128)S(1)}, f32[13,8,128]{2,1,0:T(8,128)S(1)}, u32[]{:S(2)}, u32[]{:S(2)}) collective-permute-start(f32[13,8,128]{2,1,0:T(8,128)S(1)} %get-tuple-element.21.sent0), channel_id=1, source_target_pairs={{8,0},{4,8},{12,4},{0,12},{9,1},{5,9},{13,5},{1,13},{10,2},{6,10},... | collective-permute-start | bytes 159752 | tf_op jit(solution)/shard_map/ppermute | solution.py:500
  6.8 5.8 %collective-permute-start.5 = (f32[11,8,128]{2,1,0:T(8,128)S(1)}, f32[11,8,128]{2,1,0:T(8,128)S(1)}, u32[]{:S(2)}, u32[]{:S(2)}) collective-permute-start(f32[11,8,128]{2,1,0:T(8,128)S(1)} %get-tuple-element.25), channel_id=1, source_target_pairs={{0,4},{4,0},{8,12},{12,8},{1,5},{5,1},{9,13},{13,9},{2,6},{6,2},{1... | collective-permute-start | bytes 135176 | tf_op jit(solution)/shard_map/ppermute | solution.py:500
  7.3 7.4 %collective-permute-start.4 = (f32[11,8,128]{2,1,0:T(8,128)S(1)}, f32[11,8,128]{2,1,0:T(8,128)S(1)}, u32[]{:S(2)}, u32[]{:S(2)}) collective-permute-start(f32[11,8,128]{2,1,0:T(8,128)S(1)} %get-tuple-element.24), channel_id=1, source_target_pairs={{0,6},{2,4},{4,2},{6,0},{8,14},{10,12},{12,10},{14,8},{1,7},{3,5},... | collective-permute-start | bytes 135176 | tf_op jit(solution)/shard_map/ppermute | solution.py:511
  9.9 4.3 %collective-permute-start.1 = (f32[13,8,128]{2,1,0:T(8,128)S(1)}, f32[13,8,128]{2,1,0:T(8,128)S(1)}, u32[]{:S(2)}, u32[]{:S(2)}) collective-permute-start(f32[13,8,128]{2,1,0:T(8,128)S(1)} %shard_map.95.after_ref), channel_id=1, source_target_pairs={{0,2},{2,0},{1,3},{3,1},{4,6},{6,4},{5,7},{7,5},{8,10},{10,8},{9,1... | collective-permute-start | bytes 159752 | tf_op jit(solution)/shard_map/ppermute | solution.py:503
  10.9 4.5 %collective-permute-start.3 = (f32[19,8,128]{2,1,0:T(8,128)S(1)}, f32[19,8,128]{2,1,0:T(8,128)S(1)}, u32[]{:S(2)}, u32[]{:S(2)}) collective-permute-start(f32[19,8,128]{2,1,0:T(8,128)S(1)} %shard_map.96.after_ref), channel_id=1, source_target_pairs={{0,2},{2,0},{1,3},{3,1},{4,6},{6,4},{5,7},{7,5},{8,10},{10,8},{9,1... | collective-permute-start | bytes 233480 | tf_op jit(solution)/shard_map/ppermute | solution.py:503
  16.0 1.2 %collective-permute-start.6 = (f32[16,128]{1,0:T(8,128)S(1)}, f32[16,128]{1,0:T(8,128)S(1)}, u32[]{:S(2)}, u32[]{:S(2)}) collective-permute-start(f32[16,128]{1,0:T(8,128)S(1)} %shard_map.100.mine_ref), channel_id=1, source_target_pairs={{0,1},{1,0},{2,3},{3,2},{4,5},{5,4},{6,7},{7,6},{8,9},{9,8},{10,11... | collective-permute-start | bytes 24584 | tf_op jit(solution)/shard_map/ppermute | solution.py:535

commit v15 on v13

--- a/solution.py
+++ b/solution.py
@@ -381,7 +381,7 @@
     out_ref[...] = scatter(index, jnp.concatenate(grads, axis=0), out_ref.shape[0])
 
 
-def late_kernel(
+def late_sums(
     own_ref,
     sent0,
     sent1,
@@ -422,6 +422,28 @@
     total = scatter(index, grads, garm_out.shape[1])
     for c in range(3):
         garm_out[c] = total[:, c * BLOCK : (c + 1) * BLOCK]
+
+
+def before_kernel(*refs):
+    *work, stiff_ref, body_out, garm_out, stiff_out = refs
+    stiff_out[...] = stiff_ref[...]
+
+    @pl.when(lax.axis_index("frame") == 1)
+    def _():
+        late_sums(*work, body_out, garm_out)
+
+
+def beside_kernel(*refs):
+    *work, body_ref, garm_ref, body_out, garm_out = refs
+
+    @pl.when(lax.axis_index("frame") == 0)
+    def _():
+        late_sums(*work, body_out, garm_out)
+
+    @pl.when(lax.axis_index("frame") == 1)
+    def _():
+        body_out[...] = body_ref[...]
+        garm_out[...] = garm_ref[...]
 
 
 def final_kernel(garm_ref, body_ref, mine_ref, other_ref, garm_out, body_out, stiff_out):
@@ -533,13 +555,13 @@
     stiff = call(
         stiff_kernel, stiff_shape, [], (), (own, second_other, direct, bg1, bg2, bi1, bi2)
     )
+    work = (own, *sent, near_other, second_other, direct, bg1, bg2, bi1, bi2, gg1, index)
+    body_total, garm_total, stiff = call(
+        before_kernel, (body_shape, garm_shape, stiff_shape), [], (), (*work, stiff)
+    )
     stiff_other = lax.ppermute(stiff, "frame", [(0, 1), (1, 0)])
     body_total, garm_total = call(
-        late_kernel,
-        (body_shape, garm_shape),
-        [],
-        (),
-        (own, *sent, near_other, second_other, direct, bg1, bg2, bi1, bi2, gg1, index),
+        beside_kernel, (body_shape, garm_shape), [], (), (*work, body_total, garm_total)
     )
     return call(
         final_kernel,

time: 17.8 us -> 17.7 us (level)
    pallas_call x7 -> x8, Pallas kernels: 3.89 us -> 3.9 us  [call(): pl.pallas_call(kernel, out_shape=out_shape, in_specs=specs, out_specs=jax...]
where the time goes in v15:
time: 17.7 us; the launch traced here: 17.5 us
  starting transfers between devices  10.7 us (60%)
  Pallas kernels  4.9 us (28%)
  waiting for transfers between devices  1.22 us (7%)
  between operations  0.68 us (4%)
    ppermute x3, starting transfers between devices, along_garm(): return lax.ppermute(value, 'garm', pairs)  5.67 us
    pallas_call x8, Pallas kernels, call(): pl.pallas_call(kernel, out_shape=out_shape, in_specs=specs, out_specs=jax...  3.9 us
    ppermute x1, starting transfers between devices, staged(): lax.ppermute(last_other, ('garm', 'body'), [(n, n ^ 3) for n in range(2 *...  2.61 us
    ppermute x2, starting transfers between devices, along_body(): return lax.ppermute(value, 'body', [(0, 1), (1, 0)])  2.42 us
    pallas_call x1, Pallas kernels, staged(): pl.pallas_call(stage_kernel, out_shape=[jax.ShapeDtypeStruct((garm_n, SUB...  1.01 us
    ppermute x2, waiting for transfers between devices, along_body(): return lax.ppermute(value, 'body', [(0, 1), (1, 0)])  0.9 us
  transfers between devices with their start and end apart: 7, of which 3 were waited for; matrix products, arithmetic and copies ran while one was open for 0% of the time, Pallas kernels for 15%

profile of v15, /device:TPU:0, one launch (start us, length us, event | category | flops | bytes accessed | tf_op | source)
XLA Modules:
  0.0 17.5 jit_solution(15549984079088350486)
XLA Ops:
  0.6 1.0 %shard_map.94 = (f32[4,8,128]{2,1,0:T(8,128)S(1)}, f32[11,8,128]{2,1,0:T(8,128)S(1)}, f32[11,8,128]{2,1,0:T(8,128)S(1)}, f32[13,8,128]{2,1,0:T(8,128)S(1)}, f32[...) custom-call(s32[4,8]{1,0:T(4,128)} %bitcast.18, s32[4,8]{1,0:T(4,128)} %bitcast.19, ...), custom_call_target="tpu_custom_call" | custom-call | tf_op jit(solution)/shard_map/pallas_call | solution.py:511
  1.6 4.1 %collective-permute-start = (f32[13,8,128]{2,1,0:T(8,128)S(1)}, f32[13,8,128]{2,1,0:T(8,128)S(1)}, u32[]{:S(2)}, u32[]{:S(2)}) collective-permute-start(f32[13,8,128]{2,1,0:T(8,128)S(1)} %get-tuple-element.25.sent1.refs_2_), channel_id=1, source_target_pairs={{0,8},{8,4},{4,12},{12,0},{1,9},{9,5},{5,13},{13,1},{2,10},{10,6},... | collective-permute-start | bytes 159752 | tf_op jit(solution)/shard_map/ppermute | solution.py:524
  5.7 1.1 %collective-permute-start.2 = (f32[13,8,128]{2,1,0:T(8,128)S(1)}, f32[13,8,128]{2,1,0:T(8,128)S(1)}, u32[]{:S(2)}, u32[]{:S(2)}) collective-permute-start(f32[13,8,128]{2,1,0:T(8,128)S(1)} %get-tuple-element.24.sent0.refs_1_), channel_id=1, source_target_pairs={{8,0},{4,8},{12,4},{0,12},{9,1},{5,9},{13,5},{1,13},{10,2},{6,10},... | collective-permute-start | bytes 159752 | tf_op jit(solution)/shard_map/ppermute | solution.py:524
  6.8 0.5 %collective-permute-start.5 = (f32[11,8,128]{2,1,0:T(8,128)S(1)}, f32[11,8,128]{2,1,0:T(8,128)S(1)}, u32[]{:S(2)}, u32[]{:S(2)}) collective-permute-start(f32[11,8,128]{2,1,0:T(8,128)S(1)} %get-tuple-element.28), channel_id=1, source_target_pairs={{0,4},{4,0},{8,12},{12,8},{1,5},{5,1},{9,13},{13,9},{2,6},{6,2},{1... | collective-permute-start | bytes 135176 | tf_op jit(solution)/shard_map/ppermute | solution.py:524
  7.3 2.6 %collective-permute-start.4 = (f32[11,8,128]{2,1,0:T(8,128)S(1)}, f32[11,8,128]{2,1,0:T(8,128)S(1)}, u32[]{:S(2)}, u32[]{:S(2)}) collective-permute-start(f32[11,8,128]{2,1,0:T(8,128)S(1)} %get-tuple-element.27), channel_id=1, source_target_pairs={{0,6},{2,4},{4,2},{6,0},{8,14},{10,12},{12,10},{14,8},{1,7},{3,5},... | collective-permute-start | bytes 135176 | tf_op jit(solution)/shard_map/ppermute | solution.py:535
  9.9 0.0 collective-permute-done.two_ref.got0
  9.9 0.8 %collective-permute-start.1 = (f32[21,8,128]{2,1,0:T(8,128)S(1)}, f32[21,8,128]{2,1,0:T(8,128)S(1)}, u32[]{:S(2)}, u32[]{:S(2)}) collective-permute-start(f32[21,8,128]{2,1,0:T(8,128)S(1)} %shard_map.95.after_ref), channel_id=1, source_target_pairs={{0,2},{2,0},{1,3},{3,1},{4,6},{6,4},{5,7},{7,5},{8,10},{10,8},{9,1... | collective-permute-start | bytes 258056 | tf_op jit(solution)/shard_map/ppermute | solution.py:527
  10.8 0.2 collective-permute-done.2.ref.got1
  10.9 1.6 %collective-permute-start.3 = (f32[11,8,128]{2,1,0:T(8,128)S(1)}, f32[11,8,128]{2,1,0:T(8,128)S(1)}, u32[]{:S(2)}, u32[]{:S(2)}) collective-permute-start(f32[11,8,128]{2,1,0:T(8,128)S(1)} %shard_map.96.after_ref), channel_id=1, source_target_pairs={{0,2},{2,0},{1,3},{3,1},{4,6},{6,4},{5,7},{7,5},{8,10},{10,8},{9,1... | collective-permute-start | bytes 135176 | tf_op jit(solution)/shard_map/ppermute | solution.py:527
  12.5 0.0 collective-permute-done.5.got2
  12.5 1.0 %shard_map.97 = (f32[16,512]{1,0:T(8,128)S(1)}, f32[16,128]{1,0:T(8,128)S(1)}, f32[16,384]{1,0:T(8,128)S(1)}) custom-call(f32[13,8,128]{2,1,0:T(8,128)S(1)} %get-tuple-element.23.one_ref.own_ref.refs_0_, f32[13,8,128]{2,1,0:T(8,128)S(1)} %get-tuple-element.24.sent0.refs_1_, f32[13,8,128]{2,1,0:T(8,128)S(1)} %get-tuple-element.25.sent1.refs_2_, ...), custom_call_target="tpu_custom_call" | custom-call | flops 40000000000 | bytes 1000 | tf_op jit(solution)/shard_map/pallas_call | solution.py:229
  13.6 0.9 %collective-permute-done.1.near_ref.refs_4_ = f32[21,8,128]{2,1,0:T(8,128)S(1)} collective-permute-done((f32[21,8,128]{2,1,0:T(8,128)S(1)}, f32[21,8,128]{2,1,0:T(8,128)S(1)}, u32[]{:S(2)}, u32[]{:S(2)}) %collective-permute-start.1) | collective-permute-done | bytes 86048 | tf_op jit(solution)/shard_map/ppermute | solution.py:527
  14.5 0.5 %shard_map.98 = (f32[8,512]{1,0:T(8,128)S(1)}, f32[8,128]{1,0:T(8,128)S(1)}) custom-call(f32[13,8,128]{2,1,0:T(8,128)S(1)} %get-tuple-element.23.one_ref.own_ref.refs_0_, f32[21,8,128]{2,1,0:T(8,128)S(1)} %collective-permute-done.1.near_ref.refs_4_, f32[16,512]{1,0:T(8,128)S(1)} %get-tuple-element.29.after_ref.bg1.refs_7_), custom_call_target="tpu_custom_call" | custom-call | flops 1000000000 | bytes 1000 | tf_op jit(solution)/shard_map/pallas_call | solution.py:229
  15.0 0.0 collective-permute-done.4.two_ref.refs_6_
  15.0 0.0 collective-permute-done.3.one_ref.refs_5_
  15.0 0.6 %shard_map.99.refs_13_ = f32[16,128]{1,0:T(8,128)S(1)} custom-call(f32[13,8,128]{2,1,0:T(8,128)S(1)} %get-tuple-element.23.one_ref.own_ref.refs_0_, f32[11,8,128]{2,1,0:T(8,128)S(1)} %collective-permute-done.3.one_ref.refs_5_, f32[11,8,128]{2,1,0:T(8,128)S(1)} %collective-permute-done.4.two_ref.refs_6_, ...), custom_call_target="tpu_custom_call" | custom-call | tf_op jit(solution)/shard_map/pallas_call | solution.py:229
  15.7 0.0 collective-permute-start.6
  15.7 1.0 %shard_map.101 = (f32[3,16,128]{2,1,0:T(8,128)S(1)}, f32[3,32,128]{2,1,0:T(8,128)S(1)}) custom-call(f32[13,8,128]{2,1,0:T(8,128)S(1)} %get-tuple-element.23.one_ref.own_ref.refs_0_, f32[13,8,128]{2,1,0:T(8,128)S(1)} %get-tuple-element.24.sent0.refs_1_, f32[13,8,128]{2,1,0:T(8,128)S(1)} %get-tuple-element.25.sent1.refs_2_, ...), custom_call_target="tpu_custom_call" | custom-call | tf_op jit(solution)/shard_map/pallas_call | solution.py:229
  16.7 0.1 collective-permute-done.6.other_ref
  16.9 0.6 %shard_map.102 = (f32[3,32,128]{2,1,0:T(8,128)}, f32[3,16,128]{2,1,0:T(8,128)}, f32[16,128]{1,0:T(8,128)}) custom-call(f32[3,32,128]{2,1,0:T(8,128)S(1)} %get-tuple-element.37.garm_ref, f32[3,16,128]{2,1,0:T(8,128)S(1)} %get-tuple-element.38.body_ref, f32[16,128]{1,0:T(8,128)S(1)} %get-tuple-element.39.mine_ref, f32[16,128]{1,0:T(8,128)S(1)} %collective-permute-done.6.other_ref), custom_call_target="tpu_custom_call" | custom-call | tf_op jit(solution)/shard_map/pallas_call | solution.py:229
  (3 shorter events, 0.0 us)
Async XLA Ops:
  1.6 8.3 %collective-permute-start = (f32[13,8,128]{2,1,0:T(8,128)S(1)}, f32[13,8,128]{2,1,0:T(8,128)S(1)}, u32[]{:S(2)}, u32[]{:S(2)}) collective-permute-start(f32[13,8,128]{2,1,0:T(8,128)S(1)} %get-tuple-element.25.sent1.refs_2_), channel_id=1, source_target_pairs={{0,8},{8,4},{4,12},{12,0},{1,9},{9,5},{5,13},{13,1},{2,10},{10,6},... | collective-permute-start | bytes 159752 | tf_op jit(solution)/shard_map/ppermute | solution.py:524
  5.7 5.2 %collective-permute-start.2 = (f32[13,8,128]{2,1,0:T(8,128)S(1)}, f32[13,8,128]{2,1,0:T(8,128)S(1)}, u32[]{:S(2)}, u32[]{:S(2)}) collective-permute-start(f32[13,8,128]{2,1,0:T(8,128)S(1)} %get-tuple-element.24.sent0.refs_1_), channel_id=1, source_target_pairs={{8,0},{4,8},{12,4},{0,12},{9,1},{5,9},{13,5},{1,13},{10,2},{6,10},... | collective-permute-start | bytes 159752 | tf_op jit(solution)/shard_map/ppermute | solution.py:524
  6.8 5.7 %collective-permute-start.5 = (f32[11,8,128]{2,1,0:T(8,128)S(1)}, f32[11,8,128]{2,1,0:T(8,128)S(1)}, u32[]{:S(2)}, u32[]{:S(2)}) collective-permute-start(f32[11,8,128]{2,1,0:T(8,128)S(1)} %get-tuple-element.28), channel_id=1, source_target_pairs={{0,4},{4,0},{8,12},{12,8},{1,5},{5,1},{9,13},{13,9},{2,6},{6,2},{1... | collective-permute-start | bytes 135176 | tf_op jit(solution)/shard_map/ppermute | solution.py:524
  7.3 7.7 %collective-permute-start.4 = (f32[11,8,128]{2,1,0:T(8,128)S(1)}, f32[11,8,128]{2,1,0:T(8,128)S(1)}, u32[]{:S(2)}, u32[]{:S(2)}) collective-permute-start(f32[11,8,128]{2,1,0:T(8,128)S(1)} %get-tuple-element.27), channel_id=1, source_target_pairs={{0,6},{2,4},{4,2},{6,0},{8,14},{10,12},{12,10},{14,8},{1,7},{3,5},... | collective-permute-start | bytes 135176 | tf_op jit(solution)/shard_map/ppermute | solution.py:535
  9.9 4.6 %collective-permute-start.1 = (f32[21,8,128]{2,1,0:T(8,128)S(1)}, f32[21,8,128]{2,1,0:T(8,128)S(1)}, u32[]{:S(2)}, u32[]{:S(2)}) collective-permute-start(f32[21,8,128]{2,1,0:T(8,128)S(1)} %shard_map.95.after_ref), channel_id=1, source_target_pairs={{0,2},{2,0},{1,3},{3,1},{4,6},{6,4},{5,7},{7,5},{8,10},{10,8},{9,1... | collective-permute-start | bytes 258056 | tf_op jit(solution)/shard_map/ppermute | solution.py:527
  10.9 4.1 %collective-permute-start.3 = (f32[11,8,128]{2,1,0:T(8,128)S(1)}, f32[11,8,128]{2,1,0:T(8,128)S(1)}, u32[]{:S(2)}, u32[]{:S(2)}) collective-permute-start(f32[11,8,128]{2,1,0:T(8,128)S(1)} %shard_map.96.after_ref), channel_id=1, source_target_pairs={{0,2},{2,0},{1,3},{3,1},{4,6},{6,4},{5,7},{7,5},{8,10},{10,8},{9,1... | collective-permute-start | bytes 135176 | tf_op jit(solution)/shard_map/ppermute | solution.py:527
  15.7 1.2 %collective-permute-start.6 = (f32[16,128]{1,0:T(8,128)S(1)}, f32[16,128]{1,0:T(8,128)S(1)}, u32[]{:S(2)}, u32[]{:S(2)}) collective-permute-start(f32[16,128]{1,0:T(8,128)S(1)} %get-tuple-element.39.mine_ref), channel_id=1, source_target_pairs={{0,1},{1,0},{2,3},{3,2},{4,5},{5,4},{6,7},{7,6},{8,9},{9,8},{10,11... | collective-permute-start | bytes 24584 | tf_op jit(solution)/shard_map/ppermute | solution.py:562

commit v16 on v15

--- a/solution.py
+++ b/solution.py
@@ -54,12 +54,12 @@
     )
 
 
-def pull(batches, weights_only=False):
+def pull(batches):
     made = []
     for left, right in batches:
         lfeat, rfeat = features(left, right)
         weight = left[3]
-        coeff = [weight] if weights_only else [weight * left[c] for c in range(3)] + [weight]
+        coeff = [weight * left[c] for c in range(3)] + [weight]
         chi, clo = pieces(jnp.concatenate(coeff, axis=0), 2)
         lhs = jnp.concatenate(
             [
@@ -96,6 +96,22 @@
     for work in waiting:
         sums_of(*work)
     return [[total[c * SUB : (c + 1) * SUB] for c in range(count // SUB)] for total in totals]
+
+
+def weigh(left, right):
+    lfeat, rfeat = features(left, right)
+    lfeat_t, weight_t = lfeat.T, left[3].T
+    row = lax.broadcasted_iota(jnp.int32, rfeat.shape, 0) % SUB
+    exponents = []
+    for pair in range(0, SUB, 2):
+        masks = [(row == pair + k).astype(f32).astype(bf16) for k in range(2)]
+        rhs = jnp.concatenate([rfeat * mask for mask in masks], axis=1)
+        exponents.append(jnp.dot(lfeat_t, rhs, preferred_element_type=f32))
+    rows = []
+    for n in range(SUB):
+        kernel = jnp.exp2(exponents[n // 2][:, n % 2 * BLOCK : (n % 2 + 1) * BLOCK])
+        rows.append(jnp.sum(kernel * weight_t[:, n : n + 1], axis=0, keepdims=True))
+    return jnp.concatenate(rows, axis=0)
 
 
 def gradients(batches):
@@ -375,10 +391,14 @@
 def stiff_kernel(own_ref, one_ref, two_ref, bg1, bg2, bi1, bi2, out_ref):
     tiles = late_tiles(own_ref, one_ref, two_ref)
     own = message_table(own_ref, (own_ref.shape[0] - 5) // 4)
-    [[last]] = pull([body_work(tiles, own)], weights_only=True)
-    grads = [bg1[:, 3 * BLOCK :], bg2[:, 3 * BLOCK :], amplitude * last]
-    index = jnp.concatenate([bi1[...], bi2[...], tiles[4]], axis=0)
-    out_ref[...] = scatter(index, jnp.concatenate(grads, axis=0), out_ref.shape[0])
+    index = jnp.concatenate([bi1[...], bi2[...]], axis=0)
+    grads = jnp.concatenate([bg1[:, 3 * BLOCK :], bg2[:, 3 * BLOCK :]], axis=0)
+    total = scatter(index, grads, out_ref.shape[0])
+    last = amplitude * weigh(*body_work(tiles, own))
+    block = lax.broadcasted_iota(jnp.int32, total.shape, 0).astype(f32)
+    for n in range(SUB):
+        total = total + jnp.where(block == tiles[4][n : n + 1], last[n : n + 1], 0.0)
+    out_ref[...] = total
 
 
 def late_sums(

time: 17.7 us -> 17.5 us (0.989)
  Pallas kernels: 4.9 us -> 4.7 us
    pallas_call x8, Pallas kernels: 3.9 us -> 3.7 us  [call(): pl.pallas_call(kernel, out_shape=out_shape, in_specs=specs, out_specs=jax...]
where the time goes in v16:
time: 17.5 us; the launch traced here: 17.4 us
  starting transfers between devices  10.8 us (62%)
  Pallas kernels  4.7 us (27%)
  waiting for transfers between devices  1.2 us (7%)
  between operations  0.7 us (4%)
    ppermute x3, starting transfers between devices, along_garm(): return lax.ppermute(value, 'garm', pairs)  5.67 us
    pallas_call x8, Pallas kernels, call(): pl.pallas_call(kernel, out_shape=out_shape, in_specs=specs, out_specs=jax...  3.7 us
    ppermute x1, starting transfers between devices, staged(): lax.ppermute(last_other, ('garm', 'body'), [(n, n ^ 3) for n in range(2 *...  2.61 us
    ppermute x2, starting transfers between devices, along_body(): return lax.ppermute(value, 'body', [(0, 1), (1, 0)])  2.42 us
    pallas_call x1, Pallas kernels, staged(): pl.pallas_call(stage_kernel, out_shape=[jax.ShapeDtypeStruct((garm_n, SUB...  1.01 us
    ppermute x2, waiting for transfers between devices, along_body(): return lax.ppermute(value, 'body', [(0, 1), (1, 0)])  0.9 us
  transfers between devices with their start and end apart: 7, of which 3 were waited for; matrix products, arithmetic and copies ran while one was open for 0% of the time, Pallas kernels for 15%

profile of v16, /device:TPU:0, one launch (start us, length us, event | category | flops | bytes accessed | tf_op | source)
XLA Modules:
  0.0 17.4 jit_solution(3691172131665496721)
XLA Ops:
  0.6 1.0 %shard_map.94 = (f32[4,8,128]{2,1,0:T(8,128)S(1)}, f32[11,8,128]{2,1,0:T(8,128)S(1)}, f32[11,8,128]{2,1,0:T(8,128)S(1)}, f32[13,8,128]{2,1,0:T(8,128)S(1)}, f32[...) custom-call(s32[4,8]{1,0:T(4,128)} %bitcast.18, s32[4,8]{1,0:T(4,128)} %bitcast.19, ...), custom_call_target="tpu_custom_call" | custom-call | tf_op jit(solution)/shard_map/pallas_call | solution.py:531
  1.6 4.1 %collective-permute-start = (f32[13,8,128]{2,1,0:T(8,128)S(1)}, f32[13,8,128]{2,1,0:T(8,128)S(1)}, u32[]{:S(2)}, u32[]{:S(2)}) collective-permute-start(f32[13,8,128]{2,1,0:T(8,128)S(1)} %get-tuple-element.25.sent1.refs_2_), channel_id=1, source_target_pairs={{0,8},{8,4},{4,12},{12,0},{1,9},{9,5},{5,13},{13,1},{2,10},{10,6},... | collective-permute-start | bytes 159752 | tf_op jit(solution)/shard_map/ppermute | solution.py:544
  5.7 1.1 %collective-permute-start.2 = (f32[13,8,128]{2,1,0:T(8,128)S(1)}, f32[13,8,128]{2,1,0:T(8,128)S(1)}, u32[]{:S(2)}, u32[]{:S(2)}) collective-permute-start(f32[13,8,128]{2,1,0:T(8,128)S(1)} %get-tuple-element.24.sent0.refs_1_), channel_id=1, source_target_pairs={{8,0},{4,8},{12,4},{0,12},{9,1},{5,9},{13,5},{1,13},{10,2},{6,10},... | collective-permute-start | bytes 159752 | tf_op jit(solution)/shard_map/ppermute | solution.py:544
  6.8 0.5 %collective-permute-start.5 = (f32[11,8,128]{2,1,0:T(8,128)S(1)}, f32[11,8,128]{2,1,0:T(8,128)S(1)}, u32[]{:S(2)}, u32[]{:S(2)}) collective-permute-start(f32[11,8,128]{2,1,0:T(8,128)S(1)} %get-tuple-element.28), channel_id=1, source_target_pairs={{0,4},{4,0},{8,12},{12,8},{1,5},{5,1},{9,13},{13,9},{2,6},{6,2},{1... | collective-permute-start | bytes 135176 | tf_op jit(solution)/shard_map/ppermute | solution.py:544
  7.3 2.6 %collective-permute-start.4 = (f32[11,8,128]{2,1,0:T(8,128)S(1)}, f32[11,8,128]{2,1,0:T(8,128)S(1)}, u32[]{:S(2)}, u32[]{:S(2)}) collective-permute-start(f32[11,8,128]{2,1,0:T(8,128)S(1)} %get-tuple-element.27), channel_id=1, source_target_pairs={{0,6},{2,4},{4,2},{6,0},{8,14},{10,12},{12,10},{14,8},{1,7},{3,5},... | collective-permute-start | bytes 135176 | tf_op jit(solution)/shard_map/ppermute | solution.py:555
  9.9 0.0 collective-permute-done.two_ref.got0
  9.9 0.8 %collective-permute-start.1 = (f32[21,8,128]{2,1,0:T(8,128)S(1)}, f32[21,8,128]{2,1,0:T(8,128)S(1)}, u32[]{:S(2)}, u32[]{:S(2)}) collective-permute-start(f32[21,8,128]{2,1,0:T(8,128)S(1)} %shard_map.95.after_ref), channel_id=1, source_target_pairs={{0,2},{2,0},{1,3},{3,1},{4,6},{6,4},{5,7},{7,5},{8,10},{10,8},{9,1... | collective-permute-start | bytes 258056 | tf_op jit(solution)/shard_map/ppermute | solution.py:547
  10.8 0.2 collective-permute-done.2.ref.got1
  10.9 1.6 %collective-permute-start.3 = (f32[11,8,128]{2,1,0:T(8,128)S(1)}, f32[11,8,128]{2,1,0:T(8,128)S(1)}, u32[]{:S(2)}, u32[]{:S(2)}) collective-permute-start(f32[11,8,128]{2,1,0:T(8,128)S(1)} %shard_map.96.after_ref), channel_id=1, source_target_pairs={{0,2},{2,0},{1,3},{3,1},{4,6},{6,4},{5,7},{7,5},{8,10},{10,8},{9,1... | collective-permute-start | bytes 135176 | tf_op jit(solution)/shard_map/ppermute | solution.py:547
  12.5 0.0 collective-permute-done.5.got2
  12.5 1.0 %shard_map.97 = (f32[16,512]{1,0:T(8,128)S(1)}, f32[16,128]{1,0:T(8,128)S(1)}, f32[16,384]{1,0:T(8,128)S(1)}) custom-call(f32[13,8,128]{2,1,0:T(8,128)S(1)} %get-tuple-element.23.one_ref.own_ref.refs_0_, f32[13,8,128]{2,1,0:T(8,128)S(1)} %get-tuple-element.24.sent0.refs_1_, f32[13,8,128]{2,1,0:T(8,128)S(1)} %get-tuple-element.25.sent1.refs_2_, ...), custom_call_target="tpu_custom_call" | custom-call | flops 40000000000 | bytes 1000 | tf_op jit(solution)/shard_map/pallas_call | solution.py:245
  13.6 0.9 %collective-permute-done.1.near_ref.refs_4_ = f32[21,8,128]{2,1,0:T(8,128)S(1)} collective-permute-done((f32[21,8,128]{2,1,0:T(8,128)S(1)}, f32[21,8,128]{2,1,0:T(8,128)S(1)}, u32[]{:S(2)}, u32[]{:S(2)}) %collective-permute-start.1) | collective-permute-done | bytes 86048 | tf_op jit(solution)/shard_map/ppermute | solution.py:547
  14.5 0.5 %shard_map.98 = (f32[8,512]{1,0:T(8,128)S(1)}, f32[8,128]{1,0:T(8,128)S(1)}) custom-call(f32[13,8,128]{2,1,0:T(8,128)S(1)} %get-tuple-element.23.one_ref.own_ref.refs_0_, f32[21,8,128]{2,1,0:T(8,128)S(1)} %collective-permute-done.1.near_ref.refs_4_, f32[16,512]{1,0:T(8,128)S(1)} %get-tuple-element.29.after_ref.bg1.refs_7_), custom_call_target="tpu_custom_call" | custom-call | flops 1000000000 | bytes 1000 | tf_op jit(solution)/shard_map/pallas_call | solution.py:245
  15.0 0.0 collective-permute-done.4.two_ref.refs_6_
  15.0 0.0 collective-permute-done.3.one_ref.refs_5_
  15.0 0.4 %shard_map.99.refs_13_ = f32[16,128]{1,0:T(8,128)S(1)} custom-call(f32[13,8,128]{2,1,0:T(8,128)S(1)} %get-tuple-element.23.one_ref.own_ref.refs_0_, f32[11,8,128]{2,1,0:T(8,128)S(1)} %collective-permute-done.3.one_ref.refs_5_, f32[11,8,128]{2,1,0:T(8,128)S(1)} %collective-permute-done.4.two_ref.refs_6_, ...), custom_call_target="tpu_custom_call" | custom-call | tf_op jit(solution)/shard_map/pallas_call | solution.py:245
  15.5 0.1 collective-permute-start.6
  15.6 1.0 %shard_map.101 = (f32[3,16,128]{2,1,0:T(8,128)S(1)}, f32[3,32,128]{2,1,0:T(8,128)S(1)}) custom-call(f32[13,8,128]{2,1,0:T(8,128)S(1)} %get-tuple-element.23.one_ref.own_ref.refs_0_, f32[13,8,128]{2,1,0:T(8,128)S(1)} %get-tuple-element.24.sent0.refs_1_, f32[13,8,128]{2,1,0:T(8,128)S(1)} %get-tuple-element.25.sent1.refs_2_, ...), custom_call_target="tpu_custom_call" | custom-call | tf_op jit(solution)/shard_map/pallas_call | solution.py:245
  16.6 0.1 collective-permute-done.6.other_ref
  16.7 0.6 %shard_map.102 = (f32[3,32,128]{2,1,0:T(8,128)}, f32[3,16,128]{2,1,0:T(8,128)}, f32[16,128]{1,0:T(8,128)}) custom-call(f32[3,32,128]{2,1,0:T(8,128)S(1)} %get-tuple-element.37.garm_ref, f32[3,16,128]{2,1,0:T(8,128)S(1)} %get-tuple-element.38.body_ref, f32[16,128]{1,0:T(8,128)S(1)} %get-tuple-element.39.mine_ref, f32[16,128]{1,0:T(8,128)S(1)} %collective-permute-done.6.other_ref), custom_call_target="tpu_custom_call" | custom-call | tf_op jit(solution)/shard_map/pallas_call | solution.py:245
  (3 shorter events, 0.0 us)
Async XLA Ops:
  1.6 8.3 %collective-permute-start = (f32[13,8,128]{2,1,0:T(8,128)S(1)}, f32[13,8,128]{2,1,0:T(8,128)S(1)}, u32[]{:S(2)}, u32[]{:S(2)}) collective-permute-start(f32[13,8,128]{2,1,0:T(8,128)S(1)} %get-tuple-element.25.sent1.refs_2_), channel_id=1, source_target_pairs={{0,8},{8,4},{4,12},{12,0},{1,9},{9,5},{5,13},{13,1},{2,10},{10,6},... | collective-permute-start | bytes 159752 | tf_op jit(solution)/shard_map/ppermute | solution.py:544
  5.7 5.2 %collective-permute-start.2 = (f32[13,8,128]{2,1,0:T(8,128)S(1)}, f32[13,8,128]{2,1,0:T(8,128)S(1)}, u32[]{:S(2)}, u32[]{:S(2)}) collective-permute-start(f32[13,8,128]{2,1,0:T(8,128)S(1)} %get-tuple-element.24.sent0.refs_1_), channel_id=1, source_target_pairs={{8,0},{4,8},{12,4},{0,12},{9,1},{5,9},{13,5},{1,13},{10,2},{6,10},... | collective-permute-start | bytes 159752 | tf_op jit(solution)/shard_map/ppermute | solution.py:544
  6.8 5.7 %collective-permute-start.5 = (f32[11,8,128]{2,1,0:T(8,128)S(1)}, f32[11,8,128]{2,1,0:T(8,128)S(1)}, u32[]{:S(2)}, u32[]{:S(2)}) collective-permute-start(f32[11,8,128]{2,1,0:T(8,128)S(1)} %get-tuple-element.28), channel_id=1, source_target_pairs={{0,4},{4,0},{8,12},{12,8},{1,5},{5,1},{9,13},{13,9},{2,6},{6,2},{1... | collective-permute-start | bytes 135176 | tf_op jit(solution)/shard_map/ppermute | solution.py:544
  7.3 7.7 %collective-permute-start.4 = (f32[11,8,128]{2,1,0:T(8,128)S(1)}, f32[11,8,128]{2,1,0:T(8,128)S(1)}, u32[]{:S(2)}, u32[]{:S(2)}) collective-permute-start(f32[11,8,128]{2,1,0:T(8,128)S(1)} %get-tuple-element.27), channel_id=1, source_target_pairs={{0,6},{2,4},{4,2},{6,0},{8,14},{10,12},{12,10},{14,8},{1,7},{3,5},... | collective-permute-start | bytes 135176 | tf_op jit(solution)/shard_map/ppermute | solution.py:555
  9.9 4.6 %collective-permute-start.1 = (f32[21,8,128]{2,1,0:T(8,128)S(1)}, f32[21,8,128]{2,1,0:T(8,128)S(1)}, u32[]{:S(2)}, u32[]{:S(2)}) collective-permute-start(f32[21,8,128]{2,1,0:T(8,128)S(1)} %shard_map.95.after_ref), channel_id=1, source_target_pairs={{0,2},{2,0},{1,3},{3,1},{4,6},{6,4},{5,7},{7,5},{8,10},{10,8},{9,1... | collective-permute-start | bytes 258056 | tf_op jit(solution)/shard_map/ppermute | solution.py:547
  10.9 4.1 %collective-permute-start.3 = (f32[11,8,128]{2,1,0:T(8,128)S(1)}, f32[11,8,128]{2,1,0:T(8,128)S(1)}, u32[]{:S(2)}, u32[]{:S(2)}) collective-permute-start(f32[11,8,128]{2,1,0:T(8,128)S(1)} %shard_map.96.after_ref), channel_id=1, source_target_pairs={{0,2},{2,0},{1,3},{3,1},{4,6},{6,4},{5,7},{7,5},{8,10},{10,8},{9,1... | collective-permute-start | bytes 135176 | tf_op jit(solution)/shard_map/ppermute | solution.py:547
  15.5 1.2 %collective-permute-start.6 = (f32[16,128]{1,0:T(8,128)S(1)}, f32[16,128]{1,0:T(8,128)S(1)}, u32[]{:S(2)}, u32[]{:S(2)}) collective-permute-start(f32[16,128]{1,0:T(8,128)S(1)} %get-tuple-element.39.mine_ref), channel_id=1, source_target_pairs={{0,1},{1,0},{2,3},{3,2},{4,5},{5,4},{6,7},{7,6},{8,9},{9,8},{10,11... | collective-permute-start | bytes 24584 | tf_op jit(solution)/shard_map/ppermute | solution.py:582

commit v17 on v16

--- a/solution.py
+++ b/solution.py
@@ -380,11 +380,11 @@
     return [halves(x, y) for x, y in zip(top, bottom)]
 
 
-def near_kernel(own_ref, near_ref, after_ref, bgrad_ref, bindex_ref):
+def near_kernel(own_ref, near_ref, after_ref, stiff_ref, bindex_ref):
     del after_ref
     tiles = near_tiles(own_ref, near_ref)
     own = message_table(own_ref, (own_ref.shape[0] - 5) // 4)
-    bgrad_ref[...] = jnp.concatenate(gradients([body_work(tiles, own)])[0], axis=1)
+    stiff_ref[...] = amplitude * weigh(*body_work(tiles, own))
     bindex_ref[...] = tiles[4]
 
 
@@ -392,7 +392,7 @@
     tiles = late_tiles(own_ref, one_ref, two_ref)
     own = message_table(own_ref, (own_ref.shape[0] - 5) // 4)
     index = jnp.concatenate([bi1[...], bi2[...]], axis=0)
-    grads = jnp.concatenate([bg1[:, 3 * BLOCK :], bg2[:, 3 * BLOCK :]], axis=0)
+    grads = jnp.concatenate([bg1[:, 3 * BLOCK :], bg2[...]], axis=0)
     total = scatter(index, grads, out_ref.shape[0])
     last = amplitude * weigh(*body_work(tiles, own))
     block = lax.broadcasted_iota(jnp.int32, total.shape, 0).astype(f32)
@@ -410,9 +410,7 @@
     one_ref,
     two_ref,
     bg1,
-    bg2,
     bi1,
-    bi2,
     gg1,
     index_ref,
     body_out,
@@ -423,22 +421,24 @@
     tiles = late_tiles(own_ref, one_ref, two_ref)
     near = [read_table(near_ref, n * body, step) for n in range(2)]
     far = [read_table(ref, 0, step) for ref in (one_ref, two_ref)]
+    first = near_tiles(own_ref, near_ref)
+    own = message_table(own_ref, step)
     out = gradients(
         [
-            body_work(tiles, message_table(own_ref, step)),
+            body_work(first, own),
+            body_work(tiles, own),
             garm_work(bottom_tiles(own_ref, sent0), *near),
             garm_work(bottom_tiles(sent1, sent2), *far),
         ]
     )
     rows = [jnp.concatenate(values[:3], axis=1) for values in out]
-    width = 3 * BLOCK
-    index = jnp.concatenate([bi1[...], bi2[...], tiles[4]], axis=0)
-    grads = jnp.concatenate([bg1[:, :width], bg2[:, :width], rows[0]], axis=0)
+    index = jnp.concatenate([bi1[...], first[4], tiles[4]], axis=0)
+    grads = jnp.concatenate([bg1[:, : 3 * BLOCK], rows[0], rows[1]], axis=0)
     total = scatter(index, grads, body_out.shape[1])
     for c in range(3):
         body_out[c] = total[:, c * BLOCK : (c + 1) * BLOCK]
     index = jnp.concatenate([index_ref[k] for k in range(index_ref.shape[0])], axis=0)
-    grads = jnp.concatenate([gg1[...], rows[1], rows[2]], axis=0)
+    grads = jnp.concatenate([gg1[...], rows[2], rows[3]], axis=0)
     total = scatter(index, grads, garm_out.shape[1])
     for c in range(3):
         garm_out[c] = total[:, c * BLOCK : (c + 1) * BLOCK]
@@ -566,16 +566,15 @@
     bg1, bi1, gg1 = call(
         same_kernel, batch_shapes(2), [], (), (own, *sent, *got, second), SAME_COST
     )
-    bg2, bi2 = call(
-        near_kernel, batch_shapes(1)[:2], [], (), (own, near_other, bg1), NEAR_COST
-    )
+    tile = jax.ShapeDtypeStruct((SUB, BLOCK), f32)
+    bg2, bi2 = call(near_kernel, (tile, tile), [], (), (own, near_other, bg1), NEAR_COST)
     body_shape = jax.ShapeDtypeStruct((3, blocks, BLOCK), f32)
     stiff_shape = jax.ShapeDtypeStruct((blocks, BLOCK), f32)
     garm_shape = jax.ShapeDtypeStruct((3, verts // BLOCK, BLOCK), f32)
     stiff = call(
         stiff_kernel, stiff_shape, [], (), (own, second_other, direct, bg1, bg2, bi1, bi2)
     )
-    work = (own, *sent, near_other, second_other, direct, bg1, bg2, bi1, bi2, gg1, index)
+    work = (own, *sent, near_other, second_other, direct, bg1, bi1, gg1, index)
     body_total, garm_total, stiff = call(
         before_kernel, (body_shape, garm_shape, stiff_shape), [], (), (*work, stiff)
     )

time: 17.5 us -> 17.5 us (level)
  no operation moved by 1% of the time
where the time goes in v17:
time: 17.5 us; the launch traced here: 17.4 us
  starting transfers between devices  10.8 us (62%)
  Pallas kernels  4.75 us (27%)
  waiting for transfers between devices  1.17 us (7%)
  between operations  0.69 us (4%)
    ppermute x3, starting transfers between devices, along_garm(): return lax.ppermute(value, 'garm', pairs)  5.67 us
    pallas_call x8, Pallas kernels, call(): pl.pallas_call(kernel, out_shape=out_shape, in_specs=specs, out_specs=jax...  3.74 us
    ppermute x1, starting transfers between devices, staged(): lax.ppermute(last_other, ('garm', 'body'), [(n, n ^ 3) for n in range(2 *...  2.61 us
    ppermute x2, starting transfers between devices, along_body(): return lax.ppermute(value, 'body', [(0, 1), (1, 0)])  2.42 us
    pallas_call x1, Pallas kernels, staged(): pl.pallas_call(stage_kernel, out_shape=[jax.ShapeDtypeStruct((garm_n, SUB...  1.01 us
    ppermute x2, waiting for transfers between devices, along_body(): return lax.ppermute(value, 'body', [(0, 1), (1, 0)])  0.99 us
  transfers between devices with their start and end apart: 7, of which 3 were waited for; matrix products, arithmetic and copies ran while one was open for 0% of the time, Pallas kernels for 15%

profile of v17, /device:TPU:0, one launch (start us, length us, event | category | flops | bytes accessed | tf_op | source)
XLA Modules:
  0.0 17.4 jit_solution(3512296084303976524)
XLA Ops:
  0.6 1.0 %shard_map.94 = (f32[4,8,128]{2,1,0:T(8,128)S(1)}, f32[11,8,128]{2,1,0:T(8,128)S(1)}, f32[11,8,128]{2,1,0:T(8,128)S(1)}, f32[13,8,128]{2,1,0:T(8,128)S(1)}, f32[...) custom-call(s32[4,8]{1,0:T(4,128)} %bitcast.18, s32[4,8]{1,0:T(4,128)} %bitcast.19, ...), custom_call_target="tpu_custom_call" | custom-call | tf_op jit(solution)/shard_map/pallas_call | solution.py:531
  1.6 4.1 %collective-permute-start = (f32[13,8,128]{2,1,0:T(8,128)S(1)}, f32[13,8,128]{2,1,0:T(8,128)S(1)}, u32[]{:S(2)}, u32[]{:S(2)}) collective-permute-start(f32[13,8,128]{2,1,0:T(8,128)S(1)} %get-tuple-element.25.sent1.refs_2_), channel_id=1, source_target_pairs={{0,8},{8,4},{4,12},{12,0},{1,9},{9,5},{5,13},{13,1},{2,10},{10,6},... | collective-permute-start | bytes 159752 | tf_op jit(solution)/shard_map/ppermute | solution.py:544
  5.7 1.1 %collective-permute-start.2 = (f32[13,8,128]{2,1,0:T(8,128)S(1)}, f32[13,8,128]{2,1,0:T(8,128)S(1)}, u32[]{:S(2)}, u32[]{:S(2)}) collective-permute-start(f32[13,8,128]{2,1,0:T(8,128)S(1)} %get-tuple-element.24.sent0.refs_1_), channel_id=1, source_target_pairs={{8,0},{4,8},{12,4},{0,12},{9,1},{5,9},{13,5},{1,13},{10,2},{6,10},... | collective-permute-start | bytes 159752 | tf_op jit(solution)/shard_map/ppermute | solution.py:544
  6.8 0.5 %collective-permute-start.5 = (f32[11,8,128]{2,1,0:T(8,128)S(1)}, f32[11,8,128]{2,1,0:T(8,128)S(1)}, u32[]{:S(2)}, u32[]{:S(2)}) collective-permute-start(f32[11,8,128]{2,1,0:T(8,128)S(1)} %get-tuple-element.28), channel_id=1, source_target_pairs={{0,4},{4,0},{8,12},{12,8},{1,5},{5,1},{9,13},{13,9},{2,6},{6,2},{1... | collective-permute-start | bytes 135176 | tf_op jit(solution)/shard_map/ppermute | solution.py:544
  7.3 2.6 %collective-permute-start.4 = (f32[11,8,128]{2,1,0:T(8,128)S(1)}, f32[11,8,128]{2,1,0:T(8,128)S(1)}, u32[]{:S(2)}, u32[]{:S(2)}) collective-permute-start(f32[11,8,128]{2,1,0:T(8,128)S(1)} %get-tuple-element.27), channel_id=1, source_target_pairs={{0,6},{2,4},{4,2},{6,0},{8,14},{10,12},{12,10},{14,8},{1,7},{3,5},... | collective-permute-start | bytes 135176 | tf_op jit(solution)/shard_map/ppermute | solution.py:555
  9.9 0.0 collective-permute-done.two_ref.got0
  9.9 0.8 %collective-permute-start.1 = (f32[21,8,128]{2,1,0:T(8,128)S(1)}, f32[21,8,128]{2,1,0:T(8,128)S(1)}, u32[]{:S(2)}, u32[]{:S(2)}) collective-permute-start(f32[21,8,128]{2,1,0:T(8,128)S(1)} %shard_map.95.after_ref), channel_id=1, source_target_pairs={{0,2},{2,0},{1,3},{3,1},{4,6},{6,4},{5,7},{7,5},{8,10},{10,8},{9,1... | collective-permute-start | bytes 258056 | tf_op jit(solution)/shard_map/ppermute | solution.py:547
  10.8 0.2 collective-permute-done.2.ref.got1
  10.9 1.6 %collective-permute-start.3 = (f32[11,8,128]{2,1,0:T(8,128)S(1)}, f32[11,8,128]{2,1,0:T(8,128)S(1)}, u32[]{:S(2)}, u32[]{:S(2)}) collective-permute-start(f32[11,8,128]{2,1,0:T(8,128)S(1)} %shard_map.96.after_ref), channel_id=1, source_target_pairs={{0,2},{2,0},{1,3},{3,1},{4,6},{6,4},{5,7},{7,5},{8,10},{10,8},{9,1... | collective-permute-start | bytes 135176 | tf_op jit(solution)/shard_map/ppermute | solution.py:547
  12.5 0.0 collective-permute-done.5.got2
  12.5 1.0 %shard_map.97 = (f32[16,512]{1,0:T(8,128)S(1)}, f32[16,128]{1,0:T(8,128)S(1)}, f32[16,384]{1,0:T(8,128)S(1)}) custom-call(f32[13,8,128]{2,1,0:T(8,128)S(1)} %get-tuple-element.23.one_ref.own_ref.refs_0_, f32[13,8,128]{2,1,0:T(8,128)S(1)} %get-tuple-element.24.sent0.refs_1_, f32[13,8,128]{2,1,0:T(8,128)S(1)} %get-tuple-element.25.sent1.refs_2_, ...), custom_call_target="tpu_custom_call" | custom-call | flops 40000000000 | bytes 1000 | tf_op jit(solution)/shard_map/pallas_call | solution.py:245
  13.6 0.9 %collective-permute-done.1.near_ref.refs_4_ = f32[21,8,128]{2,1,0:T(8,128)S(1)} collective-permute-done((f32[21,8,128]{2,1,0:T(8,128)S(1)}, f32[21,8,128]{2,1,0:T(8,128)S(1)}, u32[]{:S(2)}, u32[]{:S(2)}) %collective-permute-start.1) | collective-permute-done | bytes 86048 | tf_op jit(solution)/shard_map/ppermute | solution.py:547
  14.5 0.4 %shard_map.98 = (f32[8,128]{1,0:T(8,128)S(1)}, f32[8,128]{1,0:T(8,128)S(1)}) custom-call(f32[13,8,128]{2,1,0:T(8,128)S(1)} %get-tuple-element.23.one_ref.own_ref.refs_0_, f32[21,8,128]{2,1,0:T(8,128)S(1)} %collective-permute-done.1.near_ref.refs_4_, f32[16,512]{1,0:T(8,128)S(1)} %get-tuple-element.29.after_ref.bg1.refs_7_), custom_call_target="tpu_custom_call" | custom-call | flops 1000000000 | bytes 1000 | tf_op jit(solution)/shard_map/pallas_call | solution.py:245
  14.9 0.0 collective-permute-done.4.two_ref.refs_6_
  14.9 0.1 collective-permute-done.3.one_ref.refs_5_
  15.0 0.4 %shard_map.99.refs_11_ = f32[16,128]{1,0:T(8,128)S(1)} custom-call(f32[13,8,128]{2,1,0:T(8,128)S(1)} %get-tuple-element.23.one_ref.own_ref.refs_0_, f32[11,8,128]{2,1,0:T(8,128)S(1)} %collective-permute-done.3.one_ref.refs_5_, f32[11,8,128]{2,1,0:T(8,128)S(1)} %collective-permute-done.4.two_ref.refs_6_, ...), custom_call_target="tpu_custom_call" | custom-call | tf_op jit(solution)/shard_map/pallas_call | solution.py:245
  15.4 0.1 collective-permute-start.6
  15.5 1.2 %shard_map.101 = (f32[3,16,128]{2,1,0:T(8,128)S(1)}, f32[3,32,128]{2,1,0:T(8,128)S(1)}) custom-call(f32[13,8,128]{2,1,0:T(8,128)S(1)} %get-tuple-element.23.one_ref.own_ref.refs_0_, f32[13,8,128]{2,1,0:T(8,128)S(1)} %get-tuple-element.24.sent0.refs_1_, f32[13,8,128]{2,1,0:T(8,128)S(1)} %get-tuple-element.25.sent1.refs_2_, ...), custom_call_target="tpu_custom_call" | custom-call | tf_op jit(solution)/shard_map/pallas_call | solution.py:245
  16.7 0.0 collective-permute-done.6.other_ref
  16.7 0.6 %shard_map.102 = (f32[3,32,128]{2,1,0:T(8,128)}, f32[3,16,128]{2,1,0:T(8,128)}, f32[16,128]{1,0:T(8,128)}) custom-call(f32[3,32,128]{2,1,0:T(8,128)S(1)} %get-tuple-element.37.garm_ref, f32[3,16,128]{2,1,0:T(8,128)S(1)} %get-tuple-element.38.body_ref, f32[16,128]{1,0:T(8,128)S(1)} %get-tuple-element.39.mine_ref, f32[16,128]{1,0:T(8,128)S(1)} %collective-permute-done.6.other_ref), custom_call_target="tpu_custom_call" | custom-call | tf_op jit(solution)/shard_map/pallas_call | solution.py:245
  (3 shorter events, 0.0 us)
Async XLA Ops:
  1.6 8.3 %collective-permute-start = (f32[13,8,128]{2,1,0:T(8,128)S(1)}, f32[13,8,128]{2,1,0:T(8,128)S(1)}, u32[]{:S(2)}, u32[]{:S(2)}) collective-permute-start(f32[13,8,128]{2,1,0:T(8,128)S(1)} %get-tuple-element.25.sent1.refs_2_), channel_id=1, source_target_pairs={{0,8},{8,4},{4,12},{12,0},{1,9},{9,5},{5,13},{13,1},{2,10},{10,6},... | collective-permute-start | bytes 159752 | tf_op jit(solution)/shard_map/ppermute | solution.py:544
  5.7 5.2 %collective-permute-start.2 = (f32[13,8,128]{2,1,0:T(8,128)S(1)}, f32[13,8,128]{2,1,0:T(8,128)S(1)}, u32[]{:S(2)}, u32[]{:S(2)}) collective-permute-start(f32[13,8,128]{2,1,0:T(8,128)S(1)} %get-tuple-element.24.sent0.refs_1_), channel_id=1, source_target_pairs={{8,0},{4,8},{12,4},{0,12},{9,1},{5,9},{13,5},{1,13},{10,2},{6,10},... | collective-permute-start | bytes 159752 | tf_op jit(solution)/shard_map/ppermute | solution.py:544
  6.8 5.7 %collective-permute-start.5 = (f32[11,8,128]{2,1,0:T(8,128)S(1)}, f32[11,8,128]{2,1,0:T(8,128)S(1)}, u32[]{:S(2)}, u32[]{:S(2)}) collective-permute-start(f32[11,8,128]{2,1,0:T(8,128)S(1)} %get-tuple-element.28), channel_id=1, source_target_pairs={{0,4},{4,0},{8,12},{12,8},{1,5},{5,1},{9,13},{13,9},{2,6},{6,2},{1... | collective-permute-start | bytes 135176 | tf_op jit(solution)/shard_map/ppermute | solution.py:544
  7.3 7.6 %collective-permute-start.4 = (f32[11,8,128]{2,1,0:T(8,128)S(1)}, f32[11,8,128]{2,1,0:T(8,128)S(1)}, u32[]{:S(2)}, u32[]{:S(2)}) collective-permute-start(f32[11,8,128]{2,1,0:T(8,128)S(1)} %get-tuple-element.27), channel_id=1, source_target_pairs={{0,6},{2,4},{4,2},{6,0},{8,14},{10,12},{12,10},{14,8},{1,7},{3,5},... | collective-permute-start | bytes 135176 | tf_op jit(solution)/shard_map/ppermute | solution.py:555
  9.9 4.6 %collective-permute-start.1 = (f32[21,8,128]{2,1,0:T(8,128)S(1)}, f32[21,8,128]{2,1,0:T(8,128)S(1)}, u32[]{:S(2)}, u32[]{:S(2)}) collective-permute-start(f32[21,8,128]{2,1,0:T(8,128)S(1)} %shard_map.95.after_ref), channel_id=1, source_target_pairs={{0,2},{2,0},{1,3},{3,1},{4,6},{6,4},{5,7},{7,5},{8,10},{10,8},{9,1... | collective-permute-start | bytes 258056 | tf_op jit(solution)/shard_map/ppermute | solution.py:547
  10.9 4.1 %collective-permute-start.3 = (f32[11,8,128]{2,1,0:T(8,128)S(1)}, f32[11,8,128]{2,1,0:T(8,128)S(1)}, u32[]{:S(2)}, u32[]{:S(2)}) collective-permute-start(f32[11,8,128]{2,1,0:T(8,128)S(1)} %shard_map.96.after_ref), channel_id=1, source_target_pairs={{0,2},{2,0},{1,3},{3,1},{4,6},{6,4},{5,7},{7,5},{8,10},{10,8},{9,1... | collective-permute-start | bytes 135176 | tf_op jit(solution)/shard_map/ppermute | solution.py:547
  15.4 1.3 %collective-permute-start.6 = (f32[16,128]{1,0:T(8,128)S(1)}, f32[16,128]{1,0:T(8,128)S(1)}, u32[]{:S(2)}, u32[]{:S(2)}) collective-permute-start(f32[16,128]{1,0:T(8,128)S(1)} %get-tuple-element.39.mine_ref), channel_id=1, source_target_pairs={{0,1},{1,0},{2,3},{3,2},{4,5},{5,4},{6,7},{7,6},{8,9},{9,8},{10,11... | collective-permute-start | bytes 24584 | tf_op jit(solution)/shard_map/ppermute | solution.py:581

commit v18 on v17

--- a/solution.py
+++ b/solution.py
@@ -380,25 +380,25 @@
     return [halves(x, y) for x, y in zip(top, bottom)]
 
 
-def near_kernel(own_ref, near_ref, after_ref, stiff_ref, bindex_ref):
-    del after_ref
+def add_rows(total, index, rows):
+    block = lax.broadcasted_iota(jnp.int32, total.shape, 0).astype(f32)
+    for n in range(SUB):
+        total = total + jnp.where(block == index[n : n + 1], rows[n : n + 1], 0.0)
+    return total
+
+
+def near_kernel(own_ref, near_ref, bg1, bi1, out_ref):
     tiles = near_tiles(own_ref, near_ref)
     own = message_table(own_ref, (own_ref.shape[0] - 5) // 4)
-    stiff_ref[...] = amplitude * weigh(*body_work(tiles, own))
-    bindex_ref[...] = tiles[4]
-
-
-def stiff_kernel(own_ref, one_ref, two_ref, bg1, bg2, bi1, bi2, out_ref):
+    total = scatter(bi1[...], bg1[:, 3 * BLOCK :], out_ref.shape[0])
+    out_ref[...] = add_rows(total, tiles[4], amplitude * weigh(*body_work(tiles, own)))
+
+
+def stiff_kernel(own_ref, one_ref, two_ref, total_ref, out_ref):
     tiles = late_tiles(own_ref, one_ref, two_ref)
     own = message_table(own_ref, (own_ref.shape[0] - 5) // 4)
-    index = jnp.concatenate([bi1[...], bi2[...]], axis=0)
-    grads = jnp.concatenate([bg1[:, 3 * BLOCK :], bg2[...]], axis=0)
-    total = scatter(index, grads, out_ref.shape[0])
     last = amplitude * weigh(*body_work(tiles, own))
-    block = lax.broadcasted_iota(jnp.int32, total.shape, 0).astype(f32)
-    for n in range(SUB):
-        total = total + jnp.where(block == tiles[4][n : n + 1], last[n : n + 1], 0.0)
-    out_ref[...] = total
+    out_ref[...] = add_rows(total_ref[...], tiles[4], last)
 
 
 def late_sums(
@@ -566,14 +566,11 @@
     bg1, bi1, gg1 = call(
         same_kernel, batch_shapes(2), [], (), (own, *sent, *got, second), SAME_COST
     )
-    tile = jax.ShapeDtypeStruct((SUB, BLOCK), f32)
-    bg2, bi2 = call(near_kernel, (tile, tile), [], (), (own, near_other, bg1), NEAR_COST)
     body_shape = jax.ShapeDtypeStruct((3, blocks, BLOCK), f32)
     stiff_shape = jax.ShapeDtypeStruct((blocks, BLOCK), f32)
     garm_shape = jax.ShapeDtypeStruct((3, verts // BLOCK, BLOCK), f32)
-    stiff = call(
-        stiff_kernel, stiff_shape, [], (), (own, second_other, direct, bg1, bg2, bi1, bi2)
-    )
+    so_far = call(near_kernel, stiff_shape, [], (), (own, near_other, bg1, bi1), NEAR_COST)
+    stiff = call(stiff_kernel, stiff_shape, [], (), (own, second_other, direct, so_far))
     work = (own, *sent, near_other, second_other, direct, bg1, bi1, gg1, index)
     body_total, garm_total, stiff = call(
         before_kernel, (body_shape, garm_shape, stiff_shape), [], (), (*work, stiff)

time: 17.5 us -> 17.5 us (level)
  no operation moved by 1% of the time
where the time goes in v18:
time: 17.5 us; the launch traced here: 17.4 us
  starting transfers between devices  10.8 us (62%)
  Pallas kernels  4.76 us (27%)
  waiting for transfers between devices  1.15 us (7%)
  between operations  0.68 us (4%)
    ppermute x3, starting transfers between devices, along_garm(): return lax.ppermute(value, 'garm', pairs)  5.67 us
    pallas_call x8, Pallas kernels, call(): pl.pallas_call(kernel, out_shape=out_shape, in_specs=specs, out_specs=jax...  3.76 us
    ppermute x1, starting transfers between devices, staged(): lax.ppermute(last_other, ('garm', 'body'), [(n, n ^ 3) for n in range(2 *...  2.61 us
    ppermute x2, starting transfers between devices, along_body(): return lax.ppermute(value, 'body', [(0, 1), (1, 0)])  2.42 us
    pallas_call x1, Pallas kernels, staged(): pl.pallas_call(stage_kernel, out_shape=[jax.ShapeDtypeStruct((garm_n, SUB...  1.01 us
    ppermute x2, waiting for transfers between devices, along_body(): return lax.ppermute(value, 'body', [(0, 1), (1, 0)])  0.98 us
  transfers between devices with their start and end apart: 7, of which 3 were waited for; matrix products, arithmetic and copies ran while one was open for 0% of the time, Pallas kernels for 15%

profile of v18, /device:TPU:0, one launch (start us, length us, event | category | flops | bytes accessed | tf_op | source)
XLA Modules:
  0.0 17.4 jit_solution(8735121601699771815)
XLA Ops:
  0.6 1.0 %shard_map.94 = (f32[4,8,128]{2,1,0:T(8,128)S(1)}, f32[11,8,128]{2,1,0:T(8,128)S(1)}, f32[11,8,128]{2,1,0:T(8,128)S(1)}, f32[13,8,128]{2,1,0:T(8,128)S(1)}, f32[...) custom-call(s32[4,8]{1,0:T(4,128)} %bitcast.18, s32[4,8]{1,0:T(4,128)} %bitcast.19, ...), custom_call_target="tpu_custom_call" | custom-call | tf_op jit(solution)/shard_map/pallas_call | solution.py:531
  1.6 4.1 %collective-permute-start = (f32[13,8,128]{2,1,0:T(8,128)S(1)}, f32[13,8,128]{2,1,0:T(8,128)S(1)}, u32[]{:S(2)}, u32[]{:S(2)}) collective-permute-start(f32[13,8,128]{2,1,0:T(8,128)S(1)} %get-tuple-element.23.sent1.refs_2_), channel_id=1, source_target_pairs={{0,8},{8,4},{4,12},{12,0},{1,9},{9,5},{5,13},{13,1},{2,10},{10,6},... | collective-permute-start | bytes 159752 | tf_op jit(solution)/shard_map/ppermute | solution.py:544
  5.7 1.1 %collective-permute-start.2 = (f32[13,8,128]{2,1,0:T(8,128)S(1)}, f32[13,8,128]{2,1,0:T(8,128)S(1)}, u32[]{:S(2)}, u32[]{:S(2)}) collective-permute-start(f32[13,8,128]{2,1,0:T(8,128)S(1)} %get-tuple-element.22.sent0.refs_1_), channel_id=1, source_target_pairs={{8,0},{4,8},{12,4},{0,12},{9,1},{5,9},{13,5},{1,13},{10,2},{6,10},... | collective-permute-start | bytes 159752 | tf_op jit(solution)/shard_map/ppermute | solution.py:544
  6.8 0.5 %collective-permute-start.5 = (f32[11,8,128]{2,1,0:T(8,128)S(1)}, f32[11,8,128]{2,1,0:T(8,128)S(1)}, u32[]{:S(2)}, u32[]{:S(2)}) collective-permute-start(f32[11,8,128]{2,1,0:T(8,128)S(1)} %get-tuple-element.26), channel_id=1, source_target_pairs={{0,4},{4,0},{8,12},{12,8},{1,5},{5,1},{9,13},{13,9},{2,6},{6,2},{1... | collective-permute-start | bytes 135176 | tf_op jit(solution)/shard_map/ppermute | solution.py:544
  7.3 2.6 %collective-permute-start.4 = (f32[11,8,128]{2,1,0:T(8,128)S(1)}, f32[11,8,128]{2,1,0:T(8,128)S(1)}, u32[]{:S(2)}, u32[]{:S(2)}) collective-permute-start(f32[11,8,128]{2,1,0:T(8,128)S(1)} %get-tuple-element.25), channel_id=1, source_target_pairs={{0,6},{2,4},{4,2},{6,0},{8,14},{10,12},{12,10},{14,8},{1,7},{3,5},... | collective-permute-start | bytes 135176 | tf_op jit(solution)/shard_map/ppermute | solution.py:555
  9.9 0.0 collective-permute-done.two_ref.got0
  9.9 0.8 %collective-permute-start.1 = (f32[21,8,128]{2,1,0:T(8,128)S(1)}, f32[21,8,128]{2,1,0:T(8,128)S(1)}, u32[]{:S(2)}, u32[]{:S(2)}) collective-permute-start(f32[21,8,128]{2,1,0:T(8,128)S(1)} %shard_map.95.after_ref), channel_id=1, source_target_pairs={{0,2},{2,0},{1,3},{3,1},{4,6},{6,4},{5,7},{7,5},{8,10},{10,8},{9,1... | collective-permute-start | bytes 258056 | tf_op jit(solution)/shard_map/ppermute | solution.py:547
  10.8 0.2 collective-permute-done.2.ref.got1
  10.9 1.6 %collective-permute-start.3 = (f32[11,8,128]{2,1,0:T(8,128)S(1)}, f32[11,8,128]{2,1,0:T(8,128)S(1)}, u32[]{:S(2)}, u32[]{:S(2)}) collective-permute-start(f32[11,8,128]{2,1,0:T(8,128)S(1)} %shard_map.96.after_ref), channel_id=1, source_target_pairs={{0,2},{2,0},{1,3},{3,1},{4,6},{6,4},{5,7},{7,5},{8,10},{10,8},{9,1... | collective-permute-start | bytes 135176 | tf_op jit(solution)/shard_map/ppermute | solution.py:547
  12.5 0.0 collective-permute-done.5.got2
  12.5 1.0 %shard_map.97 = (f32[16,512]{1,0:T(8,128)S(1)}, f32[16,128]{1,0:T(8,128)S(1)}, f32[16,384]{1,0:T(8,128)S(1)}) custom-call(f32[13,8,128]{2,1,0:T(8,128)S(1)} %get-tuple-element.21.one_ref.own_ref.refs_0_, f32[13,8,128]{2,1,0:T(8,128)S(1)} %get-tuple-element.22.sent0.refs_1_, f32[13,8,128]{2,1,0:T(8,128)S(1)} %get-tuple-element.23.sent1.refs_2_, ...), custom_call_target="tpu_custom_call" | custom-call | flops 40000000000 | bytes 1000 | tf_op jit(solution)/shard_map/pallas_call | solution.py:245
  13.6 0.9 %collective-permute-done.1.near_ref.refs_4_ = f32[21,8,128]{2,1,0:T(8,128)S(1)} collective-permute-done((f32[21,8,128]{2,1,0:T(8,128)S(1)}, f32[21,8,128]{2,1,0:T(8,128)S(1)}, u32[]{:S(2)}, u32[]{:S(2)}) %collective-permute-start.1) | collective-permute-done | bytes 86048 | tf_op jit(solution)/shard_map/ppermute | solution.py:547
  14.5 0.4 %shard_map.98.total_ref = f32[16,128]{1,0:T(8,128)S(1)} custom-call(f32[13,8,128]{2,1,0:T(8,128)S(1)} %get-tuple-element.21.one_ref.own_ref.refs_0_, f32[21,8,128]{2,1,0:T(8,128)S(1)} %collective-permute-done.1.near_ref.refs_4_, f32[16,512]{1,0:T(8,128)S(1)} %get-tuple-element.27.bg1.refs_7_, f32[16,128]{1,0:T(8,128)S(1)} %get-tuple-element.28.bi1.refs_8_), custom_call_target="tpu_custom_call" | custom-call | flops 1000000000 | bytes 1000 | tf_op jit(solution)/shard_map/pallas_call | solution.py:245
  14.9 0.0 collective-permute-done.4.two_ref.refs_6_
  14.9 0.1 collective-permute-done.3.one_ref.refs_5_
  15.0 0.4 %shard_map.99.refs_11_ = f32[16,128]{1,0:T(8,128)S(1)} custom-call(f32[13,8,128]{2,1,0:T(8,128)S(1)} %get-tuple-element.21.one_ref.own_ref.refs_0_, f32[11,8,128]{2,1,0:T(8,128)S(1)} %collective-permute-done.3.one_ref.refs_5_, f32[11,8,128]{2,1,0:T(8,128)S(1)} %collective-permute-done.4.two_ref.refs_6_, f32[16,128]{1,0:T(8,128)S(1)} %shard_map.98.total_ref), custom_call_target="tpu_custom_call" | custom-call | tf_op jit(solution)/shard_map/pallas_call | solution.py:245
  15.4 0.1 collective-permute-start.6
  15.5 1.2 %shard_map.101 = (f32[3,16,128]{2,1,0:T(8,128)S(1)}, f32[3,32,128]{2,1,0:T(8,128)S(1)}) custom-call(f32[13,8,128]{2,1,0:T(8,128)S(1)} %get-tuple-element.21.one_ref.own_ref.refs_0_, f32[13,8,128]{2,1,0:T(8,128)S(1)} %get-tuple-element.22.sent0.refs_1_, f32[13,8,128]{2,1,0:T(8,128)S(1)} %get-tuple-element.23.sent1.refs_2_, ...), custom_call_target="tpu_custom_call" | custom-call | tf_op jit(solution)/shard_map/pallas_call | solution.py:245
  16.7 0.0 collective-permute-done.6.other_ref
  16.7 0.6 %shard_map.102 = (f32[3,32,128]{2,1,0:T(8,128)}, f32[3,16,128]{2,1,0:T(8,128)}, f32[16,128]{1,0:T(8,128)}) custom-call(f32[3,32,128]{2,1,0:T(8,128)S(1)} %get-tuple-element.33.garm_ref, f32[3,16,128]{2,1,0:T(8,128)S(1)} %get-tuple-element.34.body_ref, f32[16,128]{1,0:T(8,128)S(1)} %get-tuple-element.35.mine_ref, f32[16,128]{1,0:T(8,128)S(1)} %collective-permute-done.6.other_ref), custom_call_target="tpu_custom_call" | custom-call | tf_op jit(solution)/shard_map/pallas_call | solution.py:245
  (3 shorter events, 0.0 us)
Async XLA Ops:
  1.6 8.3 %collective-permute-start = (f32[13,8,128]{2,1,0:T(8,128)S(1)}, f32[13,8,128]{2,1,0:T(8,128)S(1)}, u32[]{:S(2)}, u32[]{:S(2)}) collective-permute-start(f32[13,8,128]{2,1,0:T(8,128)S(1)} %get-tuple-element.23.sent1.refs_2_), channel_id=1, source_target_pairs={{0,8},{8,4},{4,12},{12,0},{1,9},{9,5},{5,13},{13,1},{2,10},{10,6},... | collective-permute-start | bytes 159752 | tf_op jit(solution)/shard_map/ppermute | solution.py:544
  5.7 5.2 %collective-permute-start.2 = (f32[13,8,128]{2,1,0:T(8,128)S(1)}, f32[13,8,128]{2,1,0:T(8,128)S(1)}, u32[]{:S(2)}, u32[]{:S(2)}) collective-permute-start(f32[13,8,128]{2,1,0:T(8,128)S(1)} %get-tuple-element.22.sent0.refs_1_), channel_id=1, source_target_pairs={{8,0},{4,8},{12,4},{0,12},{9,1},{5,9},{13,5},{1,13},{10,2},{6,10},... | collective-permute-start | bytes 159752 | tf_op jit(solution)/shard_map/ppermute | solution.py:544
  6.8 5.7 %collective-permute-start.5 = (f32[11,8,128]{2,1,0:T(8,128)S(1)}, f32[11,8,128]{2,1,0:T(8,128)S(1)}, u32[]{:S(2)}, u32[]{:S(2)}) collective-permute-start(f32[11,8,128]{2,1,0:T(8,128)S(1)} %get-tuple-element.26), channel_id=1, source_target_pairs={{0,4},{4,0},{8,12},{12,8},{1,5},{5,1},{9,13},{13,9},{2,6},{6,2},{1... | collective-permute-start | bytes 135176 | tf_op jit(solution)/shard_map/ppermute | solution.py:544
  7.3 7.6 %collective-permute-start.4 = (f32[11,8,128]{2,1,0:T(8,128)S(1)}, f32[11,8,128]{2,1,0:T(8,128)S(1)}, u32[]{:S(2)}, u32[]{:S(2)}) collective-permute-start(f32[11,8,128]{2,1,0:T(8,128)S(1)} %get-tuple-element.25), channel_id=1, source_target_pairs={{0,6},{2,4},{4,2},{6,0},{8,14},{10,12},{12,10},{14,8},{1,7},{3,5},... | collective-permute-start | bytes 135176 | tf_op jit(solution)/shard_map/ppermute | solution.py:555
  9.9 4.6 %collective-permute-start.1 = (f32[21,8,128]{2,1,0:T(8,128)S(1)}, f32[21,8,128]{2,1,0:T(8,128)S(1)}, u32[]{:S(2)}, u32[]{:S(2)}) collective-permute-start(f32[21,8,128]{2,1,0:T(8,128)S(1)} %shard_map.95.after_ref), channel_id=1, source_target_pairs={{0,2},{2,0},{1,3},{3,1},{4,6},{6,4},{5,7},{7,5},{8,10},{10,8},{9,1... | collective-permute-start | bytes 258056 | tf_op jit(solution)/shard_map/ppermute | solution.py:547
  10.9 4.1 %collective-permute-start.3 = (f32[11,8,128]{2,1,0:T(8,128)S(1)}, f32[11,8,128]{2,1,0:T(8,128)S(1)}, u32[]{:S(2)}, u32[]{:S(2)}) collective-permute-start(f32[11,8,128]{2,1,0:T(8,128)S(1)} %shard_map.96.after_ref), channel_id=1, source_target_pairs={{0,2},{2,0},{1,3},{3,1},{4,6},{6,4},{5,7},{7,5},{8,10},{10,8},{9,1... | collective-permute-start | bytes 135176 | tf_op jit(solution)/shard_map/ppermute | solution.py:547
  15.4 1.3 %collective-permute-start.6 = (f32[16,128]{1,0:T(8,128)S(1)}, f32[16,128]{1,0:T(8,128)S(1)}, u32[]{:S(2)}, u32[]{:S(2)}) collective-permute-start(f32[16,128]{1,0:T(8,128)S(1)} %get-tuple-element.35.mine_ref), channel_id=1, source_target_pairs={{0,1},{1,0},{2,3},{3,2},{4,5},{5,4},{6,7},{7,6},{8,9},{9,8},{10,11... | collective-permute-start | bytes 24584 | tf_op jit(solution)/shard_map/ppermute | solution.py:578

commit v19 on v17

--- a/solution.py
+++ b/solution.py
@@ -267,7 +267,7 @@
     onehot = onehot.astype(f32)[:, : 3 * blocks].astype(bf16)
     stack = jnp.concatenate(pieces(table, 3), axis=0).astype(bf16)
     rows = jnp.dot(onehot, stack, preferred_element_type=f32)
-    return [rows[:, c * BLOCK : (c + 1) * BLOCK] for c in range(4)]
+    return [rows[:, c * BLOCK : (c + 1) * BLOCK] for c in range(table.shape[1] // BLOCK)]
 
 
 def halves(top, bottom):
@@ -384,7 +384,7 @@
     del after_ref
     tiles = near_tiles(own_ref, near_ref)
     own = message_table(own_ref, (own_ref.shape[0] - 5) // 4)
-    stiff_ref[...] = amplitude * weigh(*body_work(tiles, own))
+    stiff_ref[...] = amplitude * weigh(*body_work(tiles, own[:, : 3 * BLOCK]))
     bindex_ref[...] = tiles[4]
 
 
@@ -394,7 +394,7 @@
     index = jnp.concatenate([bi1[...], bi2[...]], axis=0)
     grads = jnp.concatenate([bg1[:, 3 * BLOCK :], bg2[...]], axis=0)
     total = scatter(index, grads, out_ref.shape[0])
-    last = amplitude * weigh(*body_work(tiles, own))
+    last = amplitude * weigh(*body_work(tiles, own[:, : 3 * BLOCK]))
     block = lax.broadcasted_iota(jnp.int32, total.shape, 0).astype(f32)
     for n in range(SUB):
         total = total + jnp.where(block == tiles[4][n : n + 1], last[n : n + 1], 0.0)

time: 17.5 us -> 17.5 us (level)
  no operation moved by 1% of the time
where the time goes in v19:
time: 17.5 us; the launch traced here: 17.4 us
  starting transfers between devices  10.8 us (62%)
  Pallas kernels  4.75 us (27%)
  waiting for transfers between devices  1.17 us (7%)
  between operations  0.69 us (4%)
    ppermute x3, starting transfers between devices, along_garm(): return lax.ppermute(value, 'garm', pairs)  5.67 us
    pallas_call x8, Pallas kernels, call(): pl.pallas_call(kernel, out_shape=out_shape, in_specs=specs, out_specs=jax...  3.74 us
    ppermute x1, starting transfers between devices, staged(): lax.ppermute(last_other, ('garm', 'body'), [(n, n ^ 3) for n in range(2 *...  2.61 us
    ppermute x2, starting transfers between devices, along_body(): return lax.ppermute(value, 'body', [(0, 1), (1, 0)])  2.42 us
    pallas_call x1, Pallas kernels, staged(): pl.pallas_call(stage_kernel, out_shape=[jax.ShapeDtypeStruct((garm_n, SUB...  1.01 us
    ppermute x2, waiting for transfers between devices, along_body(): return lax.ppermute(value, 'body', [(0, 1), (1, 0)])  0.99 us
  transfers between devices with their start and end apart: 7, of which 3 were waited for; matrix products, arithmetic and copies ran while one was open for 0% of the time, Pallas kernels for 15%

profile of v19, /device:TPU:0, one launch (start us, length us, event | category | flops | bytes accessed | tf_op | source)
XLA Modules:
  0.0 17.4 jit_solution(33663175803986371)
XLA Ops:
  0.6 1.0 %shard_map.94 = (f32[4,8,128]{2,1,0:T(8,128)S(1)}, f32[11,8,128]{2,1,0:T(8,128)S(1)}, f32[11,8,128]{2,1,0:T(8,128)S(1)}, f32[13,8,128]{2,1,0:T(8,128)S(1)}, f32[...) custom-call(s32[4,8]{1,0:T(4,128)} %bitcast.18, s32[4,8]{1,0:T(4,128)} %bitcast.19, ...), custom_call_target="tpu_custom_call" | custom-call | tf_op jit(solution)/shard_map/pallas_call | solution.py:531
  1.6 4.1 %collective-permute-start = (f32[13,8,128]{2,1,0:T(8,128)S(1)}, f32[13,8,128]{2,1,0:T(8,128)S(1)}, u32[]{:S(2)}, u32[]{:S(2)}) collective-permute-start(f32[13,8,128]{2,1,0:T(8,128)S(1)} %get-tuple-element.25.sent1.refs_2_), channel_id=1, source_target_pairs={{0,8},{8,4},{4,12},{12,0},{1,9},{9,5},{5,13},{13,1},{2,10},{10,6},... | collective-permute-start | bytes 159752 | tf_op jit(solution)/shard_map/ppermute | solution.py:544
  5.7 1.1 %collective-permute-start.2 = (f32[13,8,128]{2,1,0:T(8,128)S(1)}, f32[13,8,128]{2,1,0:T(8,128)S(1)}, u32[]{:S(2)}, u32[]{:S(2)}) collective-permute-start(f32[13,8,128]{2,1,0:T(8,128)S(1)} %get-tuple-element.24.sent0.refs_1_), channel_id=1, source_target_pairs={{8,0},{4,8},{12,4},{0,12},{9,1},{5,9},{13,5},{1,13},{10,2},{6,10},... | collective-permute-start | bytes 159752 | tf_op jit(solution)/shard_map/ppermute | solution.py:544
  6.8 0.5 %collective-permute-start.5 = (f32[11,8,128]{2,1,0:T(8,128)S(1)}, f32[11,8,128]{2,1,0:T(8,128)S(1)}, u32[]{:S(2)}, u32[]{:S(2)}) collective-permute-start(f32[11,8,128]{2,1,0:T(8,128)S(1)} %get-tuple-element.28), channel_id=1, source_target_pairs={{0,4},{4,0},{8,12},{12,8},{1,5},{5,1},{9,13},{13,9},{2,6},{6,2},{1... | collective-permute-start | bytes 135176 | tf_op jit(solution)/shard_map/ppermute | solution.py:544
  7.3 2.6 %collective-permute-start.4 = (f32[11,8,128]{2,1,0:T(8,128)S(1)}, f32[11,8,128]{2,1,0:T(8,128)S(1)}, u32[]{:S(2)}, u32[]{:S(2)}) collective-permute-start(f32[11,8,128]{2,1,0:T(8,128)S(1)} %get-tuple-element.27), channel_id=1, source_target_pairs={{0,6},{2,4},{4,2},{6,0},{8,14},{10,12},{12,10},{14,8},{1,7},{3,5},... | collective-permute-start | bytes 135176 | tf_op jit(solution)/shard_map/ppermute | solution.py:555
  9.9 0.0 collective-permute-done.two_ref.got0
  9.9 0.8 %collective-permute-start.1 = (f32[21,8,128]{2,1,0:T(8,128)S(1)}, f32[21,8,128]{2,1,0:T(8,128)S(1)}, u32[]{:S(2)}, u32[]{:S(2)}) collective-permute-start(f32[21,8,128]{2,1,0:T(8,128)S(1)} %shard_map.95.after_ref), channel_id=1, source_target_pairs={{0,2},{2,0},{1,3},{3,1},{4,6},{6,4},{5,7},{7,5},{8,10},{10,8},{9,1... | collective-permute-start | bytes 258056 | tf_op jit(solution)/shard_map/ppermute | solution.py:547
  10.8 0.2 collective-permute-done.2.ref.got1
  10.9 1.6 %collective-permute-start.3 = (f32[11,8,128]{2,1,0:T(8,128)S(1)}, f32[11,8,128]{2,1,0:T(8,128)S(1)}, u32[]{:S(2)}, u32[]{:S(2)}) collective-permute-start(f32[11,8,128]{2,1,0:T(8,128)S(1)} %shard_map.96.after_ref), channel_id=1, source_target_pairs={{0,2},{2,0},{1,3},{3,1},{4,6},{6,4},{5,7},{7,5},{8,10},{10,8},{9,1... | collective-permute-start | bytes 135176 | tf_op jit(solution)/shard_map/ppermute | solution.py:547
  12.5 0.0 collective-permute-done.5.got2
  12.5 1.0 %shard_map.97 = (f32[16,512]{1,0:T(8,128)S(1)}, f32[16,128]{1,0:T(8,128)S(1)}, f32[16,384]{1,0:T(8,128)S(1)}) custom-call(f32[13,8,128]{2,1,0:T(8,128)S(1)} %get-tuple-element.23.one_ref.own_ref.refs_0_, f32[13,8,128]{2,1,0:T(8,128)S(1)} %get-tuple-element.24.sent0.refs_1_, f32[13,8,128]{2,1,0:T(8,128)S(1)} %get-tuple-element.25.sent1.refs_2_, ...), custom_call_target="tpu_custom_call" | custom-call | flops 40000000000 | bytes 1000 | tf_op jit(solution)/shard_map/pallas_call | solution.py:245
  13.6 0.9 %collective-permute-done.1.near_ref.refs_4_ = f32[21,8,128]{2,1,0:T(8,128)S(1)} collective-permute-done((f32[21,8,128]{2,1,0:T(8,128)S(1)}, f32[21,8,128]{2,1,0:T(8,128)S(1)}, u32[]{:S(2)}, u32[]{:S(2)}) %collective-permute-start.1) | collective-permute-done | bytes 86048 | tf_op jit(solution)/shard_map/ppermute | solution.py:547
  14.5 0.4 %shard_map.98 = (f32[8,128]{1,0:T(8,128)S(1)}, f32[8,128]{1,0:T(8,128)S(1)}) custom-call(f32[13,8,128]{2,1,0:T(8,128)S(1)} %get-tuple-element.23.one_ref.own_ref.refs_0_, f32[21,8,128]{2,1,0:T(8,128)S(1)} %collective-permute-done.1.near_ref.refs_4_, f32[16,512]{1,0:T(8,128)S(1)} %get-tuple-element.29.after_ref.bg1.refs_7_), custom_call_target="tpu_custom_call" | custom-call | flops 1000000000 | bytes 1000 | tf_op jit(solution)/shard_map/pallas_call | solution.py:245
  14.9 0.0 collective-permute-done.4.two_ref.refs_6_
  14.9 0.1 collective-permute-done.3.one_ref.refs_5_
  15.0 0.4 %shard_map.99.refs_11_ = f32[16,128]{1,0:T(8,128)S(1)} custom-call(f32[13,8,128]{2,1,0:T(8,128)S(1)} %get-tuple-element.23.one_ref.own_ref.refs_0_, f32[11,8,128]{2,1,0:T(8,128)S(1)} %collective-permute-done.3.one_ref.refs_5_, f32[11,8,128]{2,1,0:T(8,128)S(1)} %collective-permute-done.4.two_ref.refs_6_, ...), custom_call_target="tpu_custom_call" | custom-call | tf_op jit(solution)/shard_map/pallas_call | solution.py:245
  15.4 0.1 collective-permute-start.6
  15.5 1.2 %shard_map.101 = (f32[3,16,128]{2,1,0:T(8,128)S(1)}, f32[3,32,128]{2,1,0:T(8,128)S(1)}) custom-call(f32[13,8,128]{2,1,0:T(8,128)S(1)} %get-tuple-element.23.one_ref.own_ref.refs_0_, f32[13,8,128]{2,1,0:T(8,128)S(1)} %get-tuple-element.24.sent0.refs_1_, f32[13,8,128]{2,1,0:T(8,128)S(1)} %get-tuple-element.25.sent1.refs_2_, ...), custom_call_target="tpu_custom_call" | custom-call | tf_op jit(solution)/shard_map/pallas_call | solution.py:245
  16.7 0.0 collective-permute-done.6.other_ref
  16.7 0.6 %shard_map.102 = (f32[3,32,128]{2,1,0:T(8,128)}, f32[3,16,128]{2,1,0:T(8,128)}, f32[16,128]{1,0:T(8,128)}) custom-call(f32[3,32,128]{2,1,0:T(8,128)S(1)} %get-tuple-element.37.garm_ref, f32[3,16,128]{2,1,0:T(8,128)S(1)} %get-tuple-element.38.body_ref, f32[16,128]{1,0:T(8,128)S(1)} %get-tuple-element.39.mine_ref, f32[16,128]{1,0:T(8,128)S(1)} %collective-permute-done.6.other_ref), custom_call_target="tpu_custom_call" | custom-call | tf_op jit(solution)/shard_map/pallas_call | solution.py:245
  (3 shorter events, 0.0 us)
Async XLA Ops:
  1.6 8.3 %collective-permute-start = (f32[13,8,128]{2,1,0:T(8,128)S(1)}, f32[13,8,128]{2,1,0:T(8,128)S(1)}, u32[]{:S(2)}, u32[]{:S(2)}) collective-permute-start(f32[13,8,128]{2,1,0:T(8,128)S(1)} %get-tuple-element.25.sent1.refs_2_), channel_id=1, source_target_pairs={{0,8},{8,4},{4,12},{12,0},{1,9},{9,5},{5,13},{13,1},{2,10},{10,6},... | collective-permute-start | bytes 159752 | tf_op jit(solution)/shard_map/ppermute | solution.py:544
  5.7 5.2 %collective-permute-start.2 = (f32[13,8,128]{2,1,0:T(8,128)S(1)}, f32[13,8,128]{2,1,0:T(8,128)S(1)}, u32[]{:S(2)}, u32[]{:S(2)}) collective-permute-start(f32[13,8,128]{2,1,0:T(8,128)S(1)} %get-tuple-element.24.sent0.refs_1_), channel_id=1, source_target_pairs={{8,0},{4,8},{12,4},{0,12},{9,1},{5,9},{13,5},{1,13},{10,2},{6,10},... | collective-permute-start | bytes 159752 | tf_op jit(solution)/shard_map/ppermute | solution.py:544
  6.8 5.7 %collective-permute-start.5 = (f32[11,8,128]{2,1,0:T(8,128)S(1)}, f32[11,8,128]{2,1,0:T(8,128)S(1)}, u32[]{:S(2)}, u32[]{:S(2)}) collective-permute-start(f32[11,8,128]{2,1,0:T(8,128)S(1)} %get-tuple-element.28), channel_id=1, source_target_pairs={{0,4},{4,0},{8,12},{12,8},{1,5},{5,1},{9,13},{13,9},{2,6},{6,2},{1... | collective-permute-start | bytes 135176 | tf_op jit(solution)/shard_map/ppermute | solution.py:544
  7.3 7.6 %collective-permute-start.4 = (f32[11,8,128]{2,1,0:T(8,128)S(1)}, f32[11,8,128]{2,1,0:T(8,128)S(1)}, u32[]{:S(2)}, u32[]{:S(2)}) collective-permute-start(f32[11,8,128]{2,1,0:T(8,128)S(1)} %get-tuple-element.27), channel_id=1, source_target_pairs={{0,6},{2,4},{4,2},{6,0},{8,14},{10,12},{12,10},{14,8},{1,7},{3,5},... | collective-permute-start | bytes 135176 | tf_op jit(solution)/shard_map/ppermute | solution.py:555
  9.9 4.6 %collective-permute-start.1 = (f32[21,8,128]{2,1,0:T(8,128)S(1)}, f32[21,8,128]{2,1,0:T(8,128)S(1)}, u32[]{:S(2)}, u32[]{:S(2)}) collective-permute-start(f32[21,8,128]{2,1,0:T(8,128)S(1)} %shard_map.95.after_ref), channel_id=1, source_target_pairs={{0,2},{2,0},{1,3},{3,1},{4,6},{6,4},{5,7},{7,5},{8,10},{10,8},{9,1... | collective-permute-start | bytes 258056 | tf_op jit(solution)/shard_map/ppermute | solution.py:547
  10.9 4.1 %collective-permute-start.3 = (f32[11,8,128]{2,1,0:T(8,128)S(1)}, f32[11,8,128]{2,1,0:T(8,128)S(1)}, u32[]{:S(2)}, u32[]{:S(2)}) collective-permute-start(f32[11,8,128]{2,1,0:T(8,128)S(1)} %shard_map.96.after_ref), channel_id=1, source_target_pairs={{0,2},{2,0},{1,3},{3,1},{4,6},{6,4},{5,7},{7,5},{8,10},{10,8},{9,1... | collective-permute-start | bytes 135176 | tf_op jit(solution)/shard_map/ppermute | solution.py:547
  15.4 1.3 %collective-permute-start.6 = (f32[16,128]{1,0:T(8,128)S(1)}, f32[16,128]{1,0:T(8,128)S(1)}, u32[]{:S(2)}, u32[]{:S(2)}) collective-permute-start(f32[16,128]{1,0:T(8,128)S(1)} %get-tuple-element.39.mine_ref), channel_id=1, source_target_pairs={{0,1},{1,0},{2,3},{3,2},{4,5},{5,4},{6,7},{7,6},{8,9},{9,8},{10,11... | collective-permute-start | bytes 24584 | tf_op jit(solution)/shard_map/ppermute | solution.py:581
